TPU v7x, 32 devices: a whole 2x2x4 slice. The times are simulated.
32 devices in a mesh: groups: 2 (over x), ab: 8 (over z, y), cd: 2 (over core).
Axes of the slice: x: 2, y: 2, z: 4, core: 2. Of those that a mesh axis runs over, the one named last changes fastest.
Arguments:
- amplitudes: float32 [4, 128, 4096], P('groups', 'ab', 'cd'), parts along dimension 0, may hold values from -6 to 6
- integrals: float32 [16384, 4096], P(('groups', 'ab'), 'cd'), parts along dimension 0, may hold values from -0.21875 to 0.21875
- ab_irrep: int32 [128], P(('groups', 'ab')), parts along dimension 0, may hold values from 0 to 7
- cd_irrep: int32 [64], P(('groups', 'cd')), parts along dimension 0, may hold values from 0 to 7
- block_pattern: int32 [128, 32], P(('groups', 'ab'), 'cd'), parts along dimension 0, may hold values 0 or 1
Outputs:
- residual: float32 [4, 128, 8192], P('groups', 'cd', 'ab'), parts along dimension 0
There are 2 independent parts, one for each index of `groups`. A program takes and returns all parts, laid end to end along the dimension named above; each array names one. Nothing has to cross between parts.
All inputs are finite; a program needn't handle non-finite values. No bound on the sum of `block_pattern` on one device may be relied on, other than what follows from the above.
Results may differ from a plain program's by a relative error of at most 0.000071.
Values sent between devices are 32-bit elements; how exact they have to be, the bound alone decides.
No kernel may reach another device: no remote copies, remote signals or barrier semaphores. Data moves between devices by JAX's collectives and lax.ppermute only.
A program may use at most 128 MiB of HBM per device.

v0:
```python
import functools

import jax
import jax.numpy as jnp
from jax import lax
from jax.experimental import pallas as pl
from jax.experimental.pallas import tpu as pltpu
from jax.sharding import PartitionSpec as P

TILE = 128
UNROLL = 4
FLIGHT = 32
GROUP = 12
STEP_FLOPS = 1 << 30
VMEM_LIMIT = 12 * 2**20


def grid_of(count):
    bits = count.bit_length() - 1
    if count != 1 << bits or bits < 2:
        return count, 1
    rows = 1 << ((bits + 1) // 2)
    return rows, count // rows


def at_ring(place, rows, columns):
    if columns == 1:
        return place
    wide = columns - 1
    beyond = place - rows
    line = beyond // wide
    step = beyond - line * wide
    even = (line % 2) == 0
    if isinstance(place, int):
        back = (rows - 1 - line) * columns + (1 + step if even else columns - 1 - step)
        return place * columns if place < rows else back
    back = (rows - 1 - line) * columns + jnp.where(even, 1 + step, columns - 1 - step)
    return jnp.where(place < rows, place * columns, back)


def ring_of(index, rows, columns):
    if columns == 1:
        return index
    wide = columns - 1
    row = index // columns
    column = index - row * columns
    line = rows - 1 - row
    step = jnp.where((line % 2) == 0, column - 1, columns - 1 - column)
    return jnp.where(column == 0, row, rows + line * wide + step)


def place_of(count, rows, offset):
    grid = grid_of(count)
    here = ring_of(lax.axis_index("ab"), *grid)
    whole = rows * count
    start = at_ring((here + offset + count) % count, *grid) * rows + lax.axis_index("cd") * (whole // 2)
    return jnp.where(start >= whole, start - whole, start)


def cut_kernel(amplitudes, *refs):
    spans, sems = refs[:-1], refs[-1]
    copies = [pltpu.make_async_copy(amplitudes.at[pl.ds(at, 1)], span, sems.at[at]) for at, span in enumerate(spans)]
    for copy in copies:
        copy.start()
    for copy in copies:
        copy.wait()


def pick_kernel(ab_tiles, cd_tiles, pattern, ab_irrep, cd_irrep, integrals, listed, split, landed, sems):
    second = 1 + ab_tiles * cd_tiles + UNROLL

    def fetch(k):
        slot = k % FLIGHT
        return pltpu.make_async_copy(
            integrals.at[pl.ds(pl.multiple_of(listed[1 + k], TILE), TILE), pl.ds(pl.multiple_of(listed[second + k], TILE), TILE)],
            landed.at[slot],
            sems.at[slot],
        )

    def begin(k, carry):
        fetch(k).start()
        return carry

    def row(p, found):
        label = ab_irrep[p]
        before = found
        for q in range(cd_tiles):
            listed[1 + found] = p * TILE
            listed[second + found] = q * TILE
            keep = jnp.logical_and(pattern[p, q] == 1, label == cd_irrep[q])
            found = found + keep.astype(jnp.int32)
        lax.fori_loop(jnp.minimum(before, FLIGHT), jnp.minimum(found, FLIGHT), begin, 0)
        return found

    found = lax.fori_loop(0, ab_tiles, row, jnp.int32(0))
    rounds = (found + UNROLL - 1) // UNROLL
    listed[0] = rounds
    for extra in range(UNROLL):
        listed[1 + found + extra] = 0
        listed[second + found + extra] = 0
    lax.fori_loop(jnp.minimum(found, FLIGHT), jnp.minimum(rounds * UNROLL, FLIGHT), begin, 0)

    def part(round_at, carry):
        first = round_at * UNROLL
        for unrolled in range(UNROLL):
            fetch(first + unrolled).wait()
        for unrolled in range(UNROLL):
            k = first + unrolled
            tile = jnp.where(k < found, landed[k % FLIGHT], 0.0).T
            upper = tile.astype(jnp.bfloat16)
            split[k, :, :TILE] = upper
            split[k, :, TILE:] = (tile - upper.astype(jnp.float32)).astype(jnp.bfloat16)
        lax.fori_loop(
            jnp.minimum(first + FLIGHT, rounds * UNROLL), jnp.minimum(first + UNROLL + FLIGHT, rounds * UNROLL), begin, 0
        )
        return carry

    lax.fori_loop(0, rounds, part, 0)


def products(tiles, listed, split, pieces, total):
    total[...] = jnp.zeros_like(total)

    def step(round_at, carry):
        sums = []
        for unrolled in range(UNROLL):
            k = round_at * UNROLL + unrolled
            columns = pl.ds(pl.multiple_of(listed[1 + tiles + UNROLL + k], TILE), TILE)
            left = jnp.concatenate([piece[0, :, columns] for piece in pieces], axis=0)
            upper = left.astype(jnp.bfloat16)
            lower = (left - upper.astype(jnp.float32)).astype(jnp.bfloat16)
            both = jnp.dot(jnp.concatenate([upper, lower], axis=0), split[k], preferred_element_type=jnp.float32)
            high, low = both[: left.shape[0]], both[left.shape[0] :]
            sums.append((listed[1 + k], high[:, :TILE] + (high[:, TILE:] + (low[:, :TILE] + low[:, TILE:]))))
        for start, term in sums:
            total[:, pl.ds(pl.multiple_of(start, TILE), TILE)] += term
        return carry

    lax.fori_loop(0, listed[0], step, 0)


def step_kernel(count, rows, tiles, group, listed, split, *refs):
    pieces = refs[: len(group)]
    mine, send, total = refs[-3:]
    products(tiles, listed, split, pieces, total)
    half = rows * count // 2
    for at, (span, offset) in enumerate(group):
        place = place_of(count, rows, offset)
        block = total[at * rows : (at + 1) * rows, :]

        @pl.when(place < half)
        def _():
            mine[span, pl.ds(pl.multiple_of(place, rows), rows), :] = block

        @pl.when(place >= half)
        def _():
            send[span, pl.ds(pl.multiple_of(place - half, rows), rows), :] = block


def last_kernel(tiles, listed, split, *refs):
    products(tiles, listed, split, refs[:-1], refs[-1])


def merge_kernel(mine, received, out):
    out[...] = mine[...] + received[...]


def final_kernel(count, spans, rows, last, received, before, out, total, sems):
    del before
    place = place_of(count, rows, -(count // 2))

    @pl.when(place < rows * count // 2)
    def _():
        total[...] = last[...] + received[...]
        copies = []
        for span in range(spans):
            copies.append(
                pltpu.make_async_copy(
                    total.at[pl.ds(span * rows, rows), :],
                    out.at[span, pl.ds(pl.multiple_of(place, rows), rows), :],
                    sems.at[span],
                )
            )
            copies[-1].start()
        for copy in copies:
            copy.wait()


def solution(mesh):
    count = mesh.shape["ab"]
    grid = grid_of(count)
    far = count // 2
    ahead = [(at_ring(at, *grid), at_ring((at + 1) % count, *grid)) for at in range(count)]
    back = [(to, start) for start, to in ahead]
    swap = [(0, 1), (1, 0)]

    def shards(amplitudes, integrals, ab_irrep, cd_irrep, block_pattern):
        spans, rows, depth = amplitudes.shape
        slab = integrals.shape[0]
        ab_tiles, cd_tiles = block_pattern.shape
        tiles = ab_tiles * cd_tiles
        half = rows * far

        in_hbm = functools.partial(pltpu.with_memory_space_constraint, memory_space=pltpu.HBM)
        smem = pl.BlockSpec(memory_space=pltpu.SMEM)
        vmem = pl.BlockSpec(memory_space=pltpu.VMEM)
        hbm = pl.BlockSpec(memory_space=pltpu.HBM)
        params = pltpu.CompilerParams(vmem_limit_bytes=VMEM_LIMIT)
        piece = pltpu.VMEM((1, rows, depth), jnp.float32)

        own = pl.pallas_call(
            cut_kernel,
            out_shape=(piece,) * spans,
            in_specs=[hbm],
            out_specs=(vmem,) * spans,
            scratch_shapes=[pltpu.SemaphoreType.DMA((spans,))],
            compiler_params=params,
            name="cut",
        )(in_hbm(amplitudes))

        listed, split = pl.pallas_call(
            functools.partial(pick_kernel, ab_tiles, cd_tiles),
            out_shape=(
                jax.ShapeDtypeStruct((1 + 2 * (tiles + UNROLL),), jnp.int32),
                pltpu.VMEM((tiles + UNROLL, TILE, 2 * TILE), jnp.bfloat16),
            ),
            in_specs=[smem, smem, smem, hbm],
            out_specs=(smem, vmem),
            scratch_shapes=[
                pltpu.VMEM((FLIGHT, TILE, TILE), jnp.float32),
                pltpu.SemaphoreType.DMA((FLIGHT,)),
            ],
            compiler_params=params,
            cost_estimate=pl.CostEstimate(flops=0, bytes_accessed=8 << 20, transcendentals=0),
            name="pick",
        )(in_hbm(block_pattern), in_hbm(ab_irrep), in_hbm(cd_irrep), in_hbm(integrals))

        held = {}
        for span in range(spans):
            held[span, 0] = own[span]
            for pairs, sign in ((ahead, -1), (back, 1)):
                moved = own[span]
                for hop in range(1, far + 1 if (sign < 0) == (span % 2 == 0) else far):
                    if hop == 2:
                        moved, _ = lax.optimization_barrier((moved, listed))
                    moved = lax.ppermute(moved, "ab", pairs)
                    held[span, -far if hop == far else sign * hop] = moved

        def offset_of(span, hop, long):
            return -hop if (span % 2 == 0) == long else hop

        arrivals = [(span, 0) for span in range(spans)]
        for hop in range(1, far):
            arrivals += [(span, offset_of(span, hop, long)) for long in (True, False) for span in range(spans)]
        block = pltpu.VMEM((spans, half, slab), jnp.float32)
        parts = ()
        cuts = sorted({*range(0, len(arrivals) - spans, GROUP), len(arrivals) - spans, len(arrivals)})
        for start, stop in zip(cuts, cuts[1:]):
            group = arrivals[start:stop]
            pieces = [held[key] for key in group]
            parts = pl.pallas_call(
                functools.partial(step_kernel, count, rows, tiles, group),
                out_shape=(block, block),
                in_specs=[smem] + [vmem] * (1 + len(pieces) + len(parts)),
                out_specs=(vmem, vmem),
                scratch_shapes=[pltpu.VMEM((len(pieces) * rows, slab), jnp.float32)],
                compiler_params=params,
                input_output_aliases={2 + len(pieces): 0, 3 + len(pieces): 1} if parts else {},
                cost_estimate=pl.CostEstimate(flops=STEP_FLOPS, bytes_accessed=4 << 20, transcendentals=0),
                name="step",
            )(listed, split, *pieces, *parts)
        mine, send = parts
        base = pl.pallas_call(
            merge_kernel,
            out_shape=pltpu.HBM((spans, half, slab), jnp.float32),
            in_specs=[vmem, vmem],
            out_specs=vmem,
            compiler_params=params,
            name="merge",
        )(mine, lax.ppermute(send, "cd", swap))

        last = pl.pallas_call(
            functools.partial(last_kernel, tiles),
            out_shape=pltpu.VMEM((spans * rows, slab), jnp.float32),
            in_specs=[smem, vmem] + [vmem] * spans,
            out_specs=vmem,
            compiler_params=params,
            cost_estimate=pl.CostEstimate(flops=1 << 34, bytes_accessed=4 << 20, transcendentals=0),
            name="last",
        )(listed, split, *[held[span, -far] for span in range(spans)])
        return pl.pallas_call(
            functools.partial(final_kernel, count, spans, rows),
            out_shape=pltpu.HBM((spans, half, slab), jnp.float32),
            in_specs=[vmem, vmem, hbm],
            out_specs=hbm,
            scratch_shapes=[pltpu.VMEM((spans * rows, slab), jnp.float32), pltpu.SemaphoreType.DMA((spans,))],
            compiler_params=params,
            input_output_aliases={2: 0},
            name="final",
        )(last, lax.ppermute(last, "cd", swap), base)

    in_specs = (
        P("groups", "ab", "cd"),
        P(("groups", "ab"), "cd"),
        P(("groups", "ab")),
        P(("groups", "cd")),
        P(("groups", "ab"), "cd"),
    )
    out_specs = P("groups", "cd", "ab")
    return jax.shard_map(shards, mesh=mesh, in_specs=in_specs, out_specs=out_specs, check_vma=False)
```

profile of v0, /device:TPU:1, one launch (start us, length us, event | category | flops | bytes accessed | tf_op | source)
XLA Modules:
  0.0 31.8 jit_solution(15997366955191729915)
XLA Ops:
  0.0 1.0 %cut.1 = (f32[1,16,2048]{2,1,0:T(8,128)S(1)}, f32[1,16,2048]{2,1,0:T(8,128)S(1)}) custom-call(f32[2,16,2048]{2,1,0:T(8,128)} %amplitudes.1), custom_call_target="tpu_custom_call" | custom-call | tf_op jit(solution)/shard_map/cut/pallas_call | solution.py:211
  1.0 2.2 %collective-permute-start = (f32[1,16,2048]{2,1,0:T(8,128)S(1)}, f32[1,16,2048]{2,1,0:T(8,128)S(1)}, u32[]{:S(2)}, u32[]{:S(2)}) collective-permute-start(f32[1,16,2048]{2,1,0:T(8,128)S(1)} %get-tuple-element.19.refs_0_), channel_id=1, source_target_pairs={{0,4},{4,8},{8,12},{12,14},{14,10},{10,6},{6,2},{2,0},{1,5},{5,9},... | collective-permute-start | bytes 393224 | tf_op jit(solution)/shard_map/ppermute | solution.py:246
  3.2 0.0 collective-permute-start.4
  3.2 1.4 %collective-permute-start.9 = (f32[1,16,2048]{2,1,0:T(8,128)S(1)}, f32[1,16,2048]{2,1,0:T(8,128)S(1)}, u32[]{:S(2)}, u32[]{:S(2)}) collective-permute-start(f32[1,16,2048]{2,1,0:T(8,128)S(1)} %get-tuple-element.19.refs_0_), channel_id=1, source_target_pairs={{4,0},{8,4},{12,8},{14,12},{10,14},{6,10},{2,6},{0,2},{5,1},{9,5},... | collective-permute-start | bytes 393224 | tf_op jit(solution)/shard_map/ppermute | solution.py:246
  4.6 0.1 collective-permute-start.12
  4.7 3.5 %pick.1 = (s32[265]{0:T(512)S(1)}, bf16[132,128,256]{2,1,0:T(8,128)(2,1)S(1)}) custom-call(s32[8,16]{1,0:T(8,128)} %pattern.1, s32[8]{0:T(128)} %ab_irrep.1, s32[16]{0:T(128)} %cd_irrep.1, f32[1024,2048]{1,0:T(8,128)} %integrals.1), custom_call_target="tpu_custom_call" | custom-call | bytes 8388608 | tf_op jit(solution)/shard_map/pick/pallas_call | solution.py:221
  8.2 0.0 collective-permute-done.refs_2_
  8.2 1.5 %collective-permute-start.1 = (f32[1,16,2048]{2,1,0:T(8,128)S(1)}, f32[1,16,2048]{2,1,0:T(8,128)S(1)}, u32[]{:S(2)}, u32[]{:S(2)}) collective-permute-start(f32[1,16,2048]{2,1,0:T(8,128)S(1)} %collective-permute-done.refs_2_), channel_id=1, source_target_pairs={{0,4},{4,8},{8,12},{12,14},{14,10},{10,6},{6,2},{2,0},{1,5},{5,9},... | collective-permute-start | bytes 393224 | tf_op jit(solution)/shard_map/ppermute | solution.py:246
  9.7 0.0 collective-permute-done.4.refs_3_
  9.7 0.0 collective-permute-start.5
  9.7 0.3 %collective-permute-done.9.refs_4_ = f32[1,16,2048]{2,1,0:T(8,128)S(1)} collective-permute-done((f32[1,16,2048]{2,1,0:T(8,128)S(1)}, f32[1,16,2048]{2,1,0:T(8,128)S(1)}, u32[]{:S(2)}, u32[]{:S(2)}) %collective-permute-start.9) | collective-permute-done | bytes 131104 | tf_op jit(solution)/shard_map/ppermute | solution.py:246
  10.0 1.0 %collective-permute-start.10 = (f32[1,16,2048]{2,1,0:T(8,128)S(1)}, f32[1,16,2048]{2,1,0:T(8,128)S(1)}, u32[]{:S(2)}, u32[]{:S(2)}) collective-permute-start(f32[1,16,2048]{2,1,0:T(8,128)S(1)} %collective-permute-done.9.refs_4_), channel_id=1, source_target_pairs={{4,0},{8,4},{12,8},{14,12},{10,14},{6,10},{2,6},{0,2},{5,1},{9,5},... | collective-permute-start | bytes 393224 | tf_op jit(solution)/shard_map/ppermute | solution.py:246
  11.0 0.0 collective-permute-done.12.refs_5_
  11.0 0.5 %collective-permute-start.13 = (f32[1,16,2048]{2,1,0:T(8,128)S(1)}, f32[1,16,2048]{2,1,0:T(8,128)S(1)}, u32[]{:S(2)}, u32[]{:S(2)}) collective-permute-start(f32[1,16,2048]{2,1,0:T(8,128)S(1)} %collective-permute-done.12.refs_5_), channel_id=1, source_target_pairs={{0,4},{4,8},{8,12},{12,14},{14,10},{10,6},{6,2},{2,0},{1,5},{5,9},... | collective-permute-start | bytes 393224 | tf_op jit(solution)/shard_map/ppermute | solution.py:246
  11.5 0.5 %collective-permute-done.1.refs_6_ = f32[1,16,2048]{2,1,0:T(8,128)S(1)} collective-permute-done((f32[1,16,2048]{2,1,0:T(8,128)S(1)}, f32[1,16,2048]{2,1,0:T(8,128)S(1)}, u32[]{:S(2)}, u32[]{:S(2)}) %collective-permute-start.1) | collective-permute-done | bytes 131104 | tf_op jit(solution)/shard_map/ppermute | solution.py:246
  12.0 1.4 %collective-permute-start.2 = (f32[1,16,2048]{2,1,0:T(8,128)S(1)}, f32[1,16,2048]{2,1,0:T(8,128)S(1)}, u32[]{:S(2)}, u32[]{:S(2)}) collective-permute-start(f32[1,16,2048]{2,1,0:T(8,128)S(1)} %collective-permute-done.1.refs_6_), channel_id=1, source_target_pairs={{0,4},{4,8},{8,12},{12,14},{14,10},{10,6},{6,2},{2,0},{1,5},{5,9},... | collective-permute-start | bytes 393224 | tf_op jit(solution)/shard_map/ppermute | solution.py:246
  13.5 0.3 collective-permute-done.5.refs_7_
  13.8 0.0 collective-permute-start.6
  13.8 1.5 %collective-permute-done.10.refs_8_ = f32[1,16,2048]{2,1,0:T(8,128)S(1)} collective-permute-done((f32[1,16,2048]{2,1,0:T(8,128)S(1)}, f32[1,16,2048]{2,1,0:T(8,128)S(1)}, u32[]{:S(2)}, u32[]{:S(2)}) %collective-permute-start.10) | collective-permute-done | bytes 131104 | tf_op jit(solution)/shard_map/ppermute | solution.py:246
  15.3 0.3 collective-permute-start.11
  15.6 0.1 collective-permute-done.13.refs_9_
  15.8 1.0 %collective-permute-start.14 = (f32[1,16,2048]{2,1,0:T(8,128)S(1)}, f32[1,16,2048]{2,1,0:T(8,128)S(1)}, u32[]{:S(2)}, u32[]{:S(2)}) collective-permute-start(f32[1,16,2048]{2,1,0:T(8,128)S(1)} %collective-permute-done.13.refs_9_), channel_id=1, source_target_pairs={{0,4},{4,8},{8,12},{12,14},{14,10},{10,6},{6,2},{2,0},{1,5},{5,9},... | collective-permute-start | bytes 393224 | tf_op jit(solution)/shard_map/ppermute | solution.py:246
  16.8 0.6 %collective-permute-done.2.refs_10_ = f32[1,16,2048]{2,1,0:T(8,128)S(1)} collective-permute-done((f32[1,16,2048]{2,1,0:T(8,128)S(1)}, f32[1,16,2048]{2,1,0:T(8,128)S(1)}, u32[]{:S(2)}, u32[]{:S(2)}) %collective-permute-start.2) | collective-permute-done | bytes 131104 | tf_op jit(solution)/shard_map/ppermute | solution.py:246
  17.4 2.0 %collective-permute-start.3 = (f32[1,16,2048]{2,1,0:T(8,128)S(1)}, f32[1,16,2048]{2,1,0:T(8,128)S(1)}, u32[]{:S(2)}, u32[]{:S(2)}) collective-permute-start(f32[1,16,2048]{2,1,0:T(8,128)S(1)} %collective-permute-done.2.refs_10_), channel_id=1, source_target_pairs={{0,4},{4,8},{8,12},{12,14},{14,10},{10,6},{6,2},{2,0},{1,5},{5,9},... | collective-permute-start | bytes 393224 | tf_op jit(solution)/shard_map/ppermute | solution.py:246
  19.4 0.0 collective-permute-done.6.refs_11_
  19.4 0.0 collective-permute-start.7
  19.4 2.0 %step.2 = (f32[2,64,1024]{2,1,0:T(8,128)S(1)}, f32[2,64,1024]{2,1,0:T(8,128)S(1)}) custom-call(s32[265]{0:T(512)S(1)} %get-tuple-element.17.listed, bf16[132,128,256]{2,1,0:T(8,128)(2,1)S(1)} %get-tuple-element.18.split, f32[1,16,2048]{2,1,0:T(8,128)S(1)} %get-tuple-element.19.refs_0_, f32[1,16,2048]{2,1,0:T(8,128)S(1)} %get-tuple-element.21.refs_1_, ...), custom_call_target="tpu_custom_call" | custom-call | flops 1073741824 | bytes 4194304 | tf_op jit(solution)/shard_map/step/pallas_call | solution.py:261
  21.4 0.0 collective-permute-done.11.refs_0_
  21.4 0.0 collective-permute-done.14.refs_1_
  21.4 1.2 %step.3 = (f32[2,64,1024]{2,1,0:T(8,128)S(1)}, f32[2,64,1024]{2,1,0:T(8,128)S(1)}) custom-call(s32[265]{0:T(512)S(1)} %get-tuple-element.17.listed, bf16[132,128,256]{2,1,0:T(8,128)(2,1)S(1)} %get-tuple-element.18.split, f32[1,16,2048]{2,1,0:T(8,128)S(1)} %collective-permute-done.11.refs_0_, ...), custom_call_target="tpu_custom_call", output_to_operand_aliasing={{0}: (4, {}), {1}: (5, {})} | custom-call | flops 1073741824 | bytes 4194304 | tf_op jit(solution)/shard_map/step/pallas_call | solution.py:261
  22.6 5.2 %collective-permute-start.15 = (f32[2,64,1024]{2,1,0:T(8,128)S(1)}, f32[2,64,1024]{2,1,0:T(8,128)S(1)}, u32[]{:S(2)}, u32[]{:S(2)}) collective-permute-start(f32[2,64,1024]{2,1,0:T(8,128)S(1)} %get-tuple-element.28), channel_id=1, source_target_pairs={{0,1},{1,0},{2,3},{3,2},{4,5},{5,4},{6,7},{7,6},{8,9},{9,8},{10,11... | collective-permute-start | bytes 1572872 | tf_op jit(solution)/shard_map/ppermute | solution.py:280
  27.8 0.0 collective-permute-done.3.refs_0_
  27.9 0.0 collective-permute-done.7.refs_1_
  27.9 1.1 %last.1 = f32[32,1024]{1,0:T(8,128)S(1)} custom-call(s32[265]{0:T(512)S(1)} %get-tuple-element.17.listed, bf16[132,128,256]{2,1,0:T(8,128)(2,1)S(1)} %get-tuple-element.18.split, f32[1,16,2048]{2,1,0:T(8,128)S(1)} %collective-permute-done.3.refs_0_, f32[1,16,2048]{2,1,0:T(8,128)S(1)} %collective-permute-done.7.refs_1_), custom_call_target="tpu_custom_call" | custom-call | flops 17179869184 | bytes 4194304 | tf_op jit(solution)/shard_map/last/pallas_call | solution.py:282
  29.0 1.2 %collective-permute-start.8 = (f32[32,1024]{1,0:T(8,128)S(1)}, f32[32,1024]{1,0:T(8,128)S(1)}, u32[]{:S(2)}, u32[]{:S(2)}) collective-permute-start(f32[32,1024]{1,0:T(8,128)S(1)} %last.1), channel_id=1, source_target_pairs={{0,1},{1,0},{2,3},{3,2},{4,5},{5,4},{6,7},{7,6},{8,9},{9,8},{10,11... | collective-permute-start | bytes 393224 | tf_op jit(solution)/shard_map/ppermute | solution.py:300
  30.2 0.0 collective-permute-done.15.received
  30.2 0.8 %merge.1.before = f32[2,64,1024]{2,1,0:T(8,128)} custom-call(f32[2,64,1024]{2,1,0:T(8,128)S(1)} %get-tuple-element.27.mine, f32[2,64,1024]{2,1,0:T(8,128)S(1)} %collective-permute-done.15.received), custom_call_target="tpu_custom_call" | custom-call | tf_op jit(solution)/shard_map/merge/pallas_call | solution.py:273
  31.0 0.1 collective-permute-done.8.received
  31.1 0.7 %final.1 = f32[2,64,1024]{2,1,0:T(8,128)} custom-call(f32[32,1024]{1,0:T(8,128)S(1)} %last.1, f32[32,1024]{1,0:T(8,128)S(1)} %collective-permute-done.8.received, f32[2,64,1024]{2,1,0:T(8,128)} %merge.1.before), custom_call_target="tpu_custom_call", output_to_operand_aliasing={{}: (2, {})} | custom-call | tf_op jit(solution)/shard_map/final/pallas_call | solution.py:291
Async XLA Ops:
  1.0 7.2 %collective-permute-start = (f32[1,16,2048]{2,1,0:T(8,128)S(1)}, f32[1,16,2048]{2,1,0:T(8,128)S(1)}, u32[]{:S(2)}, u32[]{:S(2)}) collective-permute-start(f32[1,16,2048]{2,1,0:T(8,128)S(1)} %get-tuple-element.19.refs_0_), channel_id=1, source_target_pairs={{0,4},{4,8},{8,12},{12,14},{14,10},{10,6},{6,2},{2,0},{1,5},{5,9},... | collective-permute-start | bytes 393224 | tf_op jit(solution)/shard_map/ppermute | solution.py:246
  3.2 6.5 %collective-permute-start.4 = (f32[1,16,2048]{2,1,0:T(8,128)S(1)}, f32[1,16,2048]{2,1,0:T(8,128)S(1)}, u32[]{:S(2)}, u32[]{:S(2)}) collective-permute-start(f32[1,16,2048]{2,1,0:T(8,128)S(1)} %get-tuple-element.21.refs_1_), channel_id=1, source_target_pairs={{4,0},{8,4},{12,8},{14,12},{10,14},{6,10},{2,6},{0,2},{5,1},{9,5},... | collective-permute-start | bytes 393224 | tf_op jit(solution)/shard_map/ppermute | solution.py:246
  3.2 6.8 %collective-permute-start.9 = (f32[1,16,2048]{2,1,0:T(8,128)S(1)}, f32[1,16,2048]{2,1,0:T(8,128)S(1)}, u32[]{:S(2)}, u32[]{:S(2)}) collective-permute-start(f32[1,16,2048]{2,1,0:T(8,128)S(1)} %get-tuple-element.19.refs_0_), channel_id=1, source_target_pairs={{4,0},{8,4},{12,8},{14,12},{10,14},{6,10},{2,6},{0,2},{5,1},{9,5},... | collective-permute-start | bytes 393224 | tf_op jit(solution)/shard_map/ppermute | solution.py:246
  4.6 6.4 %collective-permute-start.12 = (f32[1,16,2048]{2,1,0:T(8,128)S(1)}, f32[1,16,2048]{2,1,0:T(8,128)S(1)}, u32[]{:S(2)}, u32[]{:S(2)}) collective-permute-start(f32[1,16,2048]{2,1,0:T(8,128)S(1)} %get-tuple-element.21.refs_1_), channel_id=1, source_target_pairs={{0,4},{4,8},{8,12},{12,14},{14,10},{10,6},{6,2},{2,0},{1,5},{5,9},... | collective-permute-start | bytes 393224 | tf_op jit(solution)/shard_map/ppermute | solution.py:246
  8.2 3.9 %collective-permute-start.1 = (f32[1,16,2048]{2,1,0:T(8,128)S(1)}, f32[1,16,2048]{2,1,0:T(8,128)S(1)}, u32[]{:S(2)}, u32[]{:S(2)}) collective-permute-start(f32[1,16,2048]{2,1,0:T(8,128)S(1)} %collective-permute-done.refs_2_), channel_id=1, source_target_pairs={{0,4},{4,8},{8,12},{12,14},{14,10},{10,6},{6,2},{2,0},{1,5},{5,9},... | collective-permute-start | bytes 393224 | tf_op jit(solution)/shard_map/ppermute | solution.py:246
  9.7 4.1 %collective-permute-start.5 = (f32[1,16,2048]{2,1,0:T(8,128)S(1)}, f32[1,16,2048]{2,1,0:T(8,128)S(1)}, u32[]{:S(2)}, u32[]{:S(2)}) collective-permute-start(f32[1,16,2048]{2,1,0:T(8,128)S(1)} %collective-permute-done.4.refs_3_), channel_id=1, source_target_pairs={{4,0},{8,4},{12,8},{14,12},{10,14},{6,10},{2,6},{0,2},{5,1},{9,5},... | collective-permute-start | bytes 393224 | tf_op jit(solution)/shard_map/ppermute | solution.py:246
  10.0 5.3 %collective-permute-start.10 = (f32[1,16,2048]{2,1,0:T(8,128)S(1)}, f32[1,16,2048]{2,1,0:T(8,128)S(1)}, u32[]{:S(2)}, u32[]{:S(2)}) collective-permute-start(f32[1,16,2048]{2,1,0:T(8,128)S(1)} %collective-permute-done.9.refs_4_), channel_id=1, source_target_pairs={{4,0},{8,4},{12,8},{14,12},{10,14},{6,10},{2,6},{0,2},{5,1},{9,5},... | collective-permute-start | bytes 393224 | tf_op jit(solution)/shard_map/ppermute | solution.py:246
  11.0 4.8 %collective-permute-start.13 = (f32[1,16,2048]{2,1,0:T(8,128)S(1)}, f32[1,16,2048]{2,1,0:T(8,128)S(1)}, u32[]{:S(2)}, u32[]{:S(2)}) collective-permute-start(f32[1,16,2048]{2,1,0:T(8,128)S(1)} %collective-permute-done.12.refs_5_), channel_id=1, source_target_pairs={{0,4},{4,8},{8,12},{12,14},{14,10},{10,6},{6,2},{2,0},{1,5},{5,9},... | collective-permute-start | bytes 393224 | tf_op jit(solution)/shard_map/ppermute | solution.py:246
  12.0 5.4 %collective-permute-start.2 = (f32[1,16,2048]{2,1,0:T(8,128)S(1)}, f32[1,16,2048]{2,1,0:T(8,128)S(1)}, u32[]{:S(2)}, u32[]{:S(2)}) collective-permute-start(f32[1,16,2048]{2,1,0:T(8,128)S(1)} %collective-permute-done.1.refs_6_), channel_id=1, source_target_pairs={{0,4},{4,8},{8,12},{12,14},{14,10},{10,6},{6,2},{2,0},{1,5},{5,9},... | collective-permute-start | bytes 393224 | tf_op jit(solution)/shard_map/ppermute | solution.py:246
  13.8 5.6 %collective-permute-start.6 = (f32[1,16,2048]{2,1,0:T(8,128)S(1)}, f32[1,16,2048]{2,1,0:T(8,128)S(1)}, u32[]{:S(2)}, u32[]{:S(2)}) collective-permute-start(f32[1,16,2048]{2,1,0:T(8,128)S(1)} %collective-permute-done.5.refs_7_), channel_id=1, source_target_pairs={{4,0},{8,4},{12,8},{14,12},{10,14},{6,10},{2,6},{0,2},{5,1},{9,5},... | collective-permute-start | bytes 393224 | tf_op jit(solution)/shard_map/ppermute | solution.py:246
  15.3 6.1 %collective-permute-start.11 = (f32[1,16,2048]{2,1,0:T(8,128)S(1)}, f32[1,16,2048]{2,1,0:T(8,128)S(1)}, u32[]{:S(2)}, u32[]{:S(2)}) collective-permute-start(f32[1,16,2048]{2,1,0:T(8,128)S(1)} %collective-permute-done.10.refs_8_), channel_id=1, source_target_pairs={{4,0},{8,4},{12,8},{14,12},{10,14},{6,10},{2,6},{0,2},{5,1},{9,5},... | collective-permute-start | bytes 393224 | tf_op jit(solution)/shard_map/ppermute | solution.py:246
  15.8 5.6 %collective-permute-start.14 = (f32[1,16,2048]{2,1,0:T(8,128)S(1)}, f32[1,16,2048]{2,1,0:T(8,128)S(1)}, u32[]{:S(2)}, u32[]{:S(2)}) collective-permute-start(f32[1,16,2048]{2,1,0:T(8,128)S(1)} %collective-permute-done.13.refs_9_), channel_id=1, source_target_pairs={{0,4},{4,8},{8,12},{12,14},{14,10},{10,6},{6,2},{2,0},{1,5},{5,9},... | collective-permute-start | bytes 393224 | tf_op jit(solution)/shard_map/ppermute | solution.py:246
  17.4 10.4 %collective-permute-start.3 = (f32[1,16,2048]{2,1,0:T(8,128)S(1)}, f32[1,16,2048]{2,1,0:T(8,128)S(1)}, u32[]{:S(2)}, u32[]{:S(2)}) collective-permute-start(f32[1,16,2048]{2,1,0:T(8,128)S(1)} %collective-permute-done.2.refs_10_), channel_id=1, source_target_pairs={{0,4},{4,8},{8,12},{12,14},{14,10},{10,6},{6,2},{2,0},{1,5},{5,9},... | collective-permute-start | bytes 393224 | tf_op jit(solution)/shard_map/ppermute | solution.py:246
  19.4 8.4 %collective-permute-start.7 = (f32[1,16,2048]{2,1,0:T(8,128)S(1)}, f32[1,16,2048]{2,1,0:T(8,128)S(1)}, u32[]{:S(2)}, u32[]{:S(2)}) collective-permute-start(f32[1,16,2048]{2,1,0:T(8,128)S(1)} %collective-permute-done.6.refs_11_), channel_id=1, source_target_pairs={{4,0},{8,4},{12,8},{14,12},{10,14},{6,10},{2,6},{0,2},{5,1},{9,5},... | collective-permute-start | bytes 393224 | tf_op jit(solution)/shard_map/ppermute | solution.py:246
  22.6 7.5 %collective-permute-start.15 = (f32[2,64,1024]{2,1,0:T(8,128)S(1)}, f32[2,64,1024]{2,1,0:T(8,128)S(1)}, u32[]{:S(2)}, u32[]{:S(2)}) collective-permute-start(f32[2,64,1024]{2,1,0:T(8,128)S(1)} %get-tuple-element.28), channel_id=1, source_target_pairs={{0,1},{1,0},{2,3},{3,2},{4,5},{5,4},{6,7},{7,6},{8,9},{9,8},{10,11... | collective-permute-start | bytes 1572872 | tf_op jit(solution)/shard_map/ppermute | solution.py:280
  29.0 2.2 %collective-permute-start.8 = (f32[32,1024]{1,0:T(8,128)S(1)}, f32[32,1024]{1,0:T(8,128)S(1)}, u32[]{:S(2)}, u32[]{:S(2)}) collective-permute-start(f32[32,1024]{1,0:T(8,128)S(1)} %last.1), channel_id=1, source_target_pairs={{0,1},{1,0},{2,3},{3,2},{4,5},{5,4},{6,7},{7,6},{8,9},{9,8},{10,11... | collective-permute-start | bytes 393224 | tf_op jit(solution)/shard_map/ppermute | solution.py:300
where the time goes:
time: 32.1 us; the launch traced here: 31.8 us
  starting transfers between devices  17.8 us (55%)
  Pallas kernels  10.3 us (32%)
  waiting for transfers between devices  3.64 us (11%)
    ppermute x14, starting transfers between devices, shards(): moved = lax.ppermute(moved, 'ab', pairs)  11.4 us
    ppermute x1, starting transfers between devices, shards(): lax.ppermute(send, 'cd', swap)  5.23 us
    ppermute x14, waiting for transfers between devices, shards(): moved = lax.ppermute(moved, 'ab', pairs)  3.5 us
    pallas_call x1, Pallas kernels, shards(): pl.pallas_call(functools.partial(pick_kernel, ab_tiles, cd_tiles), out_sh...  3.47 us
    pallas_call x2, Pallas kernels, shards(): pl.pallas_call(functools.partial(step_kernel, count, rows, tiles, group),...  3.16 us
    ppermute x1, starting transfers between devices, shards(): lax.ppermute(last, 'cd', swap)  1.17 us
    pallas_call x1, Pallas kernels, shards(): pl.pallas_call(functools.partial(last_kernel, tiles), out_shape=pltpu.VME...  1.13 us
    pallas_call x1, Pallas kernels, shards(): pl.pallas_call(cut_kernel, out_shape=(piece,) * spans, in_specs=[hbm], ou...  0.98 us
  transfers between devices with their start and end apart: 16, of which 7 were waited for; matrix products, arithmetic and copies ran while one was open for 0% of the time, Pallas kernels for 27%

commit v1 on v0

--- a/solution.py
+++ b/solution.py
@@ -49,24 +49,24 @@
     return jnp.where(column == 0, row, rows + line * wide + step)
 
 
-def place_of(count, rows, offset):
+def place_of(count, rows, chain, hop):
     grid = grid_of(count)
     here = ring_of(lax.axis_index("ab"), *grid)
+    core = lax.axis_index("cd")
+    away = (2 * core - 1) * hop if chain == 0 else (1 - 2 * core) * hop
     whole = rows * count
-    start = at_ring((here + offset + count) % count, *grid) * rows + lax.axis_index("cd") * (whole // 2)
+    start = at_ring((here + away + count) % count, *grid) * rows + core * (whole // 2)
     return jnp.where(start >= whole, start - whole, start)
 
 
-def cut_kernel(amplitudes, *refs):
-    spans, sems = refs[:-1], refs[-1]
-    copies = [pltpu.make_async_copy(amplitudes.at[pl.ds(at, 1)], span, sems.at[at]) for at, span in enumerate(spans)]
-    for copy in copies:
-        copy.start()
-    for copy in copies:
-        copy.wait()
-
-
-def pick_kernel(ab_tiles, cd_tiles, pattern, ab_irrep, cd_irrep, integrals, listed, split, landed, sems):
+def cut_kernel(chunk, *spans):
+    for at, span in enumerate(spans):
+        span[0] = chunk[at]
+
+
+def pick_kernel(ab_tiles, cd_tiles, pattern, ab_irrep, cd_irrep, integrals, amplitudes, listed, split, own, landed, sems, own_sem):
+    copy = pltpu.make_async_copy(amplitudes, own, own_sem)
+    copy.start()
     second = 1 + ab_tiles * cd_tiles + UNROLL
 
     def fetch(k):
@@ -116,6 +116,7 @@
         return carry
 
     lax.fori_loop(0, rounds, part, 0)
+    copy.wait()
 
 
 def products(tiles, listed, split, pieces, total):
@@ -126,7 +127,7 @@
         for unrolled in range(UNROLL):
             k = round_at * UNROLL + unrolled
             columns = pl.ds(pl.multiple_of(listed[1 + tiles + UNROLL + k], TILE), TILE)
-            left = jnp.concatenate([piece[0, :, columns] for piece in pieces], axis=0)
+            left = jnp.concatenate([piece[span, :, columns] for piece in pieces for span in range(piece.shape[0])], axis=0)
             upper = left.astype(jnp.bfloat16)
             lower = (left - upper.astype(jnp.float32)).astype(jnp.bfloat16)
             both = jnp.dot(jnp.concatenate([upper, lower], axis=0), split[k], preferred_element_type=jnp.float32)
@@ -144,17 +145,20 @@
     mine, send, total = refs[-3:]
     products(tiles, listed, split, pieces, total)
     half = rows * count // 2
-    for at, (span, offset) in enumerate(group):
-        place = place_of(count, rows, offset)
-        block = total[at * rows : (at + 1) * rows, :]
-
-        @pl.when(place < half)
-        def _():
-            mine[span, pl.ds(pl.multiple_of(place, rows), rows), :] = block
-
-        @pl.when(place >= half)
-        def _():
-            send[span, pl.ds(pl.multiple_of(place - half, rows), rows), :] = block
+    at = 0
+    for chain, hop, spans in group:
+        place = place_of(count, rows, chain, hop)
+        for span in spans:
+            block = total[at * rows : (at + 1) * rows, :]
+            at += 1
+
+            @pl.when(place < half)
+            def _():
+                mine[span, pl.ds(pl.multiple_of(place, rows), rows), :] = block
+
+            @pl.when(place >= half)
+            def _():
+                send[span, pl.ds(pl.multiple_of(place - half, rows), rows), :] = block
 
 
 def last_kernel(tiles, listed, split, *refs):
@@ -167,7 +171,7 @@
 
 def final_kernel(count, spans, rows, last, received, before, out, total, sems):
     del before
-    place = place_of(count, rows, -(count // 2))
+    place = place_of(count, rows, 0, count // 2)
 
     @pl.when(place < rows * count // 2)
     def _():
@@ -188,10 +192,17 @@
 
 def solution(mesh):
     count = mesh.shape["ab"]
+    cores = mesh.shape["cd"]
     grid = grid_of(count)
     far = count // 2
-    ahead = [(at_ring(at, *grid), at_ring((at + 1) % count, *grid)) for at in range(count)]
-    back = [(to, start) for start, to in ahead]
+    around = []
+    for chain in range(2):
+        pairs = []
+        for at in range(count):
+            for core in range(cores):
+                to = at + 1 if core == chain else at + count - 1
+                pairs.append((at_ring(at, *grid) * cores + core, at_ring(to % count, *grid) * cores + core))
+        around.append(pairs)
     swap = [(0, 1), (1, 0)]
 
     def shards(amplitudes, integrals, ab_irrep, cd_irrep, block_pattern):
@@ -206,69 +217,79 @@
         vmem = pl.BlockSpec(memory_space=pltpu.VMEM)
         hbm = pl.BlockSpec(memory_space=pltpu.HBM)
         params = pltpu.CompilerParams(vmem_limit_bytes=VMEM_LIMIT)
-        piece = pltpu.VMEM((1, rows, depth), jnp.float32)
-
-        own = pl.pallas_call(
-            cut_kernel,
-            out_shape=(piece,) * spans,
-            in_specs=[hbm],
-            out_specs=(vmem,) * spans,
-            scratch_shapes=[pltpu.SemaphoreType.DMA((spans,))],
-            compiler_params=params,
-            name="cut",
-        )(in_hbm(amplitudes))
-
-        listed, split = pl.pallas_call(
+
+        listed, split, own = pl.pallas_call(
             functools.partial(pick_kernel, ab_tiles, cd_tiles),
             out_shape=(
                 jax.ShapeDtypeStruct((1 + 2 * (tiles + UNROLL),), jnp.int32),
                 pltpu.VMEM((tiles + UNROLL, TILE, 2 * TILE), jnp.bfloat16),
+                pltpu.VMEM(amplitudes.shape, jnp.float32),
             ),
-            in_specs=[smem, smem, smem, hbm],
-            out_specs=(smem, vmem),
+            in_specs=[smem, smem, smem, hbm, hbm],
+            out_specs=(smem, vmem, vmem),
             scratch_shapes=[
                 pltpu.VMEM((FLIGHT, TILE, TILE), jnp.float32),
                 pltpu.SemaphoreType.DMA((FLIGHT,)),
+                pltpu.SemaphoreType.DMA,
             ],
             compiler_params=params,
             cost_estimate=pl.CostEstimate(flops=0, bytes_accessed=8 << 20, transcendentals=0),
             name="pick",
-        )(in_hbm(block_pattern), in_hbm(ab_irrep), in_hbm(cd_irrep), in_hbm(integrals))
-
-        held = {}
-        for span in range(spans):
-            held[span, 0] = own[span]
-            for pairs, sign in ((ahead, -1), (back, 1)):
-                moved = own[span]
-                for hop in range(1, far + 1 if (sign < 0) == (span % 2 == 0) else far):
-                    if hop == 2:
-                        moved, _ = lax.optimization_barrier((moved, listed))
-                    moved = lax.ppermute(moved, "ab", pairs)
-                    held[span, -far if hop == far else sign * hop] = moved
-
-        def offset_of(span, hop, long):
-            return -hop if (span % 2 == 0) == long else hop
-
-        arrivals = [(span, 0) for span in range(spans)]
-        for hop in range(1, far):
-            arrivals += [(span, offset_of(span, hop, long)) for long in (True, False) for span in range(spans)]
+        )(in_hbm(block_pattern), in_hbm(ab_irrep), in_hbm(cd_irrep), in_hbm(integrals), in_hbm(amplitudes))
+
         block = pltpu.VMEM((spans, half, slab), jnp.float32)
-        parts = ()
-        cuts = sorted({*range(0, len(arrivals) - spans, GROUP), len(arrivals) - spans, len(arrivals)})
-        for start, stop in zip(cuts, cuts[1:]):
-            group = arrivals[start:stop]
-            pieces = [held[key] for key in group]
-            parts = pl.pallas_call(
-                functools.partial(step_kernel, count, rows, tiles, group),
+
+        def step(group, parts):
+            pieces = [piece for *_, piece in group]
+            height = sum(piece.shape[0] for piece in pieces) * rows
+            return pl.pallas_call(
+                functools.partial(step_kernel, count, rows, tiles, [key for *key, _ in group]),
                 out_shape=(block, block),
                 in_specs=[smem] + [vmem] * (1 + len(pieces) + len(parts)),
                 out_specs=(vmem, vmem),
-                scratch_shapes=[pltpu.VMEM((len(pieces) * rows, slab), jnp.float32)],
+                scratch_shapes=[pltpu.VMEM((height, slab), jnp.float32)],
                 compiler_params=params,
                 input_output_aliases={2 + len(pieces): 0, 3 + len(pieces): 1} if parts else {},
                 cost_estimate=pl.CostEstimate(flops=STEP_FLOPS, bytes_accessed=4 << 20, transcendentals=0),
                 name="step",
             )(listed, split, *pieces, *parts)
+
+        def send_on(piece, chain):
+            return lax.ppermute(piece, ("ab", "cd"), around[chain])
+
+        both = tuple(range(spans))
+        parts = step([(0, 0, both, own)], ())
+        first = []
+        for chain in range(2):
+            arrived, _ = lax.optimization_barrier((send_on(amplitudes, chain), parts[0]))
+            first.append(arrived)
+        moving = {}
+        for chain in range(2):
+            cut = pl.pallas_call(
+                cut_kernel,
+                out_shape=(pltpu.VMEM((1, rows, depth), jnp.float32),) * spans,
+                in_specs=[vmem],
+                out_specs=(vmem,) * spans,
+                compiler_params=params,
+                name="cut",
+            )(first[chain])
+            for span in both:
+                moving[chain, span] = cut[span]
+        order = [(chain, span) for short in (False, True) for chain in range(2) for span in both if (span % 2 != chain) == short]
+        arrivals = [(chain, 1, both, first[chain]) for chain in range(2)]
+        final = {}
+        for hop in range(2, far + 1):
+            for chain, span in order:
+                if hop < far or span % 2 == chain:
+                    moving[chain, span] = send_on(moving[chain, span], chain)
+                    if hop < far:
+                        arrivals.append((chain, hop, (span,), moving[chain, span]))
+                    else:
+                        final[span] = moving[chain, span]
+        short = len(arrivals) - spans
+        cuts = sorted({*range(0, short, GROUP), short, len(arrivals)})
+        for start, stop in zip(cuts, cuts[1:]):
+            parts = step(arrivals[start:stop], parts)
         mine, send = parts
         base = pl.pallas_call(
             merge_kernel,
@@ -287,7 +308,7 @@
             compiler_params=params,
             cost_estimate=pl.CostEstimate(flops=1 << 34, bytes_accessed=4 << 20, transcendentals=0),
             name="last",
-        )(listed, split, *[held[span, -far] for span in range(spans)])
+        )(listed, split, *[final[span] for span in both])
         return pl.pallas_call(
             functools.partial(final_kernel, count, spans, rows),
             out_shape=pltpu.HBM((spans, half, slab), jnp.float32),

time: 32.1 us -> 32.5 us (1.012)
  the two profiles are of different devices: /device:TPU:1 before, /device:TPU:3 now
where the time goes in v1:
time: 32.5 us
  starting transfers between devices  14.3 us (44%)
  Pallas kernels  12.4 us (38%)
  waiting for transfers between devices  5.73 us (18%)
    ppermute x12, starting transfers between devices, send_on(): return lax.ppermute(piece, ('ab', 'cd'), around[chain])  9.21 us
    pallas_call x3, Pallas kernels, step(): pl.pallas_call(functools.partial(step_kernel, count, rows, tiles, [key fo...  5.66 us
    ppermute x12, waiting for transfers between devices, send_on(): return lax.ppermute(piece, ('ab', 'cd'), around[chain])  5.28 us
    ppermute x1, starting transfers between devices, shards(): lax.ppermute(send, 'cd', swap)  5.04 us
    pallas_call x1, Pallas kernels, shards(): pl.pallas_call(functools.partial(pick_kernel, ab_tiles, cd_tiles), out_sh...  3.63 us
    pallas_call x1, Pallas kernels, shards(): pl.pallas_call(functools.partial(last_kernel, tiles), out_shape=pltpu.VME...  1.51 us
    pallas_call x1, Pallas kernels, shards(): pl.pallas_call(merge_kernel, out_shape=pltpu.HBM((spans, half, slab), jnp...  0.87 us
    pallas_call x1, Pallas kernels, shards(): pl.pallas_call(functools.partial(final_kernel, count, spans, rows), out_s...  0.68 us
  transfers between devices with their start and end apart: 14, of which 6 were waited for; matrix products, arithmetic and copies ran while one was open for 0% of the time, Pallas kernels for 36%

profile of v1, /device:TPU:3, one launch (start us, length us, event | category | flops | bytes accessed | tf_op | source)
XLA Modules:
  0.0 32.5 jit_solution(17757753368618460205)
XLA Ops:
  0.0 1.3 %collective-permute-start.4 = (f32[2,16,2048]{2,1,0:T(8,128)}, f32[2,16,2048]{2,1,0:T(8,128)S(1)}, u32[]{:S(2)}, u32[]{:S(2)}) collective-permute-start(f32[2,16,2048]{2,1,0:T(8,128)} %amplitudes.1), channel_id=1, source_target_pairs={{0,2},{1,5},{4,0},{5,9},{8,4},{9,13},{12,8},{13,15},{14,12},{15,11... | collective-permute-start | bytes 786440 | tf_op jit(solution)/shard_map/ppermute | solution.py:258
  1.3 0.2 collective-permute-start
  1.5 3.6 %pick.1 = (s32[265]{0:T(512)S(1)}, bf16[132,128,256]{2,1,0:T(8,128)(2,1)S(1)}, f32[2,16,2048]{2,1,0:T(8,128)S(1)}) custom-call(s32[8,16]{1,0:T(8,128)} %pattern.1, s32[8]{0:T(128)} %ab_irrep.1, s32[16]{0:T(128)} %cd_irrep.1, f32[1024,2048]{1,0:T(8,128)} %integrals.1, f32[2,16,2048]{2,1,0:T(8,128)} %amplitudes.1), custom_call_target="tpu_custom_call" | custom-call | bytes 8388608 | tf_op jit(solution)/shard_map/pick/pallas_call | solution.py:221
  5.1 1.6 %step.3 = (f32[2,64,1024]{2,1,0:T(8,128)S(1)}, f32[2,64,1024]{2,1,0:T(8,128)S(1)}) custom-call(s32[265]{0:T(512)S(1)} %get-tuple-element.20.listed, bf16[132,128,256]{2,1,0:T(8,128)(2,1)S(1)} %get-tuple-element.21.split, f32[2,16,2048]{2,1,0:T(8,128)S(1)} %get-tuple-element.22.refs_0_), custom_call_target="tpu_custom_call" | custom-call | flops 1073741824 | bytes 4194304 | tf_op jit(solution)/shard_map/step/pallas_call | solution.py:245
  6.7 0.0 collective-permute-done.4.chunk.refs_1_
  6.7 1.5 %collective-permute-start.5 = (f32[1,16,2048]{2,1,0:T(8,128)S(1)}, f32[1,16,2048]{2,1,0:T(8,128)S(1)}, u32[]{:S(2)}, u32[]{:S(2)}) collective-permute-start(f32[1,16,2048]{2,1,0:T(8,128)S(1)} %get-tuple-element.27), channel_id=1, source_target_pairs={{0,2},{1,5},{4,0},{5,9},{8,4},{9,13},{12,8},{13,15},{14,12},{15,11... | collective-permute-start | bytes 393224 | tf_op jit(solution)/shard_map/ppermute | solution.py:258
  8.3 1.3 %collective-permute-done.chunk.refs_0_ = f32[2,16,2048]{2,1,0:T(8,128)S(1)} collective-permute-done((f32[2,16,2048]{2,1,0:T(8,128)}, f32[2,16,2048]{2,1,0:T(8,128)S(1)}, u32[]{:S(2)}, u32[]{:S(2)}) %collective-permute-start) | collective-permute-done | bytes 262176 | tf_op jit(solution)/shard_map/ppermute | solution.py:258
  9.5 0.1 collective-permute-start.1
  9.6 1.5 %collective-permute-start.11 = (f32[1,16,2048]{2,1,0:T(8,128)S(1)}, f32[1,16,2048]{2,1,0:T(8,128)S(1)}, u32[]{:S(2)}, u32[]{:S(2)}) collective-permute-start(f32[1,16,2048]{2,1,0:T(8,128)S(1)} %get-tuple-element.29), channel_id=1, source_target_pairs={{0,2},{1,5},{4,0},{5,9},{8,4},{9,13},{12,8},{13,15},{14,12},{15,11... | collective-permute-start | bytes 393224 | tf_op jit(solution)/shard_map/ppermute | solution.py:258
  11.0 0.1 collective-permute-start.9
  11.1 0.0 collective-permute-done.5.refs_3_
  11.1 1.4 %collective-permute-start.6 = (f32[1,16,2048]{2,1,0:T(8,128)S(1)}, f32[1,16,2048]{2,1,0:T(8,128)S(1)}, u32[]{:S(2)}, u32[]{:S(2)}) collective-permute-start(f32[1,16,2048]{2,1,0:T(8,128)S(1)} %collective-permute-done.5.refs_3_), channel_id=1, source_target_pairs={{0,2},{1,5},{4,0},{5,9},{8,4},{9,13},{12,8},{13,15},{14,12},{15,11... | collective-permute-start | bytes 393224 | tf_op jit(solution)/shard_map/ppermute | solution.py:258
  12.5 1.7 %collective-permute-done.1.refs_2_ = f32[1,16,2048]{2,1,0:T(8,128)S(1)} collective-permute-done((f32[1,16,2048]{2,1,0:T(8,128)S(1)}, f32[1,16,2048]{2,1,0:T(8,128)S(1)}, u32[]{:S(2)}, u32[]{:S(2)}) %collective-permute-start.1) | collective-permute-done | bytes 131104 | tf_op jit(solution)/shard_map/ppermute | solution.py:258
  14.3 0.0 collective-permute-start.2
  14.3 0.0 collective-permute-done.11.refs_5_
  14.3 1.5 %collective-permute-start.12 = (f32[1,16,2048]{2,1,0:T(8,128)S(1)}, f32[1,16,2048]{2,1,0:T(8,128)S(1)}, u32[]{:S(2)}, u32[]{:S(2)}) collective-permute-start(f32[1,16,2048]{2,1,0:T(8,128)S(1)} %collective-permute-done.11.refs_5_), channel_id=1, source_target_pairs={{0,2},{1,5},{4,0},{5,9},{8,4},{9,13},{12,8},{13,15},{14,12},{15,11... | collective-permute-start | bytes 393224 | tf_op jit(solution)/shard_map/ppermute | solution.py:258
  15.7 1.3 %collective-permute-done.9.refs_4_ = f32[1,16,2048]{2,1,0:T(8,128)S(1)} collective-permute-done((f32[1,16,2048]{2,1,0:T(8,128)S(1)}, f32[1,16,2048]{2,1,0:T(8,128)S(1)}, u32[]{:S(2)}, u32[]{:S(2)}) %collective-permute-start.9) | collective-permute-done | bytes 131104 | tf_op jit(solution)/shard_map/ppermute | solution.py:258
  17.1 0.0 collective-permute-start.10
  17.1 0.0 collective-permute-done.6.refs_7_
  17.1 1.5 %collective-permute-start.7 = (f32[1,16,2048]{2,1,0:T(8,128)S(1)}, f32[1,16,2048]{2,1,0:T(8,128)S(1)}, u32[]{:S(2)}, u32[]{:S(2)}) collective-permute-start(f32[1,16,2048]{2,1,0:T(8,128)S(1)} %collective-permute-done.6.refs_7_), channel_id=1, source_target_pairs={{0,2},{1,5},{4,0},{5,9},{8,4},{9,13},{12,8},{13,15},{14,12},{15,11... | collective-permute-start | bytes 393224 | tf_op jit(solution)/shard_map/ppermute | solution.py:258
  18.5 0.5 %collective-permute-done.2.refs_6_ = f32[1,16,2048]{2,1,0:T(8,128)S(1)} collective-permute-done((f32[1,16,2048]{2,1,0:T(8,128)S(1)}, f32[1,16,2048]{2,1,0:T(8,128)S(1)}, u32[]{:S(2)}, u32[]{:S(2)}) %collective-permute-start.2) | collective-permute-done | bytes 131104 | tf_op jit(solution)/shard_map/ppermute | solution.py:258
  19.0 0.3 collective-permute-start.3
  19.3 2.5 %step.4 = (f32[2,64,1024]{2,1,0:T(8,128)S(1)}, f32[2,64,1024]{2,1,0:T(8,128)S(1)}) custom-call(s32[265]{0:T(512)S(1)} %get-tuple-element.20.listed, bf16[132,128,256]{2,1,0:T(8,128)(2,1)S(1)} %get-tuple-element.21.split, f32[2,16,2048]{2,1,0:T(8,128)S(1)} %collective-permute-done.chunk.refs_0_, ...), custom_call_target="tpu_custom_call", output_to_operand_aliasing={{0}: (10, {}), {1}: (11, {})} | custom-call | flops 1073741824 | bytes 4194304 | tf_op jit(solution)/shard_map/step/pallas_call | solution.py:245
  21.8 0.0 collective-permute-done.12.refs_1_
  21.9 0.4 %collective-permute-done.10.refs_0_ = f32[1,16,2048]{2,1,0:T(8,128)S(1)} collective-permute-done((f32[1,16,2048]{2,1,0:T(8,128)S(1)}, f32[1,16,2048]{2,1,0:T(8,128)S(1)}, u32[]{:S(2)}, u32[]{:S(2)}) %collective-permute-start.10) | collective-permute-done | bytes 131104 | tf_op jit(solution)/shard_map/ppermute | solution.py:258
  22.3 1.6 %step.5 = (f32[2,64,1024]{2,1,0:T(8,128)S(1)}, f32[2,64,1024]{2,1,0:T(8,128)S(1)}) custom-call(s32[265]{0:T(512)S(1)} %get-tuple-element.20.listed, bf16[132,128,256]{2,1,0:T(8,128)(2,1)S(1)} %get-tuple-element.21.split, f32[1,16,2048]{2,1,0:T(8,128)S(1)} %collective-permute-done.10.refs_0_, ...), custom_call_target="tpu_custom_call", output_to_operand_aliasing={{0}: (4, {}), {1}: (5, {})} | custom-call | flops 1073741824 | bytes 4194304 | tf_op jit(solution)/shard_map/step/pallas_call | solution.py:245
  23.9 5.0 %collective-permute-start.13 = (f32[2,64,1024]{2,1,0:T(8,128)S(1)}, f32[2,64,1024]{2,1,0:T(8,128)S(1)}, u32[]{:S(2)}, u32[]{:S(2)}) collective-permute-start(f32[2,64,1024]{2,1,0:T(8,128)S(1)} %get-tuple-element.34), channel_id=1, source_target_pairs={{0,1},{1,0},{2,3},{3,2},{4,5},{5,4},{6,7},{7,6},{8,9},{9,8},{10,11... | collective-permute-start | bytes 1572872 | tf_op jit(solution)/shard_map/ppermute | solution.py:301
  28.9 0.0 collective-permute-done.7.refs_1_
  28.9 0.0 collective-permute-done.3.refs_0_
  28.9 1.5 %last.1 = f32[32,1024]{1,0:T(8,128)S(1)} custom-call(s32[265]{0:T(512)S(1)} %get-tuple-element.20.listed, bf16[132,128,256]{2,1,0:T(8,128)(2,1)S(1)} %get-tuple-element.21.split, f32[1,16,2048]{2,1,0:T(8,128)S(1)} %collective-permute-done.3.refs_0_, f32[1,16,2048]{2,1,0:T(8,128)S(1)} %collective-permute-done.7.refs_1_), custom_call_target="tpu_custom_call" | custom-call | flops 17179869184 | bytes 4194304 | tf_op jit(solution)/shard_map/last/pallas_call | solution.py:303
  30.5 0.1 collective-permute-start.8
  30.5 0.0 collective-permute-done.13.received
  30.6 0.9 %merge.1.before = f32[2,64,1024]{2,1,0:T(8,128)} custom-call(f32[2,64,1024]{2,1,0:T(8,128)S(1)} %get-tuple-element.33.mine, f32[2,64,1024]{2,1,0:T(8,128)S(1)} %collective-permute-done.13.received), custom_call_target="tpu_custom_call" | custom-call | tf_op jit(solution)/shard_map/merge/pallas_call | solution.py:294
  31.4 0.4 %collective-permute-done.8.received = f32[32,1024]{1,0:T(8,128)S(1)} collective-permute-done((f32[32,1024]{1,0:T(8,128)S(1)}, f32[32,1024]{1,0:T(8,128)S(1)}, u32[]{:S(2)}, u32[]{:S(2)}) %collective-permute-start.8) | collective-permute-done | bytes 131104 | tf_op jit(solution)/shard_map/ppermute | solution.py:321
  31.9 0.7 %final.1 = f32[2,64,1024]{2,1,0:T(8,128)} custom-call(f32[32,1024]{1,0:T(8,128)S(1)} %last.1, f32[32,1024]{1,0:T(8,128)S(1)} %collective-permute-done.8.received, f32[2,64,1024]{2,1,0:T(8,128)} %merge.1.before), custom_call_target="tpu_custom_call", output_to_operand_aliasing={{}: (2, {})} | custom-call | tf_op jit(solution)/shard_map/final/pallas_call | solution.py:312
  (2 shorter events, 0.0 us)
Async XLA Ops:
  0.0 6.7 %collective-permute-start.4 = (f32[2,16,2048]{2,1,0:T(8,128)}, f32[2,16,2048]{2,1,0:T(8,128)S(1)}, u32[]{:S(2)}, u32[]{:S(2)}) collective-permute-start(f32[2,16,2048]{2,1,0:T(8,128)} %amplitudes.1), channel_id=1, source_target_pairs={{0,2},{1,5},{4,0},{5,9},{8,4},{9,13},{12,8},{13,15},{14,12},{15,11... | collective-permute-start | bytes 786440 | tf_op jit(solution)/shard_map/ppermute | solution.py:258
  1.3 8.2 %collective-permute-start = (f32[2,16,2048]{2,1,0:T(8,128)}, f32[2,16,2048]{2,1,0:T(8,128)S(1)}, u32[]{:S(2)}, u32[]{:S(2)}) collective-permute-start(f32[2,16,2048]{2,1,0:T(8,128)} %amplitudes.1), channel_id=1, source_target_pairs={{0,4},{1,3},{4,8},{5,1},{8,12},{9,5},{12,14},{13,9},{14,10},{15,13... | collective-permute-start | bytes 786440 | tf_op jit(solution)/shard_map/ppermute | solution.py:258
  6.7 4.4 %collective-permute-start.5 = (f32[1,16,2048]{2,1,0:T(8,128)S(1)}, f32[1,16,2048]{2,1,0:T(8,128)S(1)}, u32[]{:S(2)}, u32[]{:S(2)}) collective-permute-start(f32[1,16,2048]{2,1,0:T(8,128)S(1)} %get-tuple-element.27), channel_id=1, source_target_pairs={{0,2},{1,5},{4,0},{5,9},{8,4},{9,13},{12,8},{13,15},{14,12},{15,11... | collective-permute-start | bytes 393224 | tf_op jit(solution)/shard_map/ppermute | solution.py:258
  9.5 4.7 %collective-permute-start.1 = (f32[1,16,2048]{2,1,0:T(8,128)S(1)}, f32[1,16,2048]{2,1,0:T(8,128)S(1)}, u32[]{:S(2)}, u32[]{:S(2)}) collective-permute-start(f32[1,16,2048]{2,1,0:T(8,128)S(1)} %get-tuple-element.25), channel_id=1, source_target_pairs={{0,4},{1,3},{4,8},{5,1},{8,12},{9,5},{12,14},{13,9},{14,10},{15,13... | collective-permute-start | bytes 393224 | tf_op jit(solution)/shard_map/ppermute | solution.py:258
  9.6 4.7 %collective-permute-start.11 = (f32[1,16,2048]{2,1,0:T(8,128)S(1)}, f32[1,16,2048]{2,1,0:T(8,128)S(1)}, u32[]{:S(2)}, u32[]{:S(2)}) collective-permute-start(f32[1,16,2048]{2,1,0:T(8,128)S(1)} %get-tuple-element.29), channel_id=1, source_target_pairs={{0,2},{1,5},{4,0},{5,9},{8,4},{9,13},{12,8},{13,15},{14,12},{15,11... | collective-permute-start | bytes 393224 | tf_op jit(solution)/shard_map/ppermute | solution.py:258
  11.0 6.0 %collective-permute-start.9 = (f32[1,16,2048]{2,1,0:T(8,128)S(1)}, f32[1,16,2048]{2,1,0:T(8,128)S(1)}, u32[]{:S(2)}, u32[]{:S(2)}) collective-permute-start(f32[1,16,2048]{2,1,0:T(8,128)S(1)} %get-tuple-element.28), channel_id=1, source_target_pairs={{0,4},{1,3},{4,8},{5,1},{8,12},{9,5},{12,14},{13,9},{14,10},{15,13... | collective-permute-start | bytes 393224 | tf_op jit(solution)/shard_map/ppermute | solution.py:258
  11.1 6.0 %collective-permute-start.6 = (f32[1,16,2048]{2,1,0:T(8,128)S(1)}, f32[1,16,2048]{2,1,0:T(8,128)S(1)}, u32[]{:S(2)}, u32[]{:S(2)}) collective-permute-start(f32[1,16,2048]{2,1,0:T(8,128)S(1)} %collective-permute-done.5.refs_3_), channel_id=1, source_target_pairs={{0,2},{1,5},{4,0},{5,9},{8,4},{9,13},{12,8},{13,15},{14,12},{15,11... | collective-permute-start | bytes 393224 | tf_op jit(solution)/shard_map/ppermute | solution.py:258
  14.3 4.8 %collective-permute-start.2 = (f32[1,16,2048]{2,1,0:T(8,128)S(1)}, f32[1,16,2048]{2,1,0:T(8,128)S(1)}, u32[]{:S(2)}, u32[]{:S(2)}) collective-permute-start(f32[1,16,2048]{2,1,0:T(8,128)S(1)} %collective-permute-done.1.refs_2_), channel_id=1, source_target_pairs={{0,4},{1,3},{4,8},{5,1},{8,12},{9,5},{12,14},{13,9},{14,10},{15,13... | collective-permute-start | bytes 393224 | tf_op jit(solution)/shard_map/ppermute | solution.py:258
  14.3 7.6 %collective-permute-start.12 = (f32[1,16,2048]{2,1,0:T(8,128)S(1)}, f32[1,16,2048]{2,1,0:T(8,128)S(1)}, u32[]{:S(2)}, u32[]{:S(2)}) collective-permute-start(f32[1,16,2048]{2,1,0:T(8,128)S(1)} %collective-permute-done.11.refs_5_), channel_id=1, source_target_pairs={{0,2},{1,5},{4,0},{5,9},{8,4},{9,13},{12,8},{13,15},{14,12},{15,11... | collective-permute-start | bytes 393224 | tf_op jit(solution)/shard_map/ppermute | solution.py:258
  17.1 5.2 %collective-permute-start.10 = (f32[1,16,2048]{2,1,0:T(8,128)S(1)}, f32[1,16,2048]{2,1,0:T(8,128)S(1)}, u32[]{:S(2)}, u32[]{:S(2)}) collective-permute-start(f32[1,16,2048]{2,1,0:T(8,128)S(1)} %collective-permute-done.9.refs_4_), channel_id=1, source_target_pairs={{0,4},{1,3},{4,8},{5,1},{8,12},{9,5},{12,14},{13,9},{14,10},{15,13... | collective-permute-start | bytes 393224 | tf_op jit(solution)/shard_map/ppermute | solution.py:258
  17.1 11.8 %collective-permute-start.7 = (f32[1,16,2048]{2,1,0:T(8,128)S(1)}, f32[1,16,2048]{2,1,0:T(8,128)S(1)}, u32[]{:S(2)}, u32[]{:S(2)}) collective-permute-start(f32[1,16,2048]{2,1,0:T(8,128)S(1)} %collective-permute-done.6.refs_7_), channel_id=1, source_target_pairs={{0,2},{1,5},{4,0},{5,9},{8,4},{9,13},{12,8},{13,15},{14,12},{15,11... | collective-permute-start | bytes 393224 | tf_op jit(solution)/shard_map/ppermute | solution.py:258
  19.0 9.9 %collective-permute-start.3 = (f32[1,16,2048]{2,1,0:T(8,128)S(1)}, f32[1,16,2048]{2,1,0:T(8,128)S(1)}, u32[]{:S(2)}, u32[]{:S(2)}) collective-permute-start(f32[1,16,2048]{2,1,0:T(8,128)S(1)} %collective-permute-done.2.refs_6_), channel_id=1, source_target_pairs={{0,4},{1,3},{4,8},{5,1},{8,12},{9,5},{12,14},{13,9},{14,10},{15,13... | collective-permute-start | bytes 393224 | tf_op jit(solution)/shard_map/ppermute | solution.py:258
  23.9 6.7 %collective-permute-start.13 = (f32[2,64,1024]{2,1,0:T(8,128)S(1)}, f32[2,64,1024]{2,1,0:T(8,128)S(1)}, u32[]{:S(2)}, u32[]{:S(2)}) collective-permute-start(f32[2,64,1024]{2,1,0:T(8,128)S(1)} %get-tuple-element.34), channel_id=1, source_target_pairs={{0,1},{1,0},{2,3},{3,2},{4,5},{5,4},{6,7},{7,6},{8,9},{9,8},{10,11... | collective-permute-start | bytes 1572872 | tf_op jit(solution)/shard_map/ppermute | solution.py:301
  30.5 1.4 %collective-permute-start.8 = (f32[32,1024]{1,0:T(8,128)S(1)}, f32[32,1024]{1,0:T(8,128)S(1)}, u32[]{:S(2)}, u32[]{:S(2)}) collective-permute-start(f32[32,1024]{1,0:T(8,128)S(1)} %last.1), channel_id=1, source_target_pairs={{0,1},{1,0},{2,3},{3,2},{4,5},{5,4},{6,7},{7,6},{8,9},{9,8},{10,11... | collective-permute-start | bytes 393224 | tf_op jit(solution)/shard_map/ppermute | solution.py:321

commit v2 on v0

--- a/solution.py
+++ b/solution.py
@@ -9,7 +9,9 @@
 
 TILE = 128
 UNROLL = 4
+PLACE_BITS = 12
 FLIGHT = 32
+PLACES = 1 << PLACE_BITS
 GROUP = 12
 STEP_FLOPS = 1 << 30
 VMEM_LIMIT = 12 * 2**20
@@ -57,9 +59,12 @@
     return jnp.where(start >= whole, start - whole, start)
 
 
-def cut_kernel(amplitudes, *refs):
-    spans, sems = refs[:-1], refs[-1]
-    copies = [pltpu.make_async_copy(amplitudes.at[pl.ds(at, 1)], span, sems.at[at]) for at, span in enumerate(spans)]
+def cut_kernel(amplitudes, pattern, ab_irrep, cd_irrep, *refs):
+    *outs, sems = refs
+    spans = len(outs) - 3
+    pairs = [(amplitudes.at[pl.ds(at, 1)], outs[at]) for at in range(spans)]
+    pairs += list(zip((pattern, ab_irrep, cd_irrep), outs[spans:]))
+    copies = [pltpu.make_async_copy(start, end, sems.at[at]) for at, (start, end) in enumerate(pairs)]
     for copy in copies:
         copy.start()
     for copy in copies:
@@ -67,14 +72,13 @@
 
 
 def pick_kernel(ab_tiles, cd_tiles, pattern, ab_irrep, cd_irrep, integrals, listed, split, landed, sems):
-    second = 1 + ab_tiles * cd_tiles + UNROLL
+    columns = [cd_irrep[q] for q in range(cd_tiles)]
 
     def fetch(k):
-        slot = k % FLIGHT
+        start, column = place_in(listed[1 + k])
+        slot = lax.rem(k, FLIGHT)
         return pltpu.make_async_copy(
-            integrals.at[pl.ds(pl.multiple_of(listed[1 + k], TILE), TILE), pl.ds(pl.multiple_of(listed[second + k], TILE), TILE)],
-            landed.at[slot],
-            sems.at[slot],
+            integrals.at[pl.ds(start, TILE), pl.ds(column, TILE)], landed.at[slot], sems.at[slot]
         )
 
     def begin(k, carry):
@@ -85,20 +89,19 @@
         label = ab_irrep[p]
         before = found
         for q in range(cd_tiles):
-            listed[1 + found] = p * TILE
-            listed[second + found] = q * TILE
-            keep = jnp.logical_and(pattern[p, q] == 1, label == cd_irrep[q])
+            listed[1 + found] = p * PLACES + q
+            keep = jnp.logical_and(pattern[p, q] == 1, label == columns[q])
             found = found + keep.astype(jnp.int32)
         lax.fori_loop(jnp.minimum(before, FLIGHT), jnp.minimum(found, FLIGHT), begin, 0)
         return found
 
     found = lax.fori_loop(0, ab_tiles, row, jnp.int32(0))
-    rounds = (found + UNROLL - 1) // UNROLL
+    rounds = lax.div(found + (UNROLL - 1), UNROLL)
+    last = rounds * UNROLL
     listed[0] = rounds
     for extra in range(UNROLL):
         listed[1 + found + extra] = 0
-        listed[second + found + extra] = 0
-    lax.fori_loop(jnp.minimum(found, FLIGHT), jnp.minimum(rounds * UNROLL, FLIGHT), begin, 0)
+    lax.fori_loop(jnp.minimum(found, FLIGHT), jnp.minimum(last, FLIGHT), begin, 0)
 
     def part(round_at, carry):
         first = round_at * UNROLL
@@ -106,43 +109,56 @@
             fetch(first + unrolled).wait()
         for unrolled in range(UNROLL):
             k = first + unrolled
-            tile = jnp.where(k < found, landed[k % FLIGHT], 0.0).T
+            tile = jnp.where(k < found, landed[lax.rem(k, FLIGHT)], 0.0).T
             upper = tile.astype(jnp.bfloat16)
             split[k, :, :TILE] = upper
             split[k, :, TILE:] = (tile - upper.astype(jnp.float32)).astype(jnp.bfloat16)
-        lax.fori_loop(
-            jnp.minimum(first + FLIGHT, rounds * UNROLL), jnp.minimum(first + UNROLL + FLIGHT, rounds * UNROLL), begin, 0
-        )
+        lax.fori_loop(jnp.minimum(first + FLIGHT, last), jnp.minimum(first + UNROLL + FLIGHT, last), begin, 0)
         return carry
 
     lax.fori_loop(0, rounds, part, 0)
 
 
-def products(tiles, listed, split, pieces, total):
+def place_in(code):
+    return (
+        pl.multiple_of(lax.shift_right_logical(code, PLACE_BITS) * TILE, TILE),
+        pl.multiple_of(lax.bitwise_and(code, PLACES - 1) * TILE, TILE),
+    )
+
+
+def products(listed, split, pieces, total):
     total[...] = jnp.zeros_like(total)
 
-    def step(round_at, carry):
+    def some(first, many):
         sums = []
-        for unrolled in range(UNROLL):
-            k = round_at * UNROLL + unrolled
-            columns = pl.ds(pl.multiple_of(listed[1 + tiles + UNROLL + k], TILE), TILE)
-            left = jnp.concatenate([piece[0, :, columns] for piece in pieces], axis=0)
+        for unrolled in range(many):
+            start, column = place_in(listed[1 + first + unrolled])
+            left = jnp.concatenate([piece[0, :, pl.ds(column, TILE)] for piece in pieces], axis=0)
             upper = left.astype(jnp.bfloat16)
             lower = (left - upper.astype(jnp.float32)).astype(jnp.bfloat16)
-            both = jnp.dot(jnp.concatenate([upper, lower], axis=0), split[k], preferred_element_type=jnp.float32)
+            tile = split[first + unrolled]
+            both = jnp.dot(jnp.concatenate([upper, lower], axis=0), tile, preferred_element_type=jnp.float32)
             high, low = both[: left.shape[0]], both[left.shape[0] :]
-            sums.append((listed[1 + k], high[:, :TILE] + (high[:, TILE:] + (low[:, :TILE] + low[:, TILE:]))))
+            sums.append((start, high[:, :TILE] + (high[:, TILE:] + (low[:, :TILE] + low[:, TILE:]))))
         for start, term in sums:
-            total[:, pl.ds(pl.multiple_of(start, TILE), TILE)] += term
+            total[:, pl.ds(start, TILE)] += term
+
+    def step(at, carry):
+        some(at * 2 * UNROLL, 2 * UNROLL)
         return carry
 
-    lax.fori_loop(0, listed[0], step, 0)
-
-
-def step_kernel(count, rows, tiles, group, listed, split, *refs):
+    rounds = listed[0]
+    lax.fori_loop(0, rounds // 2, step, 0)
+
+    @pl.when(rounds % 2 == 1)
+    def _():
+        some((rounds - 1) * UNROLL, UNROLL)
+
+
+def step_kernel(count, rows, group, listed, split, *refs):
     pieces = refs[: len(group)]
     mine, send, total = refs[-3:]
-    products(tiles, listed, split, pieces, total)
+    products(listed, split, pieces, total)
     half = rows * count // 2
     for at, (span, offset) in enumerate(group):
         place = place_of(count, rows, offset)
@@ -157,8 +173,8 @@
             send[span, pl.ds(pl.multiple_of(place - half, rows), rows), :] = block
 
 
-def last_kernel(tiles, listed, split, *refs):
-    products(tiles, listed, split, refs[:-1], refs[-1])
+def last_kernel(listed, split, *refs):
+    products(listed, split, refs[:-1], refs[-1])
 
 
 def merge_kernel(mine, received, out):
@@ -208,32 +224,30 @@
         params = pltpu.CompilerParams(vmem_limit_bytes=VMEM_LIMIT)
         piece = pltpu.VMEM((1, rows, depth), jnp.float32)
 
-        own = pl.pallas_call(
+        labels = (block_pattern, ab_irrep, cd_irrep)
+        *own, near_pattern, near_ab, near_cd = pl.pallas_call(
             cut_kernel,
-            out_shape=(piece,) * spans,
-            in_specs=[hbm],
-            out_specs=(vmem,) * spans,
-            scratch_shapes=[pltpu.SemaphoreType.DMA((spans,))],
+            out_shape=(piece,) * spans + tuple(pltpu.VMEM(label.shape, label.dtype) for label in labels),
+            in_specs=[hbm] * 4,
+            out_specs=(vmem,) * (spans + 3),
+            scratch_shapes=[pltpu.SemaphoreType.DMA((spans + 3,))],
             compiler_params=params,
             name="cut",
-        )(in_hbm(amplitudes))
+        )(in_hbm(amplitudes), *map(in_hbm, labels))
 
         listed, split = pl.pallas_call(
             functools.partial(pick_kernel, ab_tiles, cd_tiles),
             out_shape=(
-                jax.ShapeDtypeStruct((1 + 2 * (tiles + UNROLL),), jnp.int32),
+                jax.ShapeDtypeStruct((1 + tiles + UNROLL,), jnp.int32),
                 pltpu.VMEM((tiles + UNROLL, TILE, 2 * TILE), jnp.bfloat16),
             ),
             in_specs=[smem, smem, smem, hbm],
             out_specs=(smem, vmem),
-            scratch_shapes=[
-                pltpu.VMEM((FLIGHT, TILE, TILE), jnp.float32),
-                pltpu.SemaphoreType.DMA((FLIGHT,)),
-            ],
+            scratch_shapes=[pltpu.VMEM((FLIGHT, TILE, TILE), jnp.float32), pltpu.SemaphoreType.DMA((FLIGHT,))],
             compiler_params=params,
             cost_estimate=pl.CostEstimate(flops=0, bytes_accessed=8 << 20, transcendentals=0),
             name="pick",
-        )(in_hbm(block_pattern), in_hbm(ab_irrep), in_hbm(cd_irrep), in_hbm(integrals))
+        )(near_pattern, near_ab, near_cd, in_hbm(integrals))
 
         held = {}
         for span in range(spans):
@@ -259,7 +273,7 @@
             group = arrivals[start:stop]
             pieces = [held[key] for key in group]
             parts = pl.pallas_call(
-                functools.partial(step_kernel, count, rows, tiles, group),
+                functools.partial(step_kernel, count, rows, group),
                 out_shape=(block, block),
                 in_specs=[smem] + [vmem] * (1 + len(pieces) + len(parts)),
                 out_specs=(vmem, vmem),
@@ -280,7 +294,7 @@
         )(mine, lax.ppermute(send, "cd", swap))
 
         last = pl.pallas_call(
-            functools.partial(last_kernel, tiles),
+            last_kernel,
             out_shape=pltpu.VMEM((spans * rows, slab), jnp.float32),
             in_specs=[smem, vmem] + [vmem] * spans,
             out_specs=vmem,

time: 32.1 us -> 31 us (0.966)
  Pallas kernels: 10.3 us -> 9.62 us
  starting transfers between devices: 17.8 us -> 17.3 us
    ppermute x1, starting transfers between devices: 5.23 us -> 4.55 us  [shards(): lax.ppermute(send, 'cd', swap)]
    ppermute x1, starting transfers between devices: 1.17 us -> 1.6 us  [shards(): lax.ppermute(last, 'cd', swap)]
    pallas_call x4, Pallas kernels: 5.27 us -> 4.89 us  [the longest x2 2.9 us: shards(): pl.pallas_call(functools.partial(step_kernel, count, rows, group), out_sh...]
  transfers between devices with their start and end apart: 16 -> 16, of which waited for: 7 -> 6; matrix products, arithmetic and copies ran while one was open for 0% -> 0% of each run, Pallas kernels for 27% -> 26%
where the time goes in v2:
time: 31 us; the launch traced here: 30.9 us
  starting transfers between devices  17.3 us (56%)
  Pallas kernels  9.62 us (31%)
  waiting for transfers between devices  3.87 us (12%)
    ppermute x14, starting transfers between devices, shards(): moved = lax.ppermute(moved, 'ab', pairs)  11.1 us
    ppermute x1, starting transfers between devices, shards(): lax.ppermute(send, 'cd', swap)  4.55 us
    ppermute x14, waiting for transfers between devices, shards(): moved = lax.ppermute(moved, 'ab', pairs)  3.73 us
    pallas_call x1, Pallas kernels, shards(): pl.pallas_call(functools.partial(pick_kernel, ab_tiles, cd_tiles), out_sh...  3.2 us
    pallas_call x2, Pallas kernels, shards(): pl.pallas_call(functools.partial(step_kernel, count, rows, group), out_sh...  2.9 us
    ppermute x1, starting transfers between devices, shards(): lax.ppermute(last, 'cd', swap)  1.6 us
    pallas_call x1, Pallas kernels, shards(): pl.pallas_call(cut_kernel, out_shape=(piece,) * spans + tuple((pltpu.VMEM...  1.01 us
    pallas_call x1, Pallas kernels, shards(): pl.pallas_call(last_kernel, out_shape=pltpu.VMEM((spans * rows, slab), jn...  0.98 us
  transfers between devices with their start and end apart: 16, of which 6 were waited for; matrix products, arithmetic and copies ran while one was open for 0% of the time, Pallas kernels for 26%

profile of v2, /device:TPU:1, one launch (start us, length us, event | category | flops | bytes accessed | tf_op | source)
XLA Modules:
  0.0 30.9 jit_solution(629456774440048605)
XLA Ops:
  0.0 1.0 %cut.1 = (f32[1,16,2048]{2,1,0:T(8,128)S(1)}, f32[1,16,2048]{2,1,0:T(8,128)S(1)}, s32[8,16]{1,0:T(8,128)S(1)}, s32[8]{0:T(128)S(1)}, s32[16]{0:T(128)S(1)}) custom-call(f32[2,16,2048]{2,1,0:T(8,128)} %amplitudes.1, s32[8,16]{1,0:T(8,128)} %pattern.1, s32[8]{0:T(128)} %ab_irrep.1, s32[16]{0:T(128)} %cd_irrep.1), custom_call_target="tpu_custom_call" | custom-call | tf_op jit(solution)/shard_map/cut/pallas_call | solution.py:228
  1.0 2.1 %collective-permute-start.4 = (f32[1,16,2048]{2,1,0:T(8,128)S(1)}, f32[1,16,2048]{2,1,0:T(8,128)S(1)}, u32[]{:S(2)}, u32[]{:S(2)}) collective-permute-start(f32[1,16,2048]{2,1,0:T(8,128)S(1)} %get-tuple-element.27.refs_1_), channel_id=1, source_target_pairs={{4,0},{8,4},{12,8},{14,12},{10,14},{6,10},{2,6},{0,2},{5,1},{9,5},... | collective-permute-start | bytes 393224 | tf_op jit(solution)/shard_map/ppermute | solution.py:260
  3.1 0.1 collective-permute-start
  3.3 1.3 %collective-permute-start.9 = (f32[1,16,2048]{2,1,0:T(8,128)S(1)}, f32[1,16,2048]{2,1,0:T(8,128)S(1)}, u32[]{:S(2)}, u32[]{:S(2)}) collective-permute-start(f32[1,16,2048]{2,1,0:T(8,128)S(1)} %get-tuple-element.25.refs_0_), channel_id=1, source_target_pairs={{4,0},{8,4},{12,8},{14,12},{10,14},{6,10},{2,6},{0,2},{5,1},{9,5},... | collective-permute-start | bytes 393224 | tf_op jit(solution)/shard_map/ppermute | solution.py:260
  4.6 0.1 collective-permute-start.12
  4.7 3.2 %pick.1 = (s32[133]{0:T(256)S(1)}, bf16[132,128,256]{2,1,0:T(8,128)(2,1)S(1)}) custom-call(s32[8,16]{1,0:T(8,128)S(1)} %get-tuple-element.20.pattern, s32[8]{0:T(128)S(1)} %get-tuple-element.21.ab_irrep, s32[16]{0:T(128)S(1)} %get-tuple-element.22.cd_irrep, f32[1024,2048]{1,0:T(8,128)} %integrals.1), custom_call_target="tpu_custom_call" | custom-call | bytes 8388608 | tf_op jit(solution)/shard_map/pick/pallas_call | solution.py:238
  7.9 0.0 collective-permute-done.4.refs_3_
  8.0 1.4 %collective-permute-start.5 = (f32[1,16,2048]{2,1,0:T(8,128)S(1)}, f32[1,16,2048]{2,1,0:T(8,128)S(1)}, u32[]{:S(2)}, u32[]{:S(2)}) collective-permute-start(f32[1,16,2048]{2,1,0:T(8,128)S(1)} %collective-permute-done.4.refs_3_), channel_id=1, source_target_pairs={{4,0},{8,4},{12,8},{14,12},{10,14},{6,10},{2,6},{0,2},{5,1},{9,5},... | collective-permute-start | bytes 393224 | tf_op jit(solution)/shard_map/ppermute | solution.py:260
  9.4 0.0 collective-permute-done.refs_2_
  9.4 0.1 collective-permute-start.1
  9.5 0.0 collective-permute-done.9.refs_4_
  9.5 1.3 %collective-permute-start.10 = (f32[1,16,2048]{2,1,0:T(8,128)S(1)}, f32[1,16,2048]{2,1,0:T(8,128)S(1)}, u32[]{:S(2)}, u32[]{:S(2)}) collective-permute-start(f32[1,16,2048]{2,1,0:T(8,128)S(1)} %collective-permute-done.9.refs_4_), channel_id=1, source_target_pairs={{4,0},{8,4},{12,8},{14,12},{10,14},{6,10},{2,6},{0,2},{5,1},{9,5},... | collective-permute-start | bytes 393224 | tf_op jit(solution)/shard_map/ppermute | solution.py:260
  10.9 0.0 collective-permute-done.12.refs_5_
  10.9 0.1 collective-permute-start.13
  11.0 0.8 %collective-permute-done.5.refs_7_ = f32[1,16,2048]{2,1,0:T(8,128)S(1)} collective-permute-done((f32[1,16,2048]{2,1,0:T(8,128)S(1)}, f32[1,16,2048]{2,1,0:T(8,128)S(1)}, u32[]{:S(2)}, u32[]{:S(2)}) %collective-permute-start.5) | collective-permute-done | bytes 131104 | tf_op jit(solution)/shard_map/ppermute | solution.py:260
  11.8 1.4 %collective-permute-start.6 = (f32[1,16,2048]{2,1,0:T(8,128)S(1)}, f32[1,16,2048]{2,1,0:T(8,128)S(1)}, u32[]{:S(2)}, u32[]{:S(2)}) collective-permute-start(f32[1,16,2048]{2,1,0:T(8,128)S(1)} %collective-permute-done.5.refs_7_), channel_id=1, source_target_pairs={{4,0},{8,4},{12,8},{14,12},{10,14},{6,10},{2,6},{0,2},{5,1},{9,5},... | collective-permute-start | bytes 393224 | tf_op jit(solution)/shard_map/ppermute | solution.py:260
  13.2 0.3 collective-permute-done.1.refs_6_
  13.5 0.0 collective-permute-start.2
  13.5 1.1 %collective-permute-done.10.refs_8_ = f32[1,16,2048]{2,1,0:T(8,128)S(1)} collective-permute-done((f32[1,16,2048]{2,1,0:T(8,128)S(1)}, f32[1,16,2048]{2,1,0:T(8,128)S(1)}, u32[]{:S(2)}, u32[]{:S(2)}) %collective-permute-start.10) | collective-permute-done | bytes 131104 | tf_op jit(solution)/shard_map/ppermute | solution.py:260
  14.6 1.0 %collective-permute-start.11 = (f32[1,16,2048]{2,1,0:T(8,128)S(1)}, f32[1,16,2048]{2,1,0:T(8,128)S(1)}, u32[]{:S(2)}, u32[]{:S(2)}) collective-permute-start(f32[1,16,2048]{2,1,0:T(8,128)S(1)} %collective-permute-done.10.refs_8_), channel_id=1, source_target_pairs={{4,0},{8,4},{12,8},{14,12},{10,14},{6,10},{2,6},{0,2},{5,1},{9,5},... | collective-permute-start | bytes 393224 | tf_op jit(solution)/shard_map/ppermute | solution.py:260
  15.7 0.0 collective-permute-done.13.refs_9_
  15.7 0.4 %collective-permute-start.14 = (f32[1,16,2048]{2,1,0:T(8,128)S(1)}, f32[1,16,2048]{2,1,0:T(8,128)S(1)}, u32[]{:S(2)}, u32[]{:S(2)}) collective-permute-start(f32[1,16,2048]{2,1,0:T(8,128)S(1)} %collective-permute-done.13.refs_9_), channel_id=1, source_target_pairs={{0,4},{4,8},{8,12},{12,14},{14,10},{10,6},{6,2},{2,0},{1,5},{5,9},... | collective-permute-start | bytes 393224 | tf_op jit(solution)/shard_map/ppermute | solution.py:260
  16.1 1.3 %collective-permute-done.6.refs_11_ = f32[1,16,2048]{2,1,0:T(8,128)S(1)} collective-permute-done((f32[1,16,2048]{2,1,0:T(8,128)S(1)}, f32[1,16,2048]{2,1,0:T(8,128)S(1)}, u32[]{:S(2)}, u32[]{:S(2)}) %collective-permute-start.6) | collective-permute-done | bytes 131104 | tf_op jit(solution)/shard_map/ppermute | solution.py:260
  17.4 1.4 %collective-permute-start.7 = (f32[1,16,2048]{2,1,0:T(8,128)S(1)}, f32[1,16,2048]{2,1,0:T(8,128)S(1)}, u32[]{:S(2)}, u32[]{:S(2)}) collective-permute-start(f32[1,16,2048]{2,1,0:T(8,128)S(1)} %collective-permute-done.6.refs_11_), channel_id=1, source_target_pairs={{4,0},{8,4},{12,8},{14,12},{10,14},{6,10},{2,6},{0,2},{5,1},{9,5},... | collective-permute-start | bytes 393224 | tf_op jit(solution)/shard_map/ppermute | solution.py:260
  18.8 0.1 collective-permute-done.2.refs_10_
  18.9 0.2 collective-permute-start.3
  19.1 1.9 %step.2 = (f32[2,64,1024]{2,1,0:T(8,128)S(1)}, f32[2,64,1024]{2,1,0:T(8,128)S(1)}) custom-call(s32[133]{0:T(256)S(1)} %get-tuple-element.23.listed, bf16[132,128,256]{2,1,0:T(8,128)(2,1)S(1)} %get-tuple-element.24.split, f32[1,16,2048]{2,1,0:T(8,128)S(1)} %get-tuple-element.25.refs_0_, f32[1,16,2048]{2,1,0:T(8,128)S(1)} %get-tuple-element.27.refs_1_, ...), custom_call_target="tpu_custom_call" | custom-call | flops 1073741824 | bytes 4194304 | tf_op jit(solution)/shard_map/step/pallas_call | solution.py:275
  21.0 0.0 collective-permute-done.11.refs_0_
  21.0 0.0 collective-permute-done.14.refs_1_
  21.0 1.0 %step.3 = (f32[2,64,1024]{2,1,0:T(8,128)S(1)}, f32[2,64,1024]{2,1,0:T(8,128)S(1)}) custom-call(s32[133]{0:T(256)S(1)} %get-tuple-element.23.listed, bf16[132,128,256]{2,1,0:T(8,128)(2,1)S(1)} %get-tuple-element.24.split, f32[1,16,2048]{2,1,0:T(8,128)S(1)} %collective-permute-done.11.refs_0_, ...), custom_call_target="tpu_custom_call", output_to_operand_aliasing={{0}: (4, {}), {1}: (5, {})} | custom-call | flops 1073741824 | bytes 4194304 | tf_op jit(solution)/shard_map/step/pallas_call | solution.py:275
  22.0 4.6 %collective-permute-start.15 = (f32[2,64,1024]{2,1,0:T(8,128)S(1)}, f32[2,64,1024]{2,1,0:T(8,128)S(1)}, u32[]{:S(2)}, u32[]{:S(2)}) collective-permute-start(f32[2,64,1024]{2,1,0:T(8,128)S(1)} %get-tuple-element.34), channel_id=1, source_target_pairs={{0,1},{1,0},{2,3},{3,2},{4,5},{5,4},{6,7},{7,6},{8,9},{9,8},{10,11... | collective-permute-start | bytes 1572872 | tf_op jit(solution)/shard_map/ppermute | solution.py:294
  26.6 0.0 collective-permute-done.7.refs_1_
  26.6 0.0 collective-permute-done.3.refs_0_
  26.6 1.0 %last.1 = f32[32,1024]{1,0:T(8,128)S(1)} custom-call(s32[133]{0:T(256)S(1)} %get-tuple-element.23.listed, bf16[132,128,256]{2,1,0:T(8,128)(2,1)S(1)} %get-tuple-element.24.split, f32[1,16,2048]{2,1,0:T(8,128)S(1)} %collective-permute-done.3.refs_0_, f32[1,16,2048]{2,1,0:T(8,128)S(1)} %collective-permute-done.7.refs_1_), custom_call_target="tpu_custom_call" | custom-call | flops 17179869184 | bytes 4194304 | tf_op jit(solution)/shard_map/last/pallas_call | solution.py:296
  27.6 1.6 %collective-permute-start.8 = (f32[32,1024]{1,0:T(8,128)S(1)}, f32[32,1024]{1,0:T(8,128)S(1)}, u32[]{:S(2)}, u32[]{:S(2)}) collective-permute-start(f32[32,1024]{1,0:T(8,128)S(1)} %last.1), channel_id=1, source_target_pairs={{0,1},{1,0},{2,3},{3,2},{4,5},{5,4},{6,7},{7,6},{8,9},{9,8},{10,11... | collective-permute-start | bytes 393224 | tf_op jit(solution)/shard_map/ppermute | solution.py:314
  29.2 0.0 collective-permute-done.15.received
  29.2 0.8 %merge.1.before = f32[2,64,1024]{2,1,0:T(8,128)} custom-call(f32[2,64,1024]{2,1,0:T(8,128)S(1)} %get-tuple-element.33.mine, f32[2,64,1024]{2,1,0:T(8,128)S(1)} %collective-permute-done.15.received), custom_call_target="tpu_custom_call" | custom-call | tf_op jit(solution)/shard_map/merge/pallas_call | solution.py:287
  30.0 0.1 collective-permute-done.8.received
  30.2 0.7 %final.1 = f32[2,64,1024]{2,1,0:T(8,128)} custom-call(f32[32,1024]{1,0:T(8,128)S(1)} %last.1, f32[32,1024]{1,0:T(8,128)S(1)} %collective-permute-done.8.received, f32[2,64,1024]{2,1,0:T(8,128)} %merge.1.before), custom_call_target="tpu_custom_call", output_to_operand_aliasing={{}: (2, {})} | custom-call | tf_op jit(solution)/shard_map/final/pallas_call | solution.py:305
Async XLA Ops:
  1.0 6.9 %collective-permute-start.4 = (f32[1,16,2048]{2,1,0:T(8,128)S(1)}, f32[1,16,2048]{2,1,0:T(8,128)S(1)}, u32[]{:S(2)}, u32[]{:S(2)}) collective-permute-start(f32[1,16,2048]{2,1,0:T(8,128)S(1)} %get-tuple-element.27.refs_1_), channel_id=1, source_target_pairs={{4,0},{8,4},{12,8},{14,12},{10,14},{6,10},{2,6},{0,2},{5,1},{9,5},... | collective-permute-start | bytes 393224 | tf_op jit(solution)/shard_map/ppermute | solution.py:260
  3.1 6.3 %collective-permute-start = (f32[1,16,2048]{2,1,0:T(8,128)S(1)}, f32[1,16,2048]{2,1,0:T(8,128)S(1)}, u32[]{:S(2)}, u32[]{:S(2)}) collective-permute-start(f32[1,16,2048]{2,1,0:T(8,128)S(1)} %get-tuple-element.25.refs_0_), channel_id=1, source_target_pairs={{0,4},{4,8},{8,12},{12,14},{14,10},{10,6},{6,2},{2,0},{1,5},{5,9},... | collective-permute-start | bytes 393224 | tf_op jit(solution)/shard_map/ppermute | solution.py:260
  3.3 6.3 %collective-permute-start.9 = (f32[1,16,2048]{2,1,0:T(8,128)S(1)}, f32[1,16,2048]{2,1,0:T(8,128)S(1)}, u32[]{:S(2)}, u32[]{:S(2)}) collective-permute-start(f32[1,16,2048]{2,1,0:T(8,128)S(1)} %get-tuple-element.25.refs_0_), channel_id=1, source_target_pairs={{4,0},{8,4},{12,8},{14,12},{10,14},{6,10},{2,6},{0,2},{5,1},{9,5},... | collective-permute-start | bytes 393224 | tf_op jit(solution)/shard_map/ppermute | solution.py:260
  4.6 6.3 %collective-permute-start.12 = (f32[1,16,2048]{2,1,0:T(8,128)S(1)}, f32[1,16,2048]{2,1,0:T(8,128)S(1)}, u32[]{:S(2)}, u32[]{:S(2)}) collective-permute-start(f32[1,16,2048]{2,1,0:T(8,128)S(1)} %get-tuple-element.27.refs_1_), channel_id=1, source_target_pairs={{0,4},{4,8},{8,12},{12,14},{14,10},{10,6},{6,2},{2,0},{1,5},{5,9},... | collective-permute-start | bytes 393224 | tf_op jit(solution)/shard_map/ppermute | solution.py:260
  8.0 3.9 %collective-permute-start.5 = (f32[1,16,2048]{2,1,0:T(8,128)S(1)}, f32[1,16,2048]{2,1,0:T(8,128)S(1)}, u32[]{:S(2)}, u32[]{:S(2)}) collective-permute-start(f32[1,16,2048]{2,1,0:T(8,128)S(1)} %collective-permute-done.4.refs_3_), channel_id=1, source_target_pairs={{4,0},{8,4},{12,8},{14,12},{10,14},{6,10},{2,6},{0,2},{5,1},{9,5},... | collective-permute-start | bytes 393224 | tf_op jit(solution)/shard_map/ppermute | solution.py:260
  9.4 4.1 %collective-permute-start.1 = (f32[1,16,2048]{2,1,0:T(8,128)S(1)}, f32[1,16,2048]{2,1,0:T(8,128)S(1)}, u32[]{:S(2)}, u32[]{:S(2)}) collective-permute-start(f32[1,16,2048]{2,1,0:T(8,128)S(1)} %collective-permute-done.refs_2_), channel_id=1, source_target_pairs={{0,4},{4,8},{8,12},{12,14},{14,10},{10,6},{6,2},{2,0},{1,5},{5,9},... | collective-permute-start | bytes 393224 | tf_op jit(solution)/shard_map/ppermute | solution.py:260
  9.5 5.1 %collective-permute-start.10 = (f32[1,16,2048]{2,1,0:T(8,128)S(1)}, f32[1,16,2048]{2,1,0:T(8,128)S(1)}, u32[]{:S(2)}, u32[]{:S(2)}) collective-permute-start(f32[1,16,2048]{2,1,0:T(8,128)S(1)} %collective-permute-done.9.refs_4_), channel_id=1, source_target_pairs={{4,0},{8,4},{12,8},{14,12},{10,14},{6,10},{2,6},{0,2},{5,1},{9,5},... | collective-permute-start | bytes 393224 | tf_op jit(solution)/shard_map/ppermute | solution.py:260
  10.9 4.8 %collective-permute-start.13 = (f32[1,16,2048]{2,1,0:T(8,128)S(1)}, f32[1,16,2048]{2,1,0:T(8,128)S(1)}, u32[]{:S(2)}, u32[]{:S(2)}) collective-permute-start(f32[1,16,2048]{2,1,0:T(8,128)S(1)} %collective-permute-done.12.refs_5_), channel_id=1, source_target_pairs={{0,4},{4,8},{8,12},{12,14},{14,10},{10,6},{6,2},{2,0},{1,5},{5,9},... | collective-permute-start | bytes 393224 | tf_op jit(solution)/shard_map/ppermute | solution.py:260
  11.8 5.6 %collective-permute-start.6 = (f32[1,16,2048]{2,1,0:T(8,128)S(1)}, f32[1,16,2048]{2,1,0:T(8,128)S(1)}, u32[]{:S(2)}, u32[]{:S(2)}) collective-permute-start(f32[1,16,2048]{2,1,0:T(8,128)S(1)} %collective-permute-done.5.refs_7_), channel_id=1, source_target_pairs={{4,0},{8,4},{12,8},{14,12},{10,14},{6,10},{2,6},{0,2},{5,1},{9,5},... | collective-permute-start | bytes 393224 | tf_op jit(solution)/shard_map/ppermute | solution.py:260
  13.5 5.4 %collective-permute-start.2 = (f32[1,16,2048]{2,1,0:T(8,128)S(1)}, f32[1,16,2048]{2,1,0:T(8,128)S(1)}, u32[]{:S(2)}, u32[]{:S(2)}) collective-permute-start(f32[1,16,2048]{2,1,0:T(8,128)S(1)} %collective-permute-done.1.refs_6_), channel_id=1, source_target_pairs={{0,4},{4,8},{8,12},{12,14},{14,10},{10,6},{6,2},{2,0},{1,5},{5,9},... | collective-permute-start | bytes 393224 | tf_op jit(solution)/shard_map/ppermute | solution.py:260
  14.6 6.3 %collective-permute-start.11 = (f32[1,16,2048]{2,1,0:T(8,128)S(1)}, f32[1,16,2048]{2,1,0:T(8,128)S(1)}, u32[]{:S(2)}, u32[]{:S(2)}) collective-permute-start(f32[1,16,2048]{2,1,0:T(8,128)S(1)} %collective-permute-done.10.refs_8_), channel_id=1, source_target_pairs={{4,0},{8,4},{12,8},{14,12},{10,14},{6,10},{2,6},{0,2},{5,1},{9,5},... | collective-permute-start | bytes 393224 | tf_op jit(solution)/shard_map/ppermute | solution.py:260
  15.7 5.3 %collective-permute-start.14 = (f32[1,16,2048]{2,1,0:T(8,128)S(1)}, f32[1,16,2048]{2,1,0:T(8,128)S(1)}, u32[]{:S(2)}, u32[]{:S(2)}) collective-permute-start(f32[1,16,2048]{2,1,0:T(8,128)S(1)} %collective-permute-done.13.refs_9_), channel_id=1, source_target_pairs={{0,4},{4,8},{8,12},{12,14},{14,10},{10,6},{6,2},{2,0},{1,5},{5,9},... | collective-permute-start | bytes 393224 | tf_op jit(solution)/shard_map/ppermute | solution.py:260
  17.4 9.2 %collective-permute-start.7 = (f32[1,16,2048]{2,1,0:T(8,128)S(1)}, f32[1,16,2048]{2,1,0:T(8,128)S(1)}, u32[]{:S(2)}, u32[]{:S(2)}) collective-permute-start(f32[1,16,2048]{2,1,0:T(8,128)S(1)} %collective-permute-done.6.refs_11_), channel_id=1, source_target_pairs={{4,0},{8,4},{12,8},{14,12},{10,14},{6,10},{2,6},{0,2},{5,1},{9,5},... | collective-permute-start | bytes 393224 | tf_op jit(solution)/shard_map/ppermute | solution.py:260
  18.9 7.7 %collective-permute-start.3 = (f32[1,16,2048]{2,1,0:T(8,128)S(1)}, f32[1,16,2048]{2,1,0:T(8,128)S(1)}, u32[]{:S(2)}, u32[]{:S(2)}) collective-permute-start(f32[1,16,2048]{2,1,0:T(8,128)S(1)} %collective-permute-done.2.refs_10_), channel_id=1, source_target_pairs={{0,4},{4,8},{8,12},{12,14},{14,10},{10,6},{6,2},{2,0},{1,5},{5,9},... | collective-permute-start | bytes 393224 | tf_op jit(solution)/shard_map/ppermute | solution.py:260
  22.0 7.1 %collective-permute-start.15 = (f32[2,64,1024]{2,1,0:T(8,128)S(1)}, f32[2,64,1024]{2,1,0:T(8,128)S(1)}, u32[]{:S(2)}, u32[]{:S(2)}) collective-permute-start(f32[2,64,1024]{2,1,0:T(8,128)S(1)} %get-tuple-element.34), channel_id=1, source_target_pairs={{0,1},{1,0},{2,3},{3,2},{4,5},{5,4},{6,7},{7,6},{8,9},{9,8},{10,11... | collective-permute-start | bytes 1572872 | tf_op jit(solution)/shard_map/ppermute | solution.py:294
  27.6 2.6 %collective-permute-start.8 = (f32[32,1024]{1,0:T(8,128)S(1)}, f32[32,1024]{1,0:T(8,128)S(1)}, u32[]{:S(2)}, u32[]{:S(2)}) collective-permute-start(f32[32,1024]{1,0:T(8,128)S(1)} %last.1), channel_id=1, source_target_pairs={{0,1},{1,0},{2,3},{3,2},{4,5},{5,4},{6,7},{7,6},{8,9},{9,8},{10,11... | collective-permute-start | bytes 393224 | tf_op jit(solution)/shard_map/ppermute | solution.py:314

commit v3 on v2

--- a/solution.py
+++ b/solution.py
@@ -9,9 +9,8 @@
 
 TILE = 128
 UNROLL = 4
-PLACE_BITS = 12
+LANES = 128
 FLIGHT = 32
-PLACES = 1 << PLACE_BITS
 GROUP = 12
 STEP_FLOPS = 1 << 30
 VMEM_LIMIT = 12 * 2**20
@@ -71,11 +70,48 @@
         copy.wait()
 
 
-def pick_kernel(ab_tiles, cd_tiles, pattern, ab_irrep, cd_irrep, integrals, listed, split, landed, sems):
-    columns = [cd_irrep[q] for q in range(cd_tiles)]
+def list_kernel(ab_tiles, cd_tiles, ab_irrep, cd_irrep, pattern, listed):
+    shape = (ab_tiles, LANES)
+    lane = lax.broadcasted_iota(jnp.int32, shape, 1)
+    line = lax.broadcasted_iota(jnp.int32, shape, 0)
+    rows = jnp.full(shape, -1, jnp.int32)
+    columns = jnp.full(shape, -2, jnp.int32)
+    for p in range(ab_tiles):
+        rows = jnp.where(line == p, ab_irrep[p], rows)
+    for q in range(cd_tiles):
+        columns = jnp.where(lane == q, cd_irrep[q], columns)
+    stored = jnp.concatenate([pattern[...], jnp.zeros((ab_tiles, LANES - cd_tiles), jnp.int32)], axis=1)
+    keep = jnp.where(jnp.logical_and(stored == 1, rows == columns), 1.0, 0.0)
+
+    upto = keep
+    reach = 1
+    while reach < cd_tiles:
+        upto += jnp.where(lane >= reach, pltpu.roll(upto, reach, 1), 0.0)
+        reach *= 2
+    whole = jnp.broadcast_to(jnp.sum(keep, axis=1, keepdims=True), shape)
+    before = whole
+    reach = 1
+    while reach < ab_tiles:
+        before += jnp.where(line >= reach, pltpu.roll(before, reach, 0), 0.0)
+        reach *= 2
+    found = before[ab_tiles - 1 :, :]
+    upto += before - whole
+
+    turned = upto.T
+    order = lax.broadcasted_iota(jnp.int32, (cd_tiles, LANES), 1).astype(jnp.float32)
+    passed = jnp.zeros((cd_tiles, LANES), jnp.float32)
+    for p in range(ab_tiles):
+        passed += jnp.where(turned[:cd_tiles, p : p + 1] <= order, 1.0, 0.0)
+    places = jnp.sum(passed, axis=0, keepdims=True)
+    listed[0:1, :] = jnp.where(order[0:1, :] < found, places, 0.0).astype(jnp.int32)
+    listed[1:2, :] = ((found + (UNROLL - 1)) * (1.0 / UNROLL)).astype(jnp.int32)
+
+
+def part_kernel(cd_tiles, listed, integrals, split, landed, sems):
+    last = listed[1, 0] * UNROLL
 
     def fetch(k):
-        start, column = place_in(listed[1 + k])
+        start, column = place_in(listed[0, k], cd_tiles)
         slot = lax.rem(k, FLIGHT)
         return pltpu.make_async_copy(
             integrals.at[pl.ds(start, TILE), pl.ds(column, TILE)], landed.at[slot], sems.at[slot]
@@ -85,23 +121,7 @@
         fetch(k).start()
         return carry
 
-    def row(p, found):
-        label = ab_irrep[p]
-        before = found
-        for q in range(cd_tiles):
-            listed[1 + found] = p * PLACES + q
-            keep = jnp.logical_and(pattern[p, q] == 1, label == columns[q])
-            found = found + keep.astype(jnp.int32)
-        lax.fori_loop(jnp.minimum(before, FLIGHT), jnp.minimum(found, FLIGHT), begin, 0)
-        return found
-
-    found = lax.fori_loop(0, ab_tiles, row, jnp.int32(0))
-    rounds = lax.div(found + (UNROLL - 1), UNROLL)
-    last = rounds * UNROLL
-    listed[0] = rounds
-    for extra in range(UNROLL):
-        listed[1 + found + extra] = 0
-    lax.fori_loop(jnp.minimum(found, FLIGHT), jnp.minimum(last, FLIGHT), begin, 0)
+    lax.fori_loop(0, jnp.minimum(last, FLIGHT), begin, 0)
 
     def part(round_at, carry):
         first = round_at * UNROLL
@@ -109,30 +129,29 @@
             fetch(first + unrolled).wait()
         for unrolled in range(UNROLL):
             k = first + unrolled
-            tile = jnp.where(k < found, landed[lax.rem(k, FLIGHT)], 0.0).T
+            real = jnp.logical_or(k == 0, listed[0, k] > 0)
+            tile = jnp.where(real, landed[lax.rem(k, FLIGHT)], 0.0).T
             upper = tile.astype(jnp.bfloat16)
             split[k, :, :TILE] = upper
             split[k, :, TILE:] = (tile - upper.astype(jnp.float32)).astype(jnp.bfloat16)
         lax.fori_loop(jnp.minimum(first + FLIGHT, last), jnp.minimum(first + UNROLL + FLIGHT, last), begin, 0)
         return carry
 
-    lax.fori_loop(0, rounds, part, 0)
-
-
-def place_in(code):
-    return (
-        pl.multiple_of(lax.shift_right_logical(code, PLACE_BITS) * TILE, TILE),
-        pl.multiple_of(lax.bitwise_and(code, PLACES - 1) * TILE, TILE),
-    )
-
-
-def products(listed, split, pieces, total):
+    lax.fori_loop(0, listed[1, 0], part, 0)
+
+
+def place_in(place, cd_tiles):
+    row = lax.div(place, cd_tiles)
+    return pl.multiple_of(row * TILE, TILE), pl.multiple_of((place - row * cd_tiles) * TILE, TILE)
+
+
+def products(cd_tiles, listed, split, pieces, total):
     total[...] = jnp.zeros_like(total)
 
     def some(first, many):
         sums = []
         for unrolled in range(many):
-            start, column = place_in(listed[1 + first + unrolled])
+            start, column = place_in(listed[0, first + unrolled], cd_tiles)
             left = jnp.concatenate([piece[0, :, pl.ds(column, TILE)] for piece in pieces], axis=0)
             upper = left.astype(jnp.bfloat16)
             lower = (left - upper.astype(jnp.float32)).astype(jnp.bfloat16)
@@ -147,18 +166,18 @@
         some(at * 2 * UNROLL, 2 * UNROLL)
         return carry
 
-    rounds = listed[0]
-    lax.fori_loop(0, rounds // 2, step, 0)
-
-    @pl.when(rounds % 2 == 1)
+    rounds = listed[1, 0]
+    lax.fori_loop(0, lax.div(rounds, 2), step, 0)
+
+    @pl.when(lax.rem(rounds, 2) == 1)
     def _():
         some((rounds - 1) * UNROLL, UNROLL)
 
 
-def step_kernel(count, rows, group, listed, split, *refs):
+def step_kernel(count, rows, cd_tiles, group, listed, split, *refs):
     pieces = refs[: len(group)]
     mine, send, total = refs[-3:]
-    products(listed, split, pieces, total)
+    products(cd_tiles, listed, split, pieces, total)
     half = rows * count // 2
     for at, (span, offset) in enumerate(group):
         place = place_of(count, rows, offset)
@@ -173,8 +192,8 @@
             send[span, pl.ds(pl.multiple_of(place - half, rows), rows), :] = block
 
 
-def last_kernel(listed, split, *refs):
-    products(listed, split, refs[:-1], refs[-1])
+def last_kernel(cd_tiles, listed, split, *refs):
+    products(cd_tiles, listed, split, refs[:-1], refs[-1])
 
 
 def merge_kernel(mine, received, out):
@@ -235,19 +254,25 @@
             name="cut",
         )(in_hbm(amplitudes), *map(in_hbm, labels))
 
-        listed, split = pl.pallas_call(
-            functools.partial(pick_kernel, ab_tiles, cd_tiles),
-            out_shape=(
-                jax.ShapeDtypeStruct((1 + tiles + UNROLL,), jnp.int32),
-                pltpu.VMEM((tiles + UNROLL, TILE, 2 * TILE), jnp.bfloat16),
-            ),
-            in_specs=[smem, smem, smem, hbm],
-            out_specs=(smem, vmem),
+        listed = pl.pallas_call(
+            functools.partial(list_kernel, ab_tiles, cd_tiles),
+            out_shape=pltpu.VMEM((2, LANES), jnp.int32),
+            in_specs=[smem, smem, vmem],
+            out_specs=vmem,
+            compiler_params=params,
+            cost_estimate=pl.CostEstimate(flops=0, bytes_accessed=4 << 20, transcendentals=0),
+            name="list",
+        )(near_ab, near_cd, near_pattern)
+        split = pl.pallas_call(
+            functools.partial(part_kernel, cd_tiles),
+            out_shape=pltpu.VMEM((tiles, TILE, 2 * TILE), jnp.bfloat16),
+            in_specs=[smem, hbm],
+            out_specs=vmem,
             scratch_shapes=[pltpu.VMEM((FLIGHT, TILE, TILE), jnp.float32), pltpu.SemaphoreType.DMA((FLIGHT,))],
             compiler_params=params,
             cost_estimate=pl.CostEstimate(flops=0, bytes_accessed=8 << 20, transcendentals=0),
-            name="pick",
-        )(near_pattern, near_ab, near_cd, in_hbm(integrals))
+            name="part",
+        )(listed, in_hbm(integrals))
 
         held = {}
         for span in range(spans):
@@ -255,8 +280,8 @@
             for pairs, sign in ((ahead, -1), (back, 1)):
                 moved = own[span]
                 for hop in range(1, far + 1 if (sign < 0) == (span % 2 == 0) else far):
-                    if hop == 2:
-                        moved, _ = lax.optimization_barrier((moved, listed))
+                    if hop in (2, 3):
+                        moved, _ = lax.optimization_barrier((moved, listed if hop == 2 else split))
                     moved = lax.ppermute(moved, "ab", pairs)
                     held[span, -far if hop == far else sign * hop] = moved
 
@@ -273,7 +298,7 @@
             group = arrivals[start:stop]
             pieces = [held[key] for key in group]
             parts = pl.pallas_call(
-                functools.partial(step_kernel, count, rows, group),
+                functools.partial(step_kernel, count, rows, cd_tiles, group),
                 out_shape=(block, block),
                 in_specs=[smem] + [vmem] * (1 + len(pieces) + len(parts)),
                 out_specs=(vmem, vmem),
@@ -294,7 +319,7 @@
         )(mine, lax.ppermute(send, "cd", swap))
 
         last = pl.pallas_call(
-            last_kernel,
+            functools.partial(last_kernel, cd_tiles),
             out_shape=pltpu.VMEM((spans * rows, slab), jnp.float32),
             in_specs=[smem, vmem] + [vmem] * spans,
             out_specs=vmem,

time: 31 us -> 30.9 us (level); the launches traced: 30.9 us -> 30.4 us
  starting transfers between devices: 17.3 us -> 16.4 us
  Pallas kernels: 9.62 us -> 10.3 us
    ppermute x1, starting transfers between devices: 4.55 us -> 3.79 us  [shards(): lax.ppermute(send, 'cd', swap)]
    pallas_call x4 -> x5, Pallas kernels: 7.08 us -> 7.72 us  [the longest x2 3.26 us: shards(): pl.pallas_call(functools.partial(step_kernel, count, rows, cd_tiles, grou...]
    ppermute x1, starting transfers between devices: 1.6 us -> 1.27 us  [shards(): lax.ppermute(last, 'cd', swap)]
  transfers between devices with their start and end apart: 16 -> 16, of which waited for: 6 -> 5; matrix products, arithmetic and copies ran while one was open for 0% -> 0% of each run, Pallas kernels for 26% -> 28%
where the time goes in v3:
time: 30.9 us; the launch traced here: 30.4 us
  starting transfers between devices  16.4 us (53%)
  Pallas kernels  10.3 us (33%)
  waiting for transfers between devices  3.63 us (12%)
    ppermute x14, starting transfers between devices, shards(): moved = lax.ppermute(moved, 'ab', pairs)  11.3 us
    ppermute x1, starting transfers between devices, shards(): lax.ppermute(send, 'cd', swap)  3.79 us
    ppermute x14, waiting for transfers between devices, shards(): moved = lax.ppermute(moved, 'ab', pairs)  3.5 us
    pallas_call x2, Pallas kernels, shards(): pl.pallas_call(functools.partial(step_kernel, count, rows, cd_tiles, grou...  3.26 us
    pallas_call x1, Pallas kernels, shards(): pl.pallas_call(functools.partial(part_kernel, cd_tiles), out_shape=pltpu....  2.42 us
    ppermute x1, starting transfers between devices, shards(): lax.ppermute(last, 'cd', swap)  1.27 us
    pallas_call x1, Pallas kernels, shards(): pl.pallas_call(functools.partial(last_kernel, cd_tiles), out_shape=pltpu....  1.03 us
    pallas_call x1, Pallas kernels, shards(): pl.pallas_call(cut_kernel, out_shape=(piece,) * spans + tuple((pltpu.VMEM...  1.01 us
  transfers between devices with their start and end apart: 16, of which 5 were waited for; matrix products, arithmetic and copies ran while one was open for 0% of the time, Pallas kernels for 28%

profile of v3, /device:TPU:1, one launch (start us, length us, event | category | flops | bytes accessed | tf_op | source)
XLA Modules:
  0.0 30.4 jit_solution(5865958829326957097)
XLA Ops:
  0.0 1.0 %cut.1 = (f32[1,16,2048]{2,1,0:T(8,128)S(1)}, f32[1,16,2048]{2,1,0:T(8,128)S(1)}, s32[8,16]{1,0:T(8,128)S(1)}, s32[8]{0:T(128)S(1)}, s32[16]{0:T(128)S(1)}) custom-call(f32[2,16,2048]{2,1,0:T(8,128)} %amplitudes.1, s32[8,16]{1,0:T(8,128)} %pattern.1, s32[8]{0:T(128)} %ab_irrep.1, s32[16]{0:T(128)} %cd_irrep.1), custom_call_target="tpu_custom_call" | custom-call | tf_op jit(solution)/shard_map/cut/pallas_call | solution.py:247
  1.0 2.1 %collective-permute-start.4 = (f32[1,16,2048]{2,1,0:T(8,128)S(1)}, f32[1,16,2048]{2,1,0:T(8,128)S(1)}, u32[]{:S(2)}, u32[]{:S(2)}) collective-permute-start(f32[1,16,2048]{2,1,0:T(8,128)S(1)} %get-tuple-element.28.refs_1_), channel_id=1, source_target_pairs={{4,0},{8,4},{12,8},{14,12},{10,14},{6,10},{2,6},{0,2},{5,1},{9,5},... | collective-permute-start | bytes 393224 | tf_op jit(solution)/shard_map/ppermute | solution.py:285
  3.1 0.1 collective-permute-start
  3.3 1.3 %collective-permute-start.9 = (f32[1,16,2048]{2,1,0:T(8,128)S(1)}, f32[1,16,2048]{2,1,0:T(8,128)S(1)}, u32[]{:S(2)}, u32[]{:S(2)}) collective-permute-start(f32[1,16,2048]{2,1,0:T(8,128)S(1)} %get-tuple-element.25.refs_0_), channel_id=1, source_target_pairs={{4,0},{8,4},{12,8},{14,12},{10,14},{6,10},{2,6},{0,2},{5,1},{9,5},... | collective-permute-start | bytes 393224 | tf_op jit(solution)/shard_map/ppermute | solution.py:285
  4.6 0.1 collective-permute-start.12
  4.7 1.0 %list.1.listed = s32[2,128]{1,0:T(2,128)S(1)} custom-call(s32[8]{0:T(128)S(1)} %get-tuple-element.22.ab_irrep, s32[16]{0:T(128)S(1)} %get-tuple-element.23.cd_irrep, s32[8,16]{1,0:T(8,128)S(1)} %get-tuple-element.24.pattern), custom_call_target="tpu_custom_call" | custom-call | bytes 4194304 | tf_op jit(solution)/shard_map/list/pallas_call | solution.py:257
  5.7 0.7 %collective-permute-done.4.refs_3_ = f32[1,16,2048]{2,1,0:T(8,128)S(1)} collective-permute-done((f32[1,16,2048]{2,1,0:T(8,128)S(1)}, f32[1,16,2048]{2,1,0:T(8,128)S(1)}, u32[]{:S(2)}, u32[]{:S(2)}) %collective-permute-start.4) | collective-permute-done | bytes 131104 | tf_op jit(solution)/shard_map/ppermute | solution.py:285
  6.4 1.1 %collective-permute-start.5 = (f32[1,16,2048]{2,1,0:T(8,128)S(1)}, f32[1,16,2048]{2,1,0:T(8,128)S(1)}, u32[]{:S(2)}, u32[]{:S(2)}) collective-permute-start(f32[1,16,2048]{2,1,0:T(8,128)S(1)} %collective-permute-done.4.refs_3_), channel_id=1, source_target_pairs={{4,0},{8,4},{12,8},{14,12},{10,14},{6,10},{2,6},{0,2},{5,1},{9,5},... | collective-permute-start | bytes 393224 | tf_op jit(solution)/shard_map/ppermute | solution.py:285
  7.5 0.0 collective-permute-done.refs_2_
  7.5 0.4 %collective-permute-start.1 = (f32[1,16,2048]{2,1,0:T(8,128)S(1)}, f32[1,16,2048]{2,1,0:T(8,128)S(1)}, u32[]{:S(2)}, u32[]{:S(2)}) collective-permute-start(f32[1,16,2048]{2,1,0:T(8,128)S(1)} %collective-permute-done.refs_2_), channel_id=1, source_target_pairs={{0,4},{4,8},{8,12},{12,14},{14,10},{10,6},{6,2},{2,0},{1,5},{5,9},... | collective-permute-start | bytes 393224 | tf_op jit(solution)/shard_map/ppermute | solution.py:285
  7.9 1.3 %collective-permute-done.9.refs_4_ = f32[1,16,2048]{2,1,0:T(8,128)S(1)} collective-permute-done((f32[1,16,2048]{2,1,0:T(8,128)S(1)}, f32[1,16,2048]{2,1,0:T(8,128)S(1)}, u32[]{:S(2)}, u32[]{:S(2)}) %collective-permute-start.9) | collective-permute-done | bytes 131104 | tf_op jit(solution)/shard_map/ppermute | solution.py:285
  9.2 1.1 %collective-permute-start.10 = (f32[1,16,2048]{2,1,0:T(8,128)S(1)}, f32[1,16,2048]{2,1,0:T(8,128)S(1)}, u32[]{:S(2)}, u32[]{:S(2)}) collective-permute-start(f32[1,16,2048]{2,1,0:T(8,128)S(1)} %collective-permute-done.9.refs_4_), channel_id=1, source_target_pairs={{4,0},{8,4},{12,8},{14,12},{10,14},{6,10},{2,6},{0,2},{5,1},{9,5},... | collective-permute-start | bytes 393224 | tf_op jit(solution)/shard_map/ppermute | solution.py:285
  10.3 0.0 collective-permute-done.12.refs_5_
  10.3 0.4 %collective-permute-start.13 = (f32[1,16,2048]{2,1,0:T(8,128)S(1)}, f32[1,16,2048]{2,1,0:T(8,128)S(1)}, u32[]{:S(2)}, u32[]{:S(2)}) collective-permute-start(f32[1,16,2048]{2,1,0:T(8,128)S(1)} %collective-permute-done.12.refs_5_), channel_id=1, source_target_pairs={{0,4},{4,8},{8,12},{12,14},{14,10},{10,6},{6,2},{2,0},{1,5},{5,9},... | collective-permute-start | bytes 393224 | tf_op jit(solution)/shard_map/ppermute | solution.py:285
  10.7 2.4 %part.1.split = bf16[128,128,256]{2,1,0:T(8,128)(2,1)S(1)} custom-call(s32[2,128]{1,0:T(2,128)S(1)} %list.1.listed, f32[1024,2048]{1,0:T(8,128)} %integrals.1), custom_call_target="tpu_custom_call" | custom-call | bytes 8388608 | tf_op jit(solution)/shard_map/part/pallas_call | solution.py:266
  13.1 0.0 collective-permute-done.5.refs_7_
  13.1 1.0 %collective-permute-start.6 = (f32[1,16,2048]{2,1,0:T(8,128)S(1)}, f32[1,16,2048]{2,1,0:T(8,128)S(1)}, u32[]{:S(2)}, u32[]{:S(2)}) collective-permute-start(f32[1,16,2048]{2,1,0:T(8,128)S(1)} %collective-permute-done.5.refs_7_), channel_id=1, source_target_pairs={{4,0},{8,4},{12,8},{14,12},{10,14},{6,10},{2,6},{0,2},{5,1},{9,5},... | collective-permute-start | bytes 393224 | tf_op jit(solution)/shard_map/ppermute | solution.py:285
  14.1 0.0 collective-permute-done.1.refs_6_
  14.1 0.5 %collective-permute-start.2 = (f32[1,16,2048]{2,1,0:T(8,128)S(1)}, f32[1,16,2048]{2,1,0:T(8,128)S(1)}, u32[]{:S(2)}, u32[]{:S(2)}) collective-permute-start(f32[1,16,2048]{2,1,0:T(8,128)S(1)} %collective-permute-done.1.refs_6_), channel_id=1, source_target_pairs={{0,4},{4,8},{8,12},{12,14},{14,10},{10,6},{6,2},{2,0},{1,5},{5,9},... | collective-permute-start | bytes 393224 | tf_op jit(solution)/shard_map/ppermute | solution.py:285
  14.7 0.0 collective-permute-done.10.refs_8_
  14.7 0.9 %collective-permute-start.11 = (f32[1,16,2048]{2,1,0:T(8,128)S(1)}, f32[1,16,2048]{2,1,0:T(8,128)S(1)}, u32[]{:S(2)}, u32[]{:S(2)}) collective-permute-start(f32[1,16,2048]{2,1,0:T(8,128)S(1)} %collective-permute-done.10.refs_8_), channel_id=1, source_target_pairs={{4,0},{8,4},{12,8},{14,12},{10,14},{6,10},{2,6},{0,2},{5,1},{9,5},... | collective-permute-start | bytes 393224 | tf_op jit(solution)/shard_map/ppermute | solution.py:285
  15.6 0.0 collective-permute-done.13.refs_9_
  15.6 0.5 %collective-permute-start.14 = (f32[1,16,2048]{2,1,0:T(8,128)S(1)}, f32[1,16,2048]{2,1,0:T(8,128)S(1)}, u32[]{:S(2)}, u32[]{:S(2)}) collective-permute-start(f32[1,16,2048]{2,1,0:T(8,128)S(1)} %collective-permute-done.13.refs_9_), channel_id=1, source_target_pairs={{0,4},{4,8},{8,12},{12,14},{14,10},{10,6},{6,2},{2,0},{1,5},{5,9},... | collective-permute-start | bytes 393224 | tf_op jit(solution)/shard_map/ppermute | solution.py:285
  16.1 1.2 %collective-permute-done.6.refs_11_ = f32[1,16,2048]{2,1,0:T(8,128)S(1)} collective-permute-done((f32[1,16,2048]{2,1,0:T(8,128)S(1)}, f32[1,16,2048]{2,1,0:T(8,128)S(1)}, u32[]{:S(2)}, u32[]{:S(2)}) %collective-permute-start.6) | collective-permute-done | bytes 131104 | tf_op jit(solution)/shard_map/ppermute | solution.py:285
  17.3 1.7 %collective-permute-start.7 = (f32[1,16,2048]{2,1,0:T(8,128)S(1)}, f32[1,16,2048]{2,1,0:T(8,128)S(1)}, u32[]{:S(2)}, u32[]{:S(2)}) collective-permute-start(f32[1,16,2048]{2,1,0:T(8,128)S(1)} %collective-permute-done.6.refs_11_), channel_id=1, source_target_pairs={{4,0},{8,4},{12,8},{14,12},{10,14},{6,10},{2,6},{0,2},{5,1},{9,5},... | collective-permute-start | bytes 393224 | tf_op jit(solution)/shard_map/ppermute | solution.py:285
  19.0 0.3 collective-permute-done.2.refs_10_
  19.3 0.0 collective-permute-start.3
  19.3 2.2 %step.2 = (f32[2,64,1024]{2,1,0:T(8,128)S(1)}, f32[2,64,1024]{2,1,0:T(8,128)S(1)}) custom-call(s32[2,128]{1,0:T(2,128)S(1)} %list.1.listed, bf16[128,128,256]{2,1,0:T(8,128)(2,1)S(1)} %part.1.split, f32[1,16,2048]{2,1,0:T(8,128)S(1)} %get-tuple-element.25.refs_0_, f32[1,16,2048]{2,1,0:T(8,128)S(1)} %get-tuple-element.28.refs_1_, ...), custom_call_target="tpu_custom_call" | custom-call | flops 1073741824 | bytes 4194304 | tf_op jit(solution)/shard_map/step/pallas_call | solution.py:300
  21.5 0.0 collective-permute-done.11.refs_0_
  21.5 0.0 collective-permute-done.14.refs_1_
  21.5 1.1 %step.3 = (f32[2,64,1024]{2,1,0:T(8,128)S(1)}, f32[2,64,1024]{2,1,0:T(8,128)S(1)}) custom-call(s32[2,128]{1,0:T(2,128)S(1)} %list.1.listed, bf16[128,128,256]{2,1,0:T(8,128)(2,1)S(1)} %part.1.split, f32[1,16,2048]{2,1,0:T(8,128)S(1)} %collective-permute-done.11.refs_0_, ...), custom_call_target="tpu_custom_call", output_to_operand_aliasing={{0}: (4, {}), {1}: (5, {})} | custom-call | flops 1073741824 | bytes 4194304 | tf_op jit(solution)/shard_map/step/pallas_call | solution.py:300
  22.6 3.8 %collective-permute-start.15 = (f32[2,64,1024]{2,1,0:T(8,128)S(1)}, f32[2,64,1024]{2,1,0:T(8,128)S(1)}, u32[]{:S(2)}, u32[]{:S(2)}) collective-permute-start(f32[2,64,1024]{2,1,0:T(8,128)S(1)} %get-tuple-element.38), channel_id=1, source_target_pairs={{0,1},{1,0},{2,3},{3,2},{4,5},{5,4},{6,7},{7,6},{8,9},{9,8},{10,11... | collective-permute-start | bytes 1572872 | tf_op jit(solution)/shard_map/ppermute | solution.py:319
  26.4 0.0 collective-permute-done.7.refs_1_
  26.4 0.0 collective-permute-done.3.refs_0_
  26.4 1.0 %last.1 = f32[32,1024]{1,0:T(8,128)S(1)} custom-call(s32[2,128]{1,0:T(2,128)S(1)} %list.1.listed, bf16[128,128,256]{2,1,0:T(8,128)(2,1)S(1)} %part.1.split, f32[1,16,2048]{2,1,0:T(8,128)S(1)} %collective-permute-done.3.refs_0_, f32[1,16,2048]{2,1,0:T(8,128)S(1)} %collective-permute-done.7.refs_1_), custom_call_target="tpu_custom_call" | custom-call | flops 17179869184 | bytes 4194304 | tf_op jit(solution)/shard_map/last/pallas_call | solution.py:321
  27.4 1.3 %collective-permute-start.8 = (f32[32,1024]{1,0:T(8,128)S(1)}, f32[32,1024]{1,0:T(8,128)S(1)}, u32[]{:S(2)}, u32[]{:S(2)}) collective-permute-start(f32[32,1024]{1,0:T(8,128)S(1)} %last.1), channel_id=1, source_target_pairs={{0,1},{1,0},{2,3},{3,2},{4,5},{5,4},{6,7},{7,6},{8,9},{9,8},{10,11... | collective-permute-start | bytes 393224 | tf_op jit(solution)/shard_map/ppermute | solution.py:339
  28.7 0.0 collective-permute-done.15.received
  28.7 0.8 %merge.1.before = f32[2,64,1024]{2,1,0:T(8,128)} custom-call(f32[2,64,1024]{2,1,0:T(8,128)S(1)} %get-tuple-element.37.mine, f32[2,64,1024]{2,1,0:T(8,128)S(1)} %collective-permute-done.15.received), custom_call_target="tpu_custom_call" | custom-call | tf_op jit(solution)/shard_map/merge/pallas_call | solution.py:312
  29.5 0.1 collective-permute-done.8.received
  29.7 0.7 %final.1 = f32[2,64,1024]{2,1,0:T(8,128)} custom-call(f32[32,1024]{1,0:T(8,128)S(1)} %last.1, f32[32,1024]{1,0:T(8,128)S(1)} %collective-permute-done.8.received, f32[2,64,1024]{2,1,0:T(8,128)} %merge.1.before), custom_call_target="tpu_custom_call", output_to_operand_aliasing={{}: (2, {})} | custom-call | tf_op jit(solution)/shard_map/final/pallas_call | solution.py:330
Async XLA Ops:
  1.0 5.4 %collective-permute-start.4 = (f32[1,16,2048]{2,1,0:T(8,128)S(1)}, f32[1,16,2048]{2,1,0:T(8,128)S(1)}, u32[]{:S(2)}, u32[]{:S(2)}) collective-permute-start(f32[1,16,2048]{2,1,0:T(8,128)S(1)} %get-tuple-element.28.refs_1_), channel_id=1, source_target_pairs={{4,0},{8,4},{12,8},{14,12},{10,14},{6,10},{2,6},{0,2},{5,1},{9,5},... | collective-permute-start | bytes 393224 | tf_op jit(solution)/shard_map/ppermute | solution.py:285
  3.1 4.4 %collective-permute-start = (f32[1,16,2048]{2,1,0:T(8,128)S(1)}, f32[1,16,2048]{2,1,0:T(8,128)S(1)}, u32[]{:S(2)}, u32[]{:S(2)}) collective-permute-start(f32[1,16,2048]{2,1,0:T(8,128)S(1)} %get-tuple-element.25.refs_0_), channel_id=1, source_target_pairs={{0,4},{4,8},{8,12},{12,14},{14,10},{10,6},{6,2},{2,0},{1,5},{5,9},... | collective-permute-start | bytes 393224 | tf_op jit(solution)/shard_map/ppermute | solution.py:285
  3.3 6.0 %collective-permute-start.9 = (f32[1,16,2048]{2,1,0:T(8,128)S(1)}, f32[1,16,2048]{2,1,0:T(8,128)S(1)}, u32[]{:S(2)}, u32[]{:S(2)}) collective-permute-start(f32[1,16,2048]{2,1,0:T(8,128)S(1)} %get-tuple-element.25.refs_0_), channel_id=1, source_target_pairs={{4,0},{8,4},{12,8},{14,12},{10,14},{6,10},{2,6},{0,2},{5,1},{9,5},... | collective-permute-start | bytes 393224 | tf_op jit(solution)/shard_map/ppermute | solution.py:285
  4.6 5.7 %collective-permute-start.12 = (f32[1,16,2048]{2,1,0:T(8,128)S(1)}, f32[1,16,2048]{2,1,0:T(8,128)S(1)}, u32[]{:S(2)}, u32[]{:S(2)}) collective-permute-start(f32[1,16,2048]{2,1,0:T(8,128)S(1)} %get-tuple-element.28.refs_1_), channel_id=1, source_target_pairs={{0,4},{4,8},{8,12},{12,14},{14,10},{10,6},{6,2},{2,0},{1,5},{5,9},... | collective-permute-start | bytes 393224 | tf_op jit(solution)/shard_map/ppermute | solution.py:285
  6.4 6.7 %collective-permute-start.5 = (f32[1,16,2048]{2,1,0:T(8,128)S(1)}, f32[1,16,2048]{2,1,0:T(8,128)S(1)}, u32[]{:S(2)}, u32[]{:S(2)}) collective-permute-start(f32[1,16,2048]{2,1,0:T(8,128)S(1)} %collective-permute-done.4.refs_3_), channel_id=1, source_target_pairs={{4,0},{8,4},{12,8},{14,12},{10,14},{6,10},{2,6},{0,2},{5,1},{9,5},... | collective-permute-start | bytes 393224 | tf_op jit(solution)/shard_map/ppermute | solution.py:285
  7.5 6.6 %collective-permute-start.1 = (f32[1,16,2048]{2,1,0:T(8,128)S(1)}, f32[1,16,2048]{2,1,0:T(8,128)S(1)}, u32[]{:S(2)}, u32[]{:S(2)}) collective-permute-start(f32[1,16,2048]{2,1,0:T(8,128)S(1)} %collective-permute-done.refs_2_), channel_id=1, source_target_pairs={{0,4},{4,8},{8,12},{12,14},{14,10},{10,6},{6,2},{2,0},{1,5},{5,9},... | collective-permute-start | bytes 393224 | tf_op jit(solution)/shard_map/ppermute | solution.py:285
  9.2 5.4 %collective-permute-start.10 = (f32[1,16,2048]{2,1,0:T(8,128)S(1)}, f32[1,16,2048]{2,1,0:T(8,128)S(1)}, u32[]{:S(2)}, u32[]{:S(2)}) collective-permute-start(f32[1,16,2048]{2,1,0:T(8,128)S(1)} %collective-permute-done.9.refs_4_), channel_id=1, source_target_pairs={{4,0},{8,4},{12,8},{14,12},{10,14},{6,10},{2,6},{0,2},{5,1},{9,5},... | collective-permute-start | bytes 393224 | tf_op jit(solution)/shard_map/ppermute | solution.py:285
  10.3 5.3 %collective-permute-start.13 = (f32[1,16,2048]{2,1,0:T(8,128)S(1)}, f32[1,16,2048]{2,1,0:T(8,128)S(1)}, u32[]{:S(2)}, u32[]{:S(2)}) collective-permute-start(f32[1,16,2048]{2,1,0:T(8,128)S(1)} %collective-permute-done.12.refs_5_), channel_id=1, source_target_pairs={{0,4},{4,8},{8,12},{12,14},{14,10},{10,6},{6,2},{2,0},{1,5},{5,9},... | collective-permute-start | bytes 393224 | tf_op jit(solution)/shard_map/ppermute | solution.py:285
  13.1 4.2 %collective-permute-start.6 = (f32[1,16,2048]{2,1,0:T(8,128)S(1)}, f32[1,16,2048]{2,1,0:T(8,128)S(1)}, u32[]{:S(2)}, u32[]{:S(2)}) collective-permute-start(f32[1,16,2048]{2,1,0:T(8,128)S(1)} %collective-permute-done.5.refs_7_), channel_id=1, source_target_pairs={{4,0},{8,4},{12,8},{14,12},{10,14},{6,10},{2,6},{0,2},{5,1},{9,5},... | collective-permute-start | bytes 393224 | tf_op jit(solution)/shard_map/ppermute | solution.py:285
  14.1 5.2 %collective-permute-start.2 = (f32[1,16,2048]{2,1,0:T(8,128)S(1)}, f32[1,16,2048]{2,1,0:T(8,128)S(1)}, u32[]{:S(2)}, u32[]{:S(2)}) collective-permute-start(f32[1,16,2048]{2,1,0:T(8,128)S(1)} %collective-permute-done.1.refs_6_), channel_id=1, source_target_pairs={{0,4},{4,8},{8,12},{12,14},{14,10},{10,6},{6,2},{2,0},{1,5},{5,9},... | collective-permute-start | bytes 393224 | tf_op jit(solution)/shard_map/ppermute | solution.py:285
  14.7 6.8 %collective-permute-start.11 = (f32[1,16,2048]{2,1,0:T(8,128)S(1)}, f32[1,16,2048]{2,1,0:T(8,128)S(1)}, u32[]{:S(2)}, u32[]{:S(2)}) collective-permute-start(f32[1,16,2048]{2,1,0:T(8,128)S(1)} %collective-permute-done.10.refs_8_), channel_id=1, source_target_pairs={{4,0},{8,4},{12,8},{14,12},{10,14},{6,10},{2,6},{0,2},{5,1},{9,5},... | collective-permute-start | bytes 393224 | tf_op jit(solution)/shard_map/ppermute | solution.py:285
  15.6 5.9 %collective-permute-start.14 = (f32[1,16,2048]{2,1,0:T(8,128)S(1)}, f32[1,16,2048]{2,1,0:T(8,128)S(1)}, u32[]{:S(2)}, u32[]{:S(2)}) collective-permute-start(f32[1,16,2048]{2,1,0:T(8,128)S(1)} %collective-permute-done.13.refs_9_), channel_id=1, source_target_pairs={{0,4},{4,8},{8,12},{12,14},{14,10},{10,6},{6,2},{2,0},{1,5},{5,9},... | collective-permute-start | bytes 393224 | tf_op jit(solution)/shard_map/ppermute | solution.py:285
  17.3 9.1 %collective-permute-start.7 = (f32[1,16,2048]{2,1,0:T(8,128)S(1)}, f32[1,16,2048]{2,1,0:T(8,128)S(1)}, u32[]{:S(2)}, u32[]{:S(2)}) collective-permute-start(f32[1,16,2048]{2,1,0:T(8,128)S(1)} %collective-permute-done.6.refs_11_), channel_id=1, source_target_pairs={{4,0},{8,4},{12,8},{14,12},{10,14},{6,10},{2,6},{0,2},{5,1},{9,5},... | collective-permute-start | bytes 393224 | tf_op jit(solution)/shard_map/ppermute | solution.py:285
  19.3 7.1 %collective-permute-start.3 = (f32[1,16,2048]{2,1,0:T(8,128)S(1)}, f32[1,16,2048]{2,1,0:T(8,128)S(1)}, u32[]{:S(2)}, u32[]{:S(2)}) collective-permute-start(f32[1,16,2048]{2,1,0:T(8,128)S(1)} %collective-permute-done.2.refs_10_), channel_id=1, source_target_pairs={{0,4},{4,8},{8,12},{12,14},{14,10},{10,6},{6,2},{2,0},{1,5},{5,9},... | collective-permute-start | bytes 393224 | tf_op jit(solution)/shard_map/ppermute | solution.py:285
  22.6 6.1 %collective-permute-start.15 = (f32[2,64,1024]{2,1,0:T(8,128)S(1)}, f32[2,64,1024]{2,1,0:T(8,128)S(1)}, u32[]{:S(2)}, u32[]{:S(2)}) collective-permute-start(f32[2,64,1024]{2,1,0:T(8,128)S(1)} %get-tuple-element.38), channel_id=1, source_target_pairs={{0,1},{1,0},{2,3},{3,2},{4,5},{5,4},{6,7},{7,6},{8,9},{9,8},{10,11... | collective-permute-start | bytes 1572872 | tf_op jit(solution)/shard_map/ppermute | solution.py:319
  27.4 2.3 %collective-permute-start.8 = (f32[32,1024]{1,0:T(8,128)S(1)}, f32[32,1024]{1,0:T(8,128)S(1)}, u32[]{:S(2)}, u32[]{:S(2)}) collective-permute-start(f32[32,1024]{1,0:T(8,128)S(1)} %last.1), channel_id=1, source_target_pairs={{0,1},{1,0},{2,3},{3,2},{4,5},{5,4},{6,7},{7,6},{8,9},{9,8},{10,11... | collective-permute-start | bytes 393224 | tf_op jit(solution)/shard_map/ppermute | solution.py:339

commit v4 on v3

--- a/solution.py
+++ b/solution.py
@@ -58,19 +58,14 @@
     return jnp.where(start >= whole, start - whole, start)
 
 
-def cut_kernel(amplitudes, pattern, ab_irrep, cd_irrep, *refs):
-    *outs, sems = refs
-    spans = len(outs) - 3
-    pairs = [(amplitudes.at[pl.ds(at, 1)], outs[at]) for at in range(spans)]
-    pairs += list(zip((pattern, ab_irrep, cd_irrep), outs[spans:]))
-    copies = [pltpu.make_async_copy(start, end, sems.at[at]) for at, (start, end) in enumerate(pairs)]
-    for copy in copies:
-        copy.start()
-    for copy in copies:
-        copy.wait()
-
-
-def list_kernel(ab_tiles, cd_tiles, ab_irrep, cd_irrep, pattern, listed):
+def cut_kernel(chunk, *spans):
+    for at, span in enumerate(spans):
+        span[0] = chunk[at]
+
+
+def list_kernel(ab_tiles, cd_tiles, ab_irrep, cd_irrep, pattern, amplitudes, listed, own, own_sem):
+    copy = pltpu.make_async_copy(amplitudes, own, own_sem)
+    copy.start()
     shape = (ab_tiles, LANES)
     lane = lax.broadcasted_iota(jnp.int32, shape, 1)
     line = lax.broadcasted_iota(jnp.int32, shape, 0)
@@ -105,6 +100,7 @@
     places = jnp.sum(passed, axis=0, keepdims=True)
     listed[0:1, :] = jnp.where(order[0:1, :] < found, places, 0.0).astype(jnp.int32)
     listed[1:2, :] = ((found + (UNROLL - 1)) * (1.0 / UNROLL)).astype(jnp.int32)
+    copy.wait()
 
 
 def part_kernel(cd_tiles, listed, integrals, split, landed, sems):
@@ -152,7 +148,8 @@
         sums = []
         for unrolled in range(many):
             start, column = place_in(listed[0, first + unrolled], cd_tiles)
-            left = jnp.concatenate([piece[0, :, pl.ds(column, TILE)] for piece in pieces], axis=0)
+            rows = [piece[span, :, pl.ds(column, TILE)] for piece in pieces for span in range(piece.shape[0])]
+            left = jnp.concatenate(rows, axis=0)
             upper = left.astype(jnp.bfloat16)
             lower = (left - upper.astype(jnp.float32)).astype(jnp.bfloat16)
             tile = split[first + unrolled]
@@ -179,17 +176,20 @@
     mine, send, total = refs[-3:]
     products(cd_tiles, listed, split, pieces, total)
     half = rows * count // 2
-    for at, (span, offset) in enumerate(group):
+    at = 0
+    for offset, spans in group:
         place = place_of(count, rows, offset)
-        block = total[at * rows : (at + 1) * rows, :]
-
-        @pl.when(place < half)
-        def _():
-            mine[span, pl.ds(pl.multiple_of(place, rows), rows), :] = block
-
-        @pl.when(place >= half)
-        def _():
-            send[span, pl.ds(pl.multiple_of(place - half, rows), rows), :] = block
+        for span in spans:
+            block = total[at * rows : (at + 1) * rows, :]
+            at += 1
+
+            @pl.when(place < half)
+            def _():
+                mine[span, pl.ds(pl.multiple_of(place, rows), rows), :] = block
+
+            @pl.when(place >= half)
+            def _():
+                send[span, pl.ds(pl.multiple_of(place - half, rows), rows), :] = block
 
 
 def last_kernel(cd_tiles, listed, split, *refs):
@@ -241,28 +241,16 @@
         vmem = pl.BlockSpec(memory_space=pltpu.VMEM)
         hbm = pl.BlockSpec(memory_space=pltpu.HBM)
         params = pltpu.CompilerParams(vmem_limit_bytes=VMEM_LIMIT)
-        piece = pltpu.VMEM((1, rows, depth), jnp.float32)
-
-        labels = (block_pattern, ab_irrep, cd_irrep)
-        *own, near_pattern, near_ab, near_cd = pl.pallas_call(
-            cut_kernel,
-            out_shape=(piece,) * spans + tuple(pltpu.VMEM(label.shape, label.dtype) for label in labels),
-            in_specs=[hbm] * 4,
-            out_specs=(vmem,) * (spans + 3),
-            scratch_shapes=[pltpu.SemaphoreType.DMA((spans + 3,))],
-            compiler_params=params,
-            name="cut",
-        )(in_hbm(amplitudes), *map(in_hbm, labels))
-
-        listed = pl.pallas_call(
+        listed, own = pl.pallas_call(
             functools.partial(list_kernel, ab_tiles, cd_tiles),
-            out_shape=pltpu.VMEM((2, LANES), jnp.int32),
-            in_specs=[smem, smem, vmem],
-            out_specs=vmem,
+            out_shape=(pltpu.VMEM((2, LANES), jnp.int32), pltpu.VMEM(amplitudes.shape, jnp.float32)),
+            in_specs=[smem, smem, vmem, hbm],
+            out_specs=(vmem, vmem),
+            scratch_shapes=[pltpu.SemaphoreType.DMA],
             compiler_params=params,
             cost_estimate=pl.CostEstimate(flops=0, bytes_accessed=4 << 20, transcendentals=0),
             name="list",
-        )(near_ab, near_cd, near_pattern)
+        )(*map(in_hbm, (ab_irrep, cd_irrep, block_pattern, amplitudes)))
         split = pl.pallas_call(
             functools.partial(part_kernel, cd_tiles),
             out_shape=pltpu.VMEM((tiles, TILE, 2 * TILE), jnp.bfloat16),
@@ -274,40 +262,54 @@
             name="part",
         )(listed, in_hbm(integrals))
 
-        held = {}
-        for span in range(spans):
-            held[span, 0] = own[span]
-            for pairs, sign in ((ahead, -1), (back, 1)):
-                moved = own[span]
-                for hop in range(1, far + 1 if (sign < 0) == (span % 2 == 0) else far):
-                    if hop in (2, 3):
-                        moved, _ = lax.optimization_barrier((moved, listed if hop == 2 else split))
-                    moved = lax.ppermute(moved, "ab", pairs)
-                    held[span, -far if hop == far else sign * hop] = moved
-
-        def offset_of(span, hop, long):
-            return -hop if (span % 2 == 0) == long else hop
-
-        arrivals = [(span, 0) for span in range(spans)]
-        for hop in range(1, far):
-            arrivals += [(span, offset_of(span, hop, long)) for long in (True, False) for span in range(spans)]
         block = pltpu.VMEM((spans, half, slab), jnp.float32)
-        parts = ()
-        cuts = sorted({*range(0, len(arrivals) - spans, GROUP), len(arrivals) - spans, len(arrivals)})
-        for start, stop in zip(cuts, cuts[1:]):
-            group = arrivals[start:stop]
-            pieces = [held[key] for key in group]
-            parts = pl.pallas_call(
-                functools.partial(step_kernel, count, rows, cd_tiles, group),
+
+        def step(group, parts):
+            pieces = [piece for *_, piece in group]
+            height = sum(piece.shape[0] for piece in pieces) * rows
+            return pl.pallas_call(
+                functools.partial(step_kernel, count, rows, cd_tiles, [key for *key, _ in group]),
                 out_shape=(block, block),
                 in_specs=[smem] + [vmem] * (1 + len(pieces) + len(parts)),
                 out_specs=(vmem, vmem),
-                scratch_shapes=[pltpu.VMEM((len(pieces) * rows, slab), jnp.float32)],
+                scratch_shapes=[pltpu.VMEM((height, slab), jnp.float32)],
                 compiler_params=params,
                 input_output_aliases={2 + len(pieces): 0, 3 + len(pieces): 1} if parts else {},
                 cost_estimate=pl.CostEstimate(flops=STEP_FLOPS, bytes_accessed=4 << 20, transcendentals=0),
                 name="step",
             )(listed, split, *pieces, *parts)
+
+        both = tuple(range(spans))
+        ways = ((ahead, -1), (back, 1))
+        parts = step([(0, both, own)], ())
+        arrivals, moving = [], {}
+        for way, (pairs, sign) in enumerate(ways):
+            chunk, _ = lax.optimization_barrier((lax.ppermute(amplitudes, "ab", pairs), parts[0]))
+            arrivals.append((sign, both, chunk))
+            cut = pl.pallas_call(
+                cut_kernel,
+                out_shape=(pltpu.VMEM((1, rows, depth), jnp.float32),) * spans,
+                in_specs=[vmem],
+                out_specs=(vmem,) * spans,
+                compiler_params=params,
+                name="cut",
+            )(chunk)
+            moving.update({(way, span): cut[span] for span in both})
+        order = [(way, span) for short in (False, True) for way in range(2) for span in both if (span % 2 != way) == short]
+        final = {}
+        for hop in range(2, far + 1):
+            for way, span in order:
+                if hop < far or span % 2 == way:
+                    pairs, sign = ways[way]
+                    moving[way, span] = lax.ppermute(moving[way, span], "ab", pairs)
+                    if hop < far:
+                        arrivals.append((sign * hop, (span,), moving[way, span]))
+                    else:
+                        final[span] = moving[way, span]
+        short = len(arrivals) - spans
+        cuts = sorted({*range(0, short, GROUP), short, len(arrivals)})
+        for start, stop in zip(cuts, cuts[1:]):
+            parts = step(arrivals[start:stop], parts)
         mine, send = parts
         base = pl.pallas_call(
             merge_kernel,
@@ -326,7 +328,7 @@
             compiler_params=params,
             cost_estimate=pl.CostEstimate(flops=1 << 34, bytes_accessed=4 << 20, transcendentals=0),
             name="last",
-        )(listed, split, *[held[span, -far] for span in range(spans)])
+        )(listed, split, *[final[span] for span in both])
         return pl.pallas_call(
             functools.partial(final_kernel, count, spans, rows),
             out_shape=pltpu.HBM((spans, half, slab), jnp.float32),

time: 30.9 us -> 31.2 us (level)
  waiting for transfers between devices: 3.63 us -> 5.75 us
  starting transfers between devices: 16.4 us -> 14.8 us
    ppermute x14 -> x12, starting transfers between devices: 11.3 us -> 8.98 us  [the longest x10 6.85 us: shards(): moving[way, span] = lax.ppermute(moving[way, span], 'ab', pairs)]
    ppermute x14 -> x12, waiting for transfers between devices: 3.5 us -> 5.64 us  [the longest x10 4.37 us: shards(): moving[way, span] = lax.ppermute(moving[way, span], 'ab', pairs)]
    pallas_call x1, Pallas kernels: 1.01 us -> 1.66 us  [shards(): pl.pallas_call(functools.partial(list_kernel, ab_tiles, cd_tiles), out_sh...]
    ppermute x1, starting transfers between devices: 1.27 us -> 1.84 us  [shards(): lax.ppermute(last, 'cd', swap)]
    pallas_call x3 -> x5, Pallas kernels: 4.28 us -> 3.82 us  [the longest x3 3.78 us: step(): pl.pallas_call(functools.partial(step_kernel, count, rows, cd_tiles, [key...]
  transfers between devices with their start and end apart: 16 -> 14, of which waited for: 5 -> 7; matrix products, arithmetic and copies ran while one was open for 0% -> 0% of each run, Pallas kernels for 28% -> 31%
where the time goes in v4:
time: 31.2 us; the launch traced here: 30.9 us
  starting transfers between devices  14.8 us (47%)
  Pallas kernels  10.3 us (33%)
  waiting for transfers between devices  5.75 us (18%)
    ppermute x10, starting transfers between devices, shards(): moving[way, span] = lax.ppermute(moving[way, span], 'ab', pairs)  6.85 us
    ppermute x10, waiting for transfers between devices, shards(): moving[way, span] = lax.ppermute(moving[way, span], 'ab', pairs)  4.37 us
    ppermute x1, starting transfers between devices, shards(): lax.ppermute(send, 'cd', swap)  3.94 us
    pallas_call x3, Pallas kernels, step(): pl.pallas_call(functools.partial(step_kernel, count, rows, cd_tiles, [key...  3.78 us
    pallas_call x1, Pallas kernels, shards(): pl.pallas_call(functools.partial(part_kernel, cd_tiles), out_shape=pltpu....  2.26 us
    ppermute x2, starting transfers between devices, shards(): lax.ppermute(amplitudes, 'ab', pairs)  2.13 us
    ppermute x1, starting transfers between devices, shards(): lax.ppermute(last, 'cd', swap)  1.84 us
    pallas_call x1, Pallas kernels, shards(): pl.pallas_call(functools.partial(list_kernel, ab_tiles, cd_tiles), out_sh...  1.66 us
  transfers between devices with their start and end apart: 14, of which 7 were waited for; matrix products, arithmetic and copies ran while one was open for 0% of the time, Pallas kernels for 31%

profile of v4, /device:TPU:1, one launch (start us, length us, event | category | flops | bytes accessed | tf_op | source)
XLA Modules:
  0.0 30.9 jit_solution(648879330459221841)
XLA Ops:
  0.0 2.1 %collective-permute-start.4 = (f32[2,16,2048]{2,1,0:T(8,128)}, f32[2,16,2048]{2,1,0:T(8,128)S(1)}, u32[]{:S(2)}, u32[]{:S(2)}) collective-permute-start(f32[2,16,2048]{2,1,0:T(8,128)} %amplitudes.1), channel_id=1, source_target_pairs={{4,0},{8,4},{12,8},{14,12},{10,14},{6,10},{2,6},{0,2},{5,1},{9,5},... | collective-permute-start | bytes 786440 | tf_op jit(solution)/shard_map/ppermute | solution.py:287
  2.1 0.1 collective-permute-start
  2.1 1.7 %list.1 = (s32[2,128]{1,0:T(2,128)S(1)}, f32[2,16,2048]{2,1,0:T(8,128)S(1)}) custom-call(s32[8]{0:T(128)} %ab_irrep.1, s32[16]{0:T(128)} %cd_irrep.1, s32[8,16]{1,0:T(8,128)} %pattern.1, f32[2,16,2048]{2,1,0:T(8,128)} %amplitudes.1), custom_call_target="tpu_custom_call" | custom-call | bytes 4194304 | tf_op jit(solution)/shard_map/list/pallas_call | solution.py:244
  3.8 2.3 %part.1.split = bf16[128,128,256]{2,1,0:T(8,128)(2,1)S(1)} custom-call(s32[2,128]{1,0:T(2,128)S(1)} %get-tuple-element.19.listed, f32[1024,2048]{1,0:T(8,128)} %integrals.1), custom_call_target="tpu_custom_call" | custom-call | bytes 8388608 | tf_op jit(solution)/shard_map/part/pallas_call | solution.py:254
  6.1 1.0 %step.3 = (f32[2,64,1024]{2,1,0:T(8,128)S(1)}, f32[2,64,1024]{2,1,0:T(8,128)S(1)}) custom-call(s32[2,128]{1,0:T(2,128)S(1)} %get-tuple-element.19.listed, bf16[128,128,256]{2,1,0:T(8,128)(2,1)S(1)} %part.1.split, f32[2,16,2048]{2,1,0:T(8,128)S(1)} %get-tuple-element.20.refs_0_), custom_call_target="tpu_custom_call" | custom-call | flops 1073741824 | bytes 4194304 | tf_op jit(solution)/shard_map/step/pallas_call | solution.py:270
  7.1 1.3 %collective-permute-done.4.chunk.refs_1_ = f32[2,16,2048]{2,1,0:T(8,128)S(1)} collective-permute-done((f32[2,16,2048]{2,1,0:T(8,128)}, f32[2,16,2048]{2,1,0:T(8,128)S(1)}, u32[]{:S(2)}, u32[]{:S(2)}) %collective-permute-start.4) | collective-permute-done | bytes 262176 | tf_op jit(solution)/shard_map/ppermute | solution.py:287
  8.4 1.1 %collective-permute-start.5 = (f32[1,16,2048]{2,1,0:T(8,128)S(1)}, f32[1,16,2048]{2,1,0:T(8,128)S(1)}, u32[]{:S(2)}, u32[]{:S(2)}) collective-permute-start(f32[1,16,2048]{2,1,0:T(8,128)S(1)} %get-tuple-element.25), channel_id=1, source_target_pairs={{4,0},{8,4},{12,8},{14,12},{10,14},{6,10},{2,6},{0,2},{5,1},{9,5},... | collective-permute-start | bytes 393224 | tf_op jit(solution)/shard_map/ppermute | solution.py:304
  9.5 0.0 collective-permute-done.chunk.refs_0_
  9.6 0.4 %collective-permute-start.1 = (f32[1,16,2048]{2,1,0:T(8,128)S(1)}, f32[1,16,2048]{2,1,0:T(8,128)S(1)}, u32[]{:S(2)}, u32[]{:S(2)}) collective-permute-start(f32[1,16,2048]{2,1,0:T(8,128)S(1)} %get-tuple-element.23), channel_id=1, source_target_pairs={{0,4},{4,8},{8,12},{12,14},{14,10},{10,6},{6,2},{2,0},{1,5},{5,9},... | collective-permute-start | bytes 393224 | tf_op jit(solution)/shard_map/ppermute | solution.py:304
  10.0 1.1 %collective-permute-start.11 = (f32[1,16,2048]{2,1,0:T(8,128)S(1)}, f32[1,16,2048]{2,1,0:T(8,128)S(1)}, u32[]{:S(2)}, u32[]{:S(2)}) collective-permute-start(f32[1,16,2048]{2,1,0:T(8,128)S(1)} %get-tuple-element.27), channel_id=1, source_target_pairs={{4,0},{8,4},{12,8},{14,12},{10,14},{6,10},{2,6},{0,2},{5,1},{9,5},... | collective-permute-start | bytes 393224 | tf_op jit(solution)/shard_map/ppermute | solution.py:304
  11.1 0.4 %collective-permute-start.9 = (f32[1,16,2048]{2,1,0:T(8,128)S(1)}, f32[1,16,2048]{2,1,0:T(8,128)S(1)}, u32[]{:S(2)}, u32[]{:S(2)}) collective-permute-start(f32[1,16,2048]{2,1,0:T(8,128)S(1)} %get-tuple-element.26), channel_id=1, source_target_pairs={{0,4},{4,8},{8,12},{12,14},{14,10},{10,6},{6,2},{2,0},{1,5},{5,9},... | collective-permute-start | bytes 393224 | tf_op jit(solution)/shard_map/ppermute | solution.py:304
  11.5 0.8 %collective-permute-done.5.refs_3_ = f32[1,16,2048]{2,1,0:T(8,128)S(1)} collective-permute-done((f32[1,16,2048]{2,1,0:T(8,128)S(1)}, f32[1,16,2048]{2,1,0:T(8,128)S(1)}, u32[]{:S(2)}, u32[]{:S(2)}) %collective-permute-start.5) | collective-permute-done | bytes 131104 | tf_op jit(solution)/shard_map/ppermute | solution.py:304
  12.3 1.1 %collective-permute-start.6 = (f32[1,16,2048]{2,1,0:T(8,128)S(1)}, f32[1,16,2048]{2,1,0:T(8,128)S(1)}, u32[]{:S(2)}, u32[]{:S(2)}) collective-permute-start(f32[1,16,2048]{2,1,0:T(8,128)S(1)} %collective-permute-done.5.refs_3_), channel_id=1, source_target_pairs={{4,0},{8,4},{12,8},{14,12},{10,14},{6,10},{2,6},{0,2},{5,1},{9,5},... | collective-permute-start | bytes 393224 | tf_op jit(solution)/shard_map/ppermute | solution.py:304
  13.3 0.4 %collective-permute-done.1.refs_2_ = f32[1,16,2048]{2,1,0:T(8,128)S(1)} collective-permute-done((f32[1,16,2048]{2,1,0:T(8,128)S(1)}, f32[1,16,2048]{2,1,0:T(8,128)S(1)}, u32[]{:S(2)}, u32[]{:S(2)}) %collective-permute-start.1) | collective-permute-done | bytes 131104 | tf_op jit(solution)/shard_map/ppermute | solution.py:304
  13.7 0.1 collective-permute-start.2
  13.8 1.6 %collective-permute-done.11.refs_5_ = f32[1,16,2048]{2,1,0:T(8,128)S(1)} collective-permute-done((f32[1,16,2048]{2,1,0:T(8,128)S(1)}, f32[1,16,2048]{2,1,0:T(8,128)S(1)}, u32[]{:S(2)}, u32[]{:S(2)}) %collective-permute-start.11) | collective-permute-done | bytes 131104 | tf_op jit(solution)/shard_map/ppermute | solution.py:304
  15.4 0.8 %collective-permute-start.12 = (f32[1,16,2048]{2,1,0:T(8,128)S(1)}, f32[1,16,2048]{2,1,0:T(8,128)S(1)}, u32[]{:S(2)}, u32[]{:S(2)}) collective-permute-start(f32[1,16,2048]{2,1,0:T(8,128)S(1)} %collective-permute-done.11.refs_5_), channel_id=1, source_target_pairs={{4,0},{8,4},{12,8},{14,12},{10,14},{6,10},{2,6},{0,2},{5,1},{9,5},... | collective-permute-start | bytes 393224 | tf_op jit(solution)/shard_map/ppermute | solution.py:304
  16.2 0.0 collective-permute-done.9.refs_4_
  16.2 0.6 %collective-permute-start.10 = (f32[1,16,2048]{2,1,0:T(8,128)S(1)}, f32[1,16,2048]{2,1,0:T(8,128)S(1)}, u32[]{:S(2)}, u32[]{:S(2)}) collective-permute-start(f32[1,16,2048]{2,1,0:T(8,128)S(1)} %collective-permute-done.9.refs_4_), channel_id=1, source_target_pairs={{0,4},{4,8},{8,12},{12,14},{14,10},{10,6},{6,2},{2,0},{1,5},{5,9},... | collective-permute-start | bytes 393224 | tf_op jit(solution)/shard_map/ppermute | solution.py:304
  16.8 1.3 %collective-permute-done.6.refs_7_ = f32[1,16,2048]{2,1,0:T(8,128)S(1)} collective-permute-done((f32[1,16,2048]{2,1,0:T(8,128)S(1)}, f32[1,16,2048]{2,1,0:T(8,128)S(1)}, u32[]{:S(2)}, u32[]{:S(2)}) %collective-permute-start.6) | collective-permute-done | bytes 131104 | tf_op jit(solution)/shard_map/ppermute | solution.py:304
  18.2 0.8 %collective-permute-start.7 = (f32[1,16,2048]{2,1,0:T(8,128)S(1)}, f32[1,16,2048]{2,1,0:T(8,128)S(1)}, u32[]{:S(2)}, u32[]{:S(2)}) collective-permute-start(f32[1,16,2048]{2,1,0:T(8,128)S(1)} %collective-permute-done.6.refs_7_), channel_id=1, source_target_pairs={{4,0},{8,4},{12,8},{14,12},{10,14},{6,10},{2,6},{0,2},{5,1},{9,5},... | collective-permute-start | bytes 393224 | tf_op jit(solution)/shard_map/ppermute | solution.py:304
  19.0 0.3 collective-permute-done.2.refs_6_
  19.3 0.3 %collective-permute-start.3 = (f32[1,16,2048]{2,1,0:T(8,128)S(1)}, f32[1,16,2048]{2,1,0:T(8,128)S(1)}, u32[]{:S(2)}, u32[]{:S(2)}) collective-permute-start(f32[1,16,2048]{2,1,0:T(8,128)S(1)} %collective-permute-done.2.refs_6_), channel_id=1, source_target_pairs={{0,4},{4,8},{8,12},{12,14},{14,10},{10,6},{6,2},{2,0},{1,5},{5,9},... | collective-permute-start | bytes 393224 | tf_op jit(solution)/shard_map/ppermute | solution.py:304
  19.6 1.7 %step.4 = (f32[2,64,1024]{2,1,0:T(8,128)S(1)}, f32[2,64,1024]{2,1,0:T(8,128)S(1)}) custom-call(s32[2,128]{1,0:T(2,128)S(1)} %get-tuple-element.19.listed, bf16[128,128,256]{2,1,0:T(8,128)(2,1)S(1)} %part.1.split, f32[2,16,2048]{2,1,0:T(8,128)S(1)} %collective-permute-done.chunk.refs_0_, ...), custom_call_target="tpu_custom_call", output_to_operand_aliasing={{0}: (10, {}), {1}: (11, {})} | custom-call | flops 1073741824 | bytes 4194304 | tf_op jit(solution)/shard_map/step/pallas_call | solution.py:270
  21.4 0.0 collective-permute-done.12.refs_1_
  21.4 0.0 collective-permute-done.10.refs_0_
  21.4 1.0 %step.5 = (f32[2,64,1024]{2,1,0:T(8,128)S(1)}, f32[2,64,1024]{2,1,0:T(8,128)S(1)}) custom-call(s32[2,128]{1,0:T(2,128)S(1)} %get-tuple-element.19.listed, bf16[128,128,256]{2,1,0:T(8,128)(2,1)S(1)} %part.1.split, f32[1,16,2048]{2,1,0:T(8,128)S(1)} %collective-permute-done.10.refs_0_, ...), custom_call_target="tpu_custom_call", output_to_operand_aliasing={{0}: (4, {}), {1}: (5, {})} | custom-call | flops 1073741824 | bytes 4194304 | tf_op jit(solution)/shard_map/step/pallas_call | solution.py:270
  22.4 3.9 %collective-permute-start.13 = (f32[2,64,1024]{2,1,0:T(8,128)S(1)}, f32[2,64,1024]{2,1,0:T(8,128)S(1)}, u32[]{:S(2)}, u32[]{:S(2)}) collective-permute-start(f32[2,64,1024]{2,1,0:T(8,128)S(1)} %get-tuple-element.32), channel_id=1, source_target_pairs={{0,1},{1,0},{2,3},{3,2},{4,5},{5,4},{6,7},{7,6},{8,9},{9,8},{10,11... | collective-permute-start | bytes 1572872 | tf_op jit(solution)/shard_map/ppermute | solution.py:321
  26.4 0.0 collective-permute-done.7.refs_1_
  26.4 0.0 collective-permute-done.3.refs_0_
  26.4 1.0 %last.1 = f32[32,1024]{1,0:T(8,128)S(1)} custom-call(s32[2,128]{1,0:T(2,128)S(1)} %get-tuple-element.19.listed, bf16[128,128,256]{2,1,0:T(8,128)(2,1)S(1)} %part.1.split, f32[1,16,2048]{2,1,0:T(8,128)S(1)} %collective-permute-done.3.refs_0_, f32[1,16,2048]{2,1,0:T(8,128)S(1)} %collective-permute-done.7.refs_1_), custom_call_target="tpu_custom_call" | custom-call | flops 17179869184 | bytes 4194304 | tf_op jit(solution)/shard_map/last/pallas_call | solution.py:323
  27.3 1.8 %collective-permute-start.8 = (f32[32,1024]{1,0:T(8,128)S(1)}, f32[32,1024]{1,0:T(8,128)S(1)}, u32[]{:S(2)}, u32[]{:S(2)}) collective-permute-start(f32[32,1024]{1,0:T(8,128)S(1)} %last.1), channel_id=1, source_target_pairs={{0,1},{1,0},{2,3},{3,2},{4,5},{5,4},{6,7},{7,6},{8,9},{9,8},{10,11... | collective-permute-start | bytes 393224 | tf_op jit(solution)/shard_map/ppermute | solution.py:341
  29.2 0.0 collective-permute-done.13.received
  29.2 0.9 %merge.1.before = f32[2,64,1024]{2,1,0:T(8,128)} custom-call(f32[2,64,1024]{2,1,0:T(8,128)S(1)} %get-tuple-element.31.mine, f32[2,64,1024]{2,1,0:T(8,128)S(1)} %collective-permute-done.13.received), custom_call_target="tpu_custom_call" | custom-call | tf_op jit(solution)/shard_map/merge/pallas_call | solution.py:314
  30.1 0.1 collective-permute-done.8.received
  30.2 0.7 %final.1 = f32[2,64,1024]{2,1,0:T(8,128)} custom-call(f32[32,1024]{1,0:T(8,128)S(1)} %last.1, f32[32,1024]{1,0:T(8,128)S(1)} %collective-permute-done.8.received, f32[2,64,1024]{2,1,0:T(8,128)} %merge.1.before), custom_call_target="tpu_custom_call", output_to_operand_aliasing={{}: (2, {})} | custom-call | tf_op jit(solution)/shard_map/final/pallas_call | solution.py:332
  (2 shorter events, 0.0 us)
Async XLA Ops:
  0.0 8.4 %collective-permute-start.4 = (f32[2,16,2048]{2,1,0:T(8,128)}, f32[2,16,2048]{2,1,0:T(8,128)S(1)}, u32[]{:S(2)}, u32[]{:S(2)}) collective-permute-start(f32[2,16,2048]{2,1,0:T(8,128)} %amplitudes.1), channel_id=1, source_target_pairs={{4,0},{8,4},{12,8},{14,12},{10,14},{6,10},{2,6},{0,2},{5,1},{9,5},... | collective-permute-start | bytes 786440 | tf_op jit(solution)/shard_map/ppermute | solution.py:287
  2.1 7.5 %collective-permute-start = (f32[2,16,2048]{2,1,0:T(8,128)}, f32[2,16,2048]{2,1,0:T(8,128)S(1)}, u32[]{:S(2)}, u32[]{:S(2)}) collective-permute-start(f32[2,16,2048]{2,1,0:T(8,128)} %amplitudes.1), channel_id=1, source_target_pairs={{0,4},{4,8},{8,12},{12,14},{14,10},{10,6},{6,2},{2,0},{1,5},{5,9},... | collective-permute-start | bytes 786440 | tf_op jit(solution)/shard_map/ppermute | solution.py:287
  8.4 3.9 %collective-permute-start.5 = (f32[1,16,2048]{2,1,0:T(8,128)S(1)}, f32[1,16,2048]{2,1,0:T(8,128)S(1)}, u32[]{:S(2)}, u32[]{:S(2)}) collective-permute-start(f32[1,16,2048]{2,1,0:T(8,128)S(1)} %get-tuple-element.25), channel_id=1, source_target_pairs={{4,0},{8,4},{12,8},{14,12},{10,14},{6,10},{2,6},{0,2},{5,1},{9,5},... | collective-permute-start | bytes 393224 | tf_op jit(solution)/shard_map/ppermute | solution.py:304
  9.6 4.2 %collective-permute-start.1 = (f32[1,16,2048]{2,1,0:T(8,128)S(1)}, f32[1,16,2048]{2,1,0:T(8,128)S(1)}, u32[]{:S(2)}, u32[]{:S(2)}) collective-permute-start(f32[1,16,2048]{2,1,0:T(8,128)S(1)} %get-tuple-element.23), channel_id=1, source_target_pairs={{0,4},{4,8},{8,12},{12,14},{14,10},{10,6},{6,2},{2,0},{1,5},{5,9},... | collective-permute-start | bytes 393224 | tf_op jit(solution)/shard_map/ppermute | solution.py:304
  10.0 5.4 %collective-permute-start.11 = (f32[1,16,2048]{2,1,0:T(8,128)S(1)}, f32[1,16,2048]{2,1,0:T(8,128)S(1)}, u32[]{:S(2)}, u32[]{:S(2)}) collective-permute-start(f32[1,16,2048]{2,1,0:T(8,128)S(1)} %get-tuple-element.27), channel_id=1, source_target_pairs={{4,0},{8,4},{12,8},{14,12},{10,14},{6,10},{2,6},{0,2},{5,1},{9,5},... | collective-permute-start | bytes 393224 | tf_op jit(solution)/shard_map/ppermute | solution.py:304
  11.1 5.1 %collective-permute-start.9 = (f32[1,16,2048]{2,1,0:T(8,128)S(1)}, f32[1,16,2048]{2,1,0:T(8,128)S(1)}, u32[]{:S(2)}, u32[]{:S(2)}) collective-permute-start(f32[1,16,2048]{2,1,0:T(8,128)S(1)} %get-tuple-element.26), channel_id=1, source_target_pairs={{0,4},{4,8},{8,12},{12,14},{14,10},{10,6},{6,2},{2,0},{1,5},{5,9},... | collective-permute-start | bytes 393224 | tf_op jit(solution)/shard_map/ppermute | solution.py:304
  12.3 5.9 %collective-permute-start.6 = (f32[1,16,2048]{2,1,0:T(8,128)S(1)}, f32[1,16,2048]{2,1,0:T(8,128)S(1)}, u32[]{:S(2)}, u32[]{:S(2)}) collective-permute-start(f32[1,16,2048]{2,1,0:T(8,128)S(1)} %collective-permute-done.5.refs_3_), channel_id=1, source_target_pairs={{4,0},{8,4},{12,8},{14,12},{10,14},{6,10},{2,6},{0,2},{5,1},{9,5},... | collective-permute-start | bytes 393224 | tf_op jit(solution)/shard_map/ppermute | solution.py:304
  13.7 5.6 %collective-permute-start.2 = (f32[1,16,2048]{2,1,0:T(8,128)S(1)}, f32[1,16,2048]{2,1,0:T(8,128)S(1)}, u32[]{:S(2)}, u32[]{:S(2)}) collective-permute-start(f32[1,16,2048]{2,1,0:T(8,128)S(1)} %collective-permute-done.1.refs_2_), channel_id=1, source_target_pairs={{0,4},{4,8},{8,12},{12,14},{14,10},{10,6},{6,2},{2,0},{1,5},{5,9},... | collective-permute-start | bytes 393224 | tf_op jit(solution)/shard_map/ppermute | solution.py:304
  15.4 6.0 %collective-permute-start.12 = (f32[1,16,2048]{2,1,0:T(8,128)S(1)}, f32[1,16,2048]{2,1,0:T(8,128)S(1)}, u32[]{:S(2)}, u32[]{:S(2)}) collective-permute-start(f32[1,16,2048]{2,1,0:T(8,128)S(1)} %collective-permute-done.11.refs_5_), channel_id=1, source_target_pairs={{4,0},{8,4},{12,8},{14,12},{10,14},{6,10},{2,6},{0,2},{5,1},{9,5},... | collective-permute-start | bytes 393224 | tf_op jit(solution)/shard_map/ppermute | solution.py:304
  16.2 5.2 %collective-permute-start.10 = (f32[1,16,2048]{2,1,0:T(8,128)S(1)}, f32[1,16,2048]{2,1,0:T(8,128)S(1)}, u32[]{:S(2)}, u32[]{:S(2)}) collective-permute-start(f32[1,16,2048]{2,1,0:T(8,128)S(1)} %collective-permute-done.9.refs_4_), channel_id=1, source_target_pairs={{0,4},{4,8},{8,12},{12,14},{14,10},{10,6},{6,2},{2,0},{1,5},{5,9},... | collective-permute-start | bytes 393224 | tf_op jit(solution)/shard_map/ppermute | solution.py:304
  18.2 8.2 %collective-permute-start.7 = (f32[1,16,2048]{2,1,0:T(8,128)S(1)}, f32[1,16,2048]{2,1,0:T(8,128)S(1)}, u32[]{:S(2)}, u32[]{:S(2)}) collective-permute-start(f32[1,16,2048]{2,1,0:T(8,128)S(1)} %collective-permute-done.6.refs_7_), channel_id=1, source_target_pairs={{4,0},{8,4},{12,8},{14,12},{10,14},{6,10},{2,6},{0,2},{5,1},{9,5},... | collective-permute-start | bytes 393224 | tf_op jit(solution)/shard_map/ppermute | solution.py:304
  19.3 7.1 %collective-permute-start.3 = (f32[1,16,2048]{2,1,0:T(8,128)S(1)}, f32[1,16,2048]{2,1,0:T(8,128)S(1)}, u32[]{:S(2)}, u32[]{:S(2)}) collective-permute-start(f32[1,16,2048]{2,1,0:T(8,128)S(1)} %collective-permute-done.2.refs_6_), channel_id=1, source_target_pairs={{0,4},{4,8},{8,12},{12,14},{14,10},{10,6},{6,2},{2,0},{1,5},{5,9},... | collective-permute-start | bytes 393224 | tf_op jit(solution)/shard_map/ppermute | solution.py:304
  22.4 6.8 %collective-permute-start.13 = (f32[2,64,1024]{2,1,0:T(8,128)S(1)}, f32[2,64,1024]{2,1,0:T(8,128)S(1)}, u32[]{:S(2)}, u32[]{:S(2)}) collective-permute-start(f32[2,64,1024]{2,1,0:T(8,128)S(1)} %get-tuple-element.32), channel_id=1, source_target_pairs={{0,1},{1,0},{2,3},{3,2},{4,5},{5,4},{6,7},{7,6},{8,9},{9,8},{10,11... | collective-permute-start | bytes 1572872 | tf_op jit(solution)/shard_map/ppermute | solution.py:321
  27.3 2.8 %collective-permute-start.8 = (f32[32,1024]{1,0:T(8,128)S(1)}, f32[32,1024]{1,0:T(8,128)S(1)}, u32[]{:S(2)}, u32[]{:S(2)}) collective-permute-start(f32[32,1024]{1,0:T(8,128)S(1)} %last.1), channel_id=1, source_target_pairs={{0,1},{1,0},{2,3},{3,2},{4,5},{5,4},{6,7},{7,6},{8,9},{9,8},{10,11... | collective-permute-start | bytes 393224 | tf_op jit(solution)/shard_map/ppermute | solution.py:341

commit v5 on v4

--- a/solution.py
+++ b/solution.py
@@ -50,17 +50,22 @@
     return jnp.where(column == 0, row, rows + line * wide + step)
 
 
-def place_of(count, rows, offset):
+def place_of(count, rows, chain, hop):
     grid = grid_of(count)
     here = ring_of(lax.axis_index("ab"), *grid)
+    core = lax.axis_index("cd")
+    away = (2 * core - 1) * hop if chain == 0 else (1 - 2 * core) * hop
     whole = rows * count
-    start = at_ring((here + offset + count) % count, *grid) * rows + lax.axis_index("cd") * (whole // 2)
+    start = at_ring((here + away + count) % count, *grid) * rows + core * (whole // 2)
     return jnp.where(start >= whole, start - whole, start)
 
 
-def cut_kernel(chunk, *spans):
-    for at, span in enumerate(spans):
-        span[0] = chunk[at]
+def cut_kernel(spans, chunk, *refs):
+    outs, pack = refs[-spans - 1 : -1], refs[-1]
+    first = spans if len(refs) > spans + 1 else 0
+    for at, out in enumerate(outs):
+        out[0] = chunk[at]
+        pack[first + at] = chunk[at]
 
 
 def list_kernel(ab_tiles, cd_tiles, ab_irrep, cd_irrep, pattern, amplitudes, listed, own, own_sem):
@@ -171,14 +176,14 @@
         some((rounds - 1) * UNROLL, UNROLL)
 
 
-def step_kernel(count, rows, cd_tiles, group, listed, split, *refs):
-    pieces = refs[: len(group)]
+def step_kernel(count, rows, cd_tiles, group, many, listed, split, *refs):
+    pieces = refs[:many]
     mine, send, total = refs[-3:]
     products(cd_tiles, listed, split, pieces, total)
     half = rows * count // 2
     at = 0
-    for offset, spans in group:
-        place = place_of(count, rows, offset)
+    for chain, hop, spans in group:
+        place = place_of(count, rows, chain, hop)
         for span in spans:
             block = total[at * rows : (at + 1) * rows, :]
             at += 1
@@ -202,7 +207,7 @@
 
 def final_kernel(count, spans, rows, last, received, before, out, total, sems):
     del before
-    place = place_of(count, rows, -(count // 2))
+    place = place_of(count, rows, 0, count // 2)
 
     @pl.when(place < rows * count // 2)
     def _():
@@ -223,10 +228,19 @@
 
 def solution(mesh):
     count = mesh.shape["ab"]
+    cores = mesh.shape["cd"]
     grid = grid_of(count)
     far = count // 2
-    ahead = [(at_ring(at, *grid), at_ring((at + 1) % count, *grid)) for at in range(count)]
-    back = [(to, start) for start, to in ahead]
+
+    def around(chain, before, after):
+        pairs = []
+        for at in range(count):
+            for half in range(cores):
+                to = at + 1 if half == chain else at + count - 1
+                start, end = at_ring(at, *grid), at_ring(to % count, *grid)
+                pairs.append((start * cores + (half + before) % cores, end * cores + (half + after) % cores))
+        return pairs
+
     swap = [(0, 1), (1, 0)]
 
     def shards(amplitudes, integrals, ab_irrep, cd_irrep, block_pattern):
@@ -265,10 +279,10 @@
         block = pltpu.VMEM((spans, half, slab), jnp.float32)
 
         def step(group, parts):
-            pieces = [piece for *_, piece in group]
+            pieces = [piece for *_, piece in group if piece is not None]
             height = sum(piece.shape[0] for piece in pieces) * rows
             return pl.pallas_call(
-                functools.partial(step_kernel, count, rows, cd_tiles, [key for *key, _ in group]),
+                functools.partial(step_kernel, count, rows, cd_tiles, [key for *key, _ in group], len(pieces)),
                 out_shape=(block, block),
                 in_specs=[smem] + [vmem] * (1 + len(pieces) + len(parts)),
                 out_specs=(vmem, vmem),
@@ -279,35 +293,42 @@
                 name="step",
             )(listed, split, *pieces, *parts)
 
+        def send_on(piece, chain, hop):
+            return lax.ppermute(piece, ("ab", "cd"), around(chain, min(hop - 1, 2), min(hop, 2)))
+
         both = tuple(range(spans))
-        ways = ((ahead, -1), (back, 1))
-        parts = step([(0, both, own)], ())
-        arrivals, moving = [], {}
-        for way, (pairs, sign) in enumerate(ways):
-            chunk, _ = lax.optimization_barrier((lax.ppermute(amplitudes, "ab", pairs), parts[0]))
-            arrivals.append((sign, both, chunk))
-            cut = pl.pallas_call(
-                cut_kernel,
-                out_shape=(pltpu.VMEM((1, rows, depth), jnp.float32),) * spans,
-                in_specs=[vmem],
-                out_specs=(vmem,) * spans,
+        parts = step([(0, 0, both, own)], ())
+        pack, moving = (), {}
+        for chain in range(2):
+            chunk, _ = lax.optimization_barrier((send_on(amplitudes, chain, 1), parts[0]))
+            *cut, packed = pl.pallas_call(
+                functools.partial(cut_kernel, spans),
+                out_shape=(pltpu.VMEM((1, rows, depth), jnp.float32),) * spans
+                + (pltpu.VMEM((2 * spans, rows, depth), jnp.float32),),
+                in_specs=[vmem] * (1 + len(pack)),
+                out_specs=(vmem,) * (spans + 1),
                 compiler_params=params,
+                input_output_aliases={1: spans} if pack else {},
                 name="cut",
-            )(chunk)
-            moving.update({(way, span): cut[span] for span in both})
-        order = [(way, span) for short in (False, True) for way in range(2) for span in both if (span % 2 != way) == short]
-        final = {}
+            )(chunk, *pack)
+            pack = (packed,)
+            moving.update({(chain, span): cut[span] for span in both})
+        order = [(chain, span) for long in (True, False) for chain in range(2) for span in both if (span % 2 == chain) == long]
+        arrivals, over, final = [], [], {}
         for hop in range(2, far + 1):
-            for way, span in order:
-                if hop < far or span % 2 == way:
-                    pairs, sign = ways[way]
-                    moving[way, span] = lax.ppermute(moving[way, span], "ab", pairs)
+            for chain, span in order:
+                if hop < far or span % 2 == chain:
+                    moving[chain, span] = send_on(moving[chain, span], chain, hop)
                     if hop < far:
-                        arrivals.append((sign * hop, (span,), moving[way, span]))
+                        arrivals.append((chain, hop, (span,), moving[chain, span]))
                     else:
-                        final[span] = moving[way, span]
-        short = len(arrivals) - spans
-        cuts = sorted({*range(0, short, GROUP), short, len(arrivals)})
+                        final[span] = moving[chain, span]
+            if hop == 2:
+                packed = lax.ppermute(packed, "cd", swap)
+                over += [(0, 1, both, packed), (1, 1, both, None)]
+        late = len(arrivals) - spans
+        arrivals += over
+        cuts = sorted({*range(0, late, GROUP), late, len(arrivals)})
         for start, stop in zip(cuts, cuts[1:]):
             parts = step(arrivals[start:stop], parts)
         mine, send = parts

time: 31.2 us -> 31.7 us (1.016)
  starting transfers between devices: 14.8 us -> 19.1 us
  waiting for transfers between devices: 5.75 us -> 1.97 us
    ppermute x12 -> x13, starting transfers between devices: 8.98 us -> 17 us  [the longest x12 15.8 us: send_on(): lax.ppermute(piece, ('ab', 'cd'), around(chain, min(hop - 1, 2), min(hop,...]
    ppermute x12 -> x13, waiting for transfers between devices: 5.64 us -> 1.85 us  [the longest x12 1.85 us: send_on(): lax.ppermute(piece, ('ab', 'cd'), around(chain, min(hop - 1, 2), min(hop,...]
    ppermute x1, starting transfers between devices: 3.94 us -> 1.38 us  [shards(): lax.ppermute(send, 'cd', swap)]
    ppermute x1, starting transfers between devices: 1.84 us -> 0.73 us  [shards(): lax.ppermute(last, 'cd', swap)]
  transfers between devices with their start and end apart: 14 -> 15, of which waited for: 7 -> 6; matrix products, arithmetic and copies ran while one was open for 0% -> 0% of each run, Pallas kernels for 31% -> 30%
where the time goes in v5:
time: 31.7 us; the launch traced here: 31.4 us
  starting transfers between devices  19.1 us (60%)
  Pallas kernels  10.2 us (32%)
  waiting for transfers between devices  1.97 us (6%)
    ppermute x12, starting transfers between devices, send_on(): lax.ppermute(piece, ('ab', 'cd'), around(chain, min(hop - 1, 2), min(hop,...  15.8 us
    pallas_call x3, Pallas kernels, step(): pl.pallas_call(functools.partial(step_kernel, count, rows, cd_tiles, [key...  3.71 us
    pallas_call x1, Pallas kernels, shards(): pl.pallas_call(functools.partial(part_kernel, cd_tiles), out_shape=pltpu....  2.26 us
    ppermute x12, waiting for transfers between devices, send_on(): lax.ppermute(piece, ('ab', 'cd'), around(chain, min(hop - 1, 2), min(hop,...  1.85 us
    pallas_call x1, Pallas kernels, shards(): pl.pallas_call(functools.partial(list_kernel, ab_tiles, cd_tiles), out_sh...  1.66 us
    ppermute x1, starting transfers between devices, shards(): lax.ppermute(send, 'cd', swap)  1.38 us
    ppermute x1, starting transfers between devices, shards(): packed = lax.ppermute(packed, 'cd', swap)  1.26 us
    pallas_call x1, Pallas kernels, shards(): pl.pallas_call(functools.partial(last_kernel, cd_tiles), out_shape=pltpu....  0.97 us
  transfers between devices with their start and end apart: 15, of which 6 were waited for; matrix products, arithmetic and copies ran while one was open for 0% of the time, Pallas kernels for 30%

profile of v5, /device:TPU:1, one launch (start us, length us, event | category | flops | bytes accessed | tf_op | source)
XLA Modules:
  0.0 31.4 jit_solution(7566561955191978622)
XLA Ops:
  0.0 2.6 %collective-permute-start = (f32[2,16,2048]{2,1,0:T(8,128)}, f32[2,16,2048]{2,1,0:T(8,128)S(1)}, u32[]{:S(2)}, u32[]{:S(2)}) collective-permute-start(f32[2,16,2048]{2,1,0:T(8,128)} %amplitudes.1), channel_id=1, source_target_pairs={{0,5},{1,2},{4,9},{5,0},{8,13},{9,4},{12,15},{13,8},{14,11},{15,12... | collective-permute-start | bytes 786440 | tf_op jit(solution)/shard_map/ppermute | solution.py:297
  2.6 1.1 %collective-permute-start.4 = (f32[2,16,2048]{2,1,0:T(8,128)}, f32[2,16,2048]{2,1,0:T(8,128)S(1)}, u32[]{:S(2)}, u32[]{:S(2)}) collective-permute-start(f32[2,16,2048]{2,1,0:T(8,128)} %amplitudes.1), channel_id=1, source_target_pairs={{0,3},{1,4},{4,1},{5,8},{8,5},{9,12},{12,9},{13,14},{14,13},{15,10... | collective-permute-start | bytes 786440 | tf_op jit(solution)/shard_map/ppermute | solution.py:297
  3.7 1.7 %list.1 = (s32[2,128]{1,0:T(2,128)S(1)}, f32[2,16,2048]{2,1,0:T(8,128)S(1)}) custom-call(s32[8]{0:T(128)} %ab_irrep.1, s32[16]{0:T(128)} %cd_irrep.1, s32[8,16]{1,0:T(8,128)} %pattern.1, f32[2,16,2048]{2,1,0:T(8,128)} %amplitudes.1), custom_call_target="tpu_custom_call" | custom-call | bytes 4194304 | tf_op jit(solution)/shard_map/list/pallas_call | solution.py:258
  5.4 2.3 %part.1.split = bf16[128,128,256]{2,1,0:T(8,128)(2,1)S(1)} custom-call(s32[2,128]{1,0:T(2,128)S(1)} %get-tuple-element.21.listed, f32[1024,2048]{1,0:T(8,128)} %integrals.1), custom_call_target="tpu_custom_call" | custom-call | bytes 8388608 | tf_op jit(solution)/shard_map/part/pallas_call | solution.py:268
  7.6 1.0 %step.3 = (f32[2,64,1024]{2,1,0:T(8,128)S(1)}, f32[2,64,1024]{2,1,0:T(8,128)S(1)}) custom-call(s32[2,128]{1,0:T(2,128)S(1)} %get-tuple-element.21.listed, bf16[128,128,256]{2,1,0:T(8,128)(2,1)S(1)} %part.1.split, f32[2,16,2048]{2,1,0:T(8,128)S(1)} %get-tuple-element.22.refs_0_), custom_call_target="tpu_custom_call" | custom-call | flops 1073741824 | bytes 4194304 | tf_op jit(solution)/shard_map/step/pallas_call | solution.py:284
  8.7 0.3 collective-permute-done.chunk
  9.0 0.2 collective-permute-done.4.chunk
  9.2 1.3 %collective-permute-start.13 = (f32[4,16,2048]{2,1,0:T(8,128)S(1)}, f32[4,16,2048]{2,1,0:T(8,128)S(1)}, u32[]{:S(2)}, u32[]{:S(2)}) collective-permute-start(f32[4,16,2048]{2,1,0:T(8,128)S(1)} %get-tuple-element.31), channel_id=1, source_target_pairs={{0,1},{1,0},{2,3},{3,2},{4,5},{5,4},{6,7},{7,6},{8,9},{9,8},{10,11... | collective-permute-start | bytes 1572872 | tf_op jit(solution)/shard_map/ppermute | solution.py:327
  10.5 1.3 %collective-permute-start.5 = (f32[1,16,2048]{2,1,0:T(8,128)S(1)}, f32[1,16,2048]{2,1,0:T(8,128)S(1)}, u32[]{:S(2)}, u32[]{:S(2)}) collective-permute-start(f32[1,16,2048]{2,1,0:T(8,128)S(1)} %get-tuple-element.28), channel_id=1, source_target_pairs={{1,2},{0,5},{5,0},{4,9},{9,4},{8,13},{13,8},{12,15},{15,12},{14,11... | collective-permute-start | bytes 393224 | tf_op jit(solution)/shard_map/ppermute | solution.py:297
  11.8 1.6 %collective-permute-start.1 = (f32[1,16,2048]{2,1,0:T(8,128)S(1)}, f32[1,16,2048]{2,1,0:T(8,128)S(1)}, u32[]{:S(2)}, u32[]{:S(2)}) collective-permute-start(f32[1,16,2048]{2,1,0:T(8,128)S(1)} %get-tuple-element.25), channel_id=1, source_target_pairs={{1,4},{0,3},{5,8},{4,1},{9,12},{8,5},{13,14},{12,9},{15,10},{14,13... | collective-permute-start | bytes 393224 | tf_op jit(solution)/shard_map/ppermute | solution.py:297
  13.3 1.3 %collective-permute-start.11 = (f32[1,16,2048]{2,1,0:T(8,128)S(1)}, f32[1,16,2048]{2,1,0:T(8,128)S(1)}, u32[]{:S(2)}, u32[]{:S(2)}) collective-permute-start(f32[1,16,2048]{2,1,0:T(8,128)S(1)} %get-tuple-element.30), channel_id=1, source_target_pairs={{1,2},{0,5},{5,0},{4,9},{9,4},{8,13},{13,8},{12,15},{15,12},{14,11... | collective-permute-start | bytes 393224 | tf_op jit(solution)/shard_map/ppermute | solution.py:297
  14.7 1.5 %collective-permute-start.9 = (f32[1,16,2048]{2,1,0:T(8,128)S(1)}, f32[1,16,2048]{2,1,0:T(8,128)S(1)}, u32[]{:S(2)}, u32[]{:S(2)}) collective-permute-start(f32[1,16,2048]{2,1,0:T(8,128)S(1)} %get-tuple-element.29), channel_id=1, source_target_pairs={{1,4},{0,3},{5,8},{4,1},{9,12},{8,5},{13,14},{12,9},{15,10},{14,13... | collective-permute-start | bytes 393224 | tf_op jit(solution)/shard_map/ppermute | solution.py:297
  16.1 0.0 collective-permute-done.5.refs_1_
  16.1 0.7 %collective-permute-start.6 = (f32[1,16,2048]{2,1,0:T(8,128)S(1)}, f32[1,16,2048]{2,1,0:T(8,128)S(1)}, u32[]{:S(2)}, u32[]{:S(2)}) collective-permute-start(f32[1,16,2048]{2,1,0:T(8,128)S(1)} %collective-permute-done.5.refs_1_), channel_id=1, source_target_pairs={{0,2},{1,5},{4,0},{5,9},{8,4},{9,13},{12,8},{13,15},{14,12},{15,11... | collective-permute-start | bytes 393224 | tf_op jit(solution)/shard_map/ppermute | solution.py:297
  16.8 0.0 collective-permute-done.1.refs_0_
  16.8 1.3 %collective-permute-start.2 = (f32[1,16,2048]{2,1,0:T(8,128)S(1)}, f32[1,16,2048]{2,1,0:T(8,128)S(1)}, u32[]{:S(2)}, u32[]{:S(2)}) collective-permute-start(f32[1,16,2048]{2,1,0:T(8,128)S(1)} %collective-permute-done.1.refs_0_), channel_id=1, source_target_pairs={{0,4},{1,3},{4,8},{5,1},{8,12},{9,5},{12,14},{13,9},{14,10},{15,13... | collective-permute-start | bytes 393224 | tf_op jit(solution)/shard_map/ppermute | solution.py:297
  18.1 0.3 collective-permute-done.11.refs_3_
  18.4 1.4 %collective-permute-start.12 = (f32[1,16,2048]{2,1,0:T(8,128)S(1)}, f32[1,16,2048]{2,1,0:T(8,128)S(1)}, u32[]{:S(2)}, u32[]{:S(2)}) collective-permute-start(f32[1,16,2048]{2,1,0:T(8,128)S(1)} %collective-permute-done.11.refs_3_), channel_id=1, source_target_pairs={{0,2},{1,5},{4,0},{5,9},{8,4},{9,13},{12,8},{13,15},{14,12},{15,11... | collective-permute-start | bytes 393224 | tf_op jit(solution)/shard_map/ppermute | solution.py:297
  19.8 0.0 collective-permute-done.9.refs_2_
  19.8 0.8 %collective-permute-start.10 = (f32[1,16,2048]{2,1,0:T(8,128)S(1)}, f32[1,16,2048]{2,1,0:T(8,128)S(1)}, u32[]{:S(2)}, u32[]{:S(2)}) collective-permute-start(f32[1,16,2048]{2,1,0:T(8,128)S(1)} %collective-permute-done.9.refs_2_), channel_id=1, source_target_pairs={{0,4},{1,3},{4,8},{5,1},{8,12},{9,5},{12,14},{13,9},{14,10},{15,13... | collective-permute-start | bytes 393224 | tf_op jit(solution)/shard_map/ppermute | solution.py:297
  20.6 0.8 %collective-permute-done.6.refs_5_ = f32[1,16,2048]{2,1,0:T(8,128)S(1)} collective-permute-done((f32[1,16,2048]{2,1,0:T(8,128)S(1)}, f32[1,16,2048]{2,1,0:T(8,128)S(1)}, u32[]{:S(2)}, u32[]{:S(2)}) %collective-permute-start.6) | collective-permute-done | bytes 131104 | tf_op jit(solution)/shard_map/ppermute | solution.py:297
  21.4 1.4 %collective-permute-start.7 = (f32[1,16,2048]{2,1,0:T(8,128)S(1)}, f32[1,16,2048]{2,1,0:T(8,128)S(1)}, u32[]{:S(2)}, u32[]{:S(2)}) collective-permute-start(f32[1,16,2048]{2,1,0:T(8,128)S(1)} %collective-permute-done.6.refs_5_), channel_id=1, source_target_pairs={{0,2},{1,5},{4,0},{5,9},{8,4},{9,13},{12,8},{13,15},{14,12},{15,11... | collective-permute-start | bytes 393224 | tf_op jit(solution)/shard_map/ppermute | solution.py:297
  22.8 0.0 collective-permute-done.2.refs_4_
  22.8 0.9 %collective-permute-start.3 = (f32[1,16,2048]{2,1,0:T(8,128)S(1)}, f32[1,16,2048]{2,1,0:T(8,128)S(1)}, u32[]{:S(2)}, u32[]{:S(2)}) collective-permute-start(f32[1,16,2048]{2,1,0:T(8,128)S(1)} %collective-permute-done.2.refs_4_), channel_id=1, source_target_pairs={{0,4},{1,3},{4,8},{5,1},{8,12},{9,5},{12,14},{13,9},{14,10},{15,13... | collective-permute-start | bytes 393224 | tf_op jit(solution)/shard_map/ppermute | solution.py:297
  23.7 1.3 %step.4 = (f32[2,64,1024]{2,1,0:T(8,128)S(1)}, f32[2,64,1024]{2,1,0:T(8,128)S(1)}) custom-call(s32[2,128]{1,0:T(2,128)S(1)} %get-tuple-element.21.listed, bf16[128,128,256]{2,1,0:T(8,128)(2,1)S(1)} %part.1.split, f32[1,16,2048]{2,1,0:T(8,128)S(1)} %collective-permute-done.1.refs_0_, ...), custom_call_target="tpu_custom_call", output_to_operand_aliasing={{0}: (8, {}), {1}: (9, {})} | custom-call | flops 1073741824 | bytes 4194304 | tf_op jit(solution)/shard_map/step/pallas_call | solution.py:284
  25.1 0.0 collective-permute-done.12.refs_1_
  25.1 0.0 collective-permute-done.10.refs_0_
  25.1 0.0 collective-permute-done.13.refs_2_
  25.1 1.3 %step.5 = (f32[2,64,1024]{2,1,0:T(8,128)S(1)}, f32[2,64,1024]{2,1,0:T(8,128)S(1)}) custom-call(s32[2,128]{1,0:T(2,128)S(1)} %get-tuple-element.21.listed, bf16[128,128,256]{2,1,0:T(8,128)(2,1)S(1)} %part.1.split, f32[1,16,2048]{2,1,0:T(8,128)S(1)} %collective-permute-done.10.refs_0_, ...), custom_call_target="tpu_custom_call", output_to_operand_aliasing={{0}: (5, {}), {1}: (6, {})} | custom-call | flops 1073741824 | bytes 4194304 | tf_op jit(solution)/shard_map/step/pallas_call | solution.py:284
  26.4 1.4 %collective-permute-start.14 = (f32[2,64,1024]{2,1,0:T(8,128)S(1)}, f32[2,64,1024]{2,1,0:T(8,128)S(1)}, u32[]{:S(2)}, u32[]{:S(2)}) collective-permute-start(f32[2,64,1024]{2,1,0:T(8,128)S(1)} %get-tuple-element.36), channel_id=1, source_target_pairs={{0,1},{1,0},{2,3},{3,2},{4,5},{5,4},{6,7},{7,6},{8,9},{9,8},{10,11... | collective-permute-start | bytes 1572872 | tf_op jit(solution)/shard_map/ppermute | solution.py:342
  27.8 0.0 collective-permute-done.7.refs_1_
  27.8 0.2 collective-permute-done.3.refs_0_
  28.0 1.0 %last.1 = f32[32,1024]{1,0:T(8,128)S(1)} custom-call(s32[2,128]{1,0:T(2,128)S(1)} %get-tuple-element.21.listed, bf16[128,128,256]{2,1,0:T(8,128)(2,1)S(1)} %part.1.split, f32[1,16,2048]{2,1,0:T(8,128)S(1)} %collective-permute-done.3.refs_0_, f32[1,16,2048]{2,1,0:T(8,128)S(1)} %collective-permute-done.7.refs_1_), custom_call_target="tpu_custom_call" | custom-call | flops 17179869184 | bytes 4194304 | tf_op jit(solution)/shard_map/last/pallas_call | solution.py:344
  29.0 0.7 %collective-permute-start.8 = (f32[32,1024]{1,0:T(8,128)S(1)}, f32[32,1024]{1,0:T(8,128)S(1)}, u32[]{:S(2)}, u32[]{:S(2)}) collective-permute-start(f32[32,1024]{1,0:T(8,128)S(1)} %last.1), channel_id=1, source_target_pairs={{0,1},{1,0},{2,3},{3,2},{4,5},{5,4},{6,7},{7,6},{8,9},{9,8},{10,11... | collective-permute-start | bytes 393224 | tf_op jit(solution)/shard_map/ppermute | solution.py:362
  29.7 0.0 collective-permute-done.14.received
  29.7 0.9 %merge.1.before = f32[2,64,1024]{2,1,0:T(8,128)} custom-call(f32[2,64,1024]{2,1,0:T(8,128)S(1)} %get-tuple-element.35.mine, f32[2,64,1024]{2,1,0:T(8,128)S(1)} %collective-permute-done.14.received), custom_call_target="tpu_custom_call" | custom-call | tf_op jit(solution)/shard_map/merge/pallas_call | solution.py:335
  30.6 0.1 collective-permute-done.8.received
  30.7 0.7 %final.1 = f32[2,64,1024]{2,1,0:T(8,128)} custom-call(f32[32,1024]{1,0:T(8,128)S(1)} %last.1, f32[32,1024]{1,0:T(8,128)S(1)} %collective-permute-done.8.received, f32[2,64,1024]{2,1,0:T(8,128)} %merge.1.before), custom_call_target="tpu_custom_call", output_to_operand_aliasing={{}: (2, {})} | custom-call | tf_op jit(solution)/shard_map/final/pallas_call | solution.py:353
  (2 shorter events, 0.1 us)
Async XLA Ops:
  0.0 9.0 %collective-permute-start = (f32[2,16,2048]{2,1,0:T(8,128)}, f32[2,16,2048]{2,1,0:T(8,128)S(1)}, u32[]{:S(2)}, u32[]{:S(2)}) collective-permute-start(f32[2,16,2048]{2,1,0:T(8,128)} %amplitudes.1), channel_id=1, source_target_pairs={{0,5},{1,2},{4,9},{5,0},{8,13},{9,4},{12,15},{13,8},{14,11},{15,12... | collective-permute-start | bytes 786440 | tf_op jit(solution)/shard_map/ppermute | solution.py:297
  2.6 6.6 %collective-permute-start.4 = (f32[2,16,2048]{2,1,0:T(8,128)}, f32[2,16,2048]{2,1,0:T(8,128)S(1)}, u32[]{:S(2)}, u32[]{:S(2)}) collective-permute-start(f32[2,16,2048]{2,1,0:T(8,128)} %amplitudes.1), channel_id=1, source_target_pairs={{0,3},{1,4},{4,1},{5,8},{8,5},{9,12},{12,9},{13,14},{14,13},{15,10... | collective-permute-start | bytes 786440 | tf_op jit(solution)/shard_map/ppermute | solution.py:297
  9.2 15.8 %collective-permute-start.13 = (f32[4,16,2048]{2,1,0:T(8,128)S(1)}, f32[4,16,2048]{2,1,0:T(8,128)S(1)}, u32[]{:S(2)}, u32[]{:S(2)}) collective-permute-start(f32[4,16,2048]{2,1,0:T(8,128)S(1)} %get-tuple-element.31), channel_id=1, source_target_pairs={{0,1},{1,0},{2,3},{3,2},{4,5},{5,4},{6,7},{7,6},{8,9},{9,8},{10,11... | collective-permute-start | bytes 1572872 | tf_op jit(solution)/shard_map/ppermute | solution.py:327
  10.5 5.6 %collective-permute-start.5 = (f32[1,16,2048]{2,1,0:T(8,128)S(1)}, f32[1,16,2048]{2,1,0:T(8,128)S(1)}, u32[]{:S(2)}, u32[]{:S(2)}) collective-permute-start(f32[1,16,2048]{2,1,0:T(8,128)S(1)} %get-tuple-element.28), channel_id=1, source_target_pairs={{1,2},{0,5},{5,0},{4,9},{9,4},{8,13},{13,8},{12,15},{15,12},{14,11... | collective-permute-start | bytes 393224 | tf_op jit(solution)/shard_map/ppermute | solution.py:297
  11.8 5.1 %collective-permute-start.1 = (f32[1,16,2048]{2,1,0:T(8,128)S(1)}, f32[1,16,2048]{2,1,0:T(8,128)S(1)}, u32[]{:S(2)}, u32[]{:S(2)}) collective-permute-start(f32[1,16,2048]{2,1,0:T(8,128)S(1)} %get-tuple-element.25), channel_id=1, source_target_pairs={{1,4},{0,3},{5,8},{4,1},{9,12},{8,5},{13,14},{12,9},{15,10},{14,13... | collective-permute-start | bytes 393224 | tf_op jit(solution)/shard_map/ppermute | solution.py:297
  13.3 5.1 %collective-permute-start.11 = (f32[1,16,2048]{2,1,0:T(8,128)S(1)}, f32[1,16,2048]{2,1,0:T(8,128)S(1)}, u32[]{:S(2)}, u32[]{:S(2)}) collective-permute-start(f32[1,16,2048]{2,1,0:T(8,128)S(1)} %get-tuple-element.30), channel_id=1, source_target_pairs={{1,2},{0,5},{5,0},{4,9},{9,4},{8,13},{13,8},{12,15},{15,12},{14,11... | collective-permute-start | bytes 393224 | tf_op jit(solution)/shard_map/ppermute | solution.py:297
  14.7 5.2 %collective-permute-start.9 = (f32[1,16,2048]{2,1,0:T(8,128)S(1)}, f32[1,16,2048]{2,1,0:T(8,128)S(1)}, u32[]{:S(2)}, u32[]{:S(2)}) collective-permute-start(f32[1,16,2048]{2,1,0:T(8,128)S(1)} %get-tuple-element.29), channel_id=1, source_target_pairs={{1,4},{0,3},{5,8},{4,1},{9,12},{8,5},{13,14},{12,9},{15,10},{14,13... | collective-permute-start | bytes 393224 | tf_op jit(solution)/shard_map/ppermute | solution.py:297
  16.1 5.3 %collective-permute-start.6 = (f32[1,16,2048]{2,1,0:T(8,128)S(1)}, f32[1,16,2048]{2,1,0:T(8,128)S(1)}, u32[]{:S(2)}, u32[]{:S(2)}) collective-permute-start(f32[1,16,2048]{2,1,0:T(8,128)S(1)} %collective-permute-done.5.refs_1_), channel_id=1, source_target_pairs={{0,2},{1,5},{4,0},{5,9},{8,4},{9,13},{12,8},{13,15},{14,12},{15,11... | collective-permute-start | bytes 393224 | tf_op jit(solution)/shard_map/ppermute | solution.py:297
  16.8 5.9 %collective-permute-start.2 = (f32[1,16,2048]{2,1,0:T(8,128)S(1)}, f32[1,16,2048]{2,1,0:T(8,128)S(1)}, u32[]{:S(2)}, u32[]{:S(2)}) collective-permute-start(f32[1,16,2048]{2,1,0:T(8,128)S(1)} %collective-permute-done.1.refs_0_), channel_id=1, source_target_pairs={{0,4},{1,3},{4,8},{5,1},{8,12},{9,5},{12,14},{13,9},{14,10},{15,13... | collective-permute-start | bytes 393224 | tf_op jit(solution)/shard_map/ppermute | solution.py:297
  18.4 6.7 %collective-permute-start.12 = (f32[1,16,2048]{2,1,0:T(8,128)S(1)}, f32[1,16,2048]{2,1,0:T(8,128)S(1)}, u32[]{:S(2)}, u32[]{:S(2)}) collective-permute-start(f32[1,16,2048]{2,1,0:T(8,128)S(1)} %collective-permute-done.11.refs_3_), channel_id=1, source_target_pairs={{0,2},{1,5},{4,0},{5,9},{8,4},{9,13},{12,8},{13,15},{14,12},{15,11... | collective-permute-start | bytes 393224 | tf_op jit(solution)/shard_map/ppermute | solution.py:297
  19.8 5.3 %collective-permute-start.10 = (f32[1,16,2048]{2,1,0:T(8,128)S(1)}, f32[1,16,2048]{2,1,0:T(8,128)S(1)}, u32[]{:S(2)}, u32[]{:S(2)}) collective-permute-start(f32[1,16,2048]{2,1,0:T(8,128)S(1)} %collective-permute-done.9.refs_2_), channel_id=1, source_target_pairs={{0,4},{1,3},{4,8},{5,1},{8,12},{9,5},{12,14},{13,9},{14,10},{15,13... | collective-permute-start | bytes 393224 | tf_op jit(solution)/shard_map/ppermute | solution.py:297
  21.4 6.4 %collective-permute-start.7 = (f32[1,16,2048]{2,1,0:T(8,128)S(1)}, f32[1,16,2048]{2,1,0:T(8,128)S(1)}, u32[]{:S(2)}, u32[]{:S(2)}) collective-permute-start(f32[1,16,2048]{2,1,0:T(8,128)S(1)} %collective-permute-done.6.refs_5_), channel_id=1, source_target_pairs={{0,2},{1,5},{4,0},{5,9},{8,4},{9,13},{12,8},{13,15},{14,12},{15,11... | collective-permute-start | bytes 393224 | tf_op jit(solution)/shard_map/ppermute | solution.py:297
  22.8 5.3 %collective-permute-start.3 = (f32[1,16,2048]{2,1,0:T(8,128)S(1)}, f32[1,16,2048]{2,1,0:T(8,128)S(1)}, u32[]{:S(2)}, u32[]{:S(2)}) collective-permute-start(f32[1,16,2048]{2,1,0:T(8,128)S(1)} %collective-permute-done.2.refs_4_), channel_id=1, source_target_pairs={{0,4},{1,3},{4,8},{5,1},{8,12},{9,5},{12,14},{13,9},{14,10},{15,13... | collective-permute-start | bytes 393224 | tf_op jit(solution)/shard_map/ppermute | solution.py:297
  26.4 3.3 %collective-permute-start.14 = (f32[2,64,1024]{2,1,0:T(8,128)S(1)}, f32[2,64,1024]{2,1,0:T(8,128)S(1)}, u32[]{:S(2)}, u32[]{:S(2)}) collective-permute-start(f32[2,64,1024]{2,1,0:T(8,128)S(1)} %get-tuple-element.36), channel_id=1, source_target_pairs={{0,1},{1,0},{2,3},{3,2},{4,5},{5,4},{6,7},{7,6},{8,9},{9,8},{10,11... | collective-permute-start | bytes 1572872 | tf_op jit(solution)/shard_map/ppermute | solution.py:342
  29.0 1.7 %collective-permute-start.8 = (f32[32,1024]{1,0:T(8,128)S(1)}, f32[32,1024]{1,0:T(8,128)S(1)}, u32[]{:S(2)}, u32[]{:S(2)}) collective-permute-start(f32[32,1024]{1,0:T(8,128)S(1)} %last.1), channel_id=1, source_target_pairs={{0,1},{1,0},{2,3},{3,2},{4,5},{5,4},{6,7},{7,6},{8,9},{9,8},{10,11... | collective-permute-start | bytes 393224 | tf_op jit(solution)/shard_map/ppermute | solution.py:362

commit v6 on v5

--- a/solution.py
+++ b/solution.py
@@ -179,6 +179,9 @@
 def step_kernel(count, rows, cd_tiles, group, many, listed, split, *refs):
     pieces = refs[:many]
     mine, send, total = refs[-3:]
+    if len(refs) == many + 3:
+        mine[...] = jnp.zeros_like(mine)
+        send[...] = jnp.zeros_like(send)
     products(cd_tiles, listed, split, pieces, total)
     half = rows * count // 2
     at = 0
@@ -201,28 +204,46 @@
     products(cd_tiles, listed, split, refs[:-1], refs[-1])
 
 
-def merge_kernel(mine, received, out):
-    out[...] = mine[...] + received[...]
-
-
-def final_kernel(count, spans, rows, last, received, before, out, total, sems):
+def merge_kernel(mine, received, base, out):
+    base[...] = mine[...] + received[...]
+    out[...] = base[...]
+
+
+def final_kernel(count, rows, keys, last, received, base, before, out, total, sems):
     del before
-    place = place_of(count, rows, 0, count // 2)
-
-    @pl.when(place < rows * count // 2)
-    def _():
-        total[...] = last[...] + received[...]
-        copies = []
-        for span in range(spans):
-            copies.append(
-                pltpu.make_async_copy(
-                    total.at[pl.ds(span * rows, rows), :],
-                    out.at[span, pl.ds(pl.multiple_of(place, rows), rows), :],
-                    sems.at[span],
-                )
-            )
-            copies[-1].start()
-        for copy in copies:
+    far = count // 2
+    half = rows * far
+
+    def block(at):
+        return pl.ds(at * rows, rows)
+
+    def put(slot, key_hop, chain, span, value):
+        place = place_of(count, rows, chain, key_hop)
+
+        def to():
+            return out.at[span, pl.ds(pl.multiple_of(place, rows), rows), :]
+
+        copy = pltpu.make_async_copy(total.at[block(slot), :], to(), sems.at[slot])
+
+        @pl.when(place < half)
+        def _():
+            rest = base[span, pl.ds(pl.multiple_of(place, rows), rows), :]
+            total[block(slot), :] = rest + value()
+            copy.start()
+
+        return place < half, copy
+
+    copies = []
+    for at, (chain, hop, span) in enumerate(keys):
+        if hop == far:
+            copies.append(put(len(copies), hop, chain, span, lambda at=at: last[block(at), :] + received[block(at), :]))
+        else:
+            copies.append(put(len(copies), hop, chain, span, lambda at=at: last[block(at), :]))
+            copies.append(put(len(copies), hop, 1 - chain, span, lambda at=at: received[block(at), :]))
+    for here, copy in copies:
+
+        @pl.when(here)
+        def _():
             copy.wait()
 
 
@@ -314,52 +335,53 @@
             pack = (packed,)
             moving.update({(chain, span): cut[span] for span in both})
         order = [(chain, span) for long in (True, False) for chain in range(2) for span in both if (span % 2 == chain) == long]
-        arrivals, over, final = [], [], {}
+        arrivals, closing = [], []
         for hop in range(2, far + 1):
             for chain, span in order:
-                if hop < far or span % 2 == chain:
-                    moving[chain, span] = send_on(moving[chain, span], chain, hop)
-                    if hop < far:
-                        arrivals.append((chain, hop, (span,), moving[chain, span]))
-                    else:
-                        final[span] = moving[chain, span]
+                long = span % 2 == chain
+                if hop < far or long:
+                    piece = moving[chain, span] = send_on(moving[chain, span], chain, hop)
+                    ends = hop == far or (hop == far - 1 and not long)
+                    (closing if ends else arrivals).append((chain, hop, (span,), piece))
             if hop == 2:
                 packed = lax.ppermute(packed, "cd", swap)
-                over += [(0, 1, both, packed), (1, 1, both, None)]
-        late = len(arrivals) - spans
-        arrivals += over
-        cuts = sorted({*range(0, late, GROUP), late, len(arrivals)})
-        for start, stop in zip(cuts, cuts[1:]):
-            parts = step(arrivals[start:stop], parts)
+                arrivals += [(0, 1, both, packed), (1, 1, both, None)]
+        for start in range(0, len(arrivals), GROUP):
+            parts = step(arrivals[start : start + GROUP], parts)
         mine, send = parts
-        base = pl.pallas_call(
+        base, out = pl.pallas_call(
             merge_kernel,
-            out_shape=pltpu.HBM((spans, half, slab), jnp.float32),
+            out_shape=(
+                pltpu.VMEM((spans, half, slab), jnp.float32),
+                pltpu.HBM((spans, half, slab), jnp.float32),
+            ),
             in_specs=[vmem, vmem],
-            out_specs=vmem,
+            out_specs=(vmem, vmem),
             compiler_params=params,
             name="merge",
         )(mine, lax.ppermute(send, "cd", swap))
 
+        keys = [(chain, hop, some[0]) for chain, hop, some, _ in closing]
         last = pl.pallas_call(
             functools.partial(last_kernel, cd_tiles),
-            out_shape=pltpu.VMEM((spans * rows, slab), jnp.float32),
-            in_specs=[smem, vmem] + [vmem] * spans,
+            out_shape=pltpu.VMEM((len(keys) * rows, slab), jnp.float32),
+            in_specs=[smem, vmem] + [vmem] * len(keys),
             out_specs=vmem,
             compiler_params=params,
             cost_estimate=pl.CostEstimate(flops=1 << 34, bytes_accessed=4 << 20, transcendentals=0),
             name="last",
-        )(listed, split, *[final[span] for span in both])
+        )(listed, split, *[piece for *_, piece in closing])
+        blocks = sum(1 if hop == far else 2 for _, hop, _ in keys)
         return pl.pallas_call(
-            functools.partial(final_kernel, count, spans, rows),
+            functools.partial(final_kernel, count, rows, keys),
             out_shape=pltpu.HBM((spans, half, slab), jnp.float32),
-            in_specs=[vmem, vmem, hbm],
+            in_specs=[vmem, vmem, vmem, hbm],
             out_specs=hbm,
-            scratch_shapes=[pltpu.VMEM((spans * rows, slab), jnp.float32), pltpu.SemaphoreType.DMA((spans,))],
-            compiler_params=params,
-            input_output_aliases={2: 0},
+            scratch_shapes=[pltpu.VMEM((blocks * rows, slab), jnp.float32), pltpu.SemaphoreType.DMA((blocks,))],
+            compiler_params=params,
+            input_output_aliases={3: 0},
             name="final",
-        )(last, lax.ppermute(last, "cd", swap), base)
+        )(last, lax.ppermute(last, "cd", swap), base, out)
 
     in_specs = (
         P("groups", "ab", "cd"),

time: 31.7 us -> 32.1 us (1.013)
  waiting for transfers between devices: 1.97 us -> 2.68 us
    pallas_call x3 -> x2, Pallas kernels: 3.71 us -> 3.11 us  [step(): pl.pallas_call(functools.partial(step_kernel, count, rows, cd_tiles, [key...]
    ppermute x12, waiting for transfers between devices: 1.85 us -> 2.38 us  [send_on(): lax.ppermute(piece, ('ab', 'cd'), around(chain, min(hop - 1, 2), min(hop,...]
  transfers between devices with their start and end apart: 15 -> 15, of which waited for: 6 -> 5; matrix products, arithmetic and copies ran while one was open for 0% -> 0% of each run, Pallas kernels for 30% -> 29%
where the time goes in v6:
time: 32.1 us; the launch traced here: 31.9 us
  starting transfers between devices  19 us (59%)
  Pallas kernels  10.1 us (31%)
  waiting for transfers between devices  2.68 us (8%)
    ppermute x12, starting transfers between devices, send_on(): lax.ppermute(piece, ('ab', 'cd'), around(chain, min(hop - 1, 2), min(hop,...  15.8 us
    pallas_call x2, Pallas kernels, step(): pl.pallas_call(functools.partial(step_kernel, count, rows, cd_tiles, [key...  3.11 us
    pallas_call x1, Pallas kernels, shards(): pl.pallas_call(functools.partial(part_kernel, cd_tiles), out_shape=pltpu....  2.43 us
    ppermute x12, waiting for transfers between devices, send_on(): lax.ppermute(piece, ('ab', 'cd'), around(chain, min(hop - 1, 2), min(hop,...  2.38 us
    pallas_call x1, Pallas kernels, shards(): pl.pallas_call(functools.partial(list_kernel, ab_tiles, cd_tiles), out_sh...  1.66 us
    ppermute x1, starting transfers between devices, shards(): lax.ppermute(send, 'cd', swap)  1.3 us
    ppermute x1, starting transfers between devices, shards(): packed = lax.ppermute(packed, 'cd', swap)  1.26 us
    pallas_call x1, Pallas kernels, shards(): pl.pallas_call(functools.partial(last_kernel, cd_tiles), out_shape=pltpu....  1.17 us
  transfers between devices with their start and end apart: 15, of which 5 were waited for; matrix products, arithmetic and copies ran while one was open for 0% of the time, Pallas kernels for 29%

profile of v6, /device:TPU:1, one launch (start us, length us, event | category | flops | bytes accessed | tf_op | source)
XLA Modules:
  0.0 31.9 jit_solution(4290088714201117418)
XLA Ops:
  0.0 2.6 %collective-permute-start = (f32[2,16,2048]{2,1,0:T(8,128)}, f32[2,16,2048]{2,1,0:T(8,128)S(1)}, u32[]{:S(2)}, u32[]{:S(2)}) collective-permute-start(f32[2,16,2048]{2,1,0:T(8,128)} %amplitudes.1), channel_id=1, source_target_pairs={{0,5},{1,2},{4,9},{5,0},{8,13},{9,4},{12,15},{13,8},{14,11},{15,12... | collective-permute-start | bytes 786440 | tf_op jit(solution)/shard_map/ppermute | solution.py:318
  2.6 1.1 %collective-permute-start.3 = (f32[2,16,2048]{2,1,0:T(8,128)}, f32[2,16,2048]{2,1,0:T(8,128)S(1)}, u32[]{:S(2)}, u32[]{:S(2)}) collective-permute-start(f32[2,16,2048]{2,1,0:T(8,128)} %amplitudes.1), channel_id=1, source_target_pairs={{0,3},{1,4},{4,1},{5,8},{8,5},{9,12},{12,9},{13,14},{14,13},{15,10... | collective-permute-start | bytes 786440 | tf_op jit(solution)/shard_map/ppermute | solution.py:318
  3.7 1.7 %list.1 = (s32[2,128]{1,0:T(2,128)S(1)}, f32[2,16,2048]{2,1,0:T(8,128)S(1)}) custom-call(s32[8]{0:T(128)} %ab_irrep.1, s32[16]{0:T(128)} %cd_irrep.1, s32[8,16]{1,0:T(8,128)} %pattern.1, f32[2,16,2048]{2,1,0:T(8,128)} %amplitudes.1), custom_call_target="tpu_custom_call" | custom-call | bytes 4194304 | tf_op jit(solution)/shard_map/list/pallas_call | solution.py:279
  5.4 2.4 %part.1.split = bf16[128,128,256]{2,1,0:T(8,128)(2,1)S(1)} custom-call(s32[2,128]{1,0:T(2,128)S(1)} %get-tuple-element.21.listed, f32[1024,2048]{1,0:T(8,128)} %integrals.1), custom_call_target="tpu_custom_call" | custom-call | bytes 8388608 | tf_op jit(solution)/shard_map/part/pallas_call | solution.py:289
  7.8 1.1 %step.2 = (f32[2,64,1024]{2,1,0:T(8,128)S(1)}, f32[2,64,1024]{2,1,0:T(8,128)S(1)}) custom-call(s32[2,128]{1,0:T(2,128)S(1)} %get-tuple-element.21.listed, bf16[128,128,256]{2,1,0:T(8,128)(2,1)S(1)} %part.1.split, f32[2,16,2048]{2,1,0:T(8,128)S(1)} %get-tuple-element.22.refs_0_), custom_call_target="tpu_custom_call" | custom-call | flops 1073741824 | bytes 4194304 | tf_op jit(solution)/shard_map/step/pallas_call | solution.py:305
  9.0 0.0 collective-permute-done.chunk
  9.0 0.2 collective-permute-done.3.chunk
  9.2 1.3 %collective-permute-start.13 = (f32[4,16,2048]{2,1,0:T(8,128)S(1)}, f32[4,16,2048]{2,1,0:T(8,128)S(1)}, u32[]{:S(2)}, u32[]{:S(2)}) collective-permute-start(f32[4,16,2048]{2,1,0:T(8,128)S(1)} %get-tuple-element.31), channel_id=1, source_target_pairs={{0,1},{1,0},{2,3},{3,2},{4,5},{5,4},{6,7},{7,6},{8,9},{9,8},{10,11... | collective-permute-start | bytes 1572872 | tf_op jit(solution)/shard_map/ppermute | solution.py:347
  10.5 1.3 %collective-permute-start.9 = (f32[1,16,2048]{2,1,0:T(8,128)S(1)}, f32[1,16,2048]{2,1,0:T(8,128)S(1)}, u32[]{:S(2)}, u32[]{:S(2)}) collective-permute-start(f32[1,16,2048]{2,1,0:T(8,128)S(1)} %get-tuple-element.30), channel_id=1, source_target_pairs={{1,2},{0,5},{5,0},{4,9},{9,4},{8,13},{13,8},{12,15},{15,12},{14,11... | collective-permute-start | bytes 393224 | tf_op jit(solution)/shard_map/ppermute | solution.py:318
  11.8 1.6 %collective-permute-start.6 = (f32[1,16,2048]{2,1,0:T(8,128)S(1)}, f32[1,16,2048]{2,1,0:T(8,128)S(1)}, u32[]{:S(2)}, u32[]{:S(2)}) collective-permute-start(f32[1,16,2048]{2,1,0:T(8,128)S(1)} %get-tuple-element.29), channel_id=1, source_target_pairs={{1,4},{0,3},{5,8},{4,1},{9,12},{8,5},{13,14},{12,9},{15,10},{14,13... | collective-permute-start | bytes 393224 | tf_op jit(solution)/shard_map/ppermute | solution.py:318
  13.3 1.3 %collective-permute-start.4 = (f32[1,16,2048]{2,1,0:T(8,128)S(1)}, f32[1,16,2048]{2,1,0:T(8,128)S(1)}, u32[]{:S(2)}, u32[]{:S(2)}) collective-permute-start(f32[1,16,2048]{2,1,0:T(8,128)S(1)} %get-tuple-element.28), channel_id=1, source_target_pairs={{1,2},{0,5},{5,0},{4,9},{9,4},{8,13},{13,8},{12,15},{15,12},{14,11... | collective-permute-start | bytes 393224 | tf_op jit(solution)/shard_map/ppermute | solution.py:318
  14.7 1.5 %collective-permute-start.1 = (f32[1,16,2048]{2,1,0:T(8,128)S(1)}, f32[1,16,2048]{2,1,0:T(8,128)S(1)}, u32[]{:S(2)}, u32[]{:S(2)}) collective-permute-start(f32[1,16,2048]{2,1,0:T(8,128)S(1)} %get-tuple-element.25), channel_id=1, source_target_pairs={{1,4},{0,3},{5,8},{4,1},{9,12},{8,5},{13,14},{12,9},{15,10},{14,13... | collective-permute-start | bytes 393224 | tf_op jit(solution)/shard_map/ppermute | solution.py:318
  16.1 0.0 collective-permute-done.9.refs_1_
  16.1 0.7 %collective-permute-start.10 = (f32[1,16,2048]{2,1,0:T(8,128)S(1)}, f32[1,16,2048]{2,1,0:T(8,128)S(1)}, u32[]{:S(2)}, u32[]{:S(2)}) collective-permute-start(f32[1,16,2048]{2,1,0:T(8,128)S(1)} %collective-permute-done.9.refs_1_), channel_id=1, source_target_pairs={{0,2},{1,5},{4,0},{5,9},{8,4},{9,13},{12,8},{13,15},{14,12},{15,11... | collective-permute-start | bytes 393224 | tf_op jit(solution)/shard_map/ppermute | solution.py:318
  16.8 0.0 collective-permute-done.6.refs_0_
  16.8 1.3 %collective-permute-start.7 = (f32[1,16,2048]{2,1,0:T(8,128)S(1)}, f32[1,16,2048]{2,1,0:T(8,128)S(1)}, u32[]{:S(2)}, u32[]{:S(2)}) collective-permute-start(f32[1,16,2048]{2,1,0:T(8,128)S(1)} %collective-permute-done.6.refs_0_), channel_id=1, source_target_pairs={{0,4},{1,3},{4,8},{5,1},{8,12},{9,5},{12,14},{13,9},{14,10},{15,13... | collective-permute-start | bytes 393224 | tf_op jit(solution)/shard_map/ppermute | solution.py:318
  18.1 0.3 collective-permute-done.4.refs_3_
  18.4 1.4 %collective-permute-start.5 = (f32[1,16,2048]{2,1,0:T(8,128)S(1)}, f32[1,16,2048]{2,1,0:T(8,128)S(1)}, u32[]{:S(2)}, u32[]{:S(2)}) collective-permute-start(f32[1,16,2048]{2,1,0:T(8,128)S(1)} %collective-permute-done.4.refs_3_), channel_id=1, source_target_pairs={{0,2},{1,5},{4,0},{5,9},{8,4},{9,13},{12,8},{13,15},{14,12},{15,11... | collective-permute-start | bytes 393224 | tf_op jit(solution)/shard_map/ppermute | solution.py:318
  19.8 0.0 collective-permute-done.1.refs_2_
  19.8 0.8 %collective-permute-start.2 = (f32[1,16,2048]{2,1,0:T(8,128)S(1)}, f32[1,16,2048]{2,1,0:T(8,128)S(1)}, u32[]{:S(2)}, u32[]{:S(2)}) collective-permute-start(f32[1,16,2048]{2,1,0:T(8,128)S(1)} %collective-permute-done.1.refs_2_), channel_id=1, source_target_pairs={{0,4},{1,3},{4,8},{5,1},{8,12},{9,5},{12,14},{13,9},{14,10},{15,13... | collective-permute-start | bytes 393224 | tf_op jit(solution)/shard_map/ppermute | solution.py:318
  20.6 0.8 %collective-permute-done.10.refs_6_ = f32[1,16,2048]{2,1,0:T(8,128)S(1)} collective-permute-done((f32[1,16,2048]{2,1,0:T(8,128)S(1)}, f32[1,16,2048]{2,1,0:T(8,128)S(1)}, u32[]{:S(2)}, u32[]{:S(2)}) %collective-permute-start.10) | collective-permute-done | bytes 131104 | tf_op jit(solution)/shard_map/ppermute | solution.py:318
  21.4 1.4 %collective-permute-start.11 = (f32[1,16,2048]{2,1,0:T(8,128)S(1)}, f32[1,16,2048]{2,1,0:T(8,128)S(1)}, u32[]{:S(2)}, u32[]{:S(2)}) collective-permute-start(f32[1,16,2048]{2,1,0:T(8,128)S(1)} %collective-permute-done.10.refs_6_), channel_id=1, source_target_pairs={{0,2},{1,5},{4,0},{5,9},{8,4},{9,13},{12,8},{13,15},{14,12},{15,11... | collective-permute-start | bytes 393224 | tf_op jit(solution)/shard_map/ppermute | solution.py:318
  22.8 0.0 collective-permute-done.7.refs_5_
  22.8 0.9 %collective-permute-start.8 = (f32[1,16,2048]{2,1,0:T(8,128)S(1)}, f32[1,16,2048]{2,1,0:T(8,128)S(1)}, u32[]{:S(2)}, u32[]{:S(2)}) collective-permute-start(f32[1,16,2048]{2,1,0:T(8,128)S(1)} %collective-permute-done.7.refs_5_), channel_id=1, source_target_pairs={{0,4},{1,3},{4,8},{5,1},{8,12},{9,5},{12,14},{13,9},{14,10},{15,13... | collective-permute-start | bytes 393224 | tf_op jit(solution)/shard_map/ppermute | solution.py:318
  23.7 0.0 collective-permute-done.13.refs_4_
  23.7 2.0 %step.3 = (f32[2,64,1024]{2,1,0:T(8,128)S(1)}, f32[2,64,1024]{2,1,0:T(8,128)S(1)}) custom-call(s32[2,128]{1,0:T(2,128)S(1)} %get-tuple-element.21.listed, bf16[128,128,256]{2,1,0:T(8,128)(2,1)S(1)} %part.1.split, f32[1,16,2048]{2,1,0:T(8,128)S(1)} %collective-permute-done.6.refs_0_, ...), custom_call_target="tpu_custom_call", output_to_operand_aliasing={{0}: (9, {}), {1}: (10, {})} | custom-call | flops 1073741824 | bytes 4194304 | tf_op jit(solution)/shard_map/step/pallas_call | solution.py:305
  25.7 1.3 %collective-permute-start.14 = (f32[2,64,1024]{2,1,0:T(8,128)S(1)}, f32[2,64,1024]{2,1,0:T(8,128)S(1)}, u32[]{:S(2)}, u32[]{:S(2)}) collective-permute-start(f32[2,64,1024]{2,1,0:T(8,128)S(1)} %get-tuple-element.34), channel_id=1, source_target_pairs={{0,1},{1,0},{2,3},{3,2},{4,5},{5,4},{6,7},{7,6},{8,9},{9,8},{10,11... | collective-permute-start | bytes 1572872 | tf_op jit(solution)/shard_map/ppermute | solution.py:362
  27.0 0.0 collective-permute-done.5.refs_1_
  27.0 0.0 collective-permute-done.2.refs_0_
  27.0 0.0 collective-permute-done.11.refs_3_
  27.0 1.1 %collective-permute-done.8.refs_2_ = f32[1,16,2048]{2,1,0:T(8,128)S(1)} collective-permute-done((f32[1,16,2048]{2,1,0:T(8,128)S(1)}, f32[1,16,2048]{2,1,0:T(8,128)S(1)}, u32[]{:S(2)}, u32[]{:S(2)}) %collective-permute-start.8) | collective-permute-done | bytes 131104 | tf_op jit(solution)/shard_map/ppermute | solution.py:318
  28.0 1.2 %last.1 = f32[64,1024]{1,0:T(8,128)S(1)} custom-call(s32[2,128]{1,0:T(2,128)S(1)} %get-tuple-element.21.listed, bf16[128,128,256]{2,1,0:T(8,128)(2,1)S(1)} %part.1.split, f32[1,16,2048]{2,1,0:T(8,128)S(1)} %collective-permute-done.2.refs_0_, f32[1,16,2048]{2,1,0:T(8,128)S(1)} %collective-permute-done.5.refs_1_, ...), custom_call_target="tpu_custom_call" | custom-call | flops 17179869184 | bytes 4194304 | tf_op jit(solution)/shard_map/last/pallas_call | solution.py:365
  29.2 0.7 %collective-permute-start.12 = (f32[64,1024]{1,0:T(8,128)S(1)}, f32[64,1024]{1,0:T(8,128)S(1)}, u32[]{:S(2)}, u32[]{:S(2)}) collective-permute-start(f32[64,1024]{1,0:T(8,128)S(1)} %last.1), channel_id=1, source_target_pairs={{0,1},{1,0},{2,3},{3,2},{4,5},{5,4},{6,7},{7,6},{8,9},{9,8},{10,11... | collective-permute-start | bytes 786440 | tf_op jit(solution)/shard_map/ppermute | solution.py:384
  29.9 0.0 collective-permute-done.14.received
  29.9 0.9 %merge.1 = (f32[2,64,1024]{2,1,0:T(8,128)S(1)}, f32[2,64,1024]{2,1,0:T(8,128)}) custom-call(f32[2,64,1024]{2,1,0:T(8,128)S(1)} %get-tuple-element.33.mine, f32[2,64,1024]{2,1,0:T(8,128)S(1)} %collective-permute-done.14.received), custom_call_target="tpu_custom_call" | custom-call | tf_op jit(solution)/shard_map/merge/pallas_call | solution.py:352
  30.8 0.3 collective-permute-done.12.received
  31.1 0.8 %final.1 = f32[2,64,1024]{2,1,0:T(8,128)} custom-call(f32[64,1024]{1,0:T(8,128)S(1)} %last.1, f32[64,1024]{1,0:T(8,128)S(1)} %collective-permute-done.12.received, f32[2,64,1024]{2,1,0:T(8,128)S(1)} %get-tuple-element.35.base, f32[2,64,1024]{2,1,0:T(8,128)} %get-tuple-element.36.before), custom_call_target="tpu_custom_call", output_to_operand_aliasing={{}: (3, {})} | custom-call | tf_op jit(solution)/shard_map/final/pallas_call | solution.py:375
  (2 shorter events, 0.1 us)
Async XLA Ops:
  0.0 9.0 %collective-permute-start = (f32[2,16,2048]{2,1,0:T(8,128)}, f32[2,16,2048]{2,1,0:T(8,128)S(1)}, u32[]{:S(2)}, u32[]{:S(2)}) collective-permute-start(f32[2,16,2048]{2,1,0:T(8,128)} %amplitudes.1), channel_id=1, source_target_pairs={{0,5},{1,2},{4,9},{5,0},{8,13},{9,4},{12,15},{13,8},{14,11},{15,12... | collective-permute-start | bytes 786440 | tf_op jit(solution)/shard_map/ppermute | solution.py:318
  2.6 6.6 %collective-permute-start.3 = (f32[2,16,2048]{2,1,0:T(8,128)}, f32[2,16,2048]{2,1,0:T(8,128)S(1)}, u32[]{:S(2)}, u32[]{:S(2)}) collective-permute-start(f32[2,16,2048]{2,1,0:T(8,128)} %amplitudes.1), channel_id=1, source_target_pairs={{0,3},{1,4},{4,1},{5,8},{8,5},{9,12},{12,9},{13,14},{14,13},{15,10... | collective-permute-start | bytes 786440 | tf_op jit(solution)/shard_map/ppermute | solution.py:318
  9.2 14.5 %collective-permute-start.13 = (f32[4,16,2048]{2,1,0:T(8,128)S(1)}, f32[4,16,2048]{2,1,0:T(8,128)S(1)}, u32[]{:S(2)}, u32[]{:S(2)}) collective-permute-start(f32[4,16,2048]{2,1,0:T(8,128)S(1)} %get-tuple-element.31), channel_id=1, source_target_pairs={{0,1},{1,0},{2,3},{3,2},{4,5},{5,4},{6,7},{7,6},{8,9},{9,8},{10,11... | collective-permute-start | bytes 1572872 | tf_op jit(solution)/shard_map/ppermute | solution.py:347
  10.5 5.6 %collective-permute-start.9 = (f32[1,16,2048]{2,1,0:T(8,128)S(1)}, f32[1,16,2048]{2,1,0:T(8,128)S(1)}, u32[]{:S(2)}, u32[]{:S(2)}) collective-permute-start(f32[1,16,2048]{2,1,0:T(8,128)S(1)} %get-tuple-element.30), channel_id=1, source_target_pairs={{1,2},{0,5},{5,0},{4,9},{9,4},{8,13},{13,8},{12,15},{15,12},{14,11... | collective-permute-start | bytes 393224 | tf_op jit(solution)/shard_map/ppermute | solution.py:318
  11.8 5.1 %collective-permute-start.6 = (f32[1,16,2048]{2,1,0:T(8,128)S(1)}, f32[1,16,2048]{2,1,0:T(8,128)S(1)}, u32[]{:S(2)}, u32[]{:S(2)}) collective-permute-start(f32[1,16,2048]{2,1,0:T(8,128)S(1)} %get-tuple-element.29), channel_id=1, source_target_pairs={{1,4},{0,3},{5,8},{4,1},{9,12},{8,5},{13,14},{12,9},{15,10},{14,13... | collective-permute-start | bytes 393224 | tf_op jit(solution)/shard_map/ppermute | solution.py:318
  13.3 5.1 %collective-permute-start.4 = (f32[1,16,2048]{2,1,0:T(8,128)S(1)}, f32[1,16,2048]{2,1,0:T(8,128)S(1)}, u32[]{:S(2)}, u32[]{:S(2)}) collective-permute-start(f32[1,16,2048]{2,1,0:T(8,128)S(1)} %get-tuple-element.28), channel_id=1, source_target_pairs={{1,2},{0,5},{5,0},{4,9},{9,4},{8,13},{13,8},{12,15},{15,12},{14,11... | collective-permute-start | bytes 393224 | tf_op jit(solution)/shard_map/ppermute | solution.py:318
  14.7 5.2 %collective-permute-start.1 = (f32[1,16,2048]{2,1,0:T(8,128)S(1)}, f32[1,16,2048]{2,1,0:T(8,128)S(1)}, u32[]{:S(2)}, u32[]{:S(2)}) collective-permute-start(f32[1,16,2048]{2,1,0:T(8,128)S(1)} %get-tuple-element.25), channel_id=1, source_target_pairs={{1,4},{0,3},{5,8},{4,1},{9,12},{8,5},{13,14},{12,9},{15,10},{14,13... | collective-permute-start | bytes 393224 | tf_op jit(solution)/shard_map/ppermute | solution.py:318
  16.1 5.3 %collective-permute-start.10 = (f32[1,16,2048]{2,1,0:T(8,128)S(1)}, f32[1,16,2048]{2,1,0:T(8,128)S(1)}, u32[]{:S(2)}, u32[]{:S(2)}) collective-permute-start(f32[1,16,2048]{2,1,0:T(8,128)S(1)} %collective-permute-done.9.refs_1_), channel_id=1, source_target_pairs={{0,2},{1,5},{4,0},{5,9},{8,4},{9,13},{12,8},{13,15},{14,12},{15,11... | collective-permute-start | bytes 393224 | tf_op jit(solution)/shard_map/ppermute | solution.py:318
  16.8 5.9 %collective-permute-start.7 = (f32[1,16,2048]{2,1,0:T(8,128)S(1)}, f32[1,16,2048]{2,1,0:T(8,128)S(1)}, u32[]{:S(2)}, u32[]{:S(2)}) collective-permute-start(f32[1,16,2048]{2,1,0:T(8,128)S(1)} %collective-permute-done.6.refs_0_), channel_id=1, source_target_pairs={{0,4},{1,3},{4,8},{5,1},{8,12},{9,5},{12,14},{13,9},{14,10},{15,13... | collective-permute-start | bytes 393224 | tf_op jit(solution)/shard_map/ppermute | solution.py:318
  18.4 8.6 %collective-permute-start.5 = (f32[1,16,2048]{2,1,0:T(8,128)S(1)}, f32[1,16,2048]{2,1,0:T(8,128)S(1)}, u32[]{:S(2)}, u32[]{:S(2)}) collective-permute-start(f32[1,16,2048]{2,1,0:T(8,128)S(1)} %collective-permute-done.4.refs_3_), channel_id=1, source_target_pairs={{0,2},{1,5},{4,0},{5,9},{8,4},{9,13},{12,8},{13,15},{14,12},{15,11... | collective-permute-start | bytes 393224 | tf_op jit(solution)/shard_map/ppermute | solution.py:318
  19.8 7.2 %collective-permute-start.2 = (f32[1,16,2048]{2,1,0:T(8,128)S(1)}, f32[1,16,2048]{2,1,0:T(8,128)S(1)}, u32[]{:S(2)}, u32[]{:S(2)}) collective-permute-start(f32[1,16,2048]{2,1,0:T(8,128)S(1)} %collective-permute-done.1.refs_2_), channel_id=1, source_target_pairs={{0,4},{1,3},{4,8},{5,1},{8,12},{9,5},{12,14},{13,9},{14,10},{15,13... | collective-permute-start | bytes 393224 | tf_op jit(solution)/shard_map/ppermute | solution.py:318
  21.4 5.6 %collective-permute-start.11 = (f32[1,16,2048]{2,1,0:T(8,128)S(1)}, f32[1,16,2048]{2,1,0:T(8,128)S(1)}, u32[]{:S(2)}, u32[]{:S(2)}) collective-permute-start(f32[1,16,2048]{2,1,0:T(8,128)S(1)} %collective-permute-done.10.refs_6_), channel_id=1, source_target_pairs={{0,2},{1,5},{4,0},{5,9},{8,4},{9,13},{12,8},{13,15},{14,12},{15,11... | collective-permute-start | bytes 393224 | tf_op jit(solution)/shard_map/ppermute | solution.py:318
  22.8 5.3 %collective-permute-start.8 = (f32[1,16,2048]{2,1,0:T(8,128)S(1)}, f32[1,16,2048]{2,1,0:T(8,128)S(1)}, u32[]{:S(2)}, u32[]{:S(2)}) collective-permute-start(f32[1,16,2048]{2,1,0:T(8,128)S(1)} %collective-permute-done.7.refs_5_), channel_id=1, source_target_pairs={{0,4},{1,3},{4,8},{5,1},{8,12},{9,5},{12,14},{13,9},{14,10},{15,13... | collective-permute-start | bytes 393224 | tf_op jit(solution)/shard_map/ppermute | solution.py:318
  25.7 4.3 %collective-permute-start.14 = (f32[2,64,1024]{2,1,0:T(8,128)S(1)}, f32[2,64,1024]{2,1,0:T(8,128)S(1)}, u32[]{:S(2)}, u32[]{:S(2)}) collective-permute-start(f32[2,64,1024]{2,1,0:T(8,128)S(1)} %get-tuple-element.34), channel_id=1, source_target_pairs={{0,1},{1,0},{2,3},{3,2},{4,5},{5,4},{6,7},{7,6},{8,9},{9,8},{10,11... | collective-permute-start | bytes 1572872 | tf_op jit(solution)/shard_map/ppermute | solution.py:362
  29.2 1.9 %collective-permute-start.12 = (f32[64,1024]{1,0:T(8,128)S(1)}, f32[64,1024]{1,0:T(8,128)S(1)}, u32[]{:S(2)}, u32[]{:S(2)}) collective-permute-start(f32[64,1024]{1,0:T(8,128)S(1)} %last.1), channel_id=1, source_target_pairs={{0,1},{1,0},{2,3},{3,2},{4,5},{5,4},{6,7},{7,6},{8,9},{9,8},{10,11... | collective-permute-start | bytes 786440 | tf_op jit(solution)/shard_map/ppermute | solution.py:384

commit v7 on v3

--- a/solution.py
+++ b/solution.py
@@ -10,7 +10,8 @@
 TILE = 128
 UNROLL = 4
 LANES = 128
-FLIGHT = 32
+AHEAD = 8
+FLIGHT = AHEAD * UNROLL
 GROUP = 12
 STEP_FLOPS = 1 << 30
 VMEM_LIMIT = 12 * 2**20
@@ -108,20 +109,20 @@
 
 
 def part_kernel(cd_tiles, listed, integrals, split, landed, sems):
-    last = listed[1, 0] * UNROLL
-
     def fetch(k):
         start, column = place_in(listed[0, k], cd_tiles)
-        slot = lax.rem(k, FLIGHT)
+        slot = lax.bitwise_and(k, FLIGHT - 1)
         return pltpu.make_async_copy(
             integrals.at[pl.ds(start, TILE), pl.ds(column, TILE)], landed.at[slot], sems.at[slot]
         )
 
-    def begin(k, carry):
-        fetch(k).start()
+    def begin(round_at, carry):
+        for unrolled in range(UNROLL):
+            fetch(round_at * UNROLL + unrolled).start()
         return carry
 
-    lax.fori_loop(0, jnp.minimum(last, FLIGHT), begin, 0)
+    rounds = listed[1, 0]
+    lax.fori_loop(0, jnp.minimum(rounds, AHEAD), begin, 0)
 
     def part(round_at, carry):
         first = round_at * UNROLL
@@ -130,19 +131,27 @@
         for unrolled in range(UNROLL):
             k = first + unrolled
             real = jnp.logical_or(k == 0, listed[0, k] > 0)
-            tile = jnp.where(real, landed[lax.rem(k, FLIGHT)], 0.0).T
+            tile = jnp.where(real, landed[lax.bitwise_and(k, FLIGHT - 1)], 0.0).T
             upper = tile.astype(jnp.bfloat16)
             split[k, :, :TILE] = upper
             split[k, :, TILE:] = (tile - upper.astype(jnp.float32)).astype(jnp.bfloat16)
-        lax.fori_loop(jnp.minimum(first + FLIGHT, last), jnp.minimum(first + UNROLL + FLIGHT, last), begin, 0)
+
+        @pl.when(round_at + AHEAD < rounds)
+        def _():
+            begin(round_at + AHEAD, 0)
+
         return carry
 
-    lax.fori_loop(0, listed[1, 0], part, 0)
+    lax.fori_loop(0, rounds, part, 0)
 
 
 def place_in(place, cd_tiles):
-    row = lax.div(place, cd_tiles)
-    return pl.multiple_of(row * TILE, TILE), pl.multiple_of((place - row * cd_tiles) * TILE, TILE)
+    bits = cd_tiles.bit_length() - 1
+    if cd_tiles == 1 << bits:
+        row, column = lax.shift_right_logical(place, bits), lax.bitwise_and(place, cd_tiles - 1)
+    else:
+        row, column = lax.div(place, cd_tiles), lax.rem(place, cd_tiles)
+    return pl.multiple_of(row * TILE, TILE), pl.multiple_of(column * TILE, TILE)
 
 
 def products(cd_tiles, listed, split, pieces, total):
@@ -167,9 +176,9 @@
         return carry
 
     rounds = listed[1, 0]
-    lax.fori_loop(0, lax.div(rounds, 2), step, 0)
-
-    @pl.when(lax.rem(rounds, 2) == 1)
+    lax.fori_loop(0, lax.shift_right_logical(rounds, 1), step, 0)
+
+    @pl.when(lax.bitwise_and(rounds, 1) == 1)
     def _():
         some((rounds - 1) * UNROLL, UNROLL)
 

time: 30.9 us -> 31.2 us (level)
  Pallas kernels: 10.3 us -> 11 us
  starting transfers between devices: 16.4 us -> 16 us
    pallas_call x2, Pallas kernels: 3.26 us -> 3.75 us  [shards(): pl.pallas_call(functools.partial(step_kernel, count, rows, cd_tiles, grou...]
  transfers between devices with their start and end apart: 16 -> 16, of which waited for: 5 -> 5; matrix products, arithmetic and copies ran while one was open for 0% -> 0% of each run, Pallas kernels for 28% -> 30%
where the time goes in v7:
time: 31.2 us; the launch traced here: 30.8 us
  starting transfers between devices  16 us (51%)
  Pallas kernels  11 us (35%)
  waiting for transfers between devices  3.63 us (12%)
    ppermute x14, starting transfers between devices, shards(): moved = lax.ppermute(moved, 'ab', pairs)  11.2 us
    pallas_call x2, Pallas kernels, shards(): pl.pallas_call(functools.partial(step_kernel, count, rows, cd_tiles, grou...  3.75 us
    ppermute x1, starting transfers between devices, shards(): lax.ppermute(send, 'cd', swap)  3.59 us
    ppermute x14, waiting for transfers between devices, shards(): moved = lax.ppermute(moved, 'ab', pairs)  3.5 us
    pallas_call x1, Pallas kernels, shards(): pl.pallas_call(functools.partial(part_kernel, cd_tiles), out_shape=pltpu....  2.53 us
    ppermute x1, starting transfers between devices, shards(): lax.ppermute(last, 'cd', swap)  1.23 us
    pallas_call x1, Pallas kernels, shards(): pl.pallas_call(functools.partial(last_kernel, cd_tiles), out_shape=pltpu....  1.21 us
    pallas_call x1, Pallas kernels, shards(): pl.pallas_call(cut_kernel, out_shape=(piece,) * spans + tuple((pltpu.VMEM...  1.01 us
  transfers between devices with their start and end apart: 16, of which 5 were waited for; matrix products, arithmetic and copies ran while one was open for 0% of the time, Pallas kernels for 30%

profile of v7, /device:TPU:1, one launch (start us, length us, event | category | flops | bytes accessed | tf_op | source)
XLA Modules:
  0.0 30.8 jit_solution(11555955460693310191)
XLA Ops:
  0.0 1.0 %cut.1 = (f32[1,16,2048]{2,1,0:T(8,128)S(1)}, f32[1,16,2048]{2,1,0:T(8,128)S(1)}, s32[8,16]{1,0:T(8,128)S(1)}, s32[8]{0:T(128)S(1)}, s32[16]{0:T(128)S(1)}) custom-call(f32[2,16,2048]{2,1,0:T(8,128)} %amplitudes.1, s32[8,16]{1,0:T(8,128)} %pattern.1, s32[8]{0:T(128)} %ab_irrep.1, s32[16]{0:T(128)} %cd_irrep.1), custom_call_target="tpu_custom_call" | custom-call | tf_op jit(solution)/shard_map/cut/pallas_call | solution.py:256
  1.0 2.1 %collective-permute-start.4 = (f32[1,16,2048]{2,1,0:T(8,128)S(1)}, f32[1,16,2048]{2,1,0:T(8,128)S(1)}, u32[]{:S(2)}, u32[]{:S(2)}) collective-permute-start(f32[1,16,2048]{2,1,0:T(8,128)S(1)} %get-tuple-element.28.refs_1_), channel_id=1, source_target_pairs={{4,0},{8,4},{12,8},{14,12},{10,14},{6,10},{2,6},{0,2},{5,1},{9,5},... | collective-permute-start | bytes 393224 | tf_op jit(solution)/shard_map/ppermute | solution.py:294
  3.1 0.1 collective-permute-start
  3.3 1.3 %collective-permute-start.9 = (f32[1,16,2048]{2,1,0:T(8,128)S(1)}, f32[1,16,2048]{2,1,0:T(8,128)S(1)}, u32[]{:S(2)}, u32[]{:S(2)}) collective-permute-start(f32[1,16,2048]{2,1,0:T(8,128)S(1)} %get-tuple-element.25.refs_0_), channel_id=1, source_target_pairs={{4,0},{8,4},{12,8},{14,12},{10,14},{6,10},{2,6},{0,2},{5,1},{9,5},... | collective-permute-start | bytes 393224 | tf_op jit(solution)/shard_map/ppermute | solution.py:294
  4.6 0.1 collective-permute-start.12
  4.7 1.0 %list.1.listed = s32[2,128]{1,0:T(2,128)S(1)} custom-call(s32[8]{0:T(128)S(1)} %get-tuple-element.22.ab_irrep, s32[16]{0:T(128)S(1)} %get-tuple-element.23.cd_irrep, s32[8,16]{1,0:T(8,128)S(1)} %get-tuple-element.24.pattern), custom_call_target="tpu_custom_call" | custom-call | bytes 4194304 | tf_op jit(solution)/shard_map/list/pallas_call | solution.py:266
  5.7 0.7 %collective-permute-done.4.refs_3_ = f32[1,16,2048]{2,1,0:T(8,128)S(1)} collective-permute-done((f32[1,16,2048]{2,1,0:T(8,128)S(1)}, f32[1,16,2048]{2,1,0:T(8,128)S(1)}, u32[]{:S(2)}, u32[]{:S(2)}) %collective-permute-start.4) | collective-permute-done | bytes 131104 | tf_op jit(solution)/shard_map/ppermute | solution.py:294
  6.4 1.1 %collective-permute-start.5 = (f32[1,16,2048]{2,1,0:T(8,128)S(1)}, f32[1,16,2048]{2,1,0:T(8,128)S(1)}, u32[]{:S(2)}, u32[]{:S(2)}) collective-permute-start(f32[1,16,2048]{2,1,0:T(8,128)S(1)} %collective-permute-done.4.refs_3_), channel_id=1, source_target_pairs={{4,0},{8,4},{12,8},{14,12},{10,14},{6,10},{2,6},{0,2},{5,1},{9,5},... | collective-permute-start | bytes 393224 | tf_op jit(solution)/shard_map/ppermute | solution.py:294
  7.5 0.0 collective-permute-done.refs_2_
  7.5 0.4 %collective-permute-start.1 = (f32[1,16,2048]{2,1,0:T(8,128)S(1)}, f32[1,16,2048]{2,1,0:T(8,128)S(1)}, u32[]{:S(2)}, u32[]{:S(2)}) collective-permute-start(f32[1,16,2048]{2,1,0:T(8,128)S(1)} %collective-permute-done.refs_2_), channel_id=1, source_target_pairs={{0,4},{4,8},{8,12},{12,14},{14,10},{10,6},{6,2},{2,0},{1,5},{5,9},... | collective-permute-start | bytes 393224 | tf_op jit(solution)/shard_map/ppermute | solution.py:294
  7.9 1.3 %collective-permute-done.9.refs_4_ = f32[1,16,2048]{2,1,0:T(8,128)S(1)} collective-permute-done((f32[1,16,2048]{2,1,0:T(8,128)S(1)}, f32[1,16,2048]{2,1,0:T(8,128)S(1)}, u32[]{:S(2)}, u32[]{:S(2)}) %collective-permute-start.9) | collective-permute-done | bytes 131104 | tf_op jit(solution)/shard_map/ppermute | solution.py:294
  9.2 1.1 %collective-permute-start.10 = (f32[1,16,2048]{2,1,0:T(8,128)S(1)}, f32[1,16,2048]{2,1,0:T(8,128)S(1)}, u32[]{:S(2)}, u32[]{:S(2)}) collective-permute-start(f32[1,16,2048]{2,1,0:T(8,128)S(1)} %collective-permute-done.9.refs_4_), channel_id=1, source_target_pairs={{4,0},{8,4},{12,8},{14,12},{10,14},{6,10},{2,6},{0,2},{5,1},{9,5},... | collective-permute-start | bytes 393224 | tf_op jit(solution)/shard_map/ppermute | solution.py:294
  10.3 0.0 collective-permute-done.12.refs_5_
  10.3 0.4 %collective-permute-start.13 = (f32[1,16,2048]{2,1,0:T(8,128)S(1)}, f32[1,16,2048]{2,1,0:T(8,128)S(1)}, u32[]{:S(2)}, u32[]{:S(2)}) collective-permute-start(f32[1,16,2048]{2,1,0:T(8,128)S(1)} %collective-permute-done.12.refs_5_), channel_id=1, source_target_pairs={{0,4},{4,8},{8,12},{12,14},{14,10},{10,6},{6,2},{2,0},{1,5},{5,9},... | collective-permute-start | bytes 393224 | tf_op jit(solution)/shard_map/ppermute | solution.py:294
  10.7 2.5 %part.1.split = bf16[128,128,256]{2,1,0:T(8,128)(2,1)S(1)} custom-call(s32[2,128]{1,0:T(2,128)S(1)} %list.1.listed, f32[1024,2048]{1,0:T(8,128)} %integrals.1), custom_call_target="tpu_custom_call" | custom-call | bytes 8388608 | tf_op jit(solution)/shard_map/part/pallas_call | solution.py:275
  13.2 0.0 collective-permute-done.5.refs_7_
  13.3 0.8 %collective-permute-start.6 = (f32[1,16,2048]{2,1,0:T(8,128)S(1)}, f32[1,16,2048]{2,1,0:T(8,128)S(1)}, u32[]{:S(2)}, u32[]{:S(2)}) collective-permute-start(f32[1,16,2048]{2,1,0:T(8,128)S(1)} %collective-permute-done.5.refs_7_), channel_id=1, source_target_pairs={{4,0},{8,4},{12,8},{14,12},{10,14},{6,10},{2,6},{0,2},{5,1},{9,5},... | collective-permute-start | bytes 393224 | tf_op jit(solution)/shard_map/ppermute | solution.py:294
  14.1 0.0 collective-permute-done.1.refs_6_
  14.1 0.7 %collective-permute-start.2 = (f32[1,16,2048]{2,1,0:T(8,128)S(1)}, f32[1,16,2048]{2,1,0:T(8,128)S(1)}, u32[]{:S(2)}, u32[]{:S(2)}) collective-permute-start(f32[1,16,2048]{2,1,0:T(8,128)S(1)} %collective-permute-done.1.refs_6_), channel_id=1, source_target_pairs={{0,4},{4,8},{8,12},{12,14},{14,10},{10,6},{6,2},{2,0},{1,5},{5,9},... | collective-permute-start | bytes 393224 | tf_op jit(solution)/shard_map/ppermute | solution.py:294
  14.8 0.0 collective-permute-done.10.refs_8_
  14.8 0.8 %collective-permute-start.11 = (f32[1,16,2048]{2,1,0:T(8,128)S(1)}, f32[1,16,2048]{2,1,0:T(8,128)S(1)}, u32[]{:S(2)}, u32[]{:S(2)}) collective-permute-start(f32[1,16,2048]{2,1,0:T(8,128)S(1)} %collective-permute-done.10.refs_8_), channel_id=1, source_target_pairs={{4,0},{8,4},{12,8},{14,12},{10,14},{6,10},{2,6},{0,2},{5,1},{9,5},... | collective-permute-start | bytes 393224 | tf_op jit(solution)/shard_map/ppermute | solution.py:294
  15.6 0.0 collective-permute-done.13.refs_9_
  15.6 0.7 %collective-permute-start.14 = (f32[1,16,2048]{2,1,0:T(8,128)S(1)}, f32[1,16,2048]{2,1,0:T(8,128)S(1)}, u32[]{:S(2)}, u32[]{:S(2)}) collective-permute-start(f32[1,16,2048]{2,1,0:T(8,128)S(1)} %collective-permute-done.13.refs_9_), channel_id=1, source_target_pairs={{0,4},{4,8},{8,12},{12,14},{14,10},{10,6},{6,2},{2,0},{1,5},{5,9},... | collective-permute-start | bytes 393224 | tf_op jit(solution)/shard_map/ppermute | solution.py:294
  16.2 1.2 %collective-permute-done.6.refs_11_ = f32[1,16,2048]{2,1,0:T(8,128)S(1)} collective-permute-done((f32[1,16,2048]{2,1,0:T(8,128)S(1)}, f32[1,16,2048]{2,1,0:T(8,128)S(1)}, u32[]{:S(2)}, u32[]{:S(2)}) %collective-permute-start.6) | collective-permute-done | bytes 131104 | tf_op jit(solution)/shard_map/ppermute | solution.py:294
  17.4 1.6 %collective-permute-start.7 = (f32[1,16,2048]{2,1,0:T(8,128)S(1)}, f32[1,16,2048]{2,1,0:T(8,128)S(1)}, u32[]{:S(2)}, u32[]{:S(2)}) collective-permute-start(f32[1,16,2048]{2,1,0:T(8,128)S(1)} %collective-permute-done.6.refs_11_), channel_id=1, source_target_pairs={{4,0},{8,4},{12,8},{14,12},{10,14},{6,10},{2,6},{0,2},{5,1},{9,5},... | collective-permute-start | bytes 393224 | tf_op jit(solution)/shard_map/ppermute | solution.py:294
  19.0 0.3 collective-permute-done.2.refs_10_
  19.3 0.0 collective-permute-start.3
  19.3 2.5 %step.2 = (f32[2,64,1024]{2,1,0:T(8,128)S(1)}, f32[2,64,1024]{2,1,0:T(8,128)S(1)}) custom-call(s32[2,128]{1,0:T(2,128)S(1)} %list.1.listed, bf16[128,128,256]{2,1,0:T(8,128)(2,1)S(1)} %part.1.split, f32[1,16,2048]{2,1,0:T(8,128)S(1)} %get-tuple-element.25.refs_0_, f32[1,16,2048]{2,1,0:T(8,128)S(1)} %get-tuple-element.28.refs_1_, ...), custom_call_target="tpu_custom_call" | custom-call | flops 1073741824 | bytes 4194304 | tf_op jit(solution)/shard_map/step/pallas_call | solution.py:309
  21.8 0.0 collective-permute-done.11.refs_0_
  21.8 0.0 collective-permute-done.14.refs_1_
  21.8 1.3 %step.3 = (f32[2,64,1024]{2,1,0:T(8,128)S(1)}, f32[2,64,1024]{2,1,0:T(8,128)S(1)}) custom-call(s32[2,128]{1,0:T(2,128)S(1)} %list.1.listed, bf16[128,128,256]{2,1,0:T(8,128)(2,1)S(1)} %part.1.split, f32[1,16,2048]{2,1,0:T(8,128)S(1)} %collective-permute-done.11.refs_0_, ...), custom_call_target="tpu_custom_call", output_to_operand_aliasing={{0}: (4, {}), {1}: (5, {})} | custom-call | flops 1073741824 | bytes 4194304 | tf_op jit(solution)/shard_map/step/pallas_call | solution.py:309
  23.1 3.6 %collective-permute-start.15 = (f32[2,64,1024]{2,1,0:T(8,128)S(1)}, f32[2,64,1024]{2,1,0:T(8,128)S(1)}, u32[]{:S(2)}, u32[]{:S(2)}) collective-permute-start(f32[2,64,1024]{2,1,0:T(8,128)S(1)} %get-tuple-element.38), channel_id=1, source_target_pairs={{0,1},{1,0},{2,3},{3,2},{4,5},{5,4},{6,7},{7,6},{8,9},{9,8},{10,11... | collective-permute-start | bytes 1572872 | tf_op jit(solution)/shard_map/ppermute | solution.py:328
  26.7 0.0 collective-permute-done.7.refs_1_
  26.7 0.0 collective-permute-done.3.refs_0_
  26.7 1.2 %last.1 = f32[32,1024]{1,0:T(8,128)S(1)} custom-call(s32[2,128]{1,0:T(2,128)S(1)} %list.1.listed, bf16[128,128,256]{2,1,0:T(8,128)(2,1)S(1)} %part.1.split, f32[1,16,2048]{2,1,0:T(8,128)S(1)} %collective-permute-done.3.refs_0_, f32[1,16,2048]{2,1,0:T(8,128)S(1)} %collective-permute-done.7.refs_1_), custom_call_target="tpu_custom_call" | custom-call | flops 17179869184 | bytes 4194304 | tf_op jit(solution)/shard_map/last/pallas_call | solution.py:330
  27.9 1.2 %collective-permute-start.8 = (f32[32,1024]{1,0:T(8,128)S(1)}, f32[32,1024]{1,0:T(8,128)S(1)}, u32[]{:S(2)}, u32[]{:S(2)}) collective-permute-start(f32[32,1024]{1,0:T(8,128)S(1)} %last.1), channel_id=1, source_target_pairs={{0,1},{1,0},{2,3},{3,2},{4,5},{5,4},{6,7},{7,6},{8,9},{9,8},{10,11... | collective-permute-start | bytes 393224 | tf_op jit(solution)/shard_map/ppermute | solution.py:348
  29.1 0.0 collective-permute-done.15.received
  29.1 0.8 %merge.1.before = f32[2,64,1024]{2,1,0:T(8,128)} custom-call(f32[2,64,1024]{2,1,0:T(8,128)S(1)} %get-tuple-element.37.mine, f32[2,64,1024]{2,1,0:T(8,128)S(1)} %collective-permute-done.15.received), custom_call_target="tpu_custom_call" | custom-call | tf_op jit(solution)/shard_map/merge/pallas_call | solution.py:321
  30.0 0.1 collective-permute-done.8.received
  30.1 0.7 %final.1 = f32[2,64,1024]{2,1,0:T(8,128)} custom-call(f32[32,1024]{1,0:T(8,128)S(1)} %last.1, f32[32,1024]{1,0:T(8,128)S(1)} %collective-permute-done.8.received, f32[2,64,1024]{2,1,0:T(8,128)} %merge.1.before), custom_call_target="tpu_custom_call", output_to_operand_aliasing={{}: (2, {})} | custom-call | tf_op jit(solution)/shard_map/final/pallas_call | solution.py:339
Async XLA Ops:
  1.0 5.4 %collective-permute-start.4 = (f32[1,16,2048]{2,1,0:T(8,128)S(1)}, f32[1,16,2048]{2,1,0:T(8,128)S(1)}, u32[]{:S(2)}, u32[]{:S(2)}) collective-permute-start(f32[1,16,2048]{2,1,0:T(8,128)S(1)} %get-tuple-element.28.refs_1_), channel_id=1, source_target_pairs={{4,0},{8,4},{12,8},{14,12},{10,14},{6,10},{2,6},{0,2},{5,1},{9,5},... | collective-permute-start | bytes 393224 | tf_op jit(solution)/shard_map/ppermute | solution.py:294
  3.1 4.4 %collective-permute-start = (f32[1,16,2048]{2,1,0:T(8,128)S(1)}, f32[1,16,2048]{2,1,0:T(8,128)S(1)}, u32[]{:S(2)}, u32[]{:S(2)}) collective-permute-start(f32[1,16,2048]{2,1,0:T(8,128)S(1)} %get-tuple-element.25.refs_0_), channel_id=1, source_target_pairs={{0,4},{4,8},{8,12},{12,14},{14,10},{10,6},{6,2},{2,0},{1,5},{5,9},... | collective-permute-start | bytes 393224 | tf_op jit(solution)/shard_map/ppermute | solution.py:294
  3.3 6.0 %collective-permute-start.9 = (f32[1,16,2048]{2,1,0:T(8,128)S(1)}, f32[1,16,2048]{2,1,0:T(8,128)S(1)}, u32[]{:S(2)}, u32[]{:S(2)}) collective-permute-start(f32[1,16,2048]{2,1,0:T(8,128)S(1)} %get-tuple-element.25.refs_0_), channel_id=1, source_target_pairs={{4,0},{8,4},{12,8},{14,12},{10,14},{6,10},{2,6},{0,2},{5,1},{9,5},... | collective-permute-start | bytes 393224 | tf_op jit(solution)/shard_map/ppermute | solution.py:294
  4.6 5.7 %collective-permute-start.12 = (f32[1,16,2048]{2,1,0:T(8,128)S(1)}, f32[1,16,2048]{2,1,0:T(8,128)S(1)}, u32[]{:S(2)}, u32[]{:S(2)}) collective-permute-start(f32[1,16,2048]{2,1,0:T(8,128)S(1)} %get-tuple-element.28.refs_1_), channel_id=1, source_target_pairs={{0,4},{4,8},{8,12},{12,14},{14,10},{10,6},{6,2},{2,0},{1,5},{5,9},... | collective-permute-start | bytes 393224 | tf_op jit(solution)/shard_map/ppermute | solution.py:294
  6.4 6.8 %collective-permute-start.5 = (f32[1,16,2048]{2,1,0:T(8,128)S(1)}, f32[1,16,2048]{2,1,0:T(8,128)S(1)}, u32[]{:S(2)}, u32[]{:S(2)}) collective-permute-start(f32[1,16,2048]{2,1,0:T(8,128)S(1)} %collective-permute-done.4.refs_3_), channel_id=1, source_target_pairs={{4,0},{8,4},{12,8},{14,12},{10,14},{6,10},{2,6},{0,2},{5,1},{9,5},... | collective-permute-start | bytes 393224 | tf_op jit(solution)/shard_map/ppermute | solution.py:294
  7.5 6.6 %collective-permute-start.1 = (f32[1,16,2048]{2,1,0:T(8,128)S(1)}, f32[1,16,2048]{2,1,0:T(8,128)S(1)}, u32[]{:S(2)}, u32[]{:S(2)}) collective-permute-start(f32[1,16,2048]{2,1,0:T(8,128)S(1)} %collective-permute-done.refs_2_), channel_id=1, source_target_pairs={{0,4},{4,8},{8,12},{12,14},{14,10},{10,6},{6,2},{2,0},{1,5},{5,9},... | collective-permute-start | bytes 393224 | tf_op jit(solution)/shard_map/ppermute | solution.py:294
  9.2 5.5 %collective-permute-start.10 = (f32[1,16,2048]{2,1,0:T(8,128)S(1)}, f32[1,16,2048]{2,1,0:T(8,128)S(1)}, u32[]{:S(2)}, u32[]{:S(2)}) collective-permute-start(f32[1,16,2048]{2,1,0:T(8,128)S(1)} %collective-permute-done.9.refs_4_), channel_id=1, source_target_pairs={{4,0},{8,4},{12,8},{14,12},{10,14},{6,10},{2,6},{0,2},{5,1},{9,5},... | collective-permute-start | bytes 393224 | tf_op jit(solution)/shard_map/ppermute | solution.py:294
  10.3 5.2 %collective-permute-start.13 = (f32[1,16,2048]{2,1,0:T(8,128)S(1)}, f32[1,16,2048]{2,1,0:T(8,128)S(1)}, u32[]{:S(2)}, u32[]{:S(2)}) collective-permute-start(f32[1,16,2048]{2,1,0:T(8,128)S(1)} %collective-permute-done.12.refs_5_), channel_id=1, source_target_pairs={{0,4},{4,8},{8,12},{12,14},{14,10},{10,6},{6,2},{2,0},{1,5},{5,9},... | collective-permute-start | bytes 393224 | tf_op jit(solution)/shard_map/ppermute | solution.py:294
  13.3 4.2 %collective-permute-start.6 = (f32[1,16,2048]{2,1,0:T(8,128)S(1)}, f32[1,16,2048]{2,1,0:T(8,128)S(1)}, u32[]{:S(2)}, u32[]{:S(2)}) collective-permute-start(f32[1,16,2048]{2,1,0:T(8,128)S(1)} %collective-permute-done.5.refs_7_), channel_id=1, source_target_pairs={{4,0},{8,4},{12,8},{14,12},{10,14},{6,10},{2,6},{0,2},{5,1},{9,5},... | collective-permute-start | bytes 393224 | tf_op jit(solution)/shard_map/ppermute | solution.py:294
  14.1 5.2 %collective-permute-start.2 = (f32[1,16,2048]{2,1,0:T(8,128)S(1)}, f32[1,16,2048]{2,1,0:T(8,128)S(1)}, u32[]{:S(2)}, u32[]{:S(2)}) collective-permute-start(f32[1,16,2048]{2,1,0:T(8,128)S(1)} %collective-permute-done.1.refs_6_), channel_id=1, source_target_pairs={{0,4},{4,8},{8,12},{12,14},{14,10},{10,6},{6,2},{2,0},{1,5},{5,9},... | collective-permute-start | bytes 393224 | tf_op jit(solution)/shard_map/ppermute | solution.py:294
  14.8 7.0 %collective-permute-start.11 = (f32[1,16,2048]{2,1,0:T(8,128)S(1)}, f32[1,16,2048]{2,1,0:T(8,128)S(1)}, u32[]{:S(2)}, u32[]{:S(2)}) collective-permute-start(f32[1,16,2048]{2,1,0:T(8,128)S(1)} %collective-permute-done.10.refs_8_), channel_id=1, source_target_pairs={{4,0},{8,4},{12,8},{14,12},{10,14},{6,10},{2,6},{0,2},{5,1},{9,5},... | collective-permute-start | bytes 393224 | tf_op jit(solution)/shard_map/ppermute | solution.py:294
  15.6 6.2 %collective-permute-start.14 = (f32[1,16,2048]{2,1,0:T(8,128)S(1)}, f32[1,16,2048]{2,1,0:T(8,128)S(1)}, u32[]{:S(2)}, u32[]{:S(2)}) collective-permute-start(f32[1,16,2048]{2,1,0:T(8,128)S(1)} %collective-permute-done.13.refs_9_), channel_id=1, source_target_pairs={{0,4},{4,8},{8,12},{12,14},{14,10},{10,6},{6,2},{2,0},{1,5},{5,9},... | collective-permute-start | bytes 393224 | tf_op jit(solution)/shard_map/ppermute | solution.py:294
  17.4 9.2 %collective-permute-start.7 = (f32[1,16,2048]{2,1,0:T(8,128)S(1)}, f32[1,16,2048]{2,1,0:T(8,128)S(1)}, u32[]{:S(2)}, u32[]{:S(2)}) collective-permute-start(f32[1,16,2048]{2,1,0:T(8,128)S(1)} %collective-permute-done.6.refs_11_), channel_id=1, source_target_pairs={{4,0},{8,4},{12,8},{14,12},{10,14},{6,10},{2,6},{0,2},{5,1},{9,5},... | collective-permute-start | bytes 393224 | tf_op jit(solution)/shard_map/ppermute | solution.py:294
  19.3 7.4 %collective-permute-start.3 = (f32[1,16,2048]{2,1,0:T(8,128)S(1)}, f32[1,16,2048]{2,1,0:T(8,128)S(1)}, u32[]{:S(2)}, u32[]{:S(2)}) collective-permute-start(f32[1,16,2048]{2,1,0:T(8,128)S(1)} %collective-permute-done.2.refs_10_), channel_id=1, source_target_pairs={{0,4},{4,8},{8,12},{12,14},{14,10},{10,6},{6,2},{2,0},{1,5},{5,9},... | collective-permute-start | bytes 393224 | tf_op jit(solution)/shard_map/ppermute | solution.py:294
  23.1 6.0 %collective-permute-start.15 = (f32[2,64,1024]{2,1,0:T(8,128)S(1)}, f32[2,64,1024]{2,1,0:T(8,128)S(1)}, u32[]{:S(2)}, u32[]{:S(2)}) collective-permute-start(f32[2,64,1024]{2,1,0:T(8,128)S(1)} %get-tuple-element.38), channel_id=1, source_target_pairs={{0,1},{1,0},{2,3},{3,2},{4,5},{5,4},{6,7},{7,6},{8,9},{9,8},{10,11... | collective-permute-start | bytes 1572872 | tf_op jit(solution)/shard_map/ppermute | solution.py:328
  27.9 2.2 %collective-permute-start.8 = (f32[32,1024]{1,0:T(8,128)S(1)}, f32[32,1024]{1,0:T(8,128)S(1)}, u32[]{:S(2)}, u32[]{:S(2)}) collective-permute-start(f32[32,1024]{1,0:T(8,128)S(1)} %last.1), channel_id=1, source_target_pairs={{0,1},{1,0},{2,3},{3,2},{4,5},{5,4},{6,7},{7,6},{8,9},{9,8},{10,11... | collective-permute-start | bytes 393224 | tf_op jit(solution)/shard_map/ppermute | solution.py:348

commit v8 on v7

--- a/solution.py
+++ b/solution.py
@@ -71,7 +71,7 @@
         copy.wait()
 
 
-def list_kernel(ab_tiles, cd_tiles, ab_irrep, cd_irrep, pattern, listed):
+def list_kernel(ab_tiles, cd_tiles, ab_irrep, cd_irrep, pattern, integrals, listed, landed, near, near_sem, sems):
     shape = (ab_tiles, LANES)
     lane = lax.broadcasted_iota(jnp.int32, shape, 1)
     line = lax.broadcasted_iota(jnp.int32, shape, 0)
@@ -107,42 +107,49 @@
     listed[0:1, :] = jnp.where(order[0:1, :] < found, places, 0.0).astype(jnp.int32)
     listed[1:2, :] = ((found + (UNROLL - 1)) * (1.0 / UNROLL)).astype(jnp.int32)
 
-
-def part_kernel(cd_tiles, listed, integrals, split, landed, sems):
+    copy = pltpu.make_async_copy(listed, near, near_sem)
+    copy.start()
+    copy.wait()
+    rounds = near[1, 0]
+
     def fetch(k):
-        start, column = place_in(listed[0, k], cd_tiles)
-        slot = lax.bitwise_and(k, FLIGHT - 1)
+        start, column = place_in(near[0, k], cd_tiles)
         return pltpu.make_async_copy(
-            integrals.at[pl.ds(start, TILE), pl.ds(column, TILE)], landed.at[slot], sems.at[slot]
+            integrals.at[pl.ds(start, TILE), pl.ds(column, TILE)],
+            landed.at[k],
+            sems.at[lax.bitwise_and(k, FLIGHT - 1)],
         )
 
+    def finish(round_at, carry):
+        for unrolled in range(UNROLL):
+            fetch(round_at * UNROLL + unrolled).wait()
+        return carry
+
     def begin(round_at, carry):
+        @pl.when(round_at >= AHEAD)
+        def _():
+            finish(round_at - AHEAD, 0)
+
         for unrolled in range(UNROLL):
             fetch(round_at * UNROLL + unrolled).start()
         return carry
 
-    rounds = listed[1, 0]
-    lax.fori_loop(0, jnp.minimum(rounds, AHEAD), begin, 0)
-
+    lax.fori_loop(0, rounds, begin, 0)
+    lax.fori_loop(jnp.maximum(rounds - AHEAD, 0), rounds, finish, 0)
+
+
+def part_kernel(listed, landed, split):
     def part(round_at, carry):
-        first = round_at * UNROLL
         for unrolled in range(UNROLL):
-            fetch(first + unrolled).wait()
-        for unrolled in range(UNROLL):
-            k = first + unrolled
+            k = round_at * UNROLL + unrolled
             real = jnp.logical_or(k == 0, listed[0, k] > 0)
-            tile = jnp.where(real, landed[lax.bitwise_and(k, FLIGHT - 1)], 0.0).T
+            tile = jnp.where(real, landed[k], 0.0).T
             upper = tile.astype(jnp.bfloat16)
             split[k, :, :TILE] = upper
             split[k, :, TILE:] = (tile - upper.astype(jnp.float32)).astype(jnp.bfloat16)
-
-        @pl.when(round_at + AHEAD < rounds)
-        def _():
-            begin(round_at + AHEAD, 0)
-
         return carry
 
-    lax.fori_loop(0, rounds, part, 0)
+    lax.fori_loop(0, listed[1, 0], part, 0)
 
 
 def place_in(place, cd_tiles):
@@ -263,25 +270,29 @@
             name="cut",
         )(in_hbm(amplitudes), *map(in_hbm, labels))
 
-        listed = pl.pallas_call(
+        listed, landed = pl.pallas_call(
             functools.partial(list_kernel, ab_tiles, cd_tiles),
-            out_shape=pltpu.VMEM((2, LANES), jnp.int32),
-            in_specs=[smem, smem, vmem],
-            out_specs=vmem,
+            out_shape=(pltpu.VMEM((2, LANES), jnp.int32), pltpu.VMEM((tiles, TILE, TILE), jnp.float32)),
+            in_specs=[smem, smem, vmem, hbm],
+            out_specs=(vmem, vmem),
+            scratch_shapes=[
+                pltpu.SMEM((2, LANES), jnp.int32),
+                pltpu.SemaphoreType.DMA,
+                pltpu.SemaphoreType.DMA((FLIGHT,)),
+            ],
             compiler_params=params,
             cost_estimate=pl.CostEstimate(flops=0, bytes_accessed=4 << 20, transcendentals=0),
             name="list",
-        )(near_ab, near_cd, near_pattern)
+        )(near_ab, near_cd, near_pattern, in_hbm(integrals))
         split = pl.pallas_call(
-            functools.partial(part_kernel, cd_tiles),
+            part_kernel,
             out_shape=pltpu.VMEM((tiles, TILE, 2 * TILE), jnp.bfloat16),
-            in_specs=[smem, hbm],
+            in_specs=[smem, vmem],
             out_specs=vmem,
-            scratch_shapes=[pltpu.VMEM((FLIGHT, TILE, TILE), jnp.float32), pltpu.SemaphoreType.DMA((FLIGHT,))],
             compiler_params=params,
             cost_estimate=pl.CostEstimate(flops=0, bytes_accessed=8 << 20, transcendentals=0),
             name="part",
-        )(listed, in_hbm(integrals))
+        )(listed, landed)
 
         held = {}
         for span in range(spans):

time: 31.2 us -> 31.3 us (level)
  starting transfers between devices: 16 us -> 19.1 us
  Pallas kernels: 11 us -> 9.46 us
  waiting for transfers between devices: 3.63 us -> 2.35 us
    pallas_call x1, Pallas kernels: 1.01 us -> 2.95 us  [shards(): pl.pallas_call(functools.partial(list_kernel, ab_tiles, cd_tiles), out_sh...]
    pallas_call x1, Pallas kernels: 2.53 us -> 0.84 us  [shards(): pl.pallas_call(part_kernel, out_shape=pltpu.VMEM((tiles, TILE, 2 * TILE),...]
    ppermute x14, starting transfers between devices: 11.2 us -> 12.7 us  [shards(): moved = lax.ppermute(moved, 'ab', pairs)]
    pallas_call x2, Pallas kernels: 3.75 us -> 2.34 us  [shards(): pl.pallas_call(functools.partial(step_kernel, count, rows, cd_tiles, grou...]
    ppermute x14, waiting for transfers between devices: 3.5 us -> 2.21 us  [shards(): moved = lax.ppermute(moved, 'ab', pairs)]
    ppermute x1, starting transfers between devices: 3.59 us -> 4.69 us  [shards(): lax.ppermute(send, 'cd', swap)]
    ppermute x1, starting transfers between devices: 1.23 us -> 1.7 us  [shards(): lax.ppermute(last, 'cd', swap)]
    pallas_call x1, Pallas kernels: 1.21 us -> 0.79 us  [shards(): pl.pallas_call(functools.partial(last_kernel, cd_tiles), out_shape=pltpu....]
  transfers between devices with their start and end apart: 16 -> 16, of which waited for: 5 -> 4; matrix products, arithmetic and copies ran while one was open for 0% -> 0% of each run, Pallas kernels for 30% -> 25%
where the time goes in v8:
time: 31.3 us; the launch traced here: 31 us
  starting transfers between devices  19.1 us (61%)
  Pallas kernels  9.46 us (30%)
  waiting for transfers between devices  2.35 us (8%)
    ppermute x14, starting transfers between devices, shards(): moved = lax.ppermute(moved, 'ab', pairs)  12.7 us
    ppermute x1, starting transfers between devices, shards(): lax.ppermute(send, 'cd', swap)  4.69 us
    pallas_call x1, Pallas kernels, shards(): pl.pallas_call(functools.partial(list_kernel, ab_tiles, cd_tiles), out_sh...  2.95 us
    pallas_call x2, Pallas kernels, shards(): pl.pallas_call(functools.partial(step_kernel, count, rows, cd_tiles, grou...  2.34 us
    ppermute x14, waiting for transfers between devices, shards(): moved = lax.ppermute(moved, 'ab', pairs)  2.21 us
    ppermute x1, starting transfers between devices, shards(): lax.ppermute(last, 'cd', swap)  1.7 us
    pallas_call x1, Pallas kernels, shards(): pl.pallas_call(cut_kernel, out_shape=(piece,) * spans + tuple((pltpu.VMEM...  1.01 us
    pallas_call x1, Pallas kernels, shards(): pl.pallas_call(merge_kernel, out_shape=pltpu.HBM((spans, half, slab), jnp...  0.85 us
  transfers between devices with their start and end apart: 16, of which 4 were waited for; matrix products, arithmetic and copies ran while one was open for 0% of the time, Pallas kernels for 25%

profile of v8, /device:TPU:1, one launch (start us, length us, event | category | flops | bytes accessed | tf_op | source)
XLA Modules:
  0.0 31.0 jit_solution(17983488991688516382)
XLA Ops:
  0.0 1.0 %cut.1 = (f32[1,16,2048]{2,1,0:T(8,128)S(1)}, f32[1,16,2048]{2,1,0:T(8,128)S(1)}, s32[8,16]{1,0:T(8,128)S(1)}, s32[8]{0:T(128)S(1)}, s32[16]{0:T(128)S(1)}) custom-call(f32[2,16,2048]{2,1,0:T(8,128)} %amplitudes.1, s32[8,16]{1,0:T(8,128)} %pattern.1, s32[8]{0:T(128)} %ab_irrep.1, s32[16]{0:T(128)} %cd_irrep.1), custom_call_target="tpu_custom_call" | custom-call | tf_op jit(solution)/shard_map/cut/pallas_call | solution.py:263
  1.0 2.1 %collective-permute-start.4 = (f32[1,16,2048]{2,1,0:T(8,128)S(1)}, f32[1,16,2048]{2,1,0:T(8,128)S(1)}, u32[]{:S(2)}, u32[]{:S(2)}) collective-permute-start(f32[1,16,2048]{2,1,0:T(8,128)S(1)} %get-tuple-element.32.refs_1_), channel_id=1, source_target_pairs={{4,0},{8,4},{12,8},{14,12},{10,14},{6,10},{2,6},{0,2},{5,1},{9,5},... | collective-permute-start | bytes 393224 | tf_op jit(solution)/shard_map/ppermute | solution.py:305
  3.1 0.1 collective-permute-start
  3.3 1.4 %collective-permute-start.12 = (f32[1,16,2048]{2,1,0:T(8,128)S(1)}, f32[1,16,2048]{2,1,0:T(8,128)S(1)}, u32[]{:S(2)}, u32[]{:S(2)}) collective-permute-start(f32[1,16,2048]{2,1,0:T(8,128)S(1)} %get-tuple-element.32.refs_1_), channel_id=1, source_target_pairs={{0,4},{4,8},{8,12},{12,14},{14,10},{10,6},{6,2},{2,0},{1,5},{5,9},... | collective-permute-start | bytes 393224 | tf_op jit(solution)/shard_map/ppermute | solution.py:305
  4.7 0.1 collective-permute-start.9
  4.7 3.0 %list.1 = (s32[2,128]{1,0:T(2,128)S(1)}, f32[128,128,128]{2,1,0:T(8,128)S(1)}) custom-call(s32[8]{0:T(128)S(1)} %get-tuple-element.24.ab_irrep, s32[16]{0:T(128)S(1)} %get-tuple-element.25.cd_irrep, s32[8,16]{1,0:T(8,128)S(1)} %get-tuple-element.26.pattern, f32[1024,2048]{1,0:T(8,128)} %integrals.1), custom_call_target="tpu_custom_call" | custom-call | bytes 4194304 | tf_op jit(solution)/shard_map/list/pallas_call | solution.py:273
  7.7 0.0 collective-permute-done.4.refs_3_
  7.7 1.5 %collective-permute-start.5 = (f32[1,16,2048]{2,1,0:T(8,128)S(1)}, f32[1,16,2048]{2,1,0:T(8,128)S(1)}, u32[]{:S(2)}, u32[]{:S(2)}) collective-permute-start(f32[1,16,2048]{2,1,0:T(8,128)S(1)} %collective-permute-done.4.refs_3_), channel_id=1, source_target_pairs={{4,0},{8,4},{12,8},{14,12},{10,14},{6,10},{2,6},{0,2},{5,1},{9,5},... | collective-permute-start | bytes 393224 | tf_op jit(solution)/shard_map/ppermute | solution.py:305
  9.2 0.0 collective-permute-done.refs_2_
  9.2 0.3 collective-permute-start.1
  9.5 0.5 %collective-permute-done.12.refs_5_ = f32[1,16,2048]{2,1,0:T(8,128)S(1)} collective-permute-done((f32[1,16,2048]{2,1,0:T(8,128)S(1)}, f32[1,16,2048]{2,1,0:T(8,128)S(1)}, u32[]{:S(2)}, u32[]{:S(2)}) %collective-permute-start.12) | collective-permute-done | bytes 131104 | tf_op jit(solution)/shard_map/ppermute | solution.py:305
  10.0 0.9 %collective-permute-start.13 = (f32[1,16,2048]{2,1,0:T(8,128)S(1)}, f32[1,16,2048]{2,1,0:T(8,128)S(1)}, u32[]{:S(2)}, u32[]{:S(2)}) collective-permute-start(f32[1,16,2048]{2,1,0:T(8,128)S(1)} %collective-permute-done.12.refs_5_), channel_id=1, source_target_pairs={{0,4},{4,8},{8,12},{12,14},{14,10},{10,6},{6,2},{2,0},{1,5},{5,9},... | collective-permute-start | bytes 393224 | tf_op jit(solution)/shard_map/ppermute | solution.py:305
  10.9 0.0 collective-permute-done.9.refs_4_
  10.9 0.6 %collective-permute-start.10 = (f32[1,16,2048]{2,1,0:T(8,128)S(1)}, f32[1,16,2048]{2,1,0:T(8,128)S(1)}, u32[]{:S(2)}, u32[]{:S(2)}) collective-permute-start(f32[1,16,2048]{2,1,0:T(8,128)S(1)} %collective-permute-done.9.refs_4_), channel_id=1, source_target_pairs={{4,0},{8,4},{12,8},{14,12},{10,14},{6,10},{2,6},{0,2},{5,1},{9,5},... | collective-permute-start | bytes 393224 | tf_op jit(solution)/shard_map/ppermute | solution.py:305
  11.5 0.8 %part.1.split = bf16[128,128,256]{2,1,0:T(8,128)(2,1)S(1)} custom-call(s32[2,128]{1,0:T(2,128)S(1)} %get-tuple-element.27.listed, f32[128,128,128]{2,1,0:T(8,128)S(1)} %get-tuple-element.28.landed), custom_call_target="tpu_custom_call" | custom-call | bytes 8388608 | tf_op jit(solution)/shard_map/part/pallas_call | solution.py:287
  12.3 0.0 collective-permute-done.5.refs_7_
  12.3 1.5 %collective-permute-start.6 = (f32[1,16,2048]{2,1,0:T(8,128)S(1)}, f32[1,16,2048]{2,1,0:T(8,128)S(1)}, u32[]{:S(2)}, u32[]{:S(2)}) collective-permute-start(f32[1,16,2048]{2,1,0:T(8,128)S(1)} %collective-permute-done.5.refs_7_), channel_id=1, source_target_pairs={{4,0},{8,4},{12,8},{14,12},{10,14},{6,10},{2,6},{0,2},{5,1},{9,5},... | collective-permute-start | bytes 393224 | tf_op jit(solution)/shard_map/ppermute | solution.py:305
  13.8 0.0 collective-permute-done.1.refs_6_
  13.8 0.0 collective-permute-start.2
  13.8 1.1 %collective-permute-done.13.refs_9_ = f32[1,16,2048]{2,1,0:T(8,128)S(1)} collective-permute-done((f32[1,16,2048]{2,1,0:T(8,128)S(1)}, f32[1,16,2048]{2,1,0:T(8,128)S(1)}, u32[]{:S(2)}, u32[]{:S(2)}) %collective-permute-start.13) | collective-permute-done | bytes 131104 | tf_op jit(solution)/shard_map/ppermute | solution.py:305
  14.9 0.7 %collective-permute-start.14 = (f32[1,16,2048]{2,1,0:T(8,128)S(1)}, f32[1,16,2048]{2,1,0:T(8,128)S(1)}, u32[]{:S(2)}, u32[]{:S(2)}) collective-permute-start(f32[1,16,2048]{2,1,0:T(8,128)S(1)} %collective-permute-done.13.refs_9_), channel_id=1, source_target_pairs={{0,4},{4,8},{8,12},{12,14},{14,10},{10,6},{6,2},{2,0},{1,5},{5,9},... | collective-permute-start | bytes 393224 | tf_op jit(solution)/shard_map/ppermute | solution.py:305
  15.6 0.0 collective-permute-done.10.refs_8_
  15.6 1.4 %collective-permute-start.11 = (f32[1,16,2048]{2,1,0:T(8,128)S(1)}, f32[1,16,2048]{2,1,0:T(8,128)S(1)}, u32[]{:S(2)}, u32[]{:S(2)}) collective-permute-start(f32[1,16,2048]{2,1,0:T(8,128)S(1)} %collective-permute-done.10.refs_8_), channel_id=1, source_target_pairs={{4,0},{8,4},{12,8},{14,12},{10,14},{6,10},{2,6},{0,2},{5,1},{9,5},... | collective-permute-start | bytes 393224 | tf_op jit(solution)/shard_map/ppermute | solution.py:305
  17.0 0.6 %collective-permute-done.6.refs_11_ = f32[1,16,2048]{2,1,0:T(8,128)S(1)} collective-permute-done((f32[1,16,2048]{2,1,0:T(8,128)S(1)}, f32[1,16,2048]{2,1,0:T(8,128)S(1)}, u32[]{:S(2)}, u32[]{:S(2)}) %collective-permute-start.6) | collective-permute-done | bytes 131104 | tf_op jit(solution)/shard_map/ppermute | solution.py:305
  17.6 2.2 %collective-permute-start.7 = (f32[1,16,2048]{2,1,0:T(8,128)S(1)}, f32[1,16,2048]{2,1,0:T(8,128)S(1)}, u32[]{:S(2)}, u32[]{:S(2)}) collective-permute-start(f32[1,16,2048]{2,1,0:T(8,128)S(1)} %collective-permute-done.6.refs_11_), channel_id=1, source_target_pairs={{4,0},{8,4},{12,8},{14,12},{10,14},{6,10},{2,6},{0,2},{5,1},{9,5},... | collective-permute-start | bytes 393224 | tf_op jit(solution)/shard_map/ppermute | solution.py:305
  19.8 0.0 collective-permute-done.2.refs_10_
  19.8 0.0 collective-permute-start.3
  19.8 1.5 %step.2 = (f32[2,64,1024]{2,1,0:T(8,128)S(1)}, f32[2,64,1024]{2,1,0:T(8,128)S(1)}) custom-call(s32[2,128]{1,0:T(2,128)S(1)} %get-tuple-element.27.listed, bf16[128,128,256]{2,1,0:T(8,128)(2,1)S(1)} %part.1.split, f32[1,16,2048]{2,1,0:T(8,128)S(1)} %get-tuple-element.29.refs_0_, f32[1,16,2048]{2,1,0:T(8,128)S(1)} %get-tuple-element.32.refs_1_, ...), custom_call_target="tpu_custom_call" | custom-call | flops 1073741824 | bytes 4194304 | tf_op jit(solution)/shard_map/step/pallas_call | solution.py:320
  21.3 0.0 collective-permute-done.14.refs_1_
  21.3 0.0 collective-permute-done.11.refs_0_
  21.3 0.9 %step.3 = (f32[2,64,1024]{2,1,0:T(8,128)S(1)}, f32[2,64,1024]{2,1,0:T(8,128)S(1)}) custom-call(s32[2,128]{1,0:T(2,128)S(1)} %get-tuple-element.27.listed, bf16[128,128,256]{2,1,0:T(8,128)(2,1)S(1)} %part.1.split, f32[1,16,2048]{2,1,0:T(8,128)S(1)} %collective-permute-done.11.refs_0_, ...), custom_call_target="tpu_custom_call", output_to_operand_aliasing={{0}: (4, {}), {1}: (5, {})} | custom-call | flops 1073741824 | bytes 4194304 | tf_op jit(solution)/shard_map/step/pallas_call | solution.py:320
  22.2 4.7 %collective-permute-start.15 = (f32[2,64,1024]{2,1,0:T(8,128)S(1)}, f32[2,64,1024]{2,1,0:T(8,128)S(1)}, u32[]{:S(2)}, u32[]{:S(2)}) collective-permute-start(f32[2,64,1024]{2,1,0:T(8,128)S(1)} %get-tuple-element.42), channel_id=1, source_target_pairs={{0,1},{1,0},{2,3},{3,2},{4,5},{5,4},{6,7},{7,6},{8,9},{9,8},{10,11... | collective-permute-start | bytes 1572872 | tf_op jit(solution)/shard_map/ppermute | solution.py:339
  26.9 0.0 collective-permute-done.7.refs_1_
  26.9 0.0 collective-permute-done.3.refs_0_
  26.9 0.8 %last.1 = f32[32,1024]{1,0:T(8,128)S(1)} custom-call(s32[2,128]{1,0:T(2,128)S(1)} %get-tuple-element.27.listed, bf16[128,128,256]{2,1,0:T(8,128)(2,1)S(1)} %part.1.split, f32[1,16,2048]{2,1,0:T(8,128)S(1)} %collective-permute-done.3.refs_0_, f32[1,16,2048]{2,1,0:T(8,128)S(1)} %collective-permute-done.7.refs_1_), custom_call_target="tpu_custom_call" | custom-call | flops 17179869184 | bytes 4194304 | tf_op jit(solution)/shard_map/last/pallas_call | solution.py:341
  27.7 1.7 %collective-permute-start.8 = (f32[32,1024]{1,0:T(8,128)S(1)}, f32[32,1024]{1,0:T(8,128)S(1)}, u32[]{:S(2)}, u32[]{:S(2)}) collective-permute-start(f32[32,1024]{1,0:T(8,128)S(1)} %last.1), channel_id=1, source_target_pairs={{0,1},{1,0},{2,3},{3,2},{4,5},{5,4},{6,7},{7,6},{8,9},{9,8},{10,11... | collective-permute-start | bytes 393224 | tf_op jit(solution)/shard_map/ppermute | solution.py:359
  29.4 0.0 collective-permute-done.15.received
  29.4 0.8 %merge.1.before = f32[2,64,1024]{2,1,0:T(8,128)} custom-call(f32[2,64,1024]{2,1,0:T(8,128)S(1)} %get-tuple-element.41.mine, f32[2,64,1024]{2,1,0:T(8,128)S(1)} %collective-permute-done.15.received), custom_call_target="tpu_custom_call" | custom-call | tf_op jit(solution)/shard_map/merge/pallas_call | solution.py:332
  30.2 0.1 collective-permute-done.8.received
  30.4 0.7 %final.1 = f32[2,64,1024]{2,1,0:T(8,128)} custom-call(f32[32,1024]{1,0:T(8,128)S(1)} %last.1, f32[32,1024]{1,0:T(8,128)S(1)} %collective-permute-done.8.received, f32[2,64,1024]{2,1,0:T(8,128)} %merge.1.before), custom_call_target="tpu_custom_call", output_to_operand_aliasing={{}: (2, {})} | custom-call | tf_op jit(solution)/shard_map/final/pallas_call | solution.py:350
Async XLA Ops:
  1.0 6.7 %collective-permute-start.4 = (f32[1,16,2048]{2,1,0:T(8,128)S(1)}, f32[1,16,2048]{2,1,0:T(8,128)S(1)}, u32[]{:S(2)}, u32[]{:S(2)}) collective-permute-start(f32[1,16,2048]{2,1,0:T(8,128)S(1)} %get-tuple-element.32.refs_1_), channel_id=1, source_target_pairs={{4,0},{8,4},{12,8},{14,12},{10,14},{6,10},{2,6},{0,2},{5,1},{9,5},... | collective-permute-start | bytes 393224 | tf_op jit(solution)/shard_map/ppermute | solution.py:305
  3.1 6.1 %collective-permute-start = (f32[1,16,2048]{2,1,0:T(8,128)S(1)}, f32[1,16,2048]{2,1,0:T(8,128)S(1)}, u32[]{:S(2)}, u32[]{:S(2)}) collective-permute-start(f32[1,16,2048]{2,1,0:T(8,128)S(1)} %get-tuple-element.29.refs_0_), channel_id=1, source_target_pairs={{0,4},{4,8},{8,12},{12,14},{14,10},{10,6},{6,2},{2,0},{1,5},{5,9},... | collective-permute-start | bytes 393224 | tf_op jit(solution)/shard_map/ppermute | solution.py:305
  3.3 6.7 %collective-permute-start.12 = (f32[1,16,2048]{2,1,0:T(8,128)S(1)}, f32[1,16,2048]{2,1,0:T(8,128)S(1)}, u32[]{:S(2)}, u32[]{:S(2)}) collective-permute-start(f32[1,16,2048]{2,1,0:T(8,128)S(1)} %get-tuple-element.32.refs_1_), channel_id=1, source_target_pairs={{0,4},{4,8},{8,12},{12,14},{14,10},{10,6},{6,2},{2,0},{1,5},{5,9},... | collective-permute-start | bytes 393224 | tf_op jit(solution)/shard_map/ppermute | solution.py:305
  4.7 6.2 %collective-permute-start.9 = (f32[1,16,2048]{2,1,0:T(8,128)S(1)}, f32[1,16,2048]{2,1,0:T(8,128)S(1)}, u32[]{:S(2)}, u32[]{:S(2)}) collective-permute-start(f32[1,16,2048]{2,1,0:T(8,128)S(1)} %get-tuple-element.29.refs_0_), channel_id=1, source_target_pairs={{4,0},{8,4},{12,8},{14,12},{10,14},{6,10},{2,6},{0,2},{5,1},{9,5},... | collective-permute-start | bytes 393224 | tf_op jit(solution)/shard_map/ppermute | solution.py:305
  7.7 4.6 %collective-permute-start.5 = (f32[1,16,2048]{2,1,0:T(8,128)S(1)}, f32[1,16,2048]{2,1,0:T(8,128)S(1)}, u32[]{:S(2)}, u32[]{:S(2)}) collective-permute-start(f32[1,16,2048]{2,1,0:T(8,128)S(1)} %collective-permute-done.4.refs_3_), channel_id=1, source_target_pairs={{4,0},{8,4},{12,8},{14,12},{10,14},{6,10},{2,6},{0,2},{5,1},{9,5},... | collective-permute-start | bytes 393224 | tf_op jit(solution)/shard_map/ppermute | solution.py:305
  9.2 4.6 %collective-permute-start.1 = (f32[1,16,2048]{2,1,0:T(8,128)S(1)}, f32[1,16,2048]{2,1,0:T(8,128)S(1)}, u32[]{:S(2)}, u32[]{:S(2)}) collective-permute-start(f32[1,16,2048]{2,1,0:T(8,128)S(1)} %collective-permute-done.refs_2_), channel_id=1, source_target_pairs={{0,4},{4,8},{8,12},{12,14},{14,10},{10,6},{6,2},{2,0},{1,5},{5,9},... | collective-permute-start | bytes 393224 | tf_op jit(solution)/shard_map/ppermute | solution.py:305
  10.0 4.9 %collective-permute-start.13 = (f32[1,16,2048]{2,1,0:T(8,128)S(1)}, f32[1,16,2048]{2,1,0:T(8,128)S(1)}, u32[]{:S(2)}, u32[]{:S(2)}) collective-permute-start(f32[1,16,2048]{2,1,0:T(8,128)S(1)} %collective-permute-done.12.refs_5_), channel_id=1, source_target_pairs={{0,4},{4,8},{8,12},{12,14},{14,10},{10,6},{6,2},{2,0},{1,5},{5,9},... | collective-permute-start | bytes 393224 | tf_op jit(solution)/shard_map/ppermute | solution.py:305
  10.9 4.7 %collective-permute-start.10 = (f32[1,16,2048]{2,1,0:T(8,128)S(1)}, f32[1,16,2048]{2,1,0:T(8,128)S(1)}, u32[]{:S(2)}, u32[]{:S(2)}) collective-permute-start(f32[1,16,2048]{2,1,0:T(8,128)S(1)} %collective-permute-done.9.refs_4_), channel_id=1, source_target_pairs={{4,0},{8,4},{12,8},{14,12},{10,14},{6,10},{2,6},{0,2},{5,1},{9,5},... | collective-permute-start | bytes 393224 | tf_op jit(solution)/shard_map/ppermute | solution.py:305
  12.3 5.3 %collective-permute-start.6 = (f32[1,16,2048]{2,1,0:T(8,128)S(1)}, f32[1,16,2048]{2,1,0:T(8,128)S(1)}, u32[]{:S(2)}, u32[]{:S(2)}) collective-permute-start(f32[1,16,2048]{2,1,0:T(8,128)S(1)} %collective-permute-done.5.refs_7_), channel_id=1, source_target_pairs={{4,0},{8,4},{12,8},{14,12},{10,14},{6,10},{2,6},{0,2},{5,1},{9,5},... | collective-permute-start | bytes 393224 | tf_op jit(solution)/shard_map/ppermute | solution.py:305
  13.8 6.0 %collective-permute-start.2 = (f32[1,16,2048]{2,1,0:T(8,128)S(1)}, f32[1,16,2048]{2,1,0:T(8,128)S(1)}, u32[]{:S(2)}, u32[]{:S(2)}) collective-permute-start(f32[1,16,2048]{2,1,0:T(8,128)S(1)} %collective-permute-done.1.refs_6_), channel_id=1, source_target_pairs={{0,4},{4,8},{8,12},{12,14},{14,10},{10,6},{6,2},{2,0},{1,5},{5,9},... | collective-permute-start | bytes 393224 | tf_op jit(solution)/shard_map/ppermute | solution.py:305
  14.9 6.4 %collective-permute-start.14 = (f32[1,16,2048]{2,1,0:T(8,128)S(1)}, f32[1,16,2048]{2,1,0:T(8,128)S(1)}, u32[]{:S(2)}, u32[]{:S(2)}) collective-permute-start(f32[1,16,2048]{2,1,0:T(8,128)S(1)} %collective-permute-done.13.refs_9_), channel_id=1, source_target_pairs={{0,4},{4,8},{8,12},{12,14},{14,10},{10,6},{6,2},{2,0},{1,5},{5,9},... | collective-permute-start | bytes 393224 | tf_op jit(solution)/shard_map/ppermute | solution.py:305
  15.6 5.7 %collective-permute-start.11 = (f32[1,16,2048]{2,1,0:T(8,128)S(1)}, f32[1,16,2048]{2,1,0:T(8,128)S(1)}, u32[]{:S(2)}, u32[]{:S(2)}) collective-permute-start(f32[1,16,2048]{2,1,0:T(8,128)S(1)} %collective-permute-done.10.refs_8_), channel_id=1, source_target_pairs={{4,0},{8,4},{12,8},{14,12},{10,14},{6,10},{2,6},{0,2},{5,1},{9,5},... | collective-permute-start | bytes 393224 | tf_op jit(solution)/shard_map/ppermute | solution.py:305
  17.6 9.3 %collective-permute-start.7 = (f32[1,16,2048]{2,1,0:T(8,128)S(1)}, f32[1,16,2048]{2,1,0:T(8,128)S(1)}, u32[]{:S(2)}, u32[]{:S(2)}) collective-permute-start(f32[1,16,2048]{2,1,0:T(8,128)S(1)} %collective-permute-done.6.refs_11_), channel_id=1, source_target_pairs={{4,0},{8,4},{12,8},{14,12},{10,14},{6,10},{2,6},{0,2},{5,1},{9,5},... | collective-permute-start | bytes 393224 | tf_op jit(solution)/shard_map/ppermute | solution.py:305
  19.8 7.1 %collective-permute-start.3 = (f32[1,16,2048]{2,1,0:T(8,128)S(1)}, f32[1,16,2048]{2,1,0:T(8,128)S(1)}, u32[]{:S(2)}, u32[]{:S(2)}) collective-permute-start(f32[1,16,2048]{2,1,0:T(8,128)S(1)} %collective-permute-done.2.refs_10_), channel_id=1, source_target_pairs={{0,4},{4,8},{8,12},{12,14},{14,10},{10,6},{6,2},{2,0},{1,5},{5,9},... | collective-permute-start | bytes 393224 | tf_op jit(solution)/shard_map/ppermute | solution.py:305
  22.2 7.2 %collective-permute-start.15 = (f32[2,64,1024]{2,1,0:T(8,128)S(1)}, f32[2,64,1024]{2,1,0:T(8,128)S(1)}, u32[]{:S(2)}, u32[]{:S(2)}) collective-permute-start(f32[2,64,1024]{2,1,0:T(8,128)S(1)} %get-tuple-element.42), channel_id=1, source_target_pairs={{0,1},{1,0},{2,3},{3,2},{4,5},{5,4},{6,7},{7,6},{8,9},{9,8},{10,11... | collective-permute-start | bytes 1572872 | tf_op jit(solution)/shard_map/ppermute | solution.py:339
  27.7 2.7 %collective-permute-start.8 = (f32[32,1024]{1,0:T(8,128)S(1)}, f32[32,1024]{1,0:T(8,128)S(1)}, u32[]{:S(2)}, u32[]{:S(2)}) collective-permute-start(f32[32,1024]{1,0:T(8,128)S(1)} %last.1), channel_id=1, source_target_pairs={{0,1},{1,0},{2,3},{3,2},{4,5},{5,4},{6,7},{7,6},{8,9},{9,8},{10,11... | collective-permute-start | bytes 393224 | tf_op jit(solution)/shard_map/ppermute | solution.py:359

commit v9 on v7

--- a/solution.py
+++ b/solution.py
@@ -59,19 +59,16 @@
     return jnp.where(start >= whole, start - whole, start)
 
 
-def cut_kernel(amplitudes, pattern, ab_irrep, cd_irrep, *refs):
-    *outs, sems = refs
-    spans = len(outs) - 3
-    pairs = [(amplitudes.at[pl.ds(at, 1)], outs[at]) for at in range(spans)]
-    pairs += list(zip((pattern, ab_irrep, cd_irrep), outs[spans:]))
+def cut_kernel(ab_tiles, cd_tiles, spans, amplitudes, labels_ab, labels_cd, labels_pattern, *refs):
+    outs, (listed, ab_irrep, cd_irrep, pattern, sems) = refs[:spans], refs[spans:]
+    pairs = [(labels_ab, ab_irrep), (labels_cd, cd_irrep), (labels_pattern, pattern)]
+    pairs += [(amplitudes.at[pl.ds(at, 1)], out) for at, out in enumerate(outs)]
     copies = [pltpu.make_async_copy(start, end, sems.at[at]) for at, (start, end) in enumerate(pairs)]
     for copy in copies:
         copy.start()
-    for copy in copies:
+    for copy in copies[:3]:
         copy.wait()
 
-
-def list_kernel(ab_tiles, cd_tiles, ab_irrep, cd_irrep, pattern, listed):
     shape = (ab_tiles, LANES)
     lane = lax.broadcasted_iota(jnp.int32, shape, 1)
     line = lax.broadcasted_iota(jnp.int32, shape, 0)
@@ -106,6 +103,8 @@
     places = jnp.sum(passed, axis=0, keepdims=True)
     listed[0:1, :] = jnp.where(order[0:1, :] < found, places, 0.0).astype(jnp.int32)
     listed[1:2, :] = ((found + (UNROLL - 1)) * (1.0 / UNROLL)).astype(jnp.int32)
+    for copy in copies[3:]:
+        copy.wait()
 
 
 def part_kernel(cd_tiles, listed, integrals, split, landed, sems):
@@ -252,26 +251,20 @@
         params = pltpu.CompilerParams(vmem_limit_bytes=VMEM_LIMIT)
         piece = pltpu.VMEM((1, rows, depth), jnp.float32)
 
-        labels = (block_pattern, ab_irrep, cd_irrep)
-        *own, near_pattern, near_ab, near_cd = pl.pallas_call(
-            cut_kernel,
-            out_shape=(piece,) * spans + tuple(pltpu.VMEM(label.shape, label.dtype) for label in labels),
+        *own, listed = pl.pallas_call(
+            functools.partial(cut_kernel, ab_tiles, cd_tiles, spans),
+            out_shape=(piece,) * spans + (pltpu.VMEM((2, LANES), jnp.int32),),
             in_specs=[hbm] * 4,
-            out_specs=(vmem,) * (spans + 3),
-            scratch_shapes=[pltpu.SemaphoreType.DMA((spans + 3,))],
+            out_specs=(vmem,) * (spans + 1),
+            scratch_shapes=[
+                pltpu.SMEM(ab_irrep.shape, jnp.int32),
+                pltpu.SMEM(cd_irrep.shape, jnp.int32),
+                pltpu.VMEM(block_pattern.shape, jnp.int32),
+                pltpu.SemaphoreType.DMA((spans + 3,)),
+            ],
             compiler_params=params,
             name="cut",
-        )(in_hbm(amplitudes), *map(in_hbm, labels))
-
-        listed = pl.pallas_call(
-            functools.partial(list_kernel, ab_tiles, cd_tiles),
-            out_shape=pltpu.VMEM((2, LANES), jnp.int32),
-            in_specs=[smem, smem, vmem],
-            out_specs=vmem,
-            compiler_params=params,
-            cost_estimate=pl.CostEstimate(flops=0, bytes_accessed=4 << 20, transcendentals=0),
-            name="list",
-        )(near_ab, near_cd, near_pattern)
+        )(*map(in_hbm, (amplitudes, ab_irrep, cd_irrep, block_pattern)))
         split = pl.pallas_call(
             functools.partial(part_kernel, cd_tiles),
             out_shape=pltpu.VMEM((tiles, TILE, 2 * TILE), jnp.bfloat16),
@@ -289,8 +282,8 @@
             for pairs, sign in ((ahead, -1), (back, 1)):
                 moved = own[span]
                 for hop in range(1, far + 1 if (sign < 0) == (span % 2 == 0) else far):
-                    if hop in (2, 3):
-                        moved, _ = lax.optimization_barrier((moved, listed if hop == 2 else split))
+                    if hop == 2:
+                        moved, _ = lax.optimization_barrier((moved, split))
                     moved = lax.ppermute(moved, "ab", pairs)
                     held[span, -far if hop == far else sign * hop] = moved
 

time: 31.2 us -> 30.4 us (0.974)
  Pallas kernels: 11 us -> 8.84 us
  starting transfers between devices: 16 us -> 17 us
  waiting for transfers between devices: 3.63 us -> 4.29 us
    pallas_call x2, Pallas kernels: 3.75 us -> 2.9 us  [shards(): pl.pallas_call(functools.partial(step_kernel, count, rows, cd_tiles, grou...]
    pallas_call x2 -> x1, Pallas kernels: 2.02 us -> 1.2 us  [shards(): pl.pallas_call(functools.partial(cut_kernel, ab_tiles, cd_tiles, spans),...]
    ppermute x14, waiting for transfers between devices: 3.5 us -> 4.15 us  [shards(): moved = lax.ppermute(moved, 'ab', pairs)]
    ppermute x1, starting transfers between devices: 3.59 us -> 3.96 us  [shards(): lax.ppermute(send, 'cd', swap)]
    ppermute x14, starting transfers between devices: 11.2 us -> 11.5 us  [shards(): moved = lax.ppermute(moved, 'ab', pairs)]
  transfers between devices with their start and end apart: 16 -> 16, of which waited for: 5 -> 5; matrix products, arithmetic and copies ran while one was open for 0% -> 0% of each run, Pallas kernels for 30% -> 23%
where the time goes in v9:
time: 30.4 us; the launch traced here: 30.2 us
  starting transfers between devices  17 us (56%)
  Pallas kernels  8.84 us (29%)
  waiting for transfers between devices  4.29 us (14%)
    ppermute x14, starting transfers between devices, shards(): moved = lax.ppermute(moved, 'ab', pairs)  11.5 us
    ppermute x14, waiting for transfers between devices, shards(): moved = lax.ppermute(moved, 'ab', pairs)  4.15 us
    ppermute x1, starting transfers between devices, shards(): lax.ppermute(send, 'cd', swap)  3.96 us
    pallas_call x2, Pallas kernels, shards(): pl.pallas_call(functools.partial(step_kernel, count, rows, cd_tiles, grou...  2.9 us
    pallas_call x1, Pallas kernels, shards(): pl.pallas_call(functools.partial(part_kernel, cd_tiles), out_shape=pltpu....  2.23 us
    ppermute x1, starting transfers between devices, shards(): lax.ppermute(last, 'cd', swap)  1.53 us
    pallas_call x1, Pallas kernels, shards(): pl.pallas_call(functools.partial(cut_kernel, ab_tiles, cd_tiles, spans),...  1.2 us
    pallas_call x1, Pallas kernels, shards(): pl.pallas_call(functools.partial(last_kernel, cd_tiles), out_shape=pltpu....  0.98 us
  transfers between devices with their start and end apart: 16, of which 5 were waited for; matrix products, arithmetic and copies ran while one was open for 0% of the time, Pallas kernels for 23%

profile of v9, /device:TPU:1, one launch (start us, length us, event | category | flops | bytes accessed | tf_op | source)
XLA Modules:
  0.0 30.2 jit_solution(6879144166033038950)
XLA Ops:
  0.0 1.2 %cut.1 = (f32[1,16,2048]{2,1,0:T(8,128)S(1)}, f32[1,16,2048]{2,1,0:T(8,128)S(1)}, s32[2,128]{1,0:T(2,128)S(1)}) custom-call(f32[2,16,2048]{2,1,0:T(8,128)} %amplitudes.1, s32[8]{0:T(128)} %labels_ab.1, s32[16]{0:T(128)} %labels_cd.1, s32[8,16]{1,0:T(8,128)} %labels_pattern.1), custom_call_target="tpu_custom_call" | custom-call | tf_op jit(solution)/shard_map/cut/pallas_call | solution.py:254
  1.2 2.1 %collective-permute-start.4 = (f32[1,16,2048]{2,1,0:T(8,128)S(1)}, f32[1,16,2048]{2,1,0:T(8,128)S(1)}, u32[]{:S(2)}, u32[]{:S(2)}) collective-permute-start(f32[1,16,2048]{2,1,0:T(8,128)S(1)} %get-tuple-element.19.refs_1_), channel_id=1, source_target_pairs={{4,0},{8,4},{12,8},{14,12},{10,14},{6,10},{2,6},{0,2},{5,1},{9,5},... | collective-permute-start | bytes 393224 | tf_op jit(solution)/shard_map/ppermute | solution.py:287
  3.3 0.1 collective-permute-start
  3.5 1.3 %collective-permute-start.9 = (f32[1,16,2048]{2,1,0:T(8,128)S(1)}, f32[1,16,2048]{2,1,0:T(8,128)S(1)}, u32[]{:S(2)}, u32[]{:S(2)}) collective-permute-start(f32[1,16,2048]{2,1,0:T(8,128)S(1)} %get-tuple-element.17.refs_0_), channel_id=1, source_target_pairs={{4,0},{8,4},{12,8},{14,12},{10,14},{6,10},{2,6},{0,2},{5,1},{9,5},... | collective-permute-start | bytes 393224 | tf_op jit(solution)/shard_map/ppermute | solution.py:287
  4.8 0.1 collective-permute-start.12
  4.9 2.2 %part.1.split = bf16[128,128,256]{2,1,0:T(8,128)(2,1)S(1)} custom-call(s32[2,128]{1,0:T(2,128)S(1)} %get-tuple-element.16.listed, f32[1024,2048]{1,0:T(8,128)} %integrals.1), custom_call_target="tpu_custom_call" | custom-call | bytes 8388608 | tf_op jit(solution)/shard_map/part/pallas_call | solution.py:268
  7.2 0.0 collective-permute-done.4.refs_3_
  7.2 1.5 %collective-permute-start.5 = (f32[1,16,2048]{2,1,0:T(8,128)S(1)}, f32[1,16,2048]{2,1,0:T(8,128)S(1)}, u32[]{:S(2)}, u32[]{:S(2)}) collective-permute-start(f32[1,16,2048]{2,1,0:T(8,128)S(1)} %collective-permute-done.4.refs_3_), channel_id=1, source_target_pairs={{4,0},{8,4},{12,8},{14,12},{10,14},{6,10},{2,6},{0,2},{5,1},{9,5},... | collective-permute-start | bytes 393224 | tf_op jit(solution)/shard_map/ppermute | solution.py:287
  8.7 0.0 collective-permute-done.refs_2_
  8.7 0.3 collective-permute-start.1
  9.0 0.4 %collective-permute-done.9.refs_4_ = f32[1,16,2048]{2,1,0:T(8,128)S(1)} collective-permute-done((f32[1,16,2048]{2,1,0:T(8,128)S(1)}, f32[1,16,2048]{2,1,0:T(8,128)S(1)}, u32[]{:S(2)}, u32[]{:S(2)}) %collective-permute-start.9) | collective-permute-done | bytes 131104 | tf_op jit(solution)/shard_map/ppermute | solution.py:287
  9.4 1.1 %collective-permute-start.10 = (f32[1,16,2048]{2,1,0:T(8,128)S(1)}, f32[1,16,2048]{2,1,0:T(8,128)S(1)}, u32[]{:S(2)}, u32[]{:S(2)}) collective-permute-start(f32[1,16,2048]{2,1,0:T(8,128)S(1)} %collective-permute-done.9.refs_4_), channel_id=1, source_target_pairs={{4,0},{8,4},{12,8},{14,12},{10,14},{6,10},{2,6},{0,2},{5,1},{9,5},... | collective-permute-start | bytes 393224 | tf_op jit(solution)/shard_map/ppermute | solution.py:287
  10.5 0.0 collective-permute-done.12.refs_5_
  10.5 0.4 %collective-permute-start.13 = (f32[1,16,2048]{2,1,0:T(8,128)S(1)}, f32[1,16,2048]{2,1,0:T(8,128)S(1)}, u32[]{:S(2)}, u32[]{:S(2)}) collective-permute-start(f32[1,16,2048]{2,1,0:T(8,128)S(1)} %collective-permute-done.12.refs_5_), channel_id=1, source_target_pairs={{0,4},{4,8},{8,12},{12,14},{14,10},{10,6},{6,2},{2,0},{1,5},{5,9},... | collective-permute-start | bytes 393224 | tf_op jit(solution)/shard_map/ppermute | solution.py:287
  10.9 0.8 %collective-permute-done.5.refs_7_ = f32[1,16,2048]{2,1,0:T(8,128)S(1)} collective-permute-done((f32[1,16,2048]{2,1,0:T(8,128)S(1)}, f32[1,16,2048]{2,1,0:T(8,128)S(1)}, u32[]{:S(2)}, u32[]{:S(2)}) %collective-permute-start.5) | collective-permute-done | bytes 131104 | tf_op jit(solution)/shard_map/ppermute | solution.py:287
  11.7 1.4 %collective-permute-start.6 = (f32[1,16,2048]{2,1,0:T(8,128)S(1)}, f32[1,16,2048]{2,1,0:T(8,128)S(1)}, u32[]{:S(2)}, u32[]{:S(2)}) collective-permute-start(f32[1,16,2048]{2,1,0:T(8,128)S(1)} %collective-permute-done.5.refs_7_), channel_id=1, source_target_pairs={{4,0},{8,4},{12,8},{14,12},{10,14},{6,10},{2,6},{0,2},{5,1},{9,5},... | collective-permute-start | bytes 393224 | tf_op jit(solution)/shard_map/ppermute | solution.py:287
  13.1 0.0 collective-permute-done.1.refs_6_
  13.1 0.1 collective-permute-start.2
  13.1 1.8 %collective-permute-done.10.refs_8_ = f32[1,16,2048]{2,1,0:T(8,128)S(1)} collective-permute-done((f32[1,16,2048]{2,1,0:T(8,128)S(1)}, f32[1,16,2048]{2,1,0:T(8,128)S(1)}, u32[]{:S(2)}, u32[]{:S(2)}) %collective-permute-start.10) | collective-permute-done | bytes 131104 | tf_op jit(solution)/shard_map/ppermute | solution.py:287
  14.9 0.7 %collective-permute-start.11 = (f32[1,16,2048]{2,1,0:T(8,128)S(1)}, f32[1,16,2048]{2,1,0:T(8,128)S(1)}, u32[]{:S(2)}, u32[]{:S(2)}) collective-permute-start(f32[1,16,2048]{2,1,0:T(8,128)S(1)} %collective-permute-done.10.refs_8_), channel_id=1, source_target_pairs={{4,0},{8,4},{12,8},{14,12},{10,14},{6,10},{2,6},{0,2},{5,1},{9,5},... | collective-permute-start | bytes 393224 | tf_op jit(solution)/shard_map/ppermute | solution.py:287
  15.6 0.0 collective-permute-done.13.refs_9_
  15.6 0.8 %collective-permute-start.14 = (f32[1,16,2048]{2,1,0:T(8,128)S(1)}, f32[1,16,2048]{2,1,0:T(8,128)S(1)}, u32[]{:S(2)}, u32[]{:S(2)}) collective-permute-start(f32[1,16,2048]{2,1,0:T(8,128)S(1)} %collective-permute-done.13.refs_9_), channel_id=1, source_target_pairs={{0,4},{4,8},{8,12},{12,14},{14,10},{10,6},{6,2},{2,0},{1,5},{5,9},... | collective-permute-start | bytes 393224 | tf_op jit(solution)/shard_map/ppermute | solution.py:287
  16.4 1.1 %collective-permute-done.6.refs_11_ = f32[1,16,2048]{2,1,0:T(8,128)S(1)} collective-permute-done((f32[1,16,2048]{2,1,0:T(8,128)S(1)}, f32[1,16,2048]{2,1,0:T(8,128)S(1)}, u32[]{:S(2)}, u32[]{:S(2)}) %collective-permute-start.6) | collective-permute-done | bytes 131104 | tf_op jit(solution)/shard_map/ppermute | solution.py:287
  17.5 1.1 %collective-permute-start.7 = (f32[1,16,2048]{2,1,0:T(8,128)S(1)}, f32[1,16,2048]{2,1,0:T(8,128)S(1)}, u32[]{:S(2)}, u32[]{:S(2)}) collective-permute-start(f32[1,16,2048]{2,1,0:T(8,128)S(1)} %collective-permute-done.6.refs_11_), channel_id=1, source_target_pairs={{4,0},{8,4},{12,8},{14,12},{10,14},{6,10},{2,6},{0,2},{5,1},{9,5},... | collective-permute-start | bytes 393224 | tf_op jit(solution)/shard_map/ppermute | solution.py:287
  18.6 0.0 collective-permute-done.2.refs_10_
  18.7 0.5 %collective-permute-start.3 = (f32[1,16,2048]{2,1,0:T(8,128)S(1)}, f32[1,16,2048]{2,1,0:T(8,128)S(1)}, u32[]{:S(2)}, u32[]{:S(2)}) collective-permute-start(f32[1,16,2048]{2,1,0:T(8,128)S(1)} %collective-permute-done.2.refs_10_), channel_id=1, source_target_pairs={{0,4},{4,8},{8,12},{12,14},{14,10},{10,6},{6,2},{2,0},{1,5},{5,9},... | collective-permute-start | bytes 393224 | tf_op jit(solution)/shard_map/ppermute | solution.py:287
  19.1 1.9 %step.2 = (f32[2,64,1024]{2,1,0:T(8,128)S(1)}, f32[2,64,1024]{2,1,0:T(8,128)S(1)}) custom-call(s32[2,128]{1,0:T(2,128)S(1)} %get-tuple-element.16.listed, bf16[128,128,256]{2,1,0:T(8,128)(2,1)S(1)} %part.1.split, f32[1,16,2048]{2,1,0:T(8,128)S(1)} %get-tuple-element.17.refs_0_, f32[1,16,2048]{2,1,0:T(8,128)S(1)} %get-tuple-element.19.refs_1_, ...), custom_call_target="tpu_custom_call" | custom-call | flops 1073741824 | bytes 4194304 | tf_op jit(solution)/shard_map/step/pallas_call | solution.py:302
  21.0 0.0 collective-permute-done.11.refs_0_
  21.0 0.0 collective-permute-done.14.refs_1_
  21.0 1.0 %step.3 = (f32[2,64,1024]{2,1,0:T(8,128)S(1)}, f32[2,64,1024]{2,1,0:T(8,128)S(1)}) custom-call(s32[2,128]{1,0:T(2,128)S(1)} %get-tuple-element.16.listed, bf16[128,128,256]{2,1,0:T(8,128)(2,1)S(1)} %part.1.split, f32[1,16,2048]{2,1,0:T(8,128)S(1)} %collective-permute-done.11.refs_0_, ...), custom_call_target="tpu_custom_call", output_to_operand_aliasing={{0}: (4, {}), {1}: (5, {})} | custom-call | flops 1073741824 | bytes 4194304 | tf_op jit(solution)/shard_map/step/pallas_call | solution.py:302
  22.1 4.0 %collective-permute-start.15 = (f32[2,64,1024]{2,1,0:T(8,128)S(1)}, f32[2,64,1024]{2,1,0:T(8,128)S(1)}, u32[]{:S(2)}, u32[]{:S(2)}) collective-permute-start(f32[2,64,1024]{2,1,0:T(8,128)S(1)} %get-tuple-element.26), channel_id=1, source_target_pairs={{0,1},{1,0},{2,3},{3,2},{4,5},{5,4},{6,7},{7,6},{8,9},{9,8},{10,11... | collective-permute-start | bytes 1572872 | tf_op jit(solution)/shard_map/ppermute | solution.py:321
  26.0 0.0 collective-permute-done.7.refs_1_
  26.0 0.0 collective-permute-done.3.refs_0_
  26.0 1.0 %last.1 = f32[32,1024]{1,0:T(8,128)S(1)} custom-call(s32[2,128]{1,0:T(2,128)S(1)} %get-tuple-element.16.listed, bf16[128,128,256]{2,1,0:T(8,128)(2,1)S(1)} %part.1.split, f32[1,16,2048]{2,1,0:T(8,128)S(1)} %collective-permute-done.3.refs_0_, f32[1,16,2048]{2,1,0:T(8,128)S(1)} %collective-permute-done.7.refs_1_), custom_call_target="tpu_custom_call" | custom-call | flops 17179869184 | bytes 4194304 | tf_op jit(solution)/shard_map/last/pallas_call | solution.py:323
  27.0 1.5 %collective-permute-start.8 = (f32[32,1024]{1,0:T(8,128)S(1)}, f32[32,1024]{1,0:T(8,128)S(1)}, u32[]{:S(2)}, u32[]{:S(2)}) collective-permute-start(f32[32,1024]{1,0:T(8,128)S(1)} %last.1), channel_id=1, source_target_pairs={{0,1},{1,0},{2,3},{3,2},{4,5},{5,4},{6,7},{7,6},{8,9},{9,8},{10,11... | collective-permute-start | bytes 393224 | tf_op jit(solution)/shard_map/ppermute | solution.py:341
  28.6 0.0 collective-permute-done.15.received
  28.6 0.8 %merge.1.before = f32[2,64,1024]{2,1,0:T(8,128)} custom-call(f32[2,64,1024]{2,1,0:T(8,128)S(1)} %get-tuple-element.25.mine, f32[2,64,1024]{2,1,0:T(8,128)S(1)} %collective-permute-done.15.received), custom_call_target="tpu_custom_call" | custom-call | tf_op jit(solution)/shard_map/merge/pallas_call | solution.py:314
  29.4 0.1 collective-permute-done.8.received
  29.5 0.7 %final.1 = f32[2,64,1024]{2,1,0:T(8,128)} custom-call(f32[32,1024]{1,0:T(8,128)S(1)} %last.1, f32[32,1024]{1,0:T(8,128)S(1)} %collective-permute-done.8.received, f32[2,64,1024]{2,1,0:T(8,128)} %merge.1.before), custom_call_target="tpu_custom_call", output_to_operand_aliasing={{}: (2, {})} | custom-call | tf_op jit(solution)/shard_map/final/pallas_call | solution.py:332
Async XLA Ops:
  1.2 5.9 %collective-permute-start.4 = (f32[1,16,2048]{2,1,0:T(8,128)S(1)}, f32[1,16,2048]{2,1,0:T(8,128)S(1)}, u32[]{:S(2)}, u32[]{:S(2)}) collective-permute-start(f32[1,16,2048]{2,1,0:T(8,128)S(1)} %get-tuple-element.19.refs_1_), channel_id=1, source_target_pairs={{4,0},{8,4},{12,8},{14,12},{10,14},{6,10},{2,6},{0,2},{5,1},{9,5},... | collective-permute-start | bytes 393224 | tf_op jit(solution)/shard_map/ppermute | solution.py:287
  3.3 5.4 %collective-permute-start = (f32[1,16,2048]{2,1,0:T(8,128)S(1)}, f32[1,16,2048]{2,1,0:T(8,128)S(1)}, u32[]{:S(2)}, u32[]{:S(2)}) collective-permute-start(f32[1,16,2048]{2,1,0:T(8,128)S(1)} %get-tuple-element.17.refs_0_), channel_id=1, source_target_pairs={{0,4},{4,8},{8,12},{12,14},{14,10},{10,6},{6,2},{2,0},{1,5},{5,9},... | collective-permute-start | bytes 393224 | tf_op jit(solution)/shard_map/ppermute | solution.py:287
  3.5 6.0 %collective-permute-start.9 = (f32[1,16,2048]{2,1,0:T(8,128)S(1)}, f32[1,16,2048]{2,1,0:T(8,128)S(1)}, u32[]{:S(2)}, u32[]{:S(2)}) collective-permute-start(f32[1,16,2048]{2,1,0:T(8,128)S(1)} %get-tuple-element.17.refs_0_), channel_id=1, source_target_pairs={{4,0},{8,4},{12,8},{14,12},{10,14},{6,10},{2,6},{0,2},{5,1},{9,5},... | collective-permute-start | bytes 393224 | tf_op jit(solution)/shard_map/ppermute | solution.py:287
  4.8 5.7 %collective-permute-start.12 = (f32[1,16,2048]{2,1,0:T(8,128)S(1)}, f32[1,16,2048]{2,1,0:T(8,128)S(1)}, u32[]{:S(2)}, u32[]{:S(2)}) collective-permute-start(f32[1,16,2048]{2,1,0:T(8,128)S(1)} %get-tuple-element.19.refs_1_), channel_id=1, source_target_pairs={{0,4},{4,8},{8,12},{12,14},{14,10},{10,6},{6,2},{2,0},{1,5},{5,9},... | collective-permute-start | bytes 393224 | tf_op jit(solution)/shard_map/ppermute | solution.py:287
  7.2 4.5 %collective-permute-start.5 = (f32[1,16,2048]{2,1,0:T(8,128)S(1)}, f32[1,16,2048]{2,1,0:T(8,128)S(1)}, u32[]{:S(2)}, u32[]{:S(2)}) collective-permute-start(f32[1,16,2048]{2,1,0:T(8,128)S(1)} %collective-permute-done.4.refs_3_), channel_id=1, source_target_pairs={{4,0},{8,4},{12,8},{14,12},{10,14},{6,10},{2,6},{0,2},{5,1},{9,5},... | collective-permute-start | bytes 393224 | tf_op jit(solution)/shard_map/ppermute | solution.py:287
  8.7 4.4 %collective-permute-start.1 = (f32[1,16,2048]{2,1,0:T(8,128)S(1)}, f32[1,16,2048]{2,1,0:T(8,128)S(1)}, u32[]{:S(2)}, u32[]{:S(2)}) collective-permute-start(f32[1,16,2048]{2,1,0:T(8,128)S(1)} %collective-permute-done.refs_2_), channel_id=1, source_target_pairs={{0,4},{4,8},{8,12},{12,14},{14,10},{10,6},{6,2},{2,0},{1,5},{5,9},... | collective-permute-start | bytes 393224 | tf_op jit(solution)/shard_map/ppermute | solution.py:287
  9.4 5.5 %collective-permute-start.10 = (f32[1,16,2048]{2,1,0:T(8,128)S(1)}, f32[1,16,2048]{2,1,0:T(8,128)S(1)}, u32[]{:S(2)}, u32[]{:S(2)}) collective-permute-start(f32[1,16,2048]{2,1,0:T(8,128)S(1)} %collective-permute-done.9.refs_4_), channel_id=1, source_target_pairs={{4,0},{8,4},{12,8},{14,12},{10,14},{6,10},{2,6},{0,2},{5,1},{9,5},... | collective-permute-start | bytes 393224 | tf_op jit(solution)/shard_map/ppermute | solution.py:287
  10.5 5.1 %collective-permute-start.13 = (f32[1,16,2048]{2,1,0:T(8,128)S(1)}, f32[1,16,2048]{2,1,0:T(8,128)S(1)}, u32[]{:S(2)}, u32[]{:S(2)}) collective-permute-start(f32[1,16,2048]{2,1,0:T(8,128)S(1)} %collective-permute-done.12.refs_5_), channel_id=1, source_target_pairs={{0,4},{4,8},{8,12},{12,14},{14,10},{10,6},{6,2},{2,0},{1,5},{5,9},... | collective-permute-start | bytes 393224 | tf_op jit(solution)/shard_map/ppermute | solution.py:287
  11.7 5.9 %collective-permute-start.6 = (f32[1,16,2048]{2,1,0:T(8,128)S(1)}, f32[1,16,2048]{2,1,0:T(8,128)S(1)}, u32[]{:S(2)}, u32[]{:S(2)}) collective-permute-start(f32[1,16,2048]{2,1,0:T(8,128)S(1)} %collective-permute-done.5.refs_7_), channel_id=1, source_target_pairs={{4,0},{8,4},{12,8},{14,12},{10,14},{6,10},{2,6},{0,2},{5,1},{9,5},... | collective-permute-start | bytes 393224 | tf_op jit(solution)/shard_map/ppermute | solution.py:287
  13.1 5.6 %collective-permute-start.2 = (f32[1,16,2048]{2,1,0:T(8,128)S(1)}, f32[1,16,2048]{2,1,0:T(8,128)S(1)}, u32[]{:S(2)}, u32[]{:S(2)}) collective-permute-start(f32[1,16,2048]{2,1,0:T(8,128)S(1)} %collective-permute-done.1.refs_6_), channel_id=1, source_target_pairs={{0,4},{4,8},{8,12},{12,14},{14,10},{10,6},{6,2},{2,0},{1,5},{5,9},... | collective-permute-start | bytes 393224 | tf_op jit(solution)/shard_map/ppermute | solution.py:287
  14.9 6.1 %collective-permute-start.11 = (f32[1,16,2048]{2,1,0:T(8,128)S(1)}, f32[1,16,2048]{2,1,0:T(8,128)S(1)}, u32[]{:S(2)}, u32[]{:S(2)}) collective-permute-start(f32[1,16,2048]{2,1,0:T(8,128)S(1)} %collective-permute-done.10.refs_8_), channel_id=1, source_target_pairs={{4,0},{8,4},{12,8},{14,12},{10,14},{6,10},{2,6},{0,2},{5,1},{9,5},... | collective-permute-start | bytes 393224 | tf_op jit(solution)/shard_map/ppermute | solution.py:287
  15.6 5.4 %collective-permute-start.14 = (f32[1,16,2048]{2,1,0:T(8,128)S(1)}, f32[1,16,2048]{2,1,0:T(8,128)S(1)}, u32[]{:S(2)}, u32[]{:S(2)}) collective-permute-start(f32[1,16,2048]{2,1,0:T(8,128)S(1)} %collective-permute-done.13.refs_9_), channel_id=1, source_target_pairs={{0,4},{4,8},{8,12},{12,14},{14,10},{10,6},{6,2},{2,0},{1,5},{5,9},... | collective-permute-start | bytes 393224 | tf_op jit(solution)/shard_map/ppermute | solution.py:287
  17.5 8.5 %collective-permute-start.7 = (f32[1,16,2048]{2,1,0:T(8,128)S(1)}, f32[1,16,2048]{2,1,0:T(8,128)S(1)}, u32[]{:S(2)}, u32[]{:S(2)}) collective-permute-start(f32[1,16,2048]{2,1,0:T(8,128)S(1)} %collective-permute-done.6.refs_11_), channel_id=1, source_target_pairs={{4,0},{8,4},{12,8},{14,12},{10,14},{6,10},{2,6},{0,2},{5,1},{9,5},... | collective-permute-start | bytes 393224 | tf_op jit(solution)/shard_map/ppermute | solution.py:287
  18.7 7.4 %collective-permute-start.3 = (f32[1,16,2048]{2,1,0:T(8,128)S(1)}, f32[1,16,2048]{2,1,0:T(8,128)S(1)}, u32[]{:S(2)}, u32[]{:S(2)}) collective-permute-start(f32[1,16,2048]{2,1,0:T(8,128)S(1)} %collective-permute-done.2.refs_10_), channel_id=1, source_target_pairs={{0,4},{4,8},{8,12},{12,14},{14,10},{10,6},{6,2},{2,0},{1,5},{5,9},... | collective-permute-start | bytes 393224 | tf_op jit(solution)/shard_map/ppermute | solution.py:287
  22.1 6.5 %collective-permute-start.15 = (f32[2,64,1024]{2,1,0:T(8,128)S(1)}, f32[2,64,1024]{2,1,0:T(8,128)S(1)}, u32[]{:S(2)}, u32[]{:S(2)}) collective-permute-start(f32[2,64,1024]{2,1,0:T(8,128)S(1)} %get-tuple-element.26), channel_id=1, source_target_pairs={{0,1},{1,0},{2,3},{3,2},{4,5},{5,4},{6,7},{7,6},{8,9},{9,8},{10,11... | collective-permute-start | bytes 1572872 | tf_op jit(solution)/shard_map/ppermute | solution.py:321
  27.0 2.5 %collective-permute-start.8 = (f32[32,1024]{1,0:T(8,128)S(1)}, f32[32,1024]{1,0:T(8,128)S(1)}, u32[]{:S(2)}, u32[]{:S(2)}) collective-permute-start(f32[32,1024]{1,0:T(8,128)S(1)} %last.1), channel_id=1, source_target_pairs={{0,1},{1,0},{2,3},{3,2},{4,5},{5,4},{6,7},{7,6},{8,9},{9,8},{10,11... | collective-permute-start | bytes 393224 | tf_op jit(solution)/shard_map/ppermute | solution.py:341

commit v10 on v9

--- a/solution.py
+++ b/solution.py
@@ -276,30 +276,11 @@
             name="part",
         )(listed, in_hbm(integrals))
 
-        held = {}
-        for span in range(spans):
-            held[span, 0] = own[span]
-            for pairs, sign in ((ahead, -1), (back, 1)):
-                moved = own[span]
-                for hop in range(1, far + 1 if (sign < 0) == (span % 2 == 0) else far):
-                    if hop == 2:
-                        moved, _ = lax.optimization_barrier((moved, split))
-                    moved = lax.ppermute(moved, "ab", pairs)
-                    held[span, -far if hop == far else sign * hop] = moved
-
-        def offset_of(span, hop, long):
-            return -hop if (span % 2 == 0) == long else hop
-
-        arrivals = [(span, 0) for span in range(spans)]
-        for hop in range(1, far):
-            arrivals += [(span, offset_of(span, hop, long)) for long in (True, False) for span in range(spans)]
         block = pltpu.VMEM((spans, half, slab), jnp.float32)
-        parts = ()
-        cuts = sorted({*range(0, len(arrivals) - spans, GROUP), len(arrivals) - spans, len(arrivals)})
-        for start, stop in zip(cuts, cuts[1:]):
-            group = arrivals[start:stop]
+
+        def step(group, parts):
             pieces = [held[key] for key in group]
-            parts = pl.pallas_call(
+            return pl.pallas_call(
                 functools.partial(step_kernel, count, rows, cd_tiles, group),
                 out_shape=(block, block),
                 in_specs=[smem] + [vmem] * (1 + len(pieces) + len(parts)),
@@ -310,6 +291,32 @@
                 cost_estimate=pl.CostEstimate(flops=STEP_FLOPS, bytes_accessed=4 << 20, transcendentals=0),
                 name="step",
             )(listed, split, *pieces, *parts)
+
+        held = {(span, 0): own[span] for span in range(spans)}
+        flows = [(span, sign) for long in (True, False) for span in range(spans) for sign in (-1, 1) if ((sign < 0) == (span % 2 == 0)) == long]
+        moving = {(span, sign): own[span] for span, sign in flows}
+        arrivals, parts = [(span, 0) for span in range(spans)], ()
+        for hop in range(1, far + 1):
+            for span, sign in flows:
+                long = (sign < 0) == (span % 2 == 0)
+                if hop < far or long:
+                    moved = moving[span, sign]
+                    if hop == 2:
+                        moved, _ = lax.optimization_barrier((moved, split))
+                    if hop == 3:
+                        moved, _ = lax.optimization_barrier((moved, parts[0]))
+                    moved = moving[span, sign] = lax.ppermute(moved, "ab", ahead if sign < 0 else back)
+                    offset = -far if hop == far else sign * hop
+                    held[span, offset] = moved
+                    if hop < far:
+                        arrivals.append((span, offset))
+            if hop == 1:
+                parts = step(arrivals, parts)
+                arrivals = []
+        late = len(arrivals) - spans
+        for start in range(0, late, GROUP):
+            parts = step(arrivals[start : min(start + GROUP, late)], parts)
+        parts = step(arrivals[late:], parts)
         mine, send = parts
         base = pl.pallas_call(
             merge_kernel,

time: 30.4 us -> 31.4 us (1.033)
  Pallas kernels: 8.84 us -> 10.1 us
    pallas_call x2 -> x3, Pallas kernels: 2.9 us -> 3.98 us  [step(): pl.pallas_call(functools.partial(step_kernel, count, rows, cd_tiles, grou...]
    ppermute x1, starting transfers between devices: 1.53 us -> 2.22 us  [shards(): lax.ppermute(last, 'cd', swap)]
    ppermute x1, starting transfers between devices: 3.96 us -> 3.51 us  [shards(): lax.ppermute(send, 'cd', swap)]
    ppermute x14, starting transfers between devices: 11.5 us -> 11.1 us  [shards(): lax.ppermute(moved, 'ab', ahead if sign < 0 else back)]
  transfers between devices with their start and end apart: 16 -> 16, of which waited for: 5 -> 6; matrix products, arithmetic and copies ran while one was open for 0% -> 0% of each run, Pallas kernels for 23% -> 26%
where the time goes in v10:
time: 31.4 us; the launch traced here: 31.3 us
  starting transfers between devices  16.9 us (54%)
  Pallas kernels  10.1 us (32%)
  waiting for transfers between devices  4.21 us (13%)
    ppermute x14, starting transfers between devices, shards(): lax.ppermute(moved, 'ab', ahead if sign < 0 else back)  11.1 us
    ppermute x14, waiting for transfers between devices, shards(): lax.ppermute(moved, 'ab', ahead if sign < 0 else back)  4.09 us
    pallas_call x3, Pallas kernels, step(): pl.pallas_call(functools.partial(step_kernel, count, rows, cd_tiles, grou...  3.98 us
    ppermute x1, starting transfers between devices, shards(): lax.ppermute(send, 'cd', swap)  3.51 us
    pallas_call x1, Pallas kernels, shards(): pl.pallas_call(functools.partial(part_kernel, cd_tiles), out_shape=pltpu....  2.38 us
    ppermute x1, starting transfers between devices, shards(): lax.ppermute(last, 'cd', swap)  2.22 us
    pallas_call x1, Pallas kernels, shards(): pl.pallas_call(functools.partial(cut_kernel, ab_tiles, cd_tiles, spans),...  1.2 us
    pallas_call x1, Pallas kernels, shards(): pl.pallas_call(functools.partial(last_kernel, cd_tiles), out_shape=pltpu....  1.03 us
  transfers between devices with their start and end apart: 16, of which 6 were waited for; matrix products, arithmetic and copies ran while one was open for 0% of the time, Pallas kernels for 26%

profile of v10, /device:TPU:1, one launch (start us, length us, event | category | flops | bytes accessed | tf_op | source)
XLA Modules:
  0.0 31.3 jit_solution(5027284573749466118)
XLA Ops:
  0.0 1.2 %cut.1 = (f32[1,16,2048]{2,1,0:T(8,128)S(1)}, f32[1,16,2048]{2,1,0:T(8,128)S(1)}, s32[2,128]{1,0:T(2,128)S(1)}) custom-call(f32[2,16,2048]{2,1,0:T(8,128)} %amplitudes.1, s32[8]{0:T(128)} %labels_ab.1, s32[16]{0:T(128)} %labels_cd.1, s32[8,16]{1,0:T(8,128)} %labels_pattern.1), custom_call_target="tpu_custom_call" | custom-call | tf_op jit(solution)/shard_map/cut/pallas_call | solution.py:254
  1.2 2.1 %collective-permute-start.2 = (f32[1,16,2048]{2,1,0:T(8,128)S(1)}, f32[1,16,2048]{2,1,0:T(8,128)S(1)}, u32[]{:S(2)}, u32[]{:S(2)}) collective-permute-start(f32[1,16,2048]{2,1,0:T(8,128)S(1)} %get-tuple-element.25.refs_1_), channel_id=1, source_target_pairs={{4,0},{8,4},{12,8},{14,12},{10,14},{6,10},{2,6},{0,2},{5,1},{9,5},... | collective-permute-start | bytes 393224 | tf_op jit(solution)/shard_map/ppermute | solution.py:308
  3.3 0.1 collective-permute-start
  3.5 1.4 %collective-permute-start.4 = (f32[1,16,2048]{2,1,0:T(8,128)S(1)}, f32[1,16,2048]{2,1,0:T(8,128)S(1)}, u32[]{:S(2)}, u32[]{:S(2)}) collective-permute-start(f32[1,16,2048]{2,1,0:T(8,128)S(1)} %get-tuple-element.25.refs_1_), channel_id=1, source_target_pairs={{0,4},{4,8},{8,12},{12,14},{14,10},{10,6},{6,2},{2,0},{1,5},{5,9},... | collective-permute-start | bytes 393224 | tf_op jit(solution)/shard_map/ppermute | solution.py:308
  4.9 0.1 collective-permute-start.3
  4.9 2.4 %part.1.split = bf16[128,128,256]{2,1,0:T(8,128)(2,1)S(1)} custom-call(s32[2,128]{1,0:T(2,128)S(1)} %get-tuple-element.22.listed, f32[1024,2048]{1,0:T(8,128)} %integrals.1), custom_call_target="tpu_custom_call" | custom-call | bytes 8388608 | tf_op jit(solution)/shard_map/part/pallas_call | solution.py:268
  7.3 0.0 collective-permute-done.2.refs_3_
  7.3 1.2 %collective-permute-start.7 = (f32[1,16,2048]{2,1,0:T(8,128)S(1)}, f32[1,16,2048]{2,1,0:T(8,128)S(1)}, u32[]{:S(2)}, u32[]{:S(2)}) collective-permute-start(f32[1,16,2048]{2,1,0:T(8,128)S(1)} %collective-permute-done.2.refs_3_), channel_id=1, source_target_pairs={{4,0},{8,4},{12,8},{14,12},{10,14},{6,10},{2,6},{0,2},{5,1},{9,5},... | collective-permute-start | bytes 393224 | tf_op jit(solution)/shard_map/ppermute | solution.py:308
  8.6 0.0 collective-permute-done.refs_2_
  8.6 0.3 collective-permute-start.1
  8.8 1.3 %collective-permute-done.4.refs_5_ = f32[1,16,2048]{2,1,0:T(8,128)S(1)} collective-permute-done((f32[1,16,2048]{2,1,0:T(8,128)S(1)}, f32[1,16,2048]{2,1,0:T(8,128)S(1)}, u32[]{:S(2)}, u32[]{:S(2)}) %collective-permute-start.4) | collective-permute-done | bytes 131104 | tf_op jit(solution)/shard_map/ppermute | solution.py:308
  10.2 0.4 %collective-permute-start.13 = (f32[1,16,2048]{2,1,0:T(8,128)S(1)}, f32[1,16,2048]{2,1,0:T(8,128)S(1)}, u32[]{:S(2)}, u32[]{:S(2)}) collective-permute-start(f32[1,16,2048]{2,1,0:T(8,128)S(1)} %collective-permute-done.4.refs_5_), channel_id=1, source_target_pairs={{0,4},{4,8},{8,12},{12,14},{14,10},{10,6},{6,2},{2,0},{1,5},{5,9},... | collective-permute-start | bytes 393224 | tf_op jit(solution)/shard_map/ppermute | solution.py:308
  10.6 0.0 collective-permute-done.3.refs_4_
  10.6 1.0 %collective-permute-start.11 = (f32[1,16,2048]{2,1,0:T(8,128)S(1)}, f32[1,16,2048]{2,1,0:T(8,128)S(1)}, u32[]{:S(2)}, u32[]{:S(2)}) collective-permute-start(f32[1,16,2048]{2,1,0:T(8,128)S(1)} %collective-permute-done.3.refs_4_), channel_id=1, source_target_pairs={{4,0},{8,4},{12,8},{14,12},{10,14},{6,10},{2,6},{0,2},{5,1},{9,5},... | collective-permute-start | bytes 393224 | tf_op jit(solution)/shard_map/ppermute | solution.py:308
  11.7 1.4 %step.3 = (f32[2,64,1024]{2,1,0:T(8,128)S(1)}, f32[2,64,1024]{2,1,0:T(8,128)S(1)}) custom-call(s32[2,128]{1,0:T(2,128)S(1)} %get-tuple-element.22.listed, bf16[128,128,256]{2,1,0:T(8,128)(2,1)S(1)} %part.1.split, f32[1,16,2048]{2,1,0:T(8,128)S(1)} %get-tuple-element.23.refs_0_, f32[1,16,2048]{2,1,0:T(8,128)S(1)} %get-tuple-element.25.refs_1_, ...), custom_call_target="tpu_custom_call" | custom-call | flops 1073741824 | bytes 4194304 | tf_op jit(solution)/shard_map/step/pallas_call | solution.py:283
  13.1 0.0 collective-permute-done.7.refs_1_
  13.1 1.2 %collective-permute-start.8 = (f32[1,16,2048]{2,1,0:T(8,128)S(1)}, f32[1,16,2048]{2,1,0:T(8,128)S(1)}, u32[]{:S(2)}, u32[]{:S(2)}) collective-permute-start(f32[1,16,2048]{2,1,0:T(8,128)S(1)} %collective-permute-done.7.refs_1_), channel_id=1, source_target_pairs={{4,0},{8,4},{12,8},{14,12},{10,14},{6,10},{2,6},{0,2},{5,1},{9,5},... | collective-permute-start | bytes 393224 | tf_op jit(solution)/shard_map/ppermute | solution.py:308
  14.4 0.0 collective-permute-done.1.refs_0_
  14.4 0.3 collective-permute-start.5
  14.6 0.3 collective-permute-done.13.refs_3_
  14.9 0.3 collective-permute-done.11.refs_2_
  15.2 1.4 %collective-permute-start.14 = (f32[1,16,2048]{2,1,0:T(8,128)S(1)}, f32[1,16,2048]{2,1,0:T(8,128)S(1)}, u32[]{:S(2)}, u32[]{:S(2)}) collective-permute-start(f32[1,16,2048]{2,1,0:T(8,128)S(1)} %collective-permute-done.13.refs_3_), channel_id=1, source_target_pairs={{0,4},{4,8},{8,12},{12,14},{14,10},{10,6},{6,2},{2,0},{1,5},{5,9},... | collective-permute-start | bytes 393224 | tf_op jit(solution)/shard_map/ppermute | solution.py:308
  16.5 0.1 collective-permute-start.12
  16.6 1.9 %collective-permute-done.8.refs_5_ = f32[1,16,2048]{2,1,0:T(8,128)S(1)} collective-permute-done((f32[1,16,2048]{2,1,0:T(8,128)S(1)}, f32[1,16,2048]{2,1,0:T(8,128)S(1)}, u32[]{:S(2)}, u32[]{:S(2)}) %collective-permute-start.8) | collective-permute-done | bytes 131104 | tf_op jit(solution)/shard_map/ppermute | solution.py:308
  18.5 1.1 %collective-permute-start.9 = (f32[1,16,2048]{2,1,0:T(8,128)S(1)}, f32[1,16,2048]{2,1,0:T(8,128)S(1)}, u32[]{:S(2)}, u32[]{:S(2)}) collective-permute-start(f32[1,16,2048]{2,1,0:T(8,128)S(1)} %collective-permute-done.8.refs_5_), channel_id=1, source_target_pairs={{4,0},{8,4},{12,8},{14,12},{10,14},{6,10},{2,6},{0,2},{5,1},{9,5},... | collective-permute-start | bytes 393224 | tf_op jit(solution)/shard_map/ppermute | solution.py:308
  19.6 0.0 collective-permute-done.5.refs_4_
  19.6 0.3 %collective-permute-start.6 = (f32[1,16,2048]{2,1,0:T(8,128)S(1)}, f32[1,16,2048]{2,1,0:T(8,128)S(1)}, u32[]{:S(2)}, u32[]{:S(2)}) collective-permute-start(f32[1,16,2048]{2,1,0:T(8,128)S(1)} %collective-permute-done.5.refs_4_), channel_id=1, source_target_pairs={{0,4},{4,8},{8,12},{12,14},{14,10},{10,6},{6,2},{2,0},{1,5},{5,9},... | collective-permute-start | bytes 393224 | tf_op jit(solution)/shard_map/ppermute | solution.py:308
  20.0 1.5 %step.4 = (f32[2,64,1024]{2,1,0:T(8,128)S(1)}, f32[2,64,1024]{2,1,0:T(8,128)S(1)}) custom-call(s32[2,128]{1,0:T(2,128)S(1)} %get-tuple-element.22.listed, bf16[128,128,256]{2,1,0:T(8,128)(2,1)S(1)} %part.1.split, f32[1,16,2048]{2,1,0:T(8,128)S(1)} %collective-permute-done.1.refs_0_, ...), custom_call_target="tpu_custom_call", output_to_operand_aliasing={{0}: (8, {}), {1}: (9, {})} | custom-call | flops 1073741824 | bytes 4194304 | tf_op jit(solution)/shard_map/step/pallas_call | solution.py:283
  21.4 0.0 collective-permute-done.14.refs_1_
  21.4 0.3 %collective-permute-done.12.refs_0_ = f32[1,16,2048]{2,1,0:T(8,128)S(1)} collective-permute-done((f32[1,16,2048]{2,1,0:T(8,128)S(1)}, f32[1,16,2048]{2,1,0:T(8,128)S(1)}, u32[]{:S(2)}, u32[]{:S(2)}) %collective-permute-start.12) | collective-permute-done | bytes 131104 | tf_op jit(solution)/shard_map/ppermute | solution.py:308
  21.8 1.1 %step.5 = (f32[2,64,1024]{2,1,0:T(8,128)S(1)}, f32[2,64,1024]{2,1,0:T(8,128)S(1)}) custom-call(s32[2,128]{1,0:T(2,128)S(1)} %get-tuple-element.22.listed, bf16[128,128,256]{2,1,0:T(8,128)(2,1)S(1)} %part.1.split, f32[1,16,2048]{2,1,0:T(8,128)S(1)} %collective-permute-done.12.refs_0_, ...), custom_call_target="tpu_custom_call", output_to_operand_aliasing={{0}: (4, {}), {1}: (5, {})} | custom-call | flops 1073741824 | bytes 4194304 | tf_op jit(solution)/shard_map/step/pallas_call | solution.py:283
  22.9 3.5 %collective-permute-start.15 = (f32[2,64,1024]{2,1,0:T(8,128)S(1)}, f32[2,64,1024]{2,1,0:T(8,128)S(1)}, u32[]{:S(2)}, u32[]{:S(2)}) collective-permute-start(f32[2,64,1024]{2,1,0:T(8,128)S(1)} %get-tuple-element.38), channel_id=1, source_target_pairs={{0,1},{1,0},{2,3},{3,2},{4,5},{5,4},{6,7},{7,6},{8,9},{9,8},{10,11... | collective-permute-start | bytes 1572872 | tf_op jit(solution)/shard_map/ppermute | solution.py:328
  26.4 0.0 collective-permute-done.9.refs_1_
  26.4 0.0 collective-permute-done.6.refs_0_
  26.4 1.0 %last.1 = f32[32,1024]{1,0:T(8,128)S(1)} custom-call(s32[2,128]{1,0:T(2,128)S(1)} %get-tuple-element.22.listed, bf16[128,128,256]{2,1,0:T(8,128)(2,1)S(1)} %part.1.split, f32[1,16,2048]{2,1,0:T(8,128)S(1)} %collective-permute-done.6.refs_0_, f32[1,16,2048]{2,1,0:T(8,128)S(1)} %collective-permute-done.9.refs_1_), custom_call_target="tpu_custom_call" | custom-call | flops 17179869184 | bytes 4194304 | tf_op jit(solution)/shard_map/last/pallas_call | solution.py:330
  27.4 2.2 %collective-permute-start.10 = (f32[32,1024]{1,0:T(8,128)S(1)}, f32[32,1024]{1,0:T(8,128)S(1)}, u32[]{:S(2)}, u32[]{:S(2)}) collective-permute-start(f32[32,1024]{1,0:T(8,128)S(1)} %last.1), channel_id=1, source_target_pairs={{0,1},{1,0},{2,3},{3,2},{4,5},{5,4},{6,7},{7,6},{8,9},{9,8},{10,11... | collective-permute-start | bytes 393224 | tf_op jit(solution)/shard_map/ppermute | solution.py:348
  29.6 0.0 collective-permute-done.15.received
  29.6 0.9 %merge.1.before = f32[2,64,1024]{2,1,0:T(8,128)} custom-call(f32[2,64,1024]{2,1,0:T(8,128)S(1)} %get-tuple-element.37.mine, f32[2,64,1024]{2,1,0:T(8,128)S(1)} %collective-permute-done.15.received), custom_call_target="tpu_custom_call" | custom-call | tf_op jit(solution)/shard_map/merge/pallas_call | solution.py:321
  30.5 0.1 collective-permute-done.10.received
  30.6 0.7 %final.1 = f32[2,64,1024]{2,1,0:T(8,128)} custom-call(f32[32,1024]{1,0:T(8,128)S(1)} %last.1, f32[32,1024]{1,0:T(8,128)S(1)} %collective-permute-done.10.received, f32[2,64,1024]{2,1,0:T(8,128)} %merge.1.before), custom_call_target="tpu_custom_call", output_to_operand_aliasing={{}: (2, {})} | custom-call | tf_op jit(solution)/shard_map/final/pallas_call | solution.py:339
Async XLA Ops:
  1.2 6.1 %collective-permute-start.2 = (f32[1,16,2048]{2,1,0:T(8,128)S(1)}, f32[1,16,2048]{2,1,0:T(8,128)S(1)}, u32[]{:S(2)}, u32[]{:S(2)}) collective-permute-start(f32[1,16,2048]{2,1,0:T(8,128)S(1)} %get-tuple-element.25.refs_1_), channel_id=1, source_target_pairs={{4,0},{8,4},{12,8},{14,12},{10,14},{6,10},{2,6},{0,2},{5,1},{9,5},... | collective-permute-start | bytes 393224 | tf_op jit(solution)/shard_map/ppermute | solution.py:308
  3.3 5.2 %collective-permute-start = (f32[1,16,2048]{2,1,0:T(8,128)S(1)}, f32[1,16,2048]{2,1,0:T(8,128)S(1)}, u32[]{:S(2)}, u32[]{:S(2)}) collective-permute-start(f32[1,16,2048]{2,1,0:T(8,128)S(1)} %get-tuple-element.23.refs_0_), channel_id=1, source_target_pairs={{0,4},{4,8},{8,12},{12,14},{14,10},{10,6},{6,2},{2,0},{1,5},{5,9},... | collective-permute-start | bytes 393224 | tf_op jit(solution)/shard_map/ppermute | solution.py:308
  3.5 6.7 %collective-permute-start.4 = (f32[1,16,2048]{2,1,0:T(8,128)S(1)}, f32[1,16,2048]{2,1,0:T(8,128)S(1)}, u32[]{:S(2)}, u32[]{:S(2)}) collective-permute-start(f32[1,16,2048]{2,1,0:T(8,128)S(1)} %get-tuple-element.25.refs_1_), channel_id=1, source_target_pairs={{0,4},{4,8},{8,12},{12,14},{14,10},{10,6},{6,2},{2,0},{1,5},{5,9},... | collective-permute-start | bytes 393224 | tf_op jit(solution)/shard_map/ppermute | solution.py:308
  4.9 5.8 %collective-permute-start.3 = (f32[1,16,2048]{2,1,0:T(8,128)S(1)}, f32[1,16,2048]{2,1,0:T(8,128)S(1)}, u32[]{:S(2)}, u32[]{:S(2)}) collective-permute-start(f32[1,16,2048]{2,1,0:T(8,128)S(1)} %get-tuple-element.23.refs_0_), channel_id=1, source_target_pairs={{4,0},{8,4},{12,8},{14,12},{10,14},{6,10},{2,6},{0,2},{5,1},{9,5},... | collective-permute-start | bytes 393224 | tf_op jit(solution)/shard_map/ppermute | solution.py:308
  7.3 5.8 %collective-permute-start.7 = (f32[1,16,2048]{2,1,0:T(8,128)S(1)}, f32[1,16,2048]{2,1,0:T(8,128)S(1)}, u32[]{:S(2)}, u32[]{:S(2)}) collective-permute-start(f32[1,16,2048]{2,1,0:T(8,128)S(1)} %collective-permute-done.2.refs_3_), channel_id=1, source_target_pairs={{4,0},{8,4},{12,8},{14,12},{10,14},{6,10},{2,6},{0,2},{5,1},{9,5},... | collective-permute-start | bytes 393224 | tf_op jit(solution)/shard_map/ppermute | solution.py:308
  8.6 5.8 %collective-permute-start.1 = (f32[1,16,2048]{2,1,0:T(8,128)S(1)}, f32[1,16,2048]{2,1,0:T(8,128)S(1)}, u32[]{:S(2)}, u32[]{:S(2)}) collective-permute-start(f32[1,16,2048]{2,1,0:T(8,128)S(1)} %collective-permute-done.refs_2_), channel_id=1, source_target_pairs={{0,4},{4,8},{8,12},{12,14},{14,10},{10,6},{6,2},{2,0},{1,5},{5,9},... | collective-permute-start | bytes 393224 | tf_op jit(solution)/shard_map/ppermute | solution.py:308
  10.2 4.7 %collective-permute-start.13 = (f32[1,16,2048]{2,1,0:T(8,128)S(1)}, f32[1,16,2048]{2,1,0:T(8,128)S(1)}, u32[]{:S(2)}, u32[]{:S(2)}) collective-permute-start(f32[1,16,2048]{2,1,0:T(8,128)S(1)} %collective-permute-done.4.refs_5_), channel_id=1, source_target_pairs={{0,4},{4,8},{8,12},{12,14},{14,10},{10,6},{6,2},{2,0},{1,5},{5,9},... | collective-permute-start | bytes 393224 | tf_op jit(solution)/shard_map/ppermute | solution.py:308
  10.6 4.5 %collective-permute-start.11 = (f32[1,16,2048]{2,1,0:T(8,128)S(1)}, f32[1,16,2048]{2,1,0:T(8,128)S(1)}, u32[]{:S(2)}, u32[]{:S(2)}) collective-permute-start(f32[1,16,2048]{2,1,0:T(8,128)S(1)} %collective-permute-done.3.refs_4_), channel_id=1, source_target_pairs={{4,0},{8,4},{12,8},{14,12},{10,14},{6,10},{2,6},{0,2},{5,1},{9,5},... | collective-permute-start | bytes 393224 | tf_op jit(solution)/shard_map/ppermute | solution.py:308
  13.1 5.4 %collective-permute-start.8 = (f32[1,16,2048]{2,1,0:T(8,128)S(1)}, f32[1,16,2048]{2,1,0:T(8,128)S(1)}, u32[]{:S(2)}, u32[]{:S(2)}) collective-permute-start(f32[1,16,2048]{2,1,0:T(8,128)S(1)} %collective-permute-done.7.refs_1_), channel_id=1, source_target_pairs={{4,0},{8,4},{12,8},{14,12},{10,14},{6,10},{2,6},{0,2},{5,1},{9,5},... | collective-permute-start | bytes 393224 | tf_op jit(solution)/shard_map/ppermute | solution.py:308
  14.4 5.3 %collective-permute-start.5 = (f32[1,16,2048]{2,1,0:T(8,128)S(1)}, f32[1,16,2048]{2,1,0:T(8,128)S(1)}, u32[]{:S(2)}, u32[]{:S(2)}) collective-permute-start(f32[1,16,2048]{2,1,0:T(8,128)S(1)} %collective-permute-done.1.refs_0_), channel_id=1, source_target_pairs={{0,4},{4,8},{8,12},{12,14},{14,10},{10,6},{6,2},{2,0},{1,5},{5,9},... | collective-permute-start | bytes 393224 | tf_op jit(solution)/shard_map/ppermute | solution.py:308
  15.2 6.3 %collective-permute-start.14 = (f32[1,16,2048]{2,1,0:T(8,128)S(1)}, f32[1,16,2048]{2,1,0:T(8,128)S(1)}, u32[]{:S(2)}, u32[]{:S(2)}) collective-permute-start(f32[1,16,2048]{2,1,0:T(8,128)S(1)} %collective-permute-done.13.refs_3_), channel_id=1, source_target_pairs={{0,4},{4,8},{8,12},{12,14},{14,10},{10,6},{6,2},{2,0},{1,5},{5,9},... | collective-permute-start | bytes 393224 | tf_op jit(solution)/shard_map/ppermute | solution.py:308
  16.5 5.2 %collective-permute-start.12 = (f32[1,16,2048]{2,1,0:T(8,128)S(1)}, f32[1,16,2048]{2,1,0:T(8,128)S(1)}, u32[]{:S(2)}, u32[]{:S(2)}) collective-permute-start(f32[1,16,2048]{2,1,0:T(8,128)S(1)} %collective-permute-done.11.refs_2_), channel_id=1, source_target_pairs={{4,0},{8,4},{12,8},{14,12},{10,14},{6,10},{2,6},{0,2},{5,1},{9,5},... | collective-permute-start | bytes 393224 | tf_op jit(solution)/shard_map/ppermute | solution.py:308
  18.5 7.9 %collective-permute-start.9 = (f32[1,16,2048]{2,1,0:T(8,128)S(1)}, f32[1,16,2048]{2,1,0:T(8,128)S(1)}, u32[]{:S(2)}, u32[]{:S(2)}) collective-permute-start(f32[1,16,2048]{2,1,0:T(8,128)S(1)} %collective-permute-done.8.refs_5_), channel_id=1, source_target_pairs={{4,0},{8,4},{12,8},{14,12},{10,14},{6,10},{2,6},{0,2},{5,1},{9,5},... | collective-permute-start | bytes 393224 | tf_op jit(solution)/shard_map/ppermute | solution.py:308
  19.6 6.7 %collective-permute-start.6 = (f32[1,16,2048]{2,1,0:T(8,128)S(1)}, f32[1,16,2048]{2,1,0:T(8,128)S(1)}, u32[]{:S(2)}, u32[]{:S(2)}) collective-permute-start(f32[1,16,2048]{2,1,0:T(8,128)S(1)} %collective-permute-done.5.refs_4_), channel_id=1, source_target_pairs={{0,4},{4,8},{8,12},{12,14},{14,10},{10,6},{6,2},{2,0},{1,5},{5,9},... | collective-permute-start | bytes 393224 | tf_op jit(solution)/shard_map/ppermute | solution.py:308
  22.9 6.8 %collective-permute-start.15 = (f32[2,64,1024]{2,1,0:T(8,128)S(1)}, f32[2,64,1024]{2,1,0:T(8,128)S(1)}, u32[]{:S(2)}, u32[]{:S(2)}) collective-permute-start(f32[2,64,1024]{2,1,0:T(8,128)S(1)} %get-tuple-element.38), channel_id=1, source_target_pairs={{0,1},{1,0},{2,3},{3,2},{4,5},{5,4},{6,7},{7,6},{8,9},{9,8},{10,11... | collective-permute-start | bytes 1572872 | tf_op jit(solution)/shard_map/ppermute | solution.py:328
  27.4 3.2 %collective-permute-start.10 = (f32[32,1024]{1,0:T(8,128)S(1)}, f32[32,1024]{1,0:T(8,128)S(1)}, u32[]{:S(2)}, u32[]{:S(2)}) collective-permute-start(f32[32,1024]{1,0:T(8,128)S(1)} %last.1), channel_id=1, source_target_pairs={{0,1},{1,0},{2,3},{3,2},{4,5},{5,4},{6,7},{7,6},{8,9},{9,8},{10,11... | collective-permute-start | bytes 393224 | tf_op jit(solution)/shard_map/ppermute | solution.py:348

commit v11 on v10

--- a/solution.py
+++ b/solution.py
@@ -303,7 +303,7 @@
                     moved = moving[span, sign]
                     if hop == 2:
                         moved, _ = lax.optimization_barrier((moved, split))
-                    if hop == 3:
+                    if hop == 3 and long:
                         moved, _ = lax.optimization_barrier((moved, parts[0]))
                     moved = moving[span, sign] = lax.ppermute(moved, "ab", ahead if sign < 0 else back)
                     offset = -far if hop == far else sign * hop

time: 31.4 us -> 30.1 us (0.959)
  waiting for transfers between devices: 4.21 us -> 3.19 us
  Pallas kernels: 10.1 us -> 9.66 us
    ppermute x14, waiting for transfers between devices: 4.09 us -> 3.08 us  [shards(): lax.ppermute(moved, 'ab', ahead if sign < 0 else back)]
    ppermute x1, starting transfers between devices: 2.22 us -> 1.41 us  [shards(): lax.ppermute(last, 'cd', swap)]
    ppermute x1, starting transfers between devices: 3.51 us -> 4.19 us  [shards(): lax.ppermute(send, 'cd', swap)]
  transfers between devices with their start and end apart: 16 -> 16, of which waited for: 6 -> 5; matrix products, arithmetic and copies ran while one was open for 0% -> 0% of each run, Pallas kernels for 26% -> 26%
where the time goes in v11:
time: 30.1 us; the launch traced here: 29.9 us
  starting transfers between devices  16.9 us (56%)
  Pallas kernels  9.66 us (32%)
  waiting for transfers between devices  3.19 us (11%)
    ppermute x14, starting transfers between devices, shards(): lax.ppermute(moved, 'ab', ahead if sign < 0 else back)  11.3 us
    ppermute x1, starting transfers between devices, shards(): lax.ppermute(send, 'cd', swap)  4.19 us
    pallas_call x3, Pallas kernels, step(): pl.pallas_call(functools.partial(step_kernel, count, rows, cd_tiles, grou...  3.7 us
    ppermute x14, waiting for transfers between devices, shards(): lax.ppermute(moved, 'ab', ahead if sign < 0 else back)  3.08 us
    pallas_call x1, Pallas kernels, shards(): pl.pallas_call(functools.partial(part_kernel, cd_tiles), out_shape=pltpu....  2.23 us
    ppermute x1, starting transfers between devices, shards(): lax.ppermute(last, 'cd', swap)  1.41 us
    pallas_call x1, Pallas kernels, shards(): pl.pallas_call(functools.partial(cut_kernel, ab_tiles, cd_tiles, spans),...  1.2 us
    pallas_call x1, Pallas kernels, shards(): pl.pallas_call(functools.partial(last_kernel, cd_tiles), out_shape=pltpu....  0.98 us
  transfers between devices with their start and end apart: 16, of which 5 were waited for; matrix products, arithmetic and copies ran while one was open for 0% of the time, Pallas kernels for 26%

profile of v11, /device:TPU:1, one launch (start us, length us, event | category | flops | bytes accessed | tf_op | source)
XLA Modules:
  0.0 29.9 jit_solution(13763707433640947582)
XLA Ops:
  0.0 1.2 %cut.1 = (f32[1,16,2048]{2,1,0:T(8,128)S(1)}, f32[1,16,2048]{2,1,0:T(8,128)S(1)}, s32[2,128]{1,0:T(2,128)S(1)}) custom-call(f32[2,16,2048]{2,1,0:T(8,128)} %amplitudes.1, s32[8]{0:T(128)} %labels_ab.1, s32[16]{0:T(128)} %labels_cd.1, s32[8,16]{1,0:T(8,128)} %labels_pattern.1), custom_call_target="tpu_custom_call" | custom-call | tf_op jit(solution)/shard_map/cut/pallas_call | solution.py:254
  1.2 2.1 %collective-permute-start.2 = (f32[1,16,2048]{2,1,0:T(8,128)S(1)}, f32[1,16,2048]{2,1,0:T(8,128)S(1)}, u32[]{:S(2)}, u32[]{:S(2)}) collective-permute-start(f32[1,16,2048]{2,1,0:T(8,128)S(1)} %get-tuple-element.23.refs_1_), channel_id=1, source_target_pairs={{4,0},{8,4},{12,8},{14,12},{10,14},{6,10},{2,6},{0,2},{5,1},{9,5},... | collective-permute-start | bytes 393224 | tf_op jit(solution)/shard_map/ppermute | solution.py:308
  3.3 0.1 collective-permute-start
  3.5 1.3 %collective-permute-start.3 = (f32[1,16,2048]{2,1,0:T(8,128)S(1)}, f32[1,16,2048]{2,1,0:T(8,128)S(1)}, u32[]{:S(2)}, u32[]{:S(2)}) collective-permute-start(f32[1,16,2048]{2,1,0:T(8,128)S(1)} %get-tuple-element.21.refs_0_), channel_id=1, source_target_pairs={{4,0},{8,4},{12,8},{14,12},{10,14},{6,10},{2,6},{0,2},{5,1},{9,5},... | collective-permute-start | bytes 393224 | tf_op jit(solution)/shard_map/ppermute | solution.py:308
  4.8 0.1 collective-permute-start.4
  4.9 2.2 %part.1.split = bf16[128,128,256]{2,1,0:T(8,128)(2,1)S(1)} custom-call(s32[2,128]{1,0:T(2,128)S(1)} %get-tuple-element.20.listed, f32[1024,2048]{1,0:T(8,128)} %integrals.1), custom_call_target="tpu_custom_call" | custom-call | bytes 8388608 | tf_op jit(solution)/shard_map/part/pallas_call | solution.py:268
  7.2 0.0 collective-permute-done.2.refs_3_
  7.2 1.4 %collective-permute-start.7 = (f32[1,16,2048]{2,1,0:T(8,128)S(1)}, f32[1,16,2048]{2,1,0:T(8,128)S(1)}, u32[]{:S(2)}, u32[]{:S(2)}) collective-permute-start(f32[1,16,2048]{2,1,0:T(8,128)S(1)} %collective-permute-done.2.refs_3_), channel_id=1, source_target_pairs={{4,0},{8,4},{12,8},{14,12},{10,14},{6,10},{2,6},{0,2},{5,1},{9,5},... | collective-permute-start | bytes 393224 | tf_op jit(solution)/shard_map/ppermute | solution.py:308
  8.6 0.0 collective-permute-done.refs_2_
  8.6 0.3 collective-permute-start.1
  8.8 0.6 %collective-permute-done.3.refs_4_ = f32[1,16,2048]{2,1,0:T(8,128)S(1)} collective-permute-done((f32[1,16,2048]{2,1,0:T(8,128)S(1)}, f32[1,16,2048]{2,1,0:T(8,128)S(1)}, u32[]{:S(2)}, u32[]{:S(2)}) %collective-permute-start.3) | collective-permute-done | bytes 131104 | tf_op jit(solution)/shard_map/ppermute | solution.py:308
  9.4 1.1 %collective-permute-start.11 = (f32[1,16,2048]{2,1,0:T(8,128)S(1)}, f32[1,16,2048]{2,1,0:T(8,128)S(1)}, u32[]{:S(2)}, u32[]{:S(2)}) collective-permute-start(f32[1,16,2048]{2,1,0:T(8,128)S(1)} %collective-permute-done.3.refs_4_), channel_id=1, source_target_pairs={{4,0},{8,4},{12,8},{14,12},{10,14},{6,10},{2,6},{0,2},{5,1},{9,5},... | collective-permute-start | bytes 393224 | tf_op jit(solution)/shard_map/ppermute | solution.py:308
  10.5 0.0 collective-permute-done.4.refs_5_
  10.5 0.4 %collective-permute-start.13 = (f32[1,16,2048]{2,1,0:T(8,128)S(1)}, f32[1,16,2048]{2,1,0:T(8,128)S(1)}, u32[]{:S(2)}, u32[]{:S(2)}) collective-permute-start(f32[1,16,2048]{2,1,0:T(8,128)S(1)} %collective-permute-done.4.refs_5_), channel_id=1, source_target_pairs={{0,4},{4,8},{8,12},{12,14},{14,10},{10,6},{6,2},{2,0},{1,5},{5,9},... | collective-permute-start | bytes 393224 | tf_op jit(solution)/shard_map/ppermute | solution.py:308
  10.9 1.3 %step.3 = (f32[2,64,1024]{2,1,0:T(8,128)S(1)}, f32[2,64,1024]{2,1,0:T(8,128)S(1)}) custom-call(s32[2,128]{1,0:T(2,128)S(1)} %get-tuple-element.20.listed, bf16[128,128,256]{2,1,0:T(8,128)(2,1)S(1)} %part.1.split, f32[1,16,2048]{2,1,0:T(8,128)S(1)} %get-tuple-element.21.refs_0_, f32[1,16,2048]{2,1,0:T(8,128)S(1)} %get-tuple-element.23.refs_1_, ...), custom_call_target="tpu_custom_call" | custom-call | flops 1073741824 | bytes 4194304 | tf_op jit(solution)/shard_map/step/pallas_call | solution.py:283
  12.2 0.0 collective-permute-done.7.refs_1_
  12.2 1.1 %collective-permute-start.8 = (f32[1,16,2048]{2,1,0:T(8,128)S(1)}, f32[1,16,2048]{2,1,0:T(8,128)S(1)}, u32[]{:S(2)}, u32[]{:S(2)}) collective-permute-start(f32[1,16,2048]{2,1,0:T(8,128)S(1)} %collective-permute-done.7.refs_1_), channel_id=1, source_target_pairs={{4,0},{8,4},{12,8},{14,12},{10,14},{6,10},{2,6},{0,2},{5,1},{9,5},... | collective-permute-start | bytes 393224 | tf_op jit(solution)/shard_map/ppermute | solution.py:308
  13.4 0.0 collective-permute-done.1.refs_0_
  13.4 0.4 %collective-permute-start.5 = (f32[1,16,2048]{2,1,0:T(8,128)S(1)}, f32[1,16,2048]{2,1,0:T(8,128)S(1)}, u32[]{:S(2)}, u32[]{:S(2)}) collective-permute-start(f32[1,16,2048]{2,1,0:T(8,128)S(1)} %collective-permute-done.1.refs_0_), channel_id=1, source_target_pairs={{0,4},{4,8},{8,12},{12,14},{14,10},{10,6},{6,2},{2,0},{1,5},{5,9},... | collective-permute-start | bytes 393224 | tf_op jit(solution)/shard_map/ppermute | solution.py:308
  13.8 1.2 %collective-permute-done.11.refs_2_ = f32[1,16,2048]{2,1,0:T(8,128)S(1)} collective-permute-done((f32[1,16,2048]{2,1,0:T(8,128)S(1)}, f32[1,16,2048]{2,1,0:T(8,128)S(1)}, u32[]{:S(2)}, u32[]{:S(2)}) %collective-permute-start.11) | collective-permute-done | bytes 131104 | tf_op jit(solution)/shard_map/ppermute | solution.py:308
  14.9 0.7 %collective-permute-start.12 = (f32[1,16,2048]{2,1,0:T(8,128)S(1)}, f32[1,16,2048]{2,1,0:T(8,128)S(1)}, u32[]{:S(2)}, u32[]{:S(2)}) collective-permute-start(f32[1,16,2048]{2,1,0:T(8,128)S(1)} %collective-permute-done.11.refs_2_), channel_id=1, source_target_pairs={{4,0},{8,4},{12,8},{14,12},{10,14},{6,10},{2,6},{0,2},{5,1},{9,5},... | collective-permute-start | bytes 393224 | tf_op jit(solution)/shard_map/ppermute | solution.py:308
  15.6 0.0 collective-permute-done.13.refs_3_
  15.6 0.8 %collective-permute-start.14 = (f32[1,16,2048]{2,1,0:T(8,128)S(1)}, f32[1,16,2048]{2,1,0:T(8,128)S(1)}, u32[]{:S(2)}, u32[]{:S(2)}) collective-permute-start(f32[1,16,2048]{2,1,0:T(8,128)S(1)} %collective-permute-done.13.refs_3_), channel_id=1, source_target_pairs={{0,4},{4,8},{8,12},{12,14},{14,10},{10,6},{6,2},{2,0},{1,5},{5,9},... | collective-permute-start | bytes 393224 | tf_op jit(solution)/shard_map/ppermute | solution.py:308
  16.4 1.2 %collective-permute-done.8.refs_5_ = f32[1,16,2048]{2,1,0:T(8,128)S(1)} collective-permute-done((f32[1,16,2048]{2,1,0:T(8,128)S(1)}, f32[1,16,2048]{2,1,0:T(8,128)S(1)}, u32[]{:S(2)}, u32[]{:S(2)}) %collective-permute-start.8) | collective-permute-done | bytes 131104 | tf_op jit(solution)/shard_map/ppermute | solution.py:308
  17.6 1.2 %collective-permute-start.9 = (f32[1,16,2048]{2,1,0:T(8,128)S(1)}, f32[1,16,2048]{2,1,0:T(8,128)S(1)}, u32[]{:S(2)}, u32[]{:S(2)}) collective-permute-start(f32[1,16,2048]{2,1,0:T(8,128)S(1)} %collective-permute-done.8.refs_5_), channel_id=1, source_target_pairs={{4,0},{8,4},{12,8},{14,12},{10,14},{6,10},{2,6},{0,2},{5,1},{9,5},... | collective-permute-start | bytes 393224 | tf_op jit(solution)/shard_map/ppermute | solution.py:308
  18.8 0.0 collective-permute-done.5.refs_4_
  18.8 0.3 collective-permute-start.6
  19.1 1.3 %step.4 = (f32[2,64,1024]{2,1,0:T(8,128)S(1)}, f32[2,64,1024]{2,1,0:T(8,128)S(1)}) custom-call(s32[2,128]{1,0:T(2,128)S(1)} %get-tuple-element.20.listed, bf16[128,128,256]{2,1,0:T(8,128)(2,1)S(1)} %part.1.split, f32[1,16,2048]{2,1,0:T(8,128)S(1)} %collective-permute-done.1.refs_0_, ...), custom_call_target="tpu_custom_call", output_to_operand_aliasing={{0}: (8, {}), {1}: (9, {})} | custom-call | flops 1073741824 | bytes 4194304 | tf_op jit(solution)/shard_map/step/pallas_call | solution.py:283
  20.4 0.0 collective-permute-done.12.refs_0_
  20.4 0.1 collective-permute-done.14.refs_1_
  20.5 1.0 %step.5 = (f32[2,64,1024]{2,1,0:T(8,128)S(1)}, f32[2,64,1024]{2,1,0:T(8,128)S(1)}) custom-call(s32[2,128]{1,0:T(2,128)S(1)} %get-tuple-element.20.listed, bf16[128,128,256]{2,1,0:T(8,128)(2,1)S(1)} %part.1.split, f32[1,16,2048]{2,1,0:T(8,128)S(1)} %collective-permute-done.12.refs_0_, ...), custom_call_target="tpu_custom_call", output_to_operand_aliasing={{0}: (4, {}), {1}: (5, {})} | custom-call | flops 1073741824 | bytes 4194304 | tf_op jit(solution)/shard_map/step/pallas_call | solution.py:283
  21.6 4.2 %collective-permute-start.15 = (f32[2,64,1024]{2,1,0:T(8,128)S(1)}, f32[2,64,1024]{2,1,0:T(8,128)S(1)}, u32[]{:S(2)}, u32[]{:S(2)}) collective-permute-start(f32[2,64,1024]{2,1,0:T(8,128)S(1)} %get-tuple-element.34), channel_id=1, source_target_pairs={{0,1},{1,0},{2,3},{3,2},{4,5},{5,4},{6,7},{7,6},{8,9},{9,8},{10,11... | collective-permute-start | bytes 1572872 | tf_op jit(solution)/shard_map/ppermute | solution.py:328
  25.8 0.0 collective-permute-done.9.refs_1_
  25.8 0.0 collective-permute-done.6.refs_0_
  25.8 1.0 %last.1 = f32[32,1024]{1,0:T(8,128)S(1)} custom-call(s32[2,128]{1,0:T(2,128)S(1)} %get-tuple-element.20.listed, bf16[128,128,256]{2,1,0:T(8,128)(2,1)S(1)} %part.1.split, f32[1,16,2048]{2,1,0:T(8,128)S(1)} %collective-permute-done.6.refs_0_, f32[1,16,2048]{2,1,0:T(8,128)S(1)} %collective-permute-done.9.refs_1_), custom_call_target="tpu_custom_call" | custom-call | flops 17179869184 | bytes 4194304 | tf_op jit(solution)/shard_map/last/pallas_call | solution.py:330
  26.8 1.4 %collective-permute-start.10 = (f32[32,1024]{1,0:T(8,128)S(1)}, f32[32,1024]{1,0:T(8,128)S(1)}, u32[]{:S(2)}, u32[]{:S(2)}) collective-permute-start(f32[32,1024]{1,0:T(8,128)S(1)} %last.1), channel_id=1, source_target_pairs={{0,1},{1,0},{2,3},{3,2},{4,5},{5,4},{6,7},{7,6},{8,9},{9,8},{10,11... | collective-permute-start | bytes 393224 | tf_op jit(solution)/shard_map/ppermute | solution.py:348
  28.2 0.0 collective-permute-done.15.received
  28.2 0.9 %merge.1.before = f32[2,64,1024]{2,1,0:T(8,128)} custom-call(f32[2,64,1024]{2,1,0:T(8,128)S(1)} %get-tuple-element.33.mine, f32[2,64,1024]{2,1,0:T(8,128)S(1)} %collective-permute-done.15.received), custom_call_target="tpu_custom_call" | custom-call | tf_op jit(solution)/shard_map/merge/pallas_call | solution.py:321
  29.1 0.1 collective-permute-done.10.received
  29.2 0.7 %final.1 = f32[2,64,1024]{2,1,0:T(8,128)} custom-call(f32[32,1024]{1,0:T(8,128)S(1)} %last.1, f32[32,1024]{1,0:T(8,128)S(1)} %collective-permute-done.10.received, f32[2,64,1024]{2,1,0:T(8,128)} %merge.1.before), custom_call_target="tpu_custom_call", output_to_operand_aliasing={{}: (2, {})} | custom-call | tf_op jit(solution)/shard_map/final/pallas_call | solution.py:339
Async XLA Ops:
  1.2 5.9 %collective-permute-start.2 = (f32[1,16,2048]{2,1,0:T(8,128)S(1)}, f32[1,16,2048]{2,1,0:T(8,128)S(1)}, u32[]{:S(2)}, u32[]{:S(2)}) collective-permute-start(f32[1,16,2048]{2,1,0:T(8,128)S(1)} %get-tuple-element.23.refs_1_), channel_id=1, source_target_pairs={{4,0},{8,4},{12,8},{14,12},{10,14},{6,10},{2,6},{0,2},{5,1},{9,5},... | collective-permute-start | bytes 393224 | tf_op jit(solution)/shard_map/ppermute | solution.py:308
  3.3 5.2 %collective-permute-start = (f32[1,16,2048]{2,1,0:T(8,128)S(1)}, f32[1,16,2048]{2,1,0:T(8,128)S(1)}, u32[]{:S(2)}, u32[]{:S(2)}) collective-permute-start(f32[1,16,2048]{2,1,0:T(8,128)S(1)} %get-tuple-element.21.refs_0_), channel_id=1, source_target_pairs={{0,4},{4,8},{8,12},{12,14},{14,10},{10,6},{6,2},{2,0},{1,5},{5,9},... | collective-permute-start | bytes 393224 | tf_op jit(solution)/shard_map/ppermute | solution.py:308
  3.5 6.0 %collective-permute-start.3 = (f32[1,16,2048]{2,1,0:T(8,128)S(1)}, f32[1,16,2048]{2,1,0:T(8,128)S(1)}, u32[]{:S(2)}, u32[]{:S(2)}) collective-permute-start(f32[1,16,2048]{2,1,0:T(8,128)S(1)} %get-tuple-element.21.refs_0_), channel_id=1, source_target_pairs={{4,0},{8,4},{12,8},{14,12},{10,14},{6,10},{2,6},{0,2},{5,1},{9,5},... | collective-permute-start | bytes 393224 | tf_op jit(solution)/shard_map/ppermute | solution.py:308
  4.8 5.7 %collective-permute-start.4 = (f32[1,16,2048]{2,1,0:T(8,128)S(1)}, f32[1,16,2048]{2,1,0:T(8,128)S(1)}, u32[]{:S(2)}, u32[]{:S(2)}) collective-permute-start(f32[1,16,2048]{2,1,0:T(8,128)S(1)} %get-tuple-element.23.refs_1_), channel_id=1, source_target_pairs={{0,4},{4,8},{8,12},{12,14},{14,10},{10,6},{6,2},{2,0},{1,5},{5,9},... | collective-permute-start | bytes 393224 | tf_op jit(solution)/shard_map/ppermute | solution.py:308
  7.2 5.1 %collective-permute-start.7 = (f32[1,16,2048]{2,1,0:T(8,128)S(1)}, f32[1,16,2048]{2,1,0:T(8,128)S(1)}, u32[]{:S(2)}, u32[]{:S(2)}) collective-permute-start(f32[1,16,2048]{2,1,0:T(8,128)S(1)} %collective-permute-done.2.refs_3_), channel_id=1, source_target_pairs={{4,0},{8,4},{12,8},{14,12},{10,14},{6,10},{2,6},{0,2},{5,1},{9,5},... | collective-permute-start | bytes 393224 | tf_op jit(solution)/shard_map/ppermute | solution.py:308
  8.6 4.8 %collective-permute-start.1 = (f32[1,16,2048]{2,1,0:T(8,128)S(1)}, f32[1,16,2048]{2,1,0:T(8,128)S(1)}, u32[]{:S(2)}, u32[]{:S(2)}) collective-permute-start(f32[1,16,2048]{2,1,0:T(8,128)S(1)} %collective-permute-done.refs_2_), channel_id=1, source_target_pairs={{0,4},{4,8},{8,12},{12,14},{14,10},{10,6},{6,2},{2,0},{1,5},{5,9},... | collective-permute-start | bytes 393224 | tf_op jit(solution)/shard_map/ppermute | solution.py:308
  9.4 5.5 %collective-permute-start.11 = (f32[1,16,2048]{2,1,0:T(8,128)S(1)}, f32[1,16,2048]{2,1,0:T(8,128)S(1)}, u32[]{:S(2)}, u32[]{:S(2)}) collective-permute-start(f32[1,16,2048]{2,1,0:T(8,128)S(1)} %collective-permute-done.3.refs_4_), channel_id=1, source_target_pairs={{4,0},{8,4},{12,8},{14,12},{10,14},{6,10},{2,6},{0,2},{5,1},{9,5},... | collective-permute-start | bytes 393224 | tf_op jit(solution)/shard_map/ppermute | solution.py:308
  10.5 5.1 %collective-permute-start.13 = (f32[1,16,2048]{2,1,0:T(8,128)S(1)}, f32[1,16,2048]{2,1,0:T(8,128)S(1)}, u32[]{:S(2)}, u32[]{:S(2)}) collective-permute-start(f32[1,16,2048]{2,1,0:T(8,128)S(1)} %collective-permute-done.4.refs_5_), channel_id=1, source_target_pairs={{0,4},{4,8},{8,12},{12,14},{14,10},{10,6},{6,2},{2,0},{1,5},{5,9},... | collective-permute-start | bytes 393224 | tf_op jit(solution)/shard_map/ppermute | solution.py:308
  12.2 5.4 %collective-permute-start.8 = (f32[1,16,2048]{2,1,0:T(8,128)S(1)}, f32[1,16,2048]{2,1,0:T(8,128)S(1)}, u32[]{:S(2)}, u32[]{:S(2)}) collective-permute-start(f32[1,16,2048]{2,1,0:T(8,128)S(1)} %collective-permute-done.7.refs_1_), channel_id=1, source_target_pairs={{4,0},{8,4},{12,8},{14,12},{10,14},{6,10},{2,6},{0,2},{5,1},{9,5},... | collective-permute-start | bytes 393224 | tf_op jit(solution)/shard_map/ppermute | solution.py:308
  13.4 5.5 %collective-permute-start.5 = (f32[1,16,2048]{2,1,0:T(8,128)S(1)}, f32[1,16,2048]{2,1,0:T(8,128)S(1)}, u32[]{:S(2)}, u32[]{:S(2)}) collective-permute-start(f32[1,16,2048]{2,1,0:T(8,128)S(1)} %collective-permute-done.1.refs_0_), channel_id=1, source_target_pairs={{0,4},{4,8},{8,12},{12,14},{14,10},{10,6},{6,2},{2,0},{1,5},{5,9},... | collective-permute-start | bytes 393224 | tf_op jit(solution)/shard_map/ppermute | solution.py:308
  14.9 5.5 %collective-permute-start.12 = (f32[1,16,2048]{2,1,0:T(8,128)S(1)}, f32[1,16,2048]{2,1,0:T(8,128)S(1)}, u32[]{:S(2)}, u32[]{:S(2)}) collective-permute-start(f32[1,16,2048]{2,1,0:T(8,128)S(1)} %collective-permute-done.11.refs_2_), channel_id=1, source_target_pairs={{4,0},{8,4},{12,8},{14,12},{10,14},{6,10},{2,6},{0,2},{5,1},{9,5},... | collective-permute-start | bytes 393224 | tf_op jit(solution)/shard_map/ppermute | solution.py:308
  15.6 4.9 %collective-permute-start.14 = (f32[1,16,2048]{2,1,0:T(8,128)S(1)}, f32[1,16,2048]{2,1,0:T(8,128)S(1)}, u32[]{:S(2)}, u32[]{:S(2)}) collective-permute-start(f32[1,16,2048]{2,1,0:T(8,128)S(1)} %collective-permute-done.13.refs_3_), channel_id=1, source_target_pairs={{0,4},{4,8},{8,12},{12,14},{14,10},{10,6},{6,2},{2,0},{1,5},{5,9},... | collective-permute-start | bytes 393224 | tf_op jit(solution)/shard_map/ppermute | solution.py:308
  17.6 8.2 %collective-permute-start.9 = (f32[1,16,2048]{2,1,0:T(8,128)S(1)}, f32[1,16,2048]{2,1,0:T(8,128)S(1)}, u32[]{:S(2)}, u32[]{:S(2)}) collective-permute-start(f32[1,16,2048]{2,1,0:T(8,128)S(1)} %collective-permute-done.8.refs_5_), channel_id=1, source_target_pairs={{4,0},{8,4},{12,8},{14,12},{10,14},{6,10},{2,6},{0,2},{5,1},{9,5},... | collective-permute-start | bytes 393224 | tf_op jit(solution)/shard_map/ppermute | solution.py:308
  18.8 6.9 %collective-permute-start.6 = (f32[1,16,2048]{2,1,0:T(8,128)S(1)}, f32[1,16,2048]{2,1,0:T(8,128)S(1)}, u32[]{:S(2)}, u32[]{:S(2)}) collective-permute-start(f32[1,16,2048]{2,1,0:T(8,128)S(1)} %collective-permute-done.5.refs_4_), channel_id=1, source_target_pairs={{0,4},{4,8},{8,12},{12,14},{14,10},{10,6},{6,2},{2,0},{1,5},{5,9},... | collective-permute-start | bytes 393224 | tf_op jit(solution)/shard_map/ppermute | solution.py:308
  21.6 6.6 %collective-permute-start.15 = (f32[2,64,1024]{2,1,0:T(8,128)S(1)}, f32[2,64,1024]{2,1,0:T(8,128)S(1)}, u32[]{:S(2)}, u32[]{:S(2)}) collective-permute-start(f32[2,64,1024]{2,1,0:T(8,128)S(1)} %get-tuple-element.34), channel_id=1, source_target_pairs={{0,1},{1,0},{2,3},{3,2},{4,5},{5,4},{6,7},{7,6},{8,9},{9,8},{10,11... | collective-permute-start | bytes 1572872 | tf_op jit(solution)/shard_map/ppermute | solution.py:328
  26.8 2.4 %collective-permute-start.10 = (f32[32,1024]{1,0:T(8,128)S(1)}, f32[32,1024]{1,0:T(8,128)S(1)}, u32[]{:S(2)}, u32[]{:S(2)}) collective-permute-start(f32[32,1024]{1,0:T(8,128)S(1)} %last.1), channel_id=1, source_target_pairs={{0,1},{1,0},{2,3},{3,2},{4,5},{5,4},{6,7},{7,6},{8,9},{9,8},{10,11... | collective-permute-start | bytes 393224 | tf_op jit(solution)/shard_map/ppermute | solution.py:348

commit v12 on v11

--- a/solution.py
+++ b/solution.py
@@ -10,6 +10,7 @@
 TILE = 128
 UNROLL = 4
 LANES = 128
+BAND = 8
 AHEAD = 8
 FLIGHT = AHEAD * UNROLL
 GROUP = 12
@@ -62,7 +63,12 @@
 def cut_kernel(ab_tiles, cd_tiles, spans, amplitudes, labels_ab, labels_cd, labels_pattern, *refs):
     outs, (listed, ab_irrep, cd_irrep, pattern, sems) = refs[:spans], refs[spans:]
     pairs = [(labels_ab, ab_irrep), (labels_cd, cd_irrep), (labels_pattern, pattern)]
-    pairs += [(amplitudes.at[pl.ds(at, 1)], out) for at, out in enumerate(outs)]
+    rows, depth = amplitudes.shape[1:]
+    for at, out in enumerate(outs):
+        for row in range(0, rows, BAND):
+            for column in range(0, depth, depth // 2):
+                part = (pl.ds(row, BAND), pl.ds(column, depth // 2))
+                pairs.append((amplitudes.at[(pl.ds(at, 1), *part)], out.at[(pl.ds(0, 1), *part)]))
     copies = [pltpu.make_async_copy(start, end, sems.at[at]) for at, (start, end) in enumerate(pairs)]
     for copy in copies:
         copy.start()
@@ -217,14 +223,15 @@
         total[...] = last[...] + received[...]
         copies = []
         for span in range(spans):
-            copies.append(
-                pltpu.make_async_copy(
-                    total.at[pl.ds(span * rows, rows), :],
-                    out.at[span, pl.ds(pl.multiple_of(place, rows), rows), :],
-                    sems.at[span],
+            for row in range(0, rows, BAND):
+                copies.append(
+                    pltpu.make_async_copy(
+                        total.at[pl.ds(span * rows + row, BAND), :],
+                        out.at[span, pl.ds(pl.multiple_of(place + row, BAND), BAND), :],
+                        sems.at[len(copies)],
+                    )
                 )
-            )
-            copies[-1].start()
+                copies[-1].start()
         for copy in copies:
             copy.wait()
 
@@ -260,7 +267,7 @@
                 pltpu.SMEM(ab_irrep.shape, jnp.int32),
                 pltpu.SMEM(cd_irrep.shape, jnp.int32),
                 pltpu.VMEM(block_pattern.shape, jnp.int32),
-                pltpu.SemaphoreType.DMA((spans + 3,)),
+                pltpu.SemaphoreType.DMA((3 + spans * 2 * rows // BAND,)),
             ],
             compiler_params=params,
             name="cut",
@@ -341,7 +348,7 @@
             out_shape=pltpu.HBM((spans, half, slab), jnp.float32),
             in_specs=[vmem, vmem, hbm],
             out_specs=hbm,
-            scratch_shapes=[pltpu.VMEM((spans * rows, slab), jnp.float32), pltpu.SemaphoreType.DMA((spans,))],
+            scratch_shapes=[pltpu.VMEM((spans * rows, slab), jnp.float32), pltpu.SemaphoreType.DMA((spans * rows // BAND,))],
             compiler_params=params,
             input_output_aliases={2: 0},
             name="final",

time: 30.1 us -> 30.3 us (level)
  no operation moved by 1% of the time
where the time goes in v12:
time: 30.3 us; the launch traced here: 29.9 us
  starting transfers between devices  16.9 us (56%)
  Pallas kernels  9.74 us (32%)
  waiting for transfers between devices  3.2 us (11%)
    ppermute x14, starting transfers between devices, shards(): lax.ppermute(moved, 'ab', ahead if sign < 0 else back)  11.3 us
    ppermute x1, starting transfers between devices, shards(): lax.ppermute(send, 'cd', swap)  4.19 us
    pallas_call x3, Pallas kernels, step(): pl.pallas_call(functools.partial(step_kernel, count, rows, cd_tiles, grou...  3.7 us
    ppermute x14, waiting for transfers between devices, shards(): lax.ppermute(moved, 'ab', ahead if sign < 0 else back)  3.09 us
    pallas_call x1, Pallas kernels, shards(): pl.pallas_call(functools.partial(part_kernel, cd_tiles), out_shape=pltpu....  2.23 us
    ppermute x1, starting transfers between devices, shards(): lax.ppermute(last, 'cd', swap)  1.42 us
    pallas_call x1, Pallas kernels, shards(): pl.pallas_call(functools.partial(cut_kernel, ab_tiles, cd_tiles, spans),...  1.27 us
    pallas_call x1, Pallas kernels, shards(): pl.pallas_call(functools.partial(last_kernel, cd_tiles), out_shape=pltpu....  0.98 us
  transfers between devices with their start and end apart: 16, of which 5 were waited for; matrix products, arithmetic and copies ran while one was open for 0% of the time, Pallas kernels for 26%

profile of v12, /device:TPU:1, one launch (start us, length us, event | category | flops | bytes accessed | tf_op | source)
XLA Modules:
  0.0 29.9 jit_solution(12315505788958144232)
XLA Ops:
  0.0 1.3 %cut.1 = (f32[1,16,2048]{2,1,0:T(8,128)S(1)}, f32[1,16,2048]{2,1,0:T(8,128)S(1)}, s32[2,128]{1,0:T(2,128)S(1)}) custom-call(f32[2,16,2048]{2,1,0:T(8,128)} %amplitudes.1, s32[8]{0:T(128)} %labels_ab.1, s32[16]{0:T(128)} %labels_cd.1, s32[8,16]{1,0:T(8,128)} %labels_pattern.1), custom_call_target="tpu_custom_call" | custom-call | tf_op jit(solution)/shard_map/cut/pallas_call | solution.py:261
  1.3 2.1 %collective-permute-start.2 = (f32[1,16,2048]{2,1,0:T(8,128)S(1)}, f32[1,16,2048]{2,1,0:T(8,128)S(1)}, u32[]{:S(2)}, u32[]{:S(2)}) collective-permute-start(f32[1,16,2048]{2,1,0:T(8,128)S(1)} %get-tuple-element.23.refs_1_), channel_id=1, source_target_pairs={{4,0},{8,4},{12,8},{14,12},{10,14},{6,10},{2,6},{0,2},{5,1},{9,5},... | collective-permute-start | bytes 393224 | tf_op jit(solution)/shard_map/ppermute | solution.py:315
  3.4 0.1 collective-permute-start
  3.5 1.3 %collective-permute-start.3 = (f32[1,16,2048]{2,1,0:T(8,128)S(1)}, f32[1,16,2048]{2,1,0:T(8,128)S(1)}, u32[]{:S(2)}, u32[]{:S(2)}) collective-permute-start(f32[1,16,2048]{2,1,0:T(8,128)S(1)} %get-tuple-element.21.refs_0_), channel_id=1, source_target_pairs={{4,0},{8,4},{12,8},{14,12},{10,14},{6,10},{2,6},{0,2},{5,1},{9,5},... | collective-permute-start | bytes 393224 | tf_op jit(solution)/shard_map/ppermute | solution.py:315
  4.9 0.1 collective-permute-start.4
  5.0 2.2 %part.1.split = bf16[128,128,256]{2,1,0:T(8,128)(2,1)S(1)} custom-call(s32[2,128]{1,0:T(2,128)S(1)} %get-tuple-element.20.listed, f32[1024,2048]{1,0:T(8,128)} %integrals.1), custom_call_target="tpu_custom_call" | custom-call | bytes 8388608 | tf_op jit(solution)/shard_map/part/pallas_call | solution.py:275
  7.2 0.0 collective-permute-done.2.refs_3_
  7.2 1.5 %collective-permute-start.7 = (f32[1,16,2048]{2,1,0:T(8,128)S(1)}, f32[1,16,2048]{2,1,0:T(8,128)S(1)}, u32[]{:S(2)}, u32[]{:S(2)}) collective-permute-start(f32[1,16,2048]{2,1,0:T(8,128)S(1)} %collective-permute-done.2.refs_3_), channel_id=1, source_target_pairs={{4,0},{8,4},{12,8},{14,12},{10,14},{6,10},{2,6},{0,2},{5,1},{9,5},... | collective-permute-start | bytes 393224 | tf_op jit(solution)/shard_map/ppermute | solution.py:315
  8.8 0.0 collective-permute-done.refs_2_
  8.8 0.0 collective-permute-start.1
  8.8 0.7 %collective-permute-done.3.refs_4_ = f32[1,16,2048]{2,1,0:T(8,128)S(1)} collective-permute-done((f32[1,16,2048]{2,1,0:T(8,128)S(1)}, f32[1,16,2048]{2,1,0:T(8,128)S(1)}, u32[]{:S(2)}, u32[]{:S(2)}) %collective-permute-start.3) | collective-permute-done | bytes 131104 | tf_op jit(solution)/shard_map/ppermute | solution.py:315
  9.5 1.1 %collective-permute-start.11 = (f32[1,16,2048]{2,1,0:T(8,128)S(1)}, f32[1,16,2048]{2,1,0:T(8,128)S(1)}, u32[]{:S(2)}, u32[]{:S(2)}) collective-permute-start(f32[1,16,2048]{2,1,0:T(8,128)S(1)} %collective-permute-done.3.refs_4_), channel_id=1, source_target_pairs={{4,0},{8,4},{12,8},{14,12},{10,14},{6,10},{2,6},{0,2},{5,1},{9,5},... | collective-permute-start | bytes 393224 | tf_op jit(solution)/shard_map/ppermute | solution.py:315
  10.6 0.0 collective-permute-done.4.refs_5_
  10.6 0.4 %collective-permute-start.13 = (f32[1,16,2048]{2,1,0:T(8,128)S(1)}, f32[1,16,2048]{2,1,0:T(8,128)S(1)}, u32[]{:S(2)}, u32[]{:S(2)}) collective-permute-start(f32[1,16,2048]{2,1,0:T(8,128)S(1)} %collective-permute-done.4.refs_5_), channel_id=1, source_target_pairs={{0,4},{4,8},{8,12},{12,14},{14,10},{10,6},{6,2},{2,0},{1,5},{5,9},... | collective-permute-start | bytes 393224 | tf_op jit(solution)/shard_map/ppermute | solution.py:315
  11.0 1.3 %step.3 = (f32[2,64,1024]{2,1,0:T(8,128)S(1)}, f32[2,64,1024]{2,1,0:T(8,128)S(1)}) custom-call(s32[2,128]{1,0:T(2,128)S(1)} %get-tuple-element.20.listed, bf16[128,128,256]{2,1,0:T(8,128)(2,1)S(1)} %part.1.split, f32[1,16,2048]{2,1,0:T(8,128)S(1)} %get-tuple-element.21.refs_0_, f32[1,16,2048]{2,1,0:T(8,128)S(1)} %get-tuple-element.23.refs_1_, ...), custom_call_target="tpu_custom_call" | custom-call | flops 1073741824 | bytes 4194304 | tf_op jit(solution)/shard_map/step/pallas_call | solution.py:290
  12.3 0.0 collective-permute-done.7.refs_1_
  12.3 1.3 %collective-permute-start.8 = (f32[1,16,2048]{2,1,0:T(8,128)S(1)}, f32[1,16,2048]{2,1,0:T(8,128)S(1)}, u32[]{:S(2)}, u32[]{:S(2)}) collective-permute-start(f32[1,16,2048]{2,1,0:T(8,128)S(1)} %collective-permute-done.7.refs_1_), channel_id=1, source_target_pairs={{4,0},{8,4},{12,8},{14,12},{10,14},{6,10},{2,6},{0,2},{5,1},{9,5},... | collective-permute-start | bytes 393224 | tf_op jit(solution)/shard_map/ppermute | solution.py:315
  13.6 0.0 collective-permute-done.1.refs_0_
  13.6 0.2 collective-permute-start.5
  13.8 1.2 %collective-permute-done.11.refs_2_ = f32[1,16,2048]{2,1,0:T(8,128)S(1)} collective-permute-done((f32[1,16,2048]{2,1,0:T(8,128)S(1)}, f32[1,16,2048]{2,1,0:T(8,128)S(1)}, u32[]{:S(2)}, u32[]{:S(2)}) %collective-permute-start.11) | collective-permute-done | bytes 131104 | tf_op jit(solution)/shard_map/ppermute | solution.py:315
  15.0 0.7 %collective-permute-start.12 = (f32[1,16,2048]{2,1,0:T(8,128)S(1)}, f32[1,16,2048]{2,1,0:T(8,128)S(1)}, u32[]{:S(2)}, u32[]{:S(2)}) collective-permute-start(f32[1,16,2048]{2,1,0:T(8,128)S(1)} %collective-permute-done.11.refs_2_), channel_id=1, source_target_pairs={{4,0},{8,4},{12,8},{14,12},{10,14},{6,10},{2,6},{0,2},{5,1},{9,5},... | collective-permute-start | bytes 393224 | tf_op jit(solution)/shard_map/ppermute | solution.py:315
  15.7 0.0 collective-permute-done.13.refs_3_
  15.7 0.7 %collective-permute-start.14 = (f32[1,16,2048]{2,1,0:T(8,128)S(1)}, f32[1,16,2048]{2,1,0:T(8,128)S(1)}, u32[]{:S(2)}, u32[]{:S(2)}) collective-permute-start(f32[1,16,2048]{2,1,0:T(8,128)S(1)} %collective-permute-done.13.refs_3_), channel_id=1, source_target_pairs={{0,4},{4,8},{8,12},{12,14},{14,10},{10,6},{6,2},{2,0},{1,5},{5,9},... | collective-permute-start | bytes 393224 | tf_op jit(solution)/shard_map/ppermute | solution.py:315
  16.5 1.1 %collective-permute-done.8.refs_5_ = f32[1,16,2048]{2,1,0:T(8,128)S(1)} collective-permute-done((f32[1,16,2048]{2,1,0:T(8,128)S(1)}, f32[1,16,2048]{2,1,0:T(8,128)S(1)}, u32[]{:S(2)}, u32[]{:S(2)}) %collective-permute-start.8) | collective-permute-done | bytes 131104 | tf_op jit(solution)/shard_map/ppermute | solution.py:315
  17.6 1.3 %collective-permute-start.9 = (f32[1,16,2048]{2,1,0:T(8,128)S(1)}, f32[1,16,2048]{2,1,0:T(8,128)S(1)}, u32[]{:S(2)}, u32[]{:S(2)}) collective-permute-start(f32[1,16,2048]{2,1,0:T(8,128)S(1)} %collective-permute-done.8.refs_5_), channel_id=1, source_target_pairs={{4,0},{8,4},{12,8},{14,12},{10,14},{6,10},{2,6},{0,2},{5,1},{9,5},... | collective-permute-start | bytes 393224 | tf_op jit(solution)/shard_map/ppermute | solution.py:315
  18.9 0.0 collective-permute-done.5.refs_4_
  18.9 0.2 collective-permute-start.6
  19.2 1.3 %step.4 = (f32[2,64,1024]{2,1,0:T(8,128)S(1)}, f32[2,64,1024]{2,1,0:T(8,128)S(1)}) custom-call(s32[2,128]{1,0:T(2,128)S(1)} %get-tuple-element.20.listed, bf16[128,128,256]{2,1,0:T(8,128)(2,1)S(1)} %part.1.split, f32[1,16,2048]{2,1,0:T(8,128)S(1)} %collective-permute-done.1.refs_0_, ...), custom_call_target="tpu_custom_call", output_to_operand_aliasing={{0}: (8, {}), {1}: (9, {})} | custom-call | flops 1073741824 | bytes 4194304 | tf_op jit(solution)/shard_map/step/pallas_call | solution.py:290
  20.5 0.0 collective-permute-done.12.refs_0_
  20.5 0.1 collective-permute-done.14.refs_1_
  20.6 1.0 %step.5 = (f32[2,64,1024]{2,1,0:T(8,128)S(1)}, f32[2,64,1024]{2,1,0:T(8,128)S(1)}) custom-call(s32[2,128]{1,0:T(2,128)S(1)} %get-tuple-element.20.listed, bf16[128,128,256]{2,1,0:T(8,128)(2,1)S(1)} %part.1.split, f32[1,16,2048]{2,1,0:T(8,128)S(1)} %collective-permute-done.12.refs_0_, ...), custom_call_target="tpu_custom_call", output_to_operand_aliasing={{0}: (4, {}), {1}: (5, {})} | custom-call | flops 1073741824 | bytes 4194304 | tf_op jit(solution)/shard_map/step/pallas_call | solution.py:290
  21.7 4.2 %collective-permute-start.15 = (f32[2,64,1024]{2,1,0:T(8,128)S(1)}, f32[2,64,1024]{2,1,0:T(8,128)S(1)}, u32[]{:S(2)}, u32[]{:S(2)}) collective-permute-start(f32[2,64,1024]{2,1,0:T(8,128)S(1)} %get-tuple-element.34), channel_id=1, source_target_pairs={{0,1},{1,0},{2,3},{3,2},{4,5},{5,4},{6,7},{7,6},{8,9},{9,8},{10,11... | collective-permute-start | bytes 1572872 | tf_op jit(solution)/shard_map/ppermute | solution.py:335
  25.8 0.0 collective-permute-done.9.refs_1_
  25.8 0.0 collective-permute-done.6.refs_0_
  25.8 1.0 %last.1 = f32[32,1024]{1,0:T(8,128)S(1)} custom-call(s32[2,128]{1,0:T(2,128)S(1)} %get-tuple-element.20.listed, bf16[128,128,256]{2,1,0:T(8,128)(2,1)S(1)} %part.1.split, f32[1,16,2048]{2,1,0:T(8,128)S(1)} %collective-permute-done.6.refs_0_, f32[1,16,2048]{2,1,0:T(8,128)S(1)} %collective-permute-done.9.refs_1_), custom_call_target="tpu_custom_call" | custom-call | flops 17179869184 | bytes 4194304 | tf_op jit(solution)/shard_map/last/pallas_call | solution.py:337
  26.8 1.4 %collective-permute-start.10 = (f32[32,1024]{1,0:T(8,128)S(1)}, f32[32,1024]{1,0:T(8,128)S(1)}, u32[]{:S(2)}, u32[]{:S(2)}) collective-permute-start(f32[32,1024]{1,0:T(8,128)S(1)} %last.1), channel_id=1, source_target_pairs={{0,1},{1,0},{2,3},{3,2},{4,5},{5,4},{6,7},{7,6},{8,9},{9,8},{10,11... | collective-permute-start | bytes 393224 | tf_op jit(solution)/shard_map/ppermute | solution.py:355
  28.2 0.0 collective-permute-done.15.received
  28.3 0.9 %merge.1.before = f32[2,64,1024]{2,1,0:T(8,128)} custom-call(f32[2,64,1024]{2,1,0:T(8,128)S(1)} %get-tuple-element.33.mine, f32[2,64,1024]{2,1,0:T(8,128)S(1)} %collective-permute-done.15.received), custom_call_target="tpu_custom_call" | custom-call | tf_op jit(solution)/shard_map/merge/pallas_call | solution.py:328
  29.1 0.1 collective-permute-done.10.received
  29.2 0.7 %final.1 = f32[2,64,1024]{2,1,0:T(8,128)} custom-call(f32[32,1024]{1,0:T(8,128)S(1)} %last.1, f32[32,1024]{1,0:T(8,128)S(1)} %collective-permute-done.10.received, f32[2,64,1024]{2,1,0:T(8,128)} %merge.1.before), custom_call_target="tpu_custom_call", output_to_operand_aliasing={{}: (2, {})} | custom-call | tf_op jit(solution)/shard_map/final/pallas_call | solution.py:346
Async XLA Ops:
  1.3 5.9 %collective-permute-start.2 = (f32[1,16,2048]{2,1,0:T(8,128)S(1)}, f32[1,16,2048]{2,1,0:T(8,128)S(1)}, u32[]{:S(2)}, u32[]{:S(2)}) collective-permute-start(f32[1,16,2048]{2,1,0:T(8,128)S(1)} %get-tuple-element.23.refs_1_), channel_id=1, source_target_pairs={{4,0},{8,4},{12,8},{14,12},{10,14},{6,10},{2,6},{0,2},{5,1},{9,5},... | collective-permute-start | bytes 393224 | tf_op jit(solution)/shard_map/ppermute | solution.py:315
  3.4 5.4 %collective-permute-start = (f32[1,16,2048]{2,1,0:T(8,128)S(1)}, f32[1,16,2048]{2,1,0:T(8,128)S(1)}, u32[]{:S(2)}, u32[]{:S(2)}) collective-permute-start(f32[1,16,2048]{2,1,0:T(8,128)S(1)} %get-tuple-element.21.refs_0_), channel_id=1, source_target_pairs={{0,4},{4,8},{8,12},{12,14},{14,10},{10,6},{6,2},{2,0},{1,5},{5,9},... | collective-permute-start | bytes 393224 | tf_op jit(solution)/shard_map/ppermute | solution.py:315
  3.5 6.0 %collective-permute-start.3 = (f32[1,16,2048]{2,1,0:T(8,128)S(1)}, f32[1,16,2048]{2,1,0:T(8,128)S(1)}, u32[]{:S(2)}, u32[]{:S(2)}) collective-permute-start(f32[1,16,2048]{2,1,0:T(8,128)S(1)} %get-tuple-element.21.refs_0_), channel_id=1, source_target_pairs={{4,0},{8,4},{12,8},{14,12},{10,14},{6,10},{2,6},{0,2},{5,1},{9,5},... | collective-permute-start | bytes 393224 | tf_op jit(solution)/shard_map/ppermute | solution.py:315
  4.9 5.7 %collective-permute-start.4 = (f32[1,16,2048]{2,1,0:T(8,128)S(1)}, f32[1,16,2048]{2,1,0:T(8,128)S(1)}, u32[]{:S(2)}, u32[]{:S(2)}) collective-permute-start(f32[1,16,2048]{2,1,0:T(8,128)S(1)} %get-tuple-element.23.refs_1_), channel_id=1, source_target_pairs={{0,4},{4,8},{8,12},{12,14},{14,10},{10,6},{6,2},{2,0},{1,5},{5,9},... | collective-permute-start | bytes 393224 | tf_op jit(solution)/shard_map/ppermute | solution.py:315
  7.2 5.1 %collective-permute-start.7 = (f32[1,16,2048]{2,1,0:T(8,128)S(1)}, f32[1,16,2048]{2,1,0:T(8,128)S(1)}, u32[]{:S(2)}, u32[]{:S(2)}) collective-permute-start(f32[1,16,2048]{2,1,0:T(8,128)S(1)} %collective-permute-done.2.refs_3_), channel_id=1, source_target_pairs={{4,0},{8,4},{12,8},{14,12},{10,14},{6,10},{2,6},{0,2},{5,1},{9,5},... | collective-permute-start | bytes 393224 | tf_op jit(solution)/shard_map/ppermute | solution.py:315
  8.8 4.8 %collective-permute-start.1 = (f32[1,16,2048]{2,1,0:T(8,128)S(1)}, f32[1,16,2048]{2,1,0:T(8,128)S(1)}, u32[]{:S(2)}, u32[]{:S(2)}) collective-permute-start(f32[1,16,2048]{2,1,0:T(8,128)S(1)} %collective-permute-done.refs_2_), channel_id=1, source_target_pairs={{0,4},{4,8},{8,12},{12,14},{14,10},{10,6},{6,2},{2,0},{1,5},{5,9},... | collective-permute-start | bytes 393224 | tf_op jit(solution)/shard_map/ppermute | solution.py:315
  9.5 5.5 %collective-permute-start.11 = (f32[1,16,2048]{2,1,0:T(8,128)S(1)}, f32[1,16,2048]{2,1,0:T(8,128)S(1)}, u32[]{:S(2)}, u32[]{:S(2)}) collective-permute-start(f32[1,16,2048]{2,1,0:T(8,128)S(1)} %collective-permute-done.3.refs_4_), channel_id=1, source_target_pairs={{4,0},{8,4},{12,8},{14,12},{10,14},{6,10},{2,6},{0,2},{5,1},{9,5},... | collective-permute-start | bytes 393224 | tf_op jit(solution)/shard_map/ppermute | solution.py:315
  10.6 5.2 %collective-permute-start.13 = (f32[1,16,2048]{2,1,0:T(8,128)S(1)}, f32[1,16,2048]{2,1,0:T(8,128)S(1)}, u32[]{:S(2)}, u32[]{:S(2)}) collective-permute-start(f32[1,16,2048]{2,1,0:T(8,128)S(1)} %collective-permute-done.4.refs_5_), channel_id=1, source_target_pairs={{0,4},{4,8},{8,12},{12,14},{14,10},{10,6},{6,2},{2,0},{1,5},{5,9},... | collective-permute-start | bytes 393224 | tf_op jit(solution)/shard_map/ppermute | solution.py:315
  12.3 5.3 %collective-permute-start.8 = (f32[1,16,2048]{2,1,0:T(8,128)S(1)}, f32[1,16,2048]{2,1,0:T(8,128)S(1)}, u32[]{:S(2)}, u32[]{:S(2)}) collective-permute-start(f32[1,16,2048]{2,1,0:T(8,128)S(1)} %collective-permute-done.7.refs_1_), channel_id=1, source_target_pairs={{4,0},{8,4},{12,8},{14,12},{10,14},{6,10},{2,6},{0,2},{5,1},{9,5},... | collective-permute-start | bytes 393224 | tf_op jit(solution)/shard_map/ppermute | solution.py:315
  13.6 5.3 %collective-permute-start.5 = (f32[1,16,2048]{2,1,0:T(8,128)S(1)}, f32[1,16,2048]{2,1,0:T(8,128)S(1)}, u32[]{:S(2)}, u32[]{:S(2)}) collective-permute-start(f32[1,16,2048]{2,1,0:T(8,128)S(1)} %collective-permute-done.1.refs_0_), channel_id=1, source_target_pairs={{0,4},{4,8},{8,12},{12,14},{14,10},{10,6},{6,2},{2,0},{1,5},{5,9},... | collective-permute-start | bytes 393224 | tf_op jit(solution)/shard_map/ppermute | solution.py:315
  15.0 5.5 %collective-permute-start.12 = (f32[1,16,2048]{2,1,0:T(8,128)S(1)}, f32[1,16,2048]{2,1,0:T(8,128)S(1)}, u32[]{:S(2)}, u32[]{:S(2)}) collective-permute-start(f32[1,16,2048]{2,1,0:T(8,128)S(1)} %collective-permute-done.11.refs_2_), channel_id=1, source_target_pairs={{4,0},{8,4},{12,8},{14,12},{10,14},{6,10},{2,6},{0,2},{5,1},{9,5},... | collective-permute-start | bytes 393224 | tf_op jit(solution)/shard_map/ppermute | solution.py:315
  15.7 4.9 %collective-permute-start.14 = (f32[1,16,2048]{2,1,0:T(8,128)S(1)}, f32[1,16,2048]{2,1,0:T(8,128)S(1)}, u32[]{:S(2)}, u32[]{:S(2)}) collective-permute-start(f32[1,16,2048]{2,1,0:T(8,128)S(1)} %collective-permute-done.13.refs_3_), channel_id=1, source_target_pairs={{0,4},{4,8},{8,12},{12,14},{14,10},{10,6},{6,2},{2,0},{1,5},{5,9},... | collective-permute-start | bytes 393224 | tf_op jit(solution)/shard_map/ppermute | solution.py:315
  17.6 8.3 %collective-permute-start.9 = (f32[1,16,2048]{2,1,0:T(8,128)S(1)}, f32[1,16,2048]{2,1,0:T(8,128)S(1)}, u32[]{:S(2)}, u32[]{:S(2)}) collective-permute-start(f32[1,16,2048]{2,1,0:T(8,128)S(1)} %collective-permute-done.8.refs_5_), channel_id=1, source_target_pairs={{4,0},{8,4},{12,8},{14,12},{10,14},{6,10},{2,6},{0,2},{5,1},{9,5},... | collective-permute-start | bytes 393224 | tf_op jit(solution)/shard_map/ppermute | solution.py:315
  18.9 6.9 %collective-permute-start.6 = (f32[1,16,2048]{2,1,0:T(8,128)S(1)}, f32[1,16,2048]{2,1,0:T(8,128)S(1)}, u32[]{:S(2)}, u32[]{:S(2)}) collective-permute-start(f32[1,16,2048]{2,1,0:T(8,128)S(1)} %collective-permute-done.5.refs_4_), channel_id=1, source_target_pairs={{0,4},{4,8},{8,12},{12,14},{14,10},{10,6},{6,2},{2,0},{1,5},{5,9},... | collective-permute-start | bytes 393224 | tf_op jit(solution)/shard_map/ppermute | solution.py:315
  21.7 6.6 %collective-permute-start.15 = (f32[2,64,1024]{2,1,0:T(8,128)S(1)}, f32[2,64,1024]{2,1,0:T(8,128)S(1)}, u32[]{:S(2)}, u32[]{:S(2)}) collective-permute-start(f32[2,64,1024]{2,1,0:T(8,128)S(1)} %get-tuple-element.34), channel_id=1, source_target_pairs={{0,1},{1,0},{2,3},{3,2},{4,5},{5,4},{6,7},{7,6},{8,9},{9,8},{10,11... | collective-permute-start | bytes 1572872 | tf_op jit(solution)/shard_map/ppermute | solution.py:335
  26.8 2.4 %collective-permute-start.10 = (f32[32,1024]{1,0:T(8,128)S(1)}, f32[32,1024]{1,0:T(8,128)S(1)}, u32[]{:S(2)}, u32[]{:S(2)}) collective-permute-start(f32[32,1024]{1,0:T(8,128)S(1)} %last.1), channel_id=1, source_target_pairs={{0,1},{1,0},{2,3},{3,2},{4,5},{5,4},{6,7},{7,6},{8,9},{9,8},{10,11... | collective-permute-start | bytes 393224 | tf_op jit(solution)/shard_map/ppermute | solution.py:355

commit v13 on v11

--- a/solution.py
+++ b/solution.py
@@ -59,16 +59,20 @@
     return jnp.where(start >= whole, start - whole, start)
 
 
-def cut_kernel(ab_tiles, cd_tiles, spans, amplitudes, labels_ab, labels_cd, labels_pattern, *refs):
-    outs, (listed, ab_irrep, cd_irrep, pattern, sems) = refs[:spans], refs[spans:]
-    pairs = [(labels_ab, ab_irrep), (labels_cd, cd_irrep), (labels_pattern, pattern)]
-    pairs += [(amplitudes.at[pl.ds(at, 1)], out) for at, out in enumerate(outs)]
+def cut_kernel(amplitudes, *refs):
+    *refs, sems = refs
+    labels, outs = refs[:3], refs[3:]
+    spans = len(outs) - 3
+    pairs = [(amplitudes.at[pl.ds(at, 1)], outs[at]) for at in range(spans)]
+    pairs += list(zip(labels, outs[spans:]))
     copies = [pltpu.make_async_copy(start, end, sems.at[at]) for at, (start, end) in enumerate(pairs)]
     for copy in copies:
         copy.start()
-    for copy in copies[:3]:
+    for copy in copies:
         copy.wait()
 
+
+def part_kernel(ab_tiles, cd_tiles, ab_irrep, cd_irrep, pattern, integrals, listed, split, near, landed, near_sem, sems):
     shape = (ab_tiles, LANES)
     lane = lax.broadcasted_iota(jnp.int32, shape, 1)
     line = lax.broadcasted_iota(jnp.int32, shape, 0)
@@ -103,13 +107,12 @@
     places = jnp.sum(passed, axis=0, keepdims=True)
     listed[0:1, :] = jnp.where(order[0:1, :] < found, places, 0.0).astype(jnp.int32)
     listed[1:2, :] = ((found + (UNROLL - 1)) * (1.0 / UNROLL)).astype(jnp.int32)
-    for copy in copies[3:]:
-        copy.wait()
-
-
-def part_kernel(cd_tiles, listed, integrals, split, landed, sems):
+    copy = pltpu.make_async_copy(listed, near, near_sem)
+    copy.start()
+    copy.wait()
+
     def fetch(k):
-        start, column = place_in(listed[0, k], cd_tiles)
+        start, column = place_in(near[0, k], cd_tiles)
         slot = lax.bitwise_and(k, FLIGHT - 1)
         return pltpu.make_async_copy(
             integrals.at[pl.ds(start, TILE), pl.ds(column, TILE)], landed.at[slot], sems.at[slot]
@@ -120,7 +123,7 @@
             fetch(round_at * UNROLL + unrolled).start()
         return carry
 
-    rounds = listed[1, 0]
+    rounds = near[1, 0]
     lax.fori_loop(0, jnp.minimum(rounds, AHEAD), begin, 0)
 
     def part(round_at, carry):
@@ -129,7 +132,7 @@
             fetch(first + unrolled).wait()
         for unrolled in range(UNROLL):
             k = first + unrolled
-            real = jnp.logical_or(k == 0, listed[0, k] > 0)
+            real = jnp.logical_or(k == 0, near[0, k] > 0)
             tile = jnp.where(real, landed[lax.bitwise_and(k, FLIGHT - 1)], 0.0).T
             upper = tile.astype(jnp.bfloat16)
             split[k, :, :TILE] = upper
@@ -251,30 +254,34 @@
         params = pltpu.CompilerParams(vmem_limit_bytes=VMEM_LIMIT)
         piece = pltpu.VMEM((1, rows, depth), jnp.float32)
 
-        *own, listed = pl.pallas_call(
-            functools.partial(cut_kernel, ab_tiles, cd_tiles, spans),
-            out_shape=(piece,) * spans + (pltpu.VMEM((2, LANES), jnp.int32),),
+        labels = (ab_irrep, cd_irrep, block_pattern)
+        *own, near_ab, near_cd, near_pattern = pl.pallas_call(
+            cut_kernel,
+            out_shape=(piece,) * spans + tuple(pltpu.VMEM(label.shape, label.dtype) for label in labels),
             in_specs=[hbm] * 4,
-            out_specs=(vmem,) * (spans + 1),
+            out_specs=(vmem,) * (spans + 3),
+            scratch_shapes=[pltpu.SemaphoreType.DMA((spans + 3,))],
+            compiler_params=params,
+            name="cut",
+        )(in_hbm(amplitudes), *map(in_hbm, labels))
+        listed, split = pl.pallas_call(
+            functools.partial(part_kernel, ab_tiles, cd_tiles),
+            out_shape=(
+                pltpu.VMEM((2, LANES), jnp.int32),
+                pltpu.VMEM((tiles, TILE, 2 * TILE), jnp.bfloat16),
+            ),
+            in_specs=[smem, smem, vmem, hbm],
+            out_specs=(vmem, vmem),
             scratch_shapes=[
-                pltpu.SMEM(ab_irrep.shape, jnp.int32),
-                pltpu.SMEM(cd_irrep.shape, jnp.int32),
-                pltpu.VMEM(block_pattern.shape, jnp.int32),
-                pltpu.SemaphoreType.DMA((spans + 3,)),
+                pltpu.SMEM((2, LANES), jnp.int32),
+                pltpu.VMEM((FLIGHT, TILE, TILE), jnp.float32),
+                pltpu.SemaphoreType.DMA,
+                pltpu.SemaphoreType.DMA((FLIGHT,)),
             ],
-            compiler_params=params,
-            name="cut",
-        )(*map(in_hbm, (amplitudes, ab_irrep, cd_irrep, block_pattern)))
-        split = pl.pallas_call(
-            functools.partial(part_kernel, cd_tiles),
-            out_shape=pltpu.VMEM((tiles, TILE, 2 * TILE), jnp.bfloat16),
-            in_specs=[smem, hbm],
-            out_specs=vmem,
-            scratch_shapes=[pltpu.VMEM((FLIGHT, TILE, TILE), jnp.float32), pltpu.SemaphoreType.DMA((FLIGHT,))],
             compiler_params=params,
             cost_estimate=pl.CostEstimate(flops=0, bytes_accessed=8 << 20, transcendentals=0),
             name="part",
-        )(listed, in_hbm(integrals))
+        )(near_ab, near_cd, near_pattern, in_hbm(integrals))
 
         block = pltpu.VMEM((spans, half, slab), jnp.float32)
 

time: 30.1 us -> 30.8 us (1.023)
  Pallas kernels: 9.66 us -> 11 us
  waiting for transfers between devices: 3.19 us -> 2.55 us
    pallas_call x2, Pallas kernels: 3.43 us -> 4.41 us  [the longest x1 3.4 us: shards(): pl.pallas_call(functools.partial(part_kernel, ab_tiles, cd_tiles), out_sh...]
    ppermute x14, waiting for transfers between devices: 3.08 us -> 2.43 us  [shards(): lax.ppermute(moved, 'ab', ahead if sign < 0 else back)]
  transfers between devices with their start and end apart: 16 -> 16, of which waited for: 5 -> 3; matrix products, arithmetic and copies ran while one was open for 0% -> 0% of each run, Pallas kernels for 26% -> 30%
where the time goes in v13:
time: 30.8 us; the launch traced here: 30.4 us
  starting transfers between devices  16.8 us (55%)
  Pallas kernels  11 us (36%)
  waiting for transfers between devices  2.55 us (8%)
    ppermute x14, starting transfers between devices, shards(): lax.ppermute(moved, 'ab', ahead if sign < 0 else back)  11.1 us
    ppermute x1, starting transfers between devices, shards(): lax.ppermute(send, 'cd', swap)  4.15 us
    pallas_call x3, Pallas kernels, step(): pl.pallas_call(functools.partial(step_kernel, count, rows, cd_tiles, grou...  3.98 us
    pallas_call x1, Pallas kernels, shards(): pl.pallas_call(functools.partial(part_kernel, ab_tiles, cd_tiles), out_sh...  3.4 us
    ppermute x14, waiting for transfers between devices, shards(): lax.ppermute(moved, 'ab', ahead if sign < 0 else back)  2.43 us
    ppermute x1, starting transfers between devices, shards(): lax.ppermute(last, 'cd', swap)  1.47 us
    pallas_call x1, Pallas kernels, shards(): pl.pallas_call(functools.partial(last_kernel, cd_tiles), out_shape=pltpu....  1.02 us
    pallas_call x1, Pallas kernels, shards(): pl.pallas_call(cut_kernel, out_shape=(piece,) * spans + tuple((pltpu.VMEM...  1.01 us
  transfers between devices with their start and end apart: 16, of which 3 were waited for; matrix products, arithmetic and copies ran while one was open for 0% of the time, Pallas kernels for 30%

profile of v13, /device:TPU:1, one launch (start us, length us, event | category | flops | bytes accessed | tf_op | source)
XLA Modules:
  0.0 30.4 jit_solution(13424546286828857466)
XLA Ops:
  0.0 1.0 %cut.1 = (f32[1,16,2048]{2,1,0:T(8,128)S(1)}, f32[1,16,2048]{2,1,0:T(8,128)S(1)}, s32[8]{0:T(128)S(1)}, s32[16]{0:T(128)S(1)}, s32[8,16]{1,0:T(8,128)S(1)}) custom-call(f32[2,16,2048]{2,1,0:T(8,128)} %amplitudes.1, s32[8]{0:T(128)} %refs_0_.1, s32[16]{0:T(128)} %refs_1_.1, s32[8,16]{1,0:T(8,128)} %refs_2_.1), custom_call_target="tpu_custom_call" | custom-call | tf_op jit(solution)/shard_map/cut/pallas_call | solution.py:258
  1.0 2.1 %collective-permute-start.2 = (f32[1,16,2048]{2,1,0:T(8,128)S(1)}, f32[1,16,2048]{2,1,0:T(8,128)S(1)}, u32[]{:S(2)}, u32[]{:S(2)}) collective-permute-start(f32[1,16,2048]{2,1,0:T(8,128)S(1)} %get-tuple-element.31.refs_1_), channel_id=1, source_target_pairs={{4,0},{8,4},{12,8},{14,12},{10,14},{6,10},{2,6},{0,2},{5,1},{9,5},... | collective-permute-start | bytes 393224 | tf_op jit(solution)/shard_map/ppermute | solution.py:315
  3.1 0.1 collective-permute-start
  3.3 1.3 %collective-permute-start.3 = (f32[1,16,2048]{2,1,0:T(8,128)S(1)}, f32[1,16,2048]{2,1,0:T(8,128)S(1)}, u32[]{:S(2)}, u32[]{:S(2)}) collective-permute-start(f32[1,16,2048]{2,1,0:T(8,128)S(1)} %get-tuple-element.29.refs_0_), channel_id=1, source_target_pairs={{4,0},{8,4},{12,8},{14,12},{10,14},{6,10},{2,6},{0,2},{5,1},{9,5},... | collective-permute-start | bytes 393224 | tf_op jit(solution)/shard_map/ppermute | solution.py:315
  4.6 0.1 collective-permute-start.4
  4.7 3.4 %part.1 = (s32[2,128]{1,0:T(2,128)S(1)}, bf16[128,128,256]{2,1,0:T(8,128)(2,1)S(1)}) custom-call(s32[8]{0:T(128)S(1)} %get-tuple-element.24.ab_irrep, s32[16]{0:T(128)S(1)} %get-tuple-element.25.cd_irrep, s32[8,16]{1,0:T(8,128)S(1)} %get-tuple-element.26.pattern, f32[1024,2048]{1,0:T(8,128)} %integrals.1), custom_call_target="tpu_custom_call" | custom-call | bytes 8388608 | tf_op jit(solution)/shard_map/part/pallas_call | solution.py:267
  8.1 0.0 collective-permute-done.2.refs_3_
  8.2 1.2 %collective-permute-start.7 = (f32[1,16,2048]{2,1,0:T(8,128)S(1)}, f32[1,16,2048]{2,1,0:T(8,128)S(1)}, u32[]{:S(2)}, u32[]{:S(2)}) collective-permute-start(f32[1,16,2048]{2,1,0:T(8,128)S(1)} %collective-permute-done.2.refs_3_), channel_id=1, source_target_pairs={{4,0},{8,4},{12,8},{14,12},{10,14},{6,10},{2,6},{0,2},{5,1},{9,5},... | collective-permute-start | bytes 393224 | tf_op jit(solution)/shard_map/ppermute | solution.py:315
  9.4 0.0 collective-permute-done.refs_2_
  9.4 0.3 collective-permute-start.1
  9.7 0.0 collective-permute-done.3.refs_4_
  9.7 1.2 %collective-permute-start.11 = (f32[1,16,2048]{2,1,0:T(8,128)S(1)}, f32[1,16,2048]{2,1,0:T(8,128)S(1)}, u32[]{:S(2)}, u32[]{:S(2)}) collective-permute-start(f32[1,16,2048]{2,1,0:T(8,128)S(1)} %collective-permute-done.3.refs_4_), channel_id=1, source_target_pairs={{4,0},{8,4},{12,8},{14,12},{10,14},{6,10},{2,6},{0,2},{5,1},{9,5},... | collective-permute-start | bytes 393224 | tf_op jit(solution)/shard_map/ppermute | solution.py:315
  10.9 0.0 collective-permute-done.4.refs_5_
  10.9 0.3 collective-permute-start.13
  11.1 1.4 %step.3 = (f32[2,64,1024]{2,1,0:T(8,128)S(1)}, f32[2,64,1024]{2,1,0:T(8,128)S(1)}) custom-call(s32[2,128]{1,0:T(2,128)S(1)} %get-tuple-element.27.listed, bf16[128,128,256]{2,1,0:T(8,128)(2,1)S(1)} %get-tuple-element.28.split, f32[1,16,2048]{2,1,0:T(8,128)S(1)} %get-tuple-element.29.refs_0_, f32[1,16,2048]{2,1,0:T(8,128)S(1)} %get-tuple-element.31.refs_1_, ...), custom_call_target="tpu_custom_call" | custom-call | flops 1073741824 | bytes 4194304 | tf_op jit(solution)/shard_map/step/pallas_call | solution.py:290
  12.6 0.0 collective-permute-done.7.refs_1_
  12.6 1.1 %collective-permute-start.8 = (f32[1,16,2048]{2,1,0:T(8,128)S(1)}, f32[1,16,2048]{2,1,0:T(8,128)S(1)}, u32[]{:S(2)}, u32[]{:S(2)}) collective-permute-start(f32[1,16,2048]{2,1,0:T(8,128)S(1)} %collective-permute-done.7.refs_1_), channel_id=1, source_target_pairs={{4,0},{8,4},{12,8},{14,12},{10,14},{6,10},{2,6},{0,2},{5,1},{9,5},... | collective-permute-start | bytes 393224 | tf_op jit(solution)/shard_map/ppermute | solution.py:315
  13.7 0.0 collective-permute-done.1.refs_0_
  13.7 0.4 %collective-permute-start.5 = (f32[1,16,2048]{2,1,0:T(8,128)S(1)}, f32[1,16,2048]{2,1,0:T(8,128)S(1)}, u32[]{:S(2)}, u32[]{:S(2)}) collective-permute-start(f32[1,16,2048]{2,1,0:T(8,128)S(1)} %collective-permute-done.1.refs_0_), channel_id=1, source_target_pairs={{0,4},{4,8},{8,12},{12,14},{14,10},{10,6},{6,2},{2,0},{1,5},{5,9},... | collective-permute-start | bytes 393224 | tf_op jit(solution)/shard_map/ppermute | solution.py:315
  14.1 0.7 %collective-permute-done.11.refs_2_ = f32[1,16,2048]{2,1,0:T(8,128)S(1)} collective-permute-done((f32[1,16,2048]{2,1,0:T(8,128)S(1)}, f32[1,16,2048]{2,1,0:T(8,128)S(1)}, u32[]{:S(2)}, u32[]{:S(2)}) %collective-permute-start.11) | collective-permute-done | bytes 131104 | tf_op jit(solution)/shard_map/ppermute | solution.py:315
  14.8 0.6 %collective-permute-start.12 = (f32[1,16,2048]{2,1,0:T(8,128)S(1)}, f32[1,16,2048]{2,1,0:T(8,128)S(1)}, u32[]{:S(2)}, u32[]{:S(2)}) collective-permute-start(f32[1,16,2048]{2,1,0:T(8,128)S(1)} %collective-permute-done.11.refs_2_), channel_id=1, source_target_pairs={{4,0},{8,4},{12,8},{14,12},{10,14},{6,10},{2,6},{0,2},{5,1},{9,5},... | collective-permute-start | bytes 393224 | tf_op jit(solution)/shard_map/ppermute | solution.py:315
  15.5 0.0 collective-permute-done.13.refs_3_
  15.5 0.8 %collective-permute-start.14 = (f32[1,16,2048]{2,1,0:T(8,128)S(1)}, f32[1,16,2048]{2,1,0:T(8,128)S(1)}, u32[]{:S(2)}, u32[]{:S(2)}) collective-permute-start(f32[1,16,2048]{2,1,0:T(8,128)S(1)} %collective-permute-done.13.refs_3_), channel_id=1, source_target_pairs={{0,4},{4,8},{8,12},{12,14},{14,10},{10,6},{6,2},{2,0},{1,5},{5,9},... | collective-permute-start | bytes 393224 | tf_op jit(solution)/shard_map/ppermute | solution.py:315
  16.3 1.7 %collective-permute-done.8.refs_5_ = f32[1,16,2048]{2,1,0:T(8,128)S(1)} collective-permute-done((f32[1,16,2048]{2,1,0:T(8,128)S(1)}, f32[1,16,2048]{2,1,0:T(8,128)S(1)}, u32[]{:S(2)}, u32[]{:S(2)}) %collective-permute-start.8) | collective-permute-done | bytes 131104 | tf_op jit(solution)/shard_map/ppermute | solution.py:315
  18.0 1.2 %collective-permute-start.9 = (f32[1,16,2048]{2,1,0:T(8,128)S(1)}, f32[1,16,2048]{2,1,0:T(8,128)S(1)}, u32[]{:S(2)}, u32[]{:S(2)}) collective-permute-start(f32[1,16,2048]{2,1,0:T(8,128)S(1)} %collective-permute-done.8.refs_5_), channel_id=1, source_target_pairs={{4,0},{8,4},{12,8},{14,12},{10,14},{6,10},{2,6},{0,2},{5,1},{9,5},... | collective-permute-start | bytes 393224 | tf_op jit(solution)/shard_map/ppermute | solution.py:315
  19.2 0.0 collective-permute-done.5.refs_4_
  19.2 0.3 %collective-permute-start.6 = (f32[1,16,2048]{2,1,0:T(8,128)S(1)}, f32[1,16,2048]{2,1,0:T(8,128)S(1)}, u32[]{:S(2)}, u32[]{:S(2)}) collective-permute-start(f32[1,16,2048]{2,1,0:T(8,128)S(1)} %collective-permute-done.5.refs_4_), channel_id=1, source_target_pairs={{0,4},{4,8},{8,12},{12,14},{14,10},{10,6},{6,2},{2,0},{1,5},{5,9},... | collective-permute-start | bytes 393224 | tf_op jit(solution)/shard_map/ppermute | solution.py:315
  19.5 1.4 %step.4 = (f32[2,64,1024]{2,1,0:T(8,128)S(1)}, f32[2,64,1024]{2,1,0:T(8,128)S(1)}) custom-call(s32[2,128]{1,0:T(2,128)S(1)} %get-tuple-element.27.listed, bf16[128,128,256]{2,1,0:T(8,128)(2,1)S(1)} %get-tuple-element.28.split, f32[1,16,2048]{2,1,0:T(8,128)S(1)} %collective-permute-done.1.refs_0_, ...), custom_call_target="tpu_custom_call", output_to_operand_aliasing={{0}: (8, {}), {1}: (9, {})} | custom-call | flops 1073741824 | bytes 4194304 | tf_op jit(solution)/shard_map/step/pallas_call | solution.py:290
  20.9 0.0 collective-permute-done.12.refs_0_
  20.9 0.0 collective-permute-done.14.refs_1_
  21.0 1.1 %step.5 = (f32[2,64,1024]{2,1,0:T(8,128)S(1)}, f32[2,64,1024]{2,1,0:T(8,128)S(1)}) custom-call(s32[2,128]{1,0:T(2,128)S(1)} %get-tuple-element.27.listed, bf16[128,128,256]{2,1,0:T(8,128)(2,1)S(1)} %get-tuple-element.28.split, f32[1,16,2048]{2,1,0:T(8,128)S(1)} %collective-permute-done.12.refs_0_, ...), custom_call_target="tpu_custom_call", output_to_operand_aliasing={{0}: (4, {}), {1}: (5, {})} | custom-call | flops 1073741824 | bytes 4194304 | tf_op jit(solution)/shard_map/step/pallas_call | solution.py:290
  22.0 4.2 %collective-permute-start.15 = (f32[2,64,1024]{2,1,0:T(8,128)S(1)}, f32[2,64,1024]{2,1,0:T(8,128)S(1)}, u32[]{:S(2)}, u32[]{:S(2)}) collective-permute-start(f32[2,64,1024]{2,1,0:T(8,128)S(1)} %get-tuple-element.42), channel_id=1, source_target_pairs={{0,1},{1,0},{2,3},{3,2},{4,5},{5,4},{6,7},{7,6},{8,9},{9,8},{10,11... | collective-permute-start | bytes 1572872 | tf_op jit(solution)/shard_map/ppermute | solution.py:335
  26.2 0.0 collective-permute-done.9.refs_1_
  26.2 0.0 collective-permute-done.6.refs_0_
  26.2 1.0 %last.1 = f32[32,1024]{1,0:T(8,128)S(1)} custom-call(s32[2,128]{1,0:T(2,128)S(1)} %get-tuple-element.27.listed, bf16[128,128,256]{2,1,0:T(8,128)(2,1)S(1)} %get-tuple-element.28.split, f32[1,16,2048]{2,1,0:T(8,128)S(1)} %collective-permute-done.6.refs_0_, f32[1,16,2048]{2,1,0:T(8,128)S(1)} %collective-permute-done.9.refs_1_), custom_call_target="tpu_custom_call" | custom-call | flops 17179869184 | bytes 4194304 | tf_op jit(solution)/shard_map/last/pallas_call | solution.py:337
  27.2 1.5 %collective-permute-start.10 = (f32[32,1024]{1,0:T(8,128)S(1)}, f32[32,1024]{1,0:T(8,128)S(1)}, u32[]{:S(2)}, u32[]{:S(2)}) collective-permute-start(f32[32,1024]{1,0:T(8,128)S(1)} %last.1), channel_id=1, source_target_pairs={{0,1},{1,0},{2,3},{3,2},{4,5},{5,4},{6,7},{7,6},{8,9},{9,8},{10,11... | collective-permute-start | bytes 393224 | tf_op jit(solution)/shard_map/ppermute | solution.py:355
  28.7 0.0 collective-permute-done.15.received
  28.7 0.9 %merge.1.before = f32[2,64,1024]{2,1,0:T(8,128)} custom-call(f32[2,64,1024]{2,1,0:T(8,128)S(1)} %get-tuple-element.41.mine, f32[2,64,1024]{2,1,0:T(8,128)S(1)} %collective-permute-done.15.received), custom_call_target="tpu_custom_call" | custom-call | tf_op jit(solution)/shard_map/merge/pallas_call | solution.py:328
  29.6 0.1 collective-permute-done.10.received
  29.7 0.7 %final.1 = f32[2,64,1024]{2,1,0:T(8,128)} custom-call(f32[32,1024]{1,0:T(8,128)S(1)} %last.1, f32[32,1024]{1,0:T(8,128)S(1)} %collective-permute-done.10.received, f32[2,64,1024]{2,1,0:T(8,128)} %merge.1.before), custom_call_target="tpu_custom_call", output_to_operand_aliasing={{}: (2, {})} | custom-call | tf_op jit(solution)/shard_map/final/pallas_call | solution.py:346
Async XLA Ops:
  1.0 7.1 %collective-permute-start.2 = (f32[1,16,2048]{2,1,0:T(8,128)S(1)}, f32[1,16,2048]{2,1,0:T(8,128)S(1)}, u32[]{:S(2)}, u32[]{:S(2)}) collective-permute-start(f32[1,16,2048]{2,1,0:T(8,128)S(1)} %get-tuple-element.31.refs_1_), channel_id=1, source_target_pairs={{4,0},{8,4},{12,8},{14,12},{10,14},{6,10},{2,6},{0,2},{5,1},{9,5},... | collective-permute-start | bytes 393224 | tf_op jit(solution)/shard_map/ppermute | solution.py:315
  3.1 6.3 %collective-permute-start = (f32[1,16,2048]{2,1,0:T(8,128)S(1)}, f32[1,16,2048]{2,1,0:T(8,128)S(1)}, u32[]{:S(2)}, u32[]{:S(2)}) collective-permute-start(f32[1,16,2048]{2,1,0:T(8,128)S(1)} %get-tuple-element.29.refs_0_), channel_id=1, source_target_pairs={{0,4},{4,8},{8,12},{12,14},{14,10},{10,6},{6,2},{2,0},{1,5},{5,9},... | collective-permute-start | bytes 393224 | tf_op jit(solution)/shard_map/ppermute | solution.py:315
  3.3 6.4 %collective-permute-start.3 = (f32[1,16,2048]{2,1,0:T(8,128)S(1)}, f32[1,16,2048]{2,1,0:T(8,128)S(1)}, u32[]{:S(2)}, u32[]{:S(2)}) collective-permute-start(f32[1,16,2048]{2,1,0:T(8,128)S(1)} %get-tuple-element.29.refs_0_), channel_id=1, source_target_pairs={{4,0},{8,4},{12,8},{14,12},{10,14},{6,10},{2,6},{0,2},{5,1},{9,5},... | collective-permute-start | bytes 393224 | tf_op jit(solution)/shard_map/ppermute | solution.py:315
  4.6 6.3 %collective-permute-start.4 = (f32[1,16,2048]{2,1,0:T(8,128)S(1)}, f32[1,16,2048]{2,1,0:T(8,128)S(1)}, u32[]{:S(2)}, u32[]{:S(2)}) collective-permute-start(f32[1,16,2048]{2,1,0:T(8,128)S(1)} %get-tuple-element.31.refs_1_), channel_id=1, source_target_pairs={{0,4},{4,8},{8,12},{12,14},{14,10},{10,6},{6,2},{2,0},{1,5},{5,9},... | collective-permute-start | bytes 393224 | tf_op jit(solution)/shard_map/ppermute | solution.py:315
  8.2 4.5 %collective-permute-start.7 = (f32[1,16,2048]{2,1,0:T(8,128)S(1)}, f32[1,16,2048]{2,1,0:T(8,128)S(1)}, u32[]{:S(2)}, u32[]{:S(2)}) collective-permute-start(f32[1,16,2048]{2,1,0:T(8,128)S(1)} %collective-permute-done.2.refs_3_), channel_id=1, source_target_pairs={{4,0},{8,4},{12,8},{14,12},{10,14},{6,10},{2,6},{0,2},{5,1},{9,5},... | collective-permute-start | bytes 393224 | tf_op jit(solution)/shard_map/ppermute | solution.py:315
  9.4 4.3 %collective-permute-start.1 = (f32[1,16,2048]{2,1,0:T(8,128)S(1)}, f32[1,16,2048]{2,1,0:T(8,128)S(1)}, u32[]{:S(2)}, u32[]{:S(2)}) collective-permute-start(f32[1,16,2048]{2,1,0:T(8,128)S(1)} %collective-permute-done.refs_2_), channel_id=1, source_target_pairs={{0,4},{4,8},{8,12},{12,14},{14,10},{10,6},{6,2},{2,0},{1,5},{5,9},... | collective-permute-start | bytes 393224 | tf_op jit(solution)/shard_map/ppermute | solution.py:315
  9.7 5.2 %collective-permute-start.11 = (f32[1,16,2048]{2,1,0:T(8,128)S(1)}, f32[1,16,2048]{2,1,0:T(8,128)S(1)}, u32[]{:S(2)}, u32[]{:S(2)}) collective-permute-start(f32[1,16,2048]{2,1,0:T(8,128)S(1)} %collective-permute-done.3.refs_4_), channel_id=1, source_target_pairs={{4,0},{8,4},{12,8},{14,12},{10,14},{6,10},{2,6},{0,2},{5,1},{9,5},... | collective-permute-start | bytes 393224 | tf_op jit(solution)/shard_map/ppermute | solution.py:315
  10.9 4.6 %collective-permute-start.13 = (f32[1,16,2048]{2,1,0:T(8,128)S(1)}, f32[1,16,2048]{2,1,0:T(8,128)S(1)}, u32[]{:S(2)}, u32[]{:S(2)}) collective-permute-start(f32[1,16,2048]{2,1,0:T(8,128)S(1)} %collective-permute-done.4.refs_5_), channel_id=1, source_target_pairs={{0,4},{4,8},{8,12},{12,14},{14,10},{10,6},{6,2},{2,0},{1,5},{5,9},... | collective-permute-start | bytes 393224 | tf_op jit(solution)/shard_map/ppermute | solution.py:315
  12.6 5.4 %collective-permute-start.8 = (f32[1,16,2048]{2,1,0:T(8,128)S(1)}, f32[1,16,2048]{2,1,0:T(8,128)S(1)}, u32[]{:S(2)}, u32[]{:S(2)}) collective-permute-start(f32[1,16,2048]{2,1,0:T(8,128)S(1)} %collective-permute-done.7.refs_1_), channel_id=1, source_target_pairs={{4,0},{8,4},{12,8},{14,12},{10,14},{6,10},{2,6},{0,2},{5,1},{9,5},... | collective-permute-start | bytes 393224 | tf_op jit(solution)/shard_map/ppermute | solution.py:315
  13.7 5.4 %collective-permute-start.5 = (f32[1,16,2048]{2,1,0:T(8,128)S(1)}, f32[1,16,2048]{2,1,0:T(8,128)S(1)}, u32[]{:S(2)}, u32[]{:S(2)}) collective-permute-start(f32[1,16,2048]{2,1,0:T(8,128)S(1)} %collective-permute-done.1.refs_0_), channel_id=1, source_target_pairs={{0,4},{4,8},{8,12},{12,14},{14,10},{10,6},{6,2},{2,0},{1,5},{5,9},... | collective-permute-start | bytes 393224 | tf_op jit(solution)/shard_map/ppermute | solution.py:315
  14.8 6.1 %collective-permute-start.12 = (f32[1,16,2048]{2,1,0:T(8,128)S(1)}, f32[1,16,2048]{2,1,0:T(8,128)S(1)}, u32[]{:S(2)}, u32[]{:S(2)}) collective-permute-start(f32[1,16,2048]{2,1,0:T(8,128)S(1)} %collective-permute-done.11.refs_2_), channel_id=1, source_target_pairs={{4,0},{8,4},{12,8},{14,12},{10,14},{6,10},{2,6},{0,2},{5,1},{9,5},... | collective-permute-start | bytes 393224 | tf_op jit(solution)/shard_map/ppermute | solution.py:315
  15.5 5.5 %collective-permute-start.14 = (f32[1,16,2048]{2,1,0:T(8,128)S(1)}, f32[1,16,2048]{2,1,0:T(8,128)S(1)}, u32[]{:S(2)}, u32[]{:S(2)}) collective-permute-start(f32[1,16,2048]{2,1,0:T(8,128)S(1)} %collective-permute-done.13.refs_3_), channel_id=1, source_target_pairs={{0,4},{4,8},{8,12},{12,14},{14,10},{10,6},{6,2},{2,0},{1,5},{5,9},... | collective-permute-start | bytes 393224 | tf_op jit(solution)/shard_map/ppermute | solution.py:315
  18.0 8.2 %collective-permute-start.9 = (f32[1,16,2048]{2,1,0:T(8,128)S(1)}, f32[1,16,2048]{2,1,0:T(8,128)S(1)}, u32[]{:S(2)}, u32[]{:S(2)}) collective-permute-start(f32[1,16,2048]{2,1,0:T(8,128)S(1)} %collective-permute-done.8.refs_5_), channel_id=1, source_target_pairs={{4,0},{8,4},{12,8},{14,12},{10,14},{6,10},{2,6},{0,2},{5,1},{9,5},... | collective-permute-start | bytes 393224 | tf_op jit(solution)/shard_map/ppermute | solution.py:315
  19.2 7.0 %collective-permute-start.6 = (f32[1,16,2048]{2,1,0:T(8,128)S(1)}, f32[1,16,2048]{2,1,0:T(8,128)S(1)}, u32[]{:S(2)}, u32[]{:S(2)}) collective-permute-start(f32[1,16,2048]{2,1,0:T(8,128)S(1)} %collective-permute-done.5.refs_4_), channel_id=1, source_target_pairs={{0,4},{4,8},{8,12},{12,14},{14,10},{10,6},{6,2},{2,0},{1,5},{5,9},... | collective-permute-start | bytes 393224 | tf_op jit(solution)/shard_map/ppermute | solution.py:315
  22.0 6.7 %collective-permute-start.15 = (f32[2,64,1024]{2,1,0:T(8,128)S(1)}, f32[2,64,1024]{2,1,0:T(8,128)S(1)}, u32[]{:S(2)}, u32[]{:S(2)}) collective-permute-start(f32[2,64,1024]{2,1,0:T(8,128)S(1)} %get-tuple-element.42), channel_id=1, source_target_pairs={{0,1},{1,0},{2,3},{3,2},{4,5},{5,4},{6,7},{7,6},{8,9},{9,8},{10,11... | collective-permute-start | bytes 1572872 | tf_op jit(solution)/shard_map/ppermute | solution.py:335
  27.2 2.5 %collective-permute-start.10 = (f32[32,1024]{1,0:T(8,128)S(1)}, f32[32,1024]{1,0:T(8,128)S(1)}, u32[]{:S(2)}, u32[]{:S(2)}) collective-permute-start(f32[32,1024]{1,0:T(8,128)S(1)} %last.1), channel_id=1, source_target_pairs={{0,1},{1,0},{2,3},{3,2},{4,5},{5,4},{6,7},{7,6},{8,9},{9,8},{10,11... | collective-permute-start | bytes 393224 | tf_op jit(solution)/shard_map/ppermute | solution.py:355

commit v14 on v11

--- a/solution.py
+++ b/solution.py
@@ -64,8 +64,8 @@
     pairs = [(labels_ab, ab_irrep), (labels_cd, cd_irrep), (labels_pattern, pattern)]
     pairs += [(amplitudes.at[pl.ds(at, 1)], out) for at, out in enumerate(outs)]
     copies = [pltpu.make_async_copy(start, end, sems.at[at]) for at, (start, end) in enumerate(pairs)]
-    for copy in copies:
-        copy.start()
+    for at, copy in enumerate(copies):
+        copy.start(priority=at % 2)
     for copy in copies[:3]:
         copy.wait()
 
@@ -117,7 +117,7 @@
 
     def begin(round_at, carry):
         for unrolled in range(UNROLL):
-            fetch(round_at * UNROLL + unrolled).start()
+            fetch(round_at * UNROLL + unrolled).start(priority=unrolled % 2)
         return carry
 
     rounds = listed[1, 0]

time: 30.1 us -> 30.1 us (level)
  waiting for transfers between devices: 3.19 us -> 3.59 us
    ppermute x14, waiting for transfers between devices: 3.08 us -> 3.47 us  [shards(): lax.ppermute(moved, 'ab', ahead if sign < 0 else back)]
  transfers between devices with their start and end apart: 16 -> 16, of which waited for: 5 -> 6; matrix products, arithmetic and copies ran while one was open for 0% -> 0% of each run, Pallas kernels for 26% -> 26%
where the time goes in v14:
time: 30.1 us
  starting transfers between devices  16.6 us (55%)
  Pallas kernels  9.79 us (33%)
  waiting for transfers between devices  3.59 us (12%)
    ppermute x14, starting transfers between devices, shards(): lax.ppermute(moved, 'ab', ahead if sign < 0 else back)  11.1 us
    ppermute x1, starting transfers between devices, shards(): lax.ppermute(send, 'cd', swap)  4.27 us
    pallas_call x3, Pallas kernels, step(): pl.pallas_call(functools.partial(step_kernel, count, rows, cd_tiles, grou...  3.72 us
    ppermute x14, waiting for transfers between devices, shards(): lax.ppermute(moved, 'ab', ahead if sign < 0 else back)  3.47 us
    pallas_call x1, Pallas kernels, shards(): pl.pallas_call(functools.partial(part_kernel, cd_tiles), out_shape=pltpu....  2.35 us
    ppermute x1, starting transfers between devices, shards(): lax.ppermute(last, 'cd', swap)  1.27 us
    pallas_call x1, Pallas kernels, shards(): pl.pallas_call(functools.partial(cut_kernel, ab_tiles, cd_tiles, spans),...  1.2 us
    pallas_call x1, Pallas kernels, shards(): pl.pallas_call(functools.partial(last_kernel, cd_tiles), out_shape=pltpu....  0.97 us
  transfers between devices with their start and end apart: 16, of which 6 were waited for; matrix products, arithmetic and copies ran while one was open for 0% of the time, Pallas kernels for 26%

profile of v14, /device:TPU:1, one launch (start us, length us, event | category | flops | bytes accessed | tf_op | source)
XLA Modules:
  0.0 30.1 jit_solution(778269806456952534)
XLA Ops:
  0.0 1.2 %cut.1 = (f32[1,16,2048]{2,1,0:T(8,128)S(1)}, f32[1,16,2048]{2,1,0:T(8,128)S(1)}, s32[2,128]{1,0:T(2,128)S(1)}) custom-call(f32[2,16,2048]{2,1,0:T(8,128)} %amplitudes.1, s32[8]{0:T(128)} %labels_ab.1, s32[16]{0:T(128)} %labels_cd.1, s32[8,16]{1,0:T(8,128)} %labels_pattern.1), custom_call_target="tpu_custom_call" | custom-call | tf_op jit(solution)/shard_map/cut/pallas_call | solution.py:254
  1.2 2.1 %collective-permute-start.2 = (f32[1,16,2048]{2,1,0:T(8,128)S(1)}, f32[1,16,2048]{2,1,0:T(8,128)S(1)}, u32[]{:S(2)}, u32[]{:S(2)}) collective-permute-start(f32[1,16,2048]{2,1,0:T(8,128)S(1)} %get-tuple-element.23.refs_1_), channel_id=1, source_target_pairs={{4,0},{8,4},{12,8},{14,12},{10,14},{6,10},{2,6},{0,2},{5,1},{9,5},... | collective-permute-start | bytes 393224 | tf_op jit(solution)/shard_map/ppermute | solution.py:308
  3.3 0.1 collective-permute-start
  3.5 1.3 %collective-permute-start.3 = (f32[1,16,2048]{2,1,0:T(8,128)S(1)}, f32[1,16,2048]{2,1,0:T(8,128)S(1)}, u32[]{:S(2)}, u32[]{:S(2)}) collective-permute-start(f32[1,16,2048]{2,1,0:T(8,128)S(1)} %get-tuple-element.21.refs_0_), channel_id=1, source_target_pairs={{4,0},{8,4},{12,8},{14,12},{10,14},{6,10},{2,6},{0,2},{5,1},{9,5},... | collective-permute-start | bytes 393224 | tf_op jit(solution)/shard_map/ppermute | solution.py:308
  4.8 0.1 collective-permute-start.4
  4.9 2.4 %part.1.split = bf16[128,128,256]{2,1,0:T(8,128)(2,1)S(1)} custom-call(s32[2,128]{1,0:T(2,128)S(1)} %get-tuple-element.20.listed, f32[1024,2048]{1,0:T(8,128)} %integrals.1), custom_call_target="tpu_custom_call" | custom-call | bytes 8388608 | tf_op jit(solution)/shard_map/part/pallas_call | solution.py:268
  7.3 0.0 collective-permute-done.2.refs_3_
  7.3 1.6 %collective-permute-start.7 = (f32[1,16,2048]{2,1,0:T(8,128)S(1)}, f32[1,16,2048]{2,1,0:T(8,128)S(1)}, u32[]{:S(2)}, u32[]{:S(2)}) collective-permute-start(f32[1,16,2048]{2,1,0:T(8,128)S(1)} %collective-permute-done.2.refs_3_), channel_id=1, source_target_pairs={{4,0},{8,4},{12,8},{14,12},{10,14},{6,10},{2,6},{0,2},{5,1},{9,5},... | collective-permute-start | bytes 393224 | tf_op jit(solution)/shard_map/ppermute | solution.py:308
  8.9 0.0 collective-permute-done.refs_2_
  8.9 0.0 collective-permute-start.1
  8.9 0.5 %collective-permute-done.3.refs_4_ = f32[1,16,2048]{2,1,0:T(8,128)S(1)} collective-permute-done((f32[1,16,2048]{2,1,0:T(8,128)S(1)}, f32[1,16,2048]{2,1,0:T(8,128)S(1)}, u32[]{:S(2)}, u32[]{:S(2)}) %collective-permute-start.3) | collective-permute-done | bytes 131104 | tf_op jit(solution)/shard_map/ppermute | solution.py:308
  9.4 1.1 %collective-permute-start.11 = (f32[1,16,2048]{2,1,0:T(8,128)S(1)}, f32[1,16,2048]{2,1,0:T(8,128)S(1)}, u32[]{:S(2)}, u32[]{:S(2)}) collective-permute-start(f32[1,16,2048]{2,1,0:T(8,128)S(1)} %collective-permute-done.3.refs_4_), channel_id=1, source_target_pairs={{4,0},{8,4},{12,8},{14,12},{10,14},{6,10},{2,6},{0,2},{5,1},{9,5},... | collective-permute-start | bytes 393224 | tf_op jit(solution)/shard_map/ppermute | solution.py:308
  10.5 0.0 collective-permute-done.4.refs_5_
  10.5 0.4 %collective-permute-start.13 = (f32[1,16,2048]{2,1,0:T(8,128)S(1)}, f32[1,16,2048]{2,1,0:T(8,128)S(1)}, u32[]{:S(2)}, u32[]{:S(2)}) collective-permute-start(f32[1,16,2048]{2,1,0:T(8,128)S(1)} %collective-permute-done.4.refs_5_), channel_id=1, source_target_pairs={{0,4},{4,8},{8,12},{12,14},{14,10},{10,6},{6,2},{2,0},{1,5},{5,9},... | collective-permute-start | bytes 393224 | tf_op jit(solution)/shard_map/ppermute | solution.py:308
  10.9 1.3 %step.3 = (f32[2,64,1024]{2,1,0:T(8,128)S(1)}, f32[2,64,1024]{2,1,0:T(8,128)S(1)}) custom-call(s32[2,128]{1,0:T(2,128)S(1)} %get-tuple-element.20.listed, bf16[128,128,256]{2,1,0:T(8,128)(2,1)S(1)} %part.1.split, f32[1,16,2048]{2,1,0:T(8,128)S(1)} %get-tuple-element.21.refs_0_, f32[1,16,2048]{2,1,0:T(8,128)S(1)} %get-tuple-element.23.refs_1_, ...), custom_call_target="tpu_custom_call" | custom-call | flops 1073741824 | bytes 4194304 | tf_op jit(solution)/shard_map/step/pallas_call | solution.py:283
  12.2 0.0 collective-permute-done.7.refs_1_
  12.3 1.2 %collective-permute-start.8 = (f32[1,16,2048]{2,1,0:T(8,128)S(1)}, f32[1,16,2048]{2,1,0:T(8,128)S(1)}, u32[]{:S(2)}, u32[]{:S(2)}) collective-permute-start(f32[1,16,2048]{2,1,0:T(8,128)S(1)} %collective-permute-done.7.refs_1_), channel_id=1, source_target_pairs={{4,0},{8,4},{12,8},{14,12},{10,14},{6,10},{2,6},{0,2},{5,1},{9,5},... | collective-permute-start | bytes 393224 | tf_op jit(solution)/shard_map/ppermute | solution.py:308
  13.5 0.0 collective-permute-done.1.refs_0_
  13.5 0.3 collective-permute-start.5
  13.8 1.1 %collective-permute-done.11.refs_2_ = f32[1,16,2048]{2,1,0:T(8,128)S(1)} collective-permute-done((f32[1,16,2048]{2,1,0:T(8,128)S(1)}, f32[1,16,2048]{2,1,0:T(8,128)S(1)}, u32[]{:S(2)}, u32[]{:S(2)}) %collective-permute-start.11) | collective-permute-done | bytes 131104 | tf_op jit(solution)/shard_map/ppermute | solution.py:308
  14.8 0.6 %collective-permute-start.12 = (f32[1,16,2048]{2,1,0:T(8,128)S(1)}, f32[1,16,2048]{2,1,0:T(8,128)S(1)}, u32[]{:S(2)}, u32[]{:S(2)}) collective-permute-start(f32[1,16,2048]{2,1,0:T(8,128)S(1)} %collective-permute-done.11.refs_2_), channel_id=1, source_target_pairs={{4,0},{8,4},{12,8},{14,12},{10,14},{6,10},{2,6},{0,2},{5,1},{9,5},... | collective-permute-start | bytes 393224 | tf_op jit(solution)/shard_map/ppermute | solution.py:308
  15.4 0.0 collective-permute-done.13.refs_3_
  15.4 0.9 %collective-permute-start.14 = (f32[1,16,2048]{2,1,0:T(8,128)S(1)}, f32[1,16,2048]{2,1,0:T(8,128)S(1)}, u32[]{:S(2)}, u32[]{:S(2)}) collective-permute-start(f32[1,16,2048]{2,1,0:T(8,128)S(1)} %collective-permute-done.13.refs_3_), channel_id=1, source_target_pairs={{0,4},{4,8},{8,12},{12,14},{14,10},{10,6},{6,2},{2,0},{1,5},{5,9},... | collective-permute-start | bytes 393224 | tf_op jit(solution)/shard_map/ppermute | solution.py:308
  16.3 1.5 %collective-permute-done.8.refs_5_ = f32[1,16,2048]{2,1,0:T(8,128)S(1)} collective-permute-done((f32[1,16,2048]{2,1,0:T(8,128)S(1)}, f32[1,16,2048]{2,1,0:T(8,128)S(1)}, u32[]{:S(2)}, u32[]{:S(2)}) %collective-permute-start.8) | collective-permute-done | bytes 131104 | tf_op jit(solution)/shard_map/ppermute | solution.py:308
  17.8 1.1 %collective-permute-start.9 = (f32[1,16,2048]{2,1,0:T(8,128)S(1)}, f32[1,16,2048]{2,1,0:T(8,128)S(1)}, u32[]{:S(2)}, u32[]{:S(2)}) collective-permute-start(f32[1,16,2048]{2,1,0:T(8,128)S(1)} %collective-permute-done.8.refs_5_), channel_id=1, source_target_pairs={{4,0},{8,4},{12,8},{14,12},{10,14},{6,10},{2,6},{0,2},{5,1},{9,5},... | collective-permute-start | bytes 393224 | tf_op jit(solution)/shard_map/ppermute | solution.py:308
  18.8 0.2 collective-permute-done.5.refs_4_
  19.0 0.2 collective-permute-start.6
  19.2 1.3 %step.4 = (f32[2,64,1024]{2,1,0:T(8,128)S(1)}, f32[2,64,1024]{2,1,0:T(8,128)S(1)}) custom-call(s32[2,128]{1,0:T(2,128)S(1)} %get-tuple-element.20.listed, bf16[128,128,256]{2,1,0:T(8,128)(2,1)S(1)} %part.1.split, f32[1,16,2048]{2,1,0:T(8,128)S(1)} %collective-permute-done.1.refs_0_, ...), custom_call_target="tpu_custom_call", output_to_operand_aliasing={{0}: (8, {}), {1}: (9, {})} | custom-call | flops 1073741824 | bytes 4194304 | tf_op jit(solution)/shard_map/step/pallas_call | solution.py:283
  20.6 0.0 collective-permute-done.12.refs_0_
  20.6 0.3 collective-permute-done.14.refs_1_
  20.9 1.0 %step.5 = (f32[2,64,1024]{2,1,0:T(8,128)S(1)}, f32[2,64,1024]{2,1,0:T(8,128)S(1)}) custom-call(s32[2,128]{1,0:T(2,128)S(1)} %get-tuple-element.20.listed, bf16[128,128,256]{2,1,0:T(8,128)(2,1)S(1)} %part.1.split, f32[1,16,2048]{2,1,0:T(8,128)S(1)} %collective-permute-done.12.refs_0_, ...), custom_call_target="tpu_custom_call", output_to_operand_aliasing={{0}: (4, {}), {1}: (5, {})} | custom-call | flops 1073741824 | bytes 4194304 | tf_op jit(solution)/shard_map/step/pallas_call | solution.py:283
  21.9 4.3 %collective-permute-start.15 = (f32[2,64,1024]{2,1,0:T(8,128)S(1)}, f32[2,64,1024]{2,1,0:T(8,128)S(1)}, u32[]{:S(2)}, u32[]{:S(2)}) collective-permute-start(f32[2,64,1024]{2,1,0:T(8,128)S(1)} %get-tuple-element.34), channel_id=1, source_target_pairs={{0,1},{1,0},{2,3},{3,2},{4,5},{5,4},{6,7},{7,6},{8,9},{9,8},{10,11... | collective-permute-start | bytes 1572872 | tf_op jit(solution)/shard_map/ppermute | solution.py:328
  26.2 0.0 collective-permute-done.9.refs_1_
  26.2 0.0 collective-permute-done.6.refs_0_
  26.2 1.0 %last.1 = f32[32,1024]{1,0:T(8,128)S(1)} custom-call(s32[2,128]{1,0:T(2,128)S(1)} %get-tuple-element.20.listed, bf16[128,128,256]{2,1,0:T(8,128)(2,1)S(1)} %part.1.split, f32[1,16,2048]{2,1,0:T(8,128)S(1)} %collective-permute-done.6.refs_0_, f32[1,16,2048]{2,1,0:T(8,128)S(1)} %collective-permute-done.9.refs_1_), custom_call_target="tpu_custom_call" | custom-call | flops 17179869184 | bytes 4194304 | tf_op jit(solution)/shard_map/last/pallas_call | solution.py:330
  27.1 1.3 %collective-permute-start.10 = (f32[32,1024]{1,0:T(8,128)S(1)}, f32[32,1024]{1,0:T(8,128)S(1)}, u32[]{:S(2)}, u32[]{:S(2)}) collective-permute-start(f32[32,1024]{1,0:T(8,128)S(1)} %last.1), channel_id=1, source_target_pairs={{0,1},{1,0},{2,3},{3,2},{4,5},{5,4},{6,7},{7,6},{8,9},{9,8},{10,11... | collective-permute-start | bytes 393224 | tf_op jit(solution)/shard_map/ppermute | solution.py:348
  28.4 0.0 collective-permute-done.15.received
  28.4 0.9 %merge.1.before = f32[2,64,1024]{2,1,0:T(8,128)} custom-call(f32[2,64,1024]{2,1,0:T(8,128)S(1)} %get-tuple-element.33.mine, f32[2,64,1024]{2,1,0:T(8,128)S(1)} %collective-permute-done.15.received), custom_call_target="tpu_custom_call" | custom-call | tf_op jit(solution)/shard_map/merge/pallas_call | solution.py:321
  29.3 0.1 collective-permute-done.10.received
  29.4 0.7 %final.1 = f32[2,64,1024]{2,1,0:T(8,128)} custom-call(f32[32,1024]{1,0:T(8,128)S(1)} %last.1, f32[32,1024]{1,0:T(8,128)S(1)} %collective-permute-done.10.received, f32[2,64,1024]{2,1,0:T(8,128)} %merge.1.before), custom_call_target="tpu_custom_call", output_to_operand_aliasing={{}: (2, {})} | custom-call | tf_op jit(solution)/shard_map/final/pallas_call | solution.py:339
Async XLA Ops:
  1.2 6.1 %collective-permute-start.2 = (f32[1,16,2048]{2,1,0:T(8,128)S(1)}, f32[1,16,2048]{2,1,0:T(8,128)S(1)}, u32[]{:S(2)}, u32[]{:S(2)}) collective-permute-start(f32[1,16,2048]{2,1,0:T(8,128)S(1)} %get-tuple-element.23.refs_1_), channel_id=1, source_target_pairs={{4,0},{8,4},{12,8},{14,12},{10,14},{6,10},{2,6},{0,2},{5,1},{9,5},... | collective-permute-start | bytes 393224 | tf_op jit(solution)/shard_map/ppermute | solution.py:308
  3.3 5.6 %collective-permute-start = (f32[1,16,2048]{2,1,0:T(8,128)S(1)}, f32[1,16,2048]{2,1,0:T(8,128)S(1)}, u32[]{:S(2)}, u32[]{:S(2)}) collective-permute-start(f32[1,16,2048]{2,1,0:T(8,128)S(1)} %get-tuple-element.21.refs_0_), channel_id=1, source_target_pairs={{0,4},{4,8},{8,12},{12,14},{14,10},{10,6},{6,2},{2,0},{1,5},{5,9},... | collective-permute-start | bytes 393224 | tf_op jit(solution)/shard_map/ppermute | solution.py:308
  3.5 6.0 %collective-permute-start.3 = (f32[1,16,2048]{2,1,0:T(8,128)S(1)}, f32[1,16,2048]{2,1,0:T(8,128)S(1)}, u32[]{:S(2)}, u32[]{:S(2)}) collective-permute-start(f32[1,16,2048]{2,1,0:T(8,128)S(1)} %get-tuple-element.21.refs_0_), channel_id=1, source_target_pairs={{4,0},{8,4},{12,8},{14,12},{10,14},{6,10},{2,6},{0,2},{5,1},{9,5},... | collective-permute-start | bytes 393224 | tf_op jit(solution)/shard_map/ppermute | solution.py:308
  4.8 5.7 %collective-permute-start.4 = (f32[1,16,2048]{2,1,0:T(8,128)S(1)}, f32[1,16,2048]{2,1,0:T(8,128)S(1)}, u32[]{:S(2)}, u32[]{:S(2)}) collective-permute-start(f32[1,16,2048]{2,1,0:T(8,128)S(1)} %get-tuple-element.23.refs_1_), channel_id=1, source_target_pairs={{0,4},{4,8},{8,12},{12,14},{14,10},{10,6},{6,2},{2,0},{1,5},{5,9},... | collective-permute-start | bytes 393224 | tf_op jit(solution)/shard_map/ppermute | solution.py:308
  7.3 4.9 %collective-permute-start.7 = (f32[1,16,2048]{2,1,0:T(8,128)S(1)}, f32[1,16,2048]{2,1,0:T(8,128)S(1)}, u32[]{:S(2)}, u32[]{:S(2)}) collective-permute-start(f32[1,16,2048]{2,1,0:T(8,128)S(1)} %collective-permute-done.2.refs_3_), channel_id=1, source_target_pairs={{4,0},{8,4},{12,8},{14,12},{10,14},{6,10},{2,6},{0,2},{5,1},{9,5},... | collective-permute-start | bytes 393224 | tf_op jit(solution)/shard_map/ppermute | solution.py:308
  8.9 4.6 %collective-permute-start.1 = (f32[1,16,2048]{2,1,0:T(8,128)S(1)}, f32[1,16,2048]{2,1,0:T(8,128)S(1)}, u32[]{:S(2)}, u32[]{:S(2)}) collective-permute-start(f32[1,16,2048]{2,1,0:T(8,128)S(1)} %collective-permute-done.refs_2_), channel_id=1, source_target_pairs={{0,4},{4,8},{8,12},{12,14},{14,10},{10,6},{6,2},{2,0},{1,5},{5,9},... | collective-permute-start | bytes 393224 | tf_op jit(solution)/shard_map/ppermute | solution.py:308
  9.4 5.4 %collective-permute-start.11 = (f32[1,16,2048]{2,1,0:T(8,128)S(1)}, f32[1,16,2048]{2,1,0:T(8,128)S(1)}, u32[]{:S(2)}, u32[]{:S(2)}) collective-permute-start(f32[1,16,2048]{2,1,0:T(8,128)S(1)} %collective-permute-done.3.refs_4_), channel_id=1, source_target_pairs={{4,0},{8,4},{12,8},{14,12},{10,14},{6,10},{2,6},{0,2},{5,1},{9,5},... | collective-permute-start | bytes 393224 | tf_op jit(solution)/shard_map/ppermute | solution.py:308
  10.5 4.9 %collective-permute-start.13 = (f32[1,16,2048]{2,1,0:T(8,128)S(1)}, f32[1,16,2048]{2,1,0:T(8,128)S(1)}, u32[]{:S(2)}, u32[]{:S(2)}) collective-permute-start(f32[1,16,2048]{2,1,0:T(8,128)S(1)} %collective-permute-done.4.refs_5_), channel_id=1, source_target_pairs={{0,4},{4,8},{8,12},{12,14},{14,10},{10,6},{6,2},{2,0},{1,5},{5,9},... | collective-permute-start | bytes 393224 | tf_op jit(solution)/shard_map/ppermute | solution.py:308
  12.3 5.5 %collective-permute-start.8 = (f32[1,16,2048]{2,1,0:T(8,128)S(1)}, f32[1,16,2048]{2,1,0:T(8,128)S(1)}, u32[]{:S(2)}, u32[]{:S(2)}) collective-permute-start(f32[1,16,2048]{2,1,0:T(8,128)S(1)} %collective-permute-done.7.refs_1_), channel_id=1, source_target_pairs={{4,0},{8,4},{12,8},{14,12},{10,14},{6,10},{2,6},{0,2},{5,1},{9,5},... | collective-permute-start | bytes 393224 | tf_op jit(solution)/shard_map/ppermute | solution.py:308
  13.5 5.5 %collective-permute-start.5 = (f32[1,16,2048]{2,1,0:T(8,128)S(1)}, f32[1,16,2048]{2,1,0:T(8,128)S(1)}, u32[]{:S(2)}, u32[]{:S(2)}) collective-permute-start(f32[1,16,2048]{2,1,0:T(8,128)S(1)} %collective-permute-done.1.refs_0_), channel_id=1, source_target_pairs={{0,4},{4,8},{8,12},{12,14},{14,10},{10,6},{6,2},{2,0},{1,5},{5,9},... | collective-permute-start | bytes 393224 | tf_op jit(solution)/shard_map/ppermute | solution.py:308
  14.8 5.8 %collective-permute-start.12 = (f32[1,16,2048]{2,1,0:T(8,128)S(1)}, f32[1,16,2048]{2,1,0:T(8,128)S(1)}, u32[]{:S(2)}, u32[]{:S(2)}) collective-permute-start(f32[1,16,2048]{2,1,0:T(8,128)S(1)} %collective-permute-done.11.refs_2_), channel_id=1, source_target_pairs={{4,0},{8,4},{12,8},{14,12},{10,14},{6,10},{2,6},{0,2},{5,1},{9,5},... | collective-permute-start | bytes 393224 | tf_op jit(solution)/shard_map/ppermute | solution.py:308
  15.4 5.4 %collective-permute-start.14 = (f32[1,16,2048]{2,1,0:T(8,128)S(1)}, f32[1,16,2048]{2,1,0:T(8,128)S(1)}, u32[]{:S(2)}, u32[]{:S(2)}) collective-permute-start(f32[1,16,2048]{2,1,0:T(8,128)S(1)} %collective-permute-done.13.refs_3_), channel_id=1, source_target_pairs={{0,4},{4,8},{8,12},{12,14},{14,10},{10,6},{6,2},{2,0},{1,5},{5,9},... | collective-permute-start | bytes 393224 | tf_op jit(solution)/shard_map/ppermute | solution.py:308
  17.8 8.4 %collective-permute-start.9 = (f32[1,16,2048]{2,1,0:T(8,128)S(1)}, f32[1,16,2048]{2,1,0:T(8,128)S(1)}, u32[]{:S(2)}, u32[]{:S(2)}) collective-permute-start(f32[1,16,2048]{2,1,0:T(8,128)S(1)} %collective-permute-done.8.refs_5_), channel_id=1, source_target_pairs={{4,0},{8,4},{12,8},{14,12},{10,14},{6,10},{2,6},{0,2},{5,1},{9,5},... | collective-permute-start | bytes 393224 | tf_op jit(solution)/shard_map/ppermute | solution.py:308
  19.0 7.2 %collective-permute-start.6 = (f32[1,16,2048]{2,1,0:T(8,128)S(1)}, f32[1,16,2048]{2,1,0:T(8,128)S(1)}, u32[]{:S(2)}, u32[]{:S(2)}) collective-permute-start(f32[1,16,2048]{2,1,0:T(8,128)S(1)} %collective-permute-done.5.refs_4_), channel_id=1, source_target_pairs={{0,4},{4,8},{8,12},{12,14},{14,10},{10,6},{6,2},{2,0},{1,5},{5,9},... | collective-permute-start | bytes 393224 | tf_op jit(solution)/shard_map/ppermute | solution.py:308
  21.9 6.5 %collective-permute-start.15 = (f32[2,64,1024]{2,1,0:T(8,128)S(1)}, f32[2,64,1024]{2,1,0:T(8,128)S(1)}, u32[]{:S(2)}, u32[]{:S(2)}) collective-permute-start(f32[2,64,1024]{2,1,0:T(8,128)S(1)} %get-tuple-element.34), channel_id=1, source_target_pairs={{0,1},{1,0},{2,3},{3,2},{4,5},{5,4},{6,7},{7,6},{8,9},{9,8},{10,11... | collective-permute-start | bytes 1572872 | tf_op jit(solution)/shard_map/ppermute | solution.py:328
  27.1 2.3 %collective-permute-start.10 = (f32[32,1024]{1,0:T(8,128)S(1)}, f32[32,1024]{1,0:T(8,128)S(1)}, u32[]{:S(2)}, u32[]{:S(2)}) collective-permute-start(f32[32,1024]{1,0:T(8,128)S(1)} %last.1), channel_id=1, source_target_pairs={{0,1},{1,0},{2,3},{3,2},{4,5},{5,4},{6,7},{7,6},{8,9},{9,8},{10,11... | collective-permute-start | bytes 393224 | tf_op jit(solution)/shard_map/ppermute | solution.py:348

commit v15 on v11

--- a/solution.py
+++ b/solution.py
@@ -8,9 +8,9 @@
 from jax.sharding import PartitionSpec as P
 
 TILE = 128
-UNROLL = 4
+UNROLL = 8
 LANES = 128
-AHEAD = 8
+AHEAD = 4
 FLIGHT = AHEAD * UNROLL
 GROUP = 12
 STEP_FLOPS = 1 << 30

time: 30.1 us -> 30.2 us (level)
  transfers between devices with their start and end apart: 16 -> 16, of which waited for: 5 -> 4; matrix products, arithmetic and copies ran while one was open for 0% -> 0% of each run, Pallas kernels for 26% -> 26%
where the time goes in v15:
time: 30.2 us; the launch traced here: 29.9 us
  starting transfers between devices  17 us (56%)
  Pallas kernels  9.52 us (32%)
  waiting for transfers between devices  3.29 us (11%)
    ppermute x14, starting transfers between devices, shards(): lax.ppermute(moved, 'ab', ahead if sign < 0 else back)  11.1 us
    ppermute x1, starting transfers between devices, shards(): lax.ppermute(send, 'cd', swap)  4.36 us
    pallas_call x3, Pallas kernels, step(): pl.pallas_call(functools.partial(step_kernel, count, rows, cd_tiles, grou...  3.54 us
    ppermute x14, waiting for transfers between devices, shards(): lax.ppermute(moved, 'ab', ahead if sign < 0 else back)  3.17 us
    pallas_call x1, Pallas kernels, shards(): pl.pallas_call(functools.partial(part_kernel, cd_tiles), out_shape=pltpu....  2.36 us
    ppermute x1, starting transfers between devices, shards(): lax.ppermute(last, 'cd', swap)  1.52 us
    pallas_call x1, Pallas kernels, shards(): pl.pallas_call(functools.partial(cut_kernel, ab_tiles, cd_tiles, spans),...  1.2 us
    pallas_call x1, Pallas kernels, shards(): pl.pallas_call(functools.partial(last_kernel, cd_tiles), out_shape=pltpu....  0.87 us
  transfers between devices with their start and end apart: 16, of which 4 were waited for; matrix products, arithmetic and copies ran while one was open for 0% of the time, Pallas kernels for 26%

profile of v15, /device:TPU:1, one launch (start us, length us, event | category | flops | bytes accessed | tf_op | source)
XLA Modules:
  0.0 29.9 jit_solution(8921542896355838057)
XLA Ops:
  0.0 1.2 %cut.1 = (f32[1,16,2048]{2,1,0:T(8,128)S(1)}, f32[1,16,2048]{2,1,0:T(8,128)S(1)}, s32[2,128]{1,0:T(2,128)S(1)}) custom-call(f32[2,16,2048]{2,1,0:T(8,128)} %amplitudes.1, s32[8]{0:T(128)} %labels_ab.1, s32[16]{0:T(128)} %labels_cd.1, s32[8,16]{1,0:T(8,128)} %labels_pattern.1), custom_call_target="tpu_custom_call" | custom-call | tf_op jit(solution)/shard_map/cut/pallas_call | solution.py:254
  1.2 2.1 %collective-permute-start.2 = (f32[1,16,2048]{2,1,0:T(8,128)S(1)}, f32[1,16,2048]{2,1,0:T(8,128)S(1)}, u32[]{:S(2)}, u32[]{:S(2)}) collective-permute-start(f32[1,16,2048]{2,1,0:T(8,128)S(1)} %get-tuple-element.23.refs_1_), channel_id=1, source_target_pairs={{4,0},{8,4},{12,8},{14,12},{10,14},{6,10},{2,6},{0,2},{5,1},{9,5},... | collective-permute-start | bytes 393224 | tf_op jit(solution)/shard_map/ppermute | solution.py:308
  3.3 0.1 collective-permute-start
  3.5 1.3 %collective-permute-start.3 = (f32[1,16,2048]{2,1,0:T(8,128)S(1)}, f32[1,16,2048]{2,1,0:T(8,128)S(1)}, u32[]{:S(2)}, u32[]{:S(2)}) collective-permute-start(f32[1,16,2048]{2,1,0:T(8,128)S(1)} %get-tuple-element.21.refs_0_), channel_id=1, source_target_pairs={{4,0},{8,4},{12,8},{14,12},{10,14},{6,10},{2,6},{0,2},{5,1},{9,5},... | collective-permute-start | bytes 393224 | tf_op jit(solution)/shard_map/ppermute | solution.py:308
  4.8 0.1 collective-permute-start.4
  4.9 2.4 %part.1.split = bf16[128,128,256]{2,1,0:T(8,128)(2,1)S(1)} custom-call(s32[2,128]{1,0:T(2,128)S(1)} %get-tuple-element.20.listed, f32[1024,2048]{1,0:T(8,128)} %integrals.1), custom_call_target="tpu_custom_call" | custom-call | bytes 8388608 | tf_op jit(solution)/shard_map/part/pallas_call | solution.py:268
  7.3 0.0 collective-permute-done.2.refs_3_
  7.3 1.4 %collective-permute-start.7 = (f32[1,16,2048]{2,1,0:T(8,128)S(1)}, f32[1,16,2048]{2,1,0:T(8,128)S(1)}, u32[]{:S(2)}, u32[]{:S(2)}) collective-permute-start(f32[1,16,2048]{2,1,0:T(8,128)S(1)} %collective-permute-done.2.refs_3_), channel_id=1, source_target_pairs={{4,0},{8,4},{12,8},{14,12},{10,14},{6,10},{2,6},{0,2},{5,1},{9,5},... | collective-permute-start | bytes 393224 | tf_op jit(solution)/shard_map/ppermute | solution.py:308
  8.7 0.0 collective-permute-done.refs_2_
  8.7 0.1 collective-permute-start.1
  8.8 0.6 %collective-permute-done.3.refs_4_ = f32[1,16,2048]{2,1,0:T(8,128)S(1)} collective-permute-done((f32[1,16,2048]{2,1,0:T(8,128)S(1)}, f32[1,16,2048]{2,1,0:T(8,128)S(1)}, u32[]{:S(2)}, u32[]{:S(2)}) %collective-permute-start.3) | collective-permute-done | bytes 131104 | tf_op jit(solution)/shard_map/ppermute | solution.py:308
  9.4 1.1 %collective-permute-start.11 = (f32[1,16,2048]{2,1,0:T(8,128)S(1)}, f32[1,16,2048]{2,1,0:T(8,128)S(1)}, u32[]{:S(2)}, u32[]{:S(2)}) collective-permute-start(f32[1,16,2048]{2,1,0:T(8,128)S(1)} %collective-permute-done.3.refs_4_), channel_id=1, source_target_pairs={{4,0},{8,4},{12,8},{14,12},{10,14},{6,10},{2,6},{0,2},{5,1},{9,5},... | collective-permute-start | bytes 393224 | tf_op jit(solution)/shard_map/ppermute | solution.py:308
  10.5 0.0 collective-permute-done.4.refs_5_
  10.5 0.4 %collective-permute-start.13 = (f32[1,16,2048]{2,1,0:T(8,128)S(1)}, f32[1,16,2048]{2,1,0:T(8,128)S(1)}, u32[]{:S(2)}, u32[]{:S(2)}) collective-permute-start(f32[1,16,2048]{2,1,0:T(8,128)S(1)} %collective-permute-done.4.refs_5_), channel_id=1, source_target_pairs={{0,4},{4,8},{8,12},{12,14},{14,10},{10,6},{6,2},{2,0},{1,5},{5,9},... | collective-permute-start | bytes 393224 | tf_op jit(solution)/shard_map/ppermute | solution.py:308
  10.9 1.3 %step.3 = (f32[2,64,1024]{2,1,0:T(8,128)S(1)}, f32[2,64,1024]{2,1,0:T(8,128)S(1)}) custom-call(s32[2,128]{1,0:T(2,128)S(1)} %get-tuple-element.20.listed, bf16[128,128,256]{2,1,0:T(8,128)(2,1)S(1)} %part.1.split, f32[1,16,2048]{2,1,0:T(8,128)S(1)} %get-tuple-element.21.refs_0_, f32[1,16,2048]{2,1,0:T(8,128)S(1)} %get-tuple-element.23.refs_1_, ...), custom_call_target="tpu_custom_call" | custom-call | flops 1073741824 | bytes 4194304 | tf_op jit(solution)/shard_map/step/pallas_call | solution.py:283
  12.2 0.0 collective-permute-done.7.refs_1_
  12.2 1.1 %collective-permute-start.8 = (f32[1,16,2048]{2,1,0:T(8,128)S(1)}, f32[1,16,2048]{2,1,0:T(8,128)S(1)}, u32[]{:S(2)}, u32[]{:S(2)}) collective-permute-start(f32[1,16,2048]{2,1,0:T(8,128)S(1)} %collective-permute-done.7.refs_1_), channel_id=1, source_target_pairs={{4,0},{8,4},{12,8},{14,12},{10,14},{6,10},{2,6},{0,2},{5,1},{9,5},... | collective-permute-start | bytes 393224 | tf_op jit(solution)/shard_map/ppermute | solution.py:308
  13.3 0.0 collective-permute-done.1.refs_0_
  13.3 0.4 %collective-permute-start.5 = (f32[1,16,2048]{2,1,0:T(8,128)S(1)}, f32[1,16,2048]{2,1,0:T(8,128)S(1)}, u32[]{:S(2)}, u32[]{:S(2)}) collective-permute-start(f32[1,16,2048]{2,1,0:T(8,128)S(1)} %collective-permute-done.1.refs_0_), channel_id=1, source_target_pairs={{0,4},{4,8},{8,12},{12,14},{14,10},{10,6},{6,2},{2,0},{1,5},{5,9},... | collective-permute-start | bytes 393224 | tf_op jit(solution)/shard_map/ppermute | solution.py:308
  13.7 1.1 %collective-permute-done.11.refs_2_ = f32[1,16,2048]{2,1,0:T(8,128)S(1)} collective-permute-done((f32[1,16,2048]{2,1,0:T(8,128)S(1)}, f32[1,16,2048]{2,1,0:T(8,128)S(1)}, u32[]{:S(2)}, u32[]{:S(2)}) %collective-permute-start.11) | collective-permute-done | bytes 131104 | tf_op jit(solution)/shard_map/ppermute | solution.py:308
  14.8 0.8 %collective-permute-start.12 = (f32[1,16,2048]{2,1,0:T(8,128)S(1)}, f32[1,16,2048]{2,1,0:T(8,128)S(1)}, u32[]{:S(2)}, u32[]{:S(2)}) collective-permute-start(f32[1,16,2048]{2,1,0:T(8,128)S(1)} %collective-permute-done.11.refs_2_), channel_id=1, source_target_pairs={{4,0},{8,4},{12,8},{14,12},{10,14},{6,10},{2,6},{0,2},{5,1},{9,5},... | collective-permute-start | bytes 393224 | tf_op jit(solution)/shard_map/ppermute | solution.py:308
  15.6 0.0 collective-permute-done.13.refs_3_
  15.6 0.6 %collective-permute-start.14 = (f32[1,16,2048]{2,1,0:T(8,128)S(1)}, f32[1,16,2048]{2,1,0:T(8,128)S(1)}, u32[]{:S(2)}, u32[]{:S(2)}) collective-permute-start(f32[1,16,2048]{2,1,0:T(8,128)S(1)} %collective-permute-done.13.refs_3_), channel_id=1, source_target_pairs={{0,4},{4,8},{8,12},{12,14},{14,10},{10,6},{6,2},{2,0},{1,5},{5,9},... | collective-permute-start | bytes 393224 | tf_op jit(solution)/shard_map/ppermute | solution.py:308
  16.3 1.5 %collective-permute-done.8.refs_5_ = f32[1,16,2048]{2,1,0:T(8,128)S(1)} collective-permute-done((f32[1,16,2048]{2,1,0:T(8,128)S(1)}, f32[1,16,2048]{2,1,0:T(8,128)S(1)}, u32[]{:S(2)}, u32[]{:S(2)}) %collective-permute-start.8) | collective-permute-done | bytes 131104 | tf_op jit(solution)/shard_map/ppermute | solution.py:308
  17.8 1.1 %collective-permute-start.9 = (f32[1,16,2048]{2,1,0:T(8,128)S(1)}, f32[1,16,2048]{2,1,0:T(8,128)S(1)}, u32[]{:S(2)}, u32[]{:S(2)}) collective-permute-start(f32[1,16,2048]{2,1,0:T(8,128)S(1)} %collective-permute-done.8.refs_5_), channel_id=1, source_target_pairs={{4,0},{8,4},{12,8},{14,12},{10,14},{6,10},{2,6},{0,2},{5,1},{9,5},... | collective-permute-start | bytes 393224 | tf_op jit(solution)/shard_map/ppermute | solution.py:308
  18.8 0.0 collective-permute-done.5.refs_4_
  18.8 0.4 %collective-permute-start.6 = (f32[1,16,2048]{2,1,0:T(8,128)S(1)}, f32[1,16,2048]{2,1,0:T(8,128)S(1)}, u32[]{:S(2)}, u32[]{:S(2)}) collective-permute-start(f32[1,16,2048]{2,1,0:T(8,128)S(1)} %collective-permute-done.5.refs_4_), channel_id=1, source_target_pairs={{0,4},{4,8},{8,12},{12,14},{14,10},{10,6},{6,2},{2,0},{1,5},{5,9},... | collective-permute-start | bytes 393224 | tf_op jit(solution)/shard_map/ppermute | solution.py:308
  19.2 1.3 %step.4 = (f32[2,64,1024]{2,1,0:T(8,128)S(1)}, f32[2,64,1024]{2,1,0:T(8,128)S(1)}) custom-call(s32[2,128]{1,0:T(2,128)S(1)} %get-tuple-element.20.listed, bf16[128,128,256]{2,1,0:T(8,128)(2,1)S(1)} %part.1.split, f32[1,16,2048]{2,1,0:T(8,128)S(1)} %collective-permute-done.1.refs_0_, ...), custom_call_target="tpu_custom_call", output_to_operand_aliasing={{0}: (8, {}), {1}: (9, {})} | custom-call | flops 1073741824 | bytes 4194304 | tf_op jit(solution)/shard_map/step/pallas_call | solution.py:283
  20.5 0.0 collective-permute-done.12.refs_0_
  20.5 0.0 collective-permute-done.14.refs_1_
  20.6 0.9 %step.5 = (f32[2,64,1024]{2,1,0:T(8,128)S(1)}, f32[2,64,1024]{2,1,0:T(8,128)S(1)}) custom-call(s32[2,128]{1,0:T(2,128)S(1)} %get-tuple-element.20.listed, bf16[128,128,256]{2,1,0:T(8,128)(2,1)S(1)} %part.1.split, f32[1,16,2048]{2,1,0:T(8,128)S(1)} %collective-permute-done.12.refs_0_, ...), custom_call_target="tpu_custom_call", output_to_operand_aliasing={{0}: (4, {}), {1}: (5, {})} | custom-call | flops 1073741824 | bytes 4194304 | tf_op jit(solution)/shard_map/step/pallas_call | solution.py:283
  21.5 4.4 %collective-permute-start.15 = (f32[2,64,1024]{2,1,0:T(8,128)S(1)}, f32[2,64,1024]{2,1,0:T(8,128)S(1)}, u32[]{:S(2)}, u32[]{:S(2)}) collective-permute-start(f32[2,64,1024]{2,1,0:T(8,128)S(1)} %get-tuple-element.34), channel_id=1, source_target_pairs={{0,1},{1,0},{2,3},{3,2},{4,5},{5,4},{6,7},{7,6},{8,9},{9,8},{10,11... | collective-permute-start | bytes 1572872 | tf_op jit(solution)/shard_map/ppermute | solution.py:328
  25.9 0.0 collective-permute-done.9.refs_1_
  25.9 0.0 collective-permute-done.6.refs_0_
  25.9 0.9 %last.1 = f32[32,1024]{1,0:T(8,128)S(1)} custom-call(s32[2,128]{1,0:T(2,128)S(1)} %get-tuple-element.20.listed, bf16[128,128,256]{2,1,0:T(8,128)(2,1)S(1)} %part.1.split, f32[1,16,2048]{2,1,0:T(8,128)S(1)} %collective-permute-done.6.refs_0_, f32[1,16,2048]{2,1,0:T(8,128)S(1)} %collective-permute-done.9.refs_1_), custom_call_target="tpu_custom_call" | custom-call | flops 17179869184 | bytes 4194304 | tf_op jit(solution)/shard_map/last/pallas_call | solution.py:330
  26.7 1.5 %collective-permute-start.10 = (f32[32,1024]{1,0:T(8,128)S(1)}, f32[32,1024]{1,0:T(8,128)S(1)}, u32[]{:S(2)}, u32[]{:S(2)}) collective-permute-start(f32[32,1024]{1,0:T(8,128)S(1)} %last.1), channel_id=1, source_target_pairs={{0,1},{1,0},{2,3},{3,2},{4,5},{5,4},{6,7},{7,6},{8,9},{9,8},{10,11... | collective-permute-start | bytes 393224 | tf_op jit(solution)/shard_map/ppermute | solution.py:348
  28.3 0.0 collective-permute-done.15.received
  28.3 0.9 %merge.1.before = f32[2,64,1024]{2,1,0:T(8,128)} custom-call(f32[2,64,1024]{2,1,0:T(8,128)S(1)} %get-tuple-element.33.mine, f32[2,64,1024]{2,1,0:T(8,128)S(1)} %collective-permute-done.15.received), custom_call_target="tpu_custom_call" | custom-call | tf_op jit(solution)/shard_map/merge/pallas_call | solution.py:321
  29.1 0.1 collective-permute-done.10.received
  29.3 0.7 %final.1 = f32[2,64,1024]{2,1,0:T(8,128)} custom-call(f32[32,1024]{1,0:T(8,128)S(1)} %last.1, f32[32,1024]{1,0:T(8,128)S(1)} %collective-permute-done.10.received, f32[2,64,1024]{2,1,0:T(8,128)} %merge.1.before), custom_call_target="tpu_custom_call", output_to_operand_aliasing={{}: (2, {})} | custom-call | tf_op jit(solution)/shard_map/final/pallas_call | solution.py:339
Async XLA Ops:
  1.2 6.1 %collective-permute-start.2 = (f32[1,16,2048]{2,1,0:T(8,128)S(1)}, f32[1,16,2048]{2,1,0:T(8,128)S(1)}, u32[]{:S(2)}, u32[]{:S(2)}) collective-permute-start(f32[1,16,2048]{2,1,0:T(8,128)S(1)} %get-tuple-element.23.refs_1_), channel_id=1, source_target_pairs={{4,0},{8,4},{12,8},{14,12},{10,14},{6,10},{2,6},{0,2},{5,1},{9,5},... | collective-permute-start | bytes 393224 | tf_op jit(solution)/shard_map/ppermute | solution.py:308
  3.3 5.4 %collective-permute-start = (f32[1,16,2048]{2,1,0:T(8,128)S(1)}, f32[1,16,2048]{2,1,0:T(8,128)S(1)}, u32[]{:S(2)}, u32[]{:S(2)}) collective-permute-start(f32[1,16,2048]{2,1,0:T(8,128)S(1)} %get-tuple-element.21.refs_0_), channel_id=1, source_target_pairs={{0,4},{4,8},{8,12},{12,14},{14,10},{10,6},{6,2},{2,0},{1,5},{5,9},... | collective-permute-start | bytes 393224 | tf_op jit(solution)/shard_map/ppermute | solution.py:308
  3.5 6.0 %collective-permute-start.3 = (f32[1,16,2048]{2,1,0:T(8,128)S(1)}, f32[1,16,2048]{2,1,0:T(8,128)S(1)}, u32[]{:S(2)}, u32[]{:S(2)}) collective-permute-start(f32[1,16,2048]{2,1,0:T(8,128)S(1)} %get-tuple-element.21.refs_0_), channel_id=1, source_target_pairs={{4,0},{8,4},{12,8},{14,12},{10,14},{6,10},{2,6},{0,2},{5,1},{9,5},... | collective-permute-start | bytes 393224 | tf_op jit(solution)/shard_map/ppermute | solution.py:308
  4.8 5.7 %collective-permute-start.4 = (f32[1,16,2048]{2,1,0:T(8,128)S(1)}, f32[1,16,2048]{2,1,0:T(8,128)S(1)}, u32[]{:S(2)}, u32[]{:S(2)}) collective-permute-start(f32[1,16,2048]{2,1,0:T(8,128)S(1)} %get-tuple-element.23.refs_1_), channel_id=1, source_target_pairs={{0,4},{4,8},{8,12},{12,14},{14,10},{10,6},{6,2},{2,0},{1,5},{5,9},... | collective-permute-start | bytes 393224 | tf_op jit(solution)/shard_map/ppermute | solution.py:308
  7.3 4.9 %collective-permute-start.7 = (f32[1,16,2048]{2,1,0:T(8,128)S(1)}, f32[1,16,2048]{2,1,0:T(8,128)S(1)}, u32[]{:S(2)}, u32[]{:S(2)}) collective-permute-start(f32[1,16,2048]{2,1,0:T(8,128)S(1)} %collective-permute-done.2.refs_3_), channel_id=1, source_target_pairs={{4,0},{8,4},{12,8},{14,12},{10,14},{6,10},{2,6},{0,2},{5,1},{9,5},... | collective-permute-start | bytes 393224 | tf_op jit(solution)/shard_map/ppermute | solution.py:308
  8.7 4.6 %collective-permute-start.1 = (f32[1,16,2048]{2,1,0:T(8,128)S(1)}, f32[1,16,2048]{2,1,0:T(8,128)S(1)}, u32[]{:S(2)}, u32[]{:S(2)}) collective-permute-start(f32[1,16,2048]{2,1,0:T(8,128)S(1)} %collective-permute-done.refs_2_), channel_id=1, source_target_pairs={{0,4},{4,8},{8,12},{12,14},{14,10},{10,6},{6,2},{2,0},{1,5},{5,9},... | collective-permute-start | bytes 393224 | tf_op jit(solution)/shard_map/ppermute | solution.py:308
  9.4 5.4 %collective-permute-start.11 = (f32[1,16,2048]{2,1,0:T(8,128)S(1)}, f32[1,16,2048]{2,1,0:T(8,128)S(1)}, u32[]{:S(2)}, u32[]{:S(2)}) collective-permute-start(f32[1,16,2048]{2,1,0:T(8,128)S(1)} %collective-permute-done.3.refs_4_), channel_id=1, source_target_pairs={{4,0},{8,4},{12,8},{14,12},{10,14},{6,10},{2,6},{0,2},{5,1},{9,5},... | collective-permute-start | bytes 393224 | tf_op jit(solution)/shard_map/ppermute | solution.py:308
  10.5 5.1 %collective-permute-start.13 = (f32[1,16,2048]{2,1,0:T(8,128)S(1)}, f32[1,16,2048]{2,1,0:T(8,128)S(1)}, u32[]{:S(2)}, u32[]{:S(2)}) collective-permute-start(f32[1,16,2048]{2,1,0:T(8,128)S(1)} %collective-permute-done.4.refs_5_), channel_id=1, source_target_pairs={{0,4},{4,8},{8,12},{12,14},{14,10},{10,6},{6,2},{2,0},{1,5},{5,9},... | collective-permute-start | bytes 393224 | tf_op jit(solution)/shard_map/ppermute | solution.py:308
  12.2 5.5 %collective-permute-start.8 = (f32[1,16,2048]{2,1,0:T(8,128)S(1)}, f32[1,16,2048]{2,1,0:T(8,128)S(1)}, u32[]{:S(2)}, u32[]{:S(2)}) collective-permute-start(f32[1,16,2048]{2,1,0:T(8,128)S(1)} %collective-permute-done.7.refs_1_), channel_id=1, source_target_pairs={{4,0},{8,4},{12,8},{14,12},{10,14},{6,10},{2,6},{0,2},{5,1},{9,5},... | collective-permute-start | bytes 393224 | tf_op jit(solution)/shard_map/ppermute | solution.py:308
  13.3 5.5 %collective-permute-start.5 = (f32[1,16,2048]{2,1,0:T(8,128)S(1)}, f32[1,16,2048]{2,1,0:T(8,128)S(1)}, u32[]{:S(2)}, u32[]{:S(2)}) collective-permute-start(f32[1,16,2048]{2,1,0:T(8,128)S(1)} %collective-permute-done.1.refs_0_), channel_id=1, source_target_pairs={{0,4},{4,8},{8,12},{12,14},{14,10},{10,6},{6,2},{2,0},{1,5},{5,9},... | collective-permute-start | bytes 393224 | tf_op jit(solution)/shard_map/ppermute | solution.py:308
  14.8 5.7 %collective-permute-start.12 = (f32[1,16,2048]{2,1,0:T(8,128)S(1)}, f32[1,16,2048]{2,1,0:T(8,128)S(1)}, u32[]{:S(2)}, u32[]{:S(2)}) collective-permute-start(f32[1,16,2048]{2,1,0:T(8,128)S(1)} %collective-permute-done.11.refs_2_), channel_id=1, source_target_pairs={{4,0},{8,4},{12,8},{14,12},{10,14},{6,10},{2,6},{0,2},{5,1},{9,5},... | collective-permute-start | bytes 393224 | tf_op jit(solution)/shard_map/ppermute | solution.py:308
  15.6 4.9 %collective-permute-start.14 = (f32[1,16,2048]{2,1,0:T(8,128)S(1)}, f32[1,16,2048]{2,1,0:T(8,128)S(1)}, u32[]{:S(2)}, u32[]{:S(2)}) collective-permute-start(f32[1,16,2048]{2,1,0:T(8,128)S(1)} %collective-permute-done.13.refs_3_), channel_id=1, source_target_pairs={{0,4},{4,8},{8,12},{12,14},{14,10},{10,6},{6,2},{2,0},{1,5},{5,9},... | collective-permute-start | bytes 393224 | tf_op jit(solution)/shard_map/ppermute | solution.py:308
  17.8 8.1 %collective-permute-start.9 = (f32[1,16,2048]{2,1,0:T(8,128)S(1)}, f32[1,16,2048]{2,1,0:T(8,128)S(1)}, u32[]{:S(2)}, u32[]{:S(2)}) collective-permute-start(f32[1,16,2048]{2,1,0:T(8,128)S(1)} %collective-permute-done.8.refs_5_), channel_id=1, source_target_pairs={{4,0},{8,4},{12,8},{14,12},{10,14},{6,10},{2,6},{0,2},{5,1},{9,5},... | collective-permute-start | bytes 393224 | tf_op jit(solution)/shard_map/ppermute | solution.py:308
  18.8 7.0 %collective-permute-start.6 = (f32[1,16,2048]{2,1,0:T(8,128)S(1)}, f32[1,16,2048]{2,1,0:T(8,128)S(1)}, u32[]{:S(2)}, u32[]{:S(2)}) collective-permute-start(f32[1,16,2048]{2,1,0:T(8,128)S(1)} %collective-permute-done.5.refs_4_), channel_id=1, source_target_pairs={{0,4},{4,8},{8,12},{12,14},{14,10},{10,6},{6,2},{2,0},{1,5},{5,9},... | collective-permute-start | bytes 393224 | tf_op jit(solution)/shard_map/ppermute | solution.py:308
  21.5 6.8 %collective-permute-start.15 = (f32[2,64,1024]{2,1,0:T(8,128)S(1)}, f32[2,64,1024]{2,1,0:T(8,128)S(1)}, u32[]{:S(2)}, u32[]{:S(2)}) collective-permute-start(f32[2,64,1024]{2,1,0:T(8,128)S(1)} %get-tuple-element.34), channel_id=1, source_target_pairs={{0,1},{1,0},{2,3},{3,2},{4,5},{5,4},{6,7},{7,6},{8,9},{9,8},{10,11... | collective-permute-start | bytes 1572872 | tf_op jit(solution)/shard_map/ppermute | solution.py:328
  26.7 2.5 %collective-permute-start.10 = (f32[32,1024]{1,0:T(8,128)S(1)}, f32[32,1024]{1,0:T(8,128)S(1)}, u32[]{:S(2)}, u32[]{:S(2)}) collective-permute-start(f32[32,1024]{1,0:T(8,128)S(1)} %last.1), channel_id=1, source_target_pairs={{0,1},{1,0},{2,3},{3,2},{4,5},{5,4},{6,7},{7,6},{8,9},{9,8},{10,11... | collective-permute-start | bytes 393224 | tf_op jit(solution)/shard_map/ppermute | solution.py:348

commit v16 on v11

--- a/solution.py
+++ b/solution.py
@@ -64,7 +64,7 @@
     pairs = [(labels_ab, ab_irrep), (labels_cd, cd_irrep), (labels_pattern, pattern)]
     pairs += [(amplitudes.at[pl.ds(at, 1)], out) for at, out in enumerate(outs)]
     copies = [pltpu.make_async_copy(start, end, sems.at[at]) for at, (start, end) in enumerate(pairs)]
-    for copy in copies:
+    for copy in reversed(copies):
         copy.start()
     for copy in copies[:3]:
         copy.wait()

time: 30.1 us -> 30.3 us (level)
  Pallas kernels: 9.66 us -> 10.3 us
  transfers between devices with their start and end apart: 16 -> 16, of which waited for: 5 -> 4; matrix products, arithmetic and copies ran while one was open for 0% -> 0% of each run, Pallas kernels for 26% -> 27%
where the time goes in v16:
time: 30.3 us; the launch traced here: 30.2 us
  starting transfers between devices  16.8 us (55%)
  Pallas kernels  10.3 us (34%)
  waiting for transfers between devices  2.99 us (10%)
    ppermute x14, starting transfers between devices, shards(): lax.ppermute(moved, 'ab', ahead if sign < 0 else back)  11.1 us
    ppermute x1, starting transfers between devices, shards(): lax.ppermute(send, 'cd', swap)  4.31 us
    pallas_call x3, Pallas kernels, step(): pl.pallas_call(functools.partial(step_kernel, count, rows, cd_tiles, grou...  3.99 us
    ppermute x14, waiting for transfers between devices, shards(): lax.ppermute(moved, 'ab', ahead if sign < 0 else back)  2.87 us
    pallas_call x1, Pallas kernels, shards(): pl.pallas_call(functools.partial(part_kernel, cd_tiles), out_shape=pltpu....  2.38 us
    ppermute x1, starting transfers between devices, shards(): lax.ppermute(last, 'cd', swap)  1.37 us
    pallas_call x1, Pallas kernels, shards(): pl.pallas_call(functools.partial(cut_kernel, ab_tiles, cd_tiles, spans),...  1.33 us
    pallas_call x1, Pallas kernels, shards(): pl.pallas_call(functools.partial(last_kernel, cd_tiles), out_shape=pltpu....  1.02 us
  transfers between devices with their start and end apart: 16, of which 4 were waited for; matrix products, arithmetic and copies ran while one was open for 0% of the time, Pallas kernels for 27%

profile of v16, /device:TPU:1, one launch (start us, length us, event | category | flops | bytes accessed | tf_op | source)
XLA Modules:
  0.0 30.2 jit_solution(10732647535263782192)
XLA Ops:
  0.0 1.3 %cut.1 = (f32[1,16,2048]{2,1,0:T(8,128)S(1)}, f32[1,16,2048]{2,1,0:T(8,128)S(1)}, s32[2,128]{1,0:T(2,128)S(1)}) custom-call(f32[2,16,2048]{2,1,0:T(8,128)} %amplitudes.1, s32[8]{0:T(128)} %labels_ab.1, s32[16]{0:T(128)} %labels_cd.1, s32[8,16]{1,0:T(8,128)} %labels_pattern.1), custom_call_target="tpu_custom_call" | custom-call | tf_op jit(solution)/shard_map/cut/pallas_call | solution.py:254
  1.3 2.1 %collective-permute-start.2 = (f32[1,16,2048]{2,1,0:T(8,128)S(1)}, f32[1,16,2048]{2,1,0:T(8,128)S(1)}, u32[]{:S(2)}, u32[]{:S(2)}) collective-permute-start(f32[1,16,2048]{2,1,0:T(8,128)S(1)} %get-tuple-element.23.refs_1_), channel_id=1, source_target_pairs={{4,0},{8,4},{12,8},{14,12},{10,14},{6,10},{2,6},{0,2},{5,1},{9,5},... | collective-permute-start | bytes 393224 | tf_op jit(solution)/shard_map/ppermute | solution.py:308
  3.5 0.1 collective-permute-start
  3.6 1.3 %collective-permute-start.3 = (f32[1,16,2048]{2,1,0:T(8,128)S(1)}, f32[1,16,2048]{2,1,0:T(8,128)S(1)}, u32[]{:S(2)}, u32[]{:S(2)}) collective-permute-start(f32[1,16,2048]{2,1,0:T(8,128)S(1)} %get-tuple-element.21.refs_0_), channel_id=1, source_target_pairs={{4,0},{8,4},{12,8},{14,12},{10,14},{6,10},{2,6},{0,2},{5,1},{9,5},... | collective-permute-start | bytes 393224 | tf_op jit(solution)/shard_map/ppermute | solution.py:308
  4.9 0.1 collective-permute-start.4
  5.1 2.4 %part.1.split = bf16[128,128,256]{2,1,0:T(8,128)(2,1)S(1)} custom-call(s32[2,128]{1,0:T(2,128)S(1)} %get-tuple-element.20.listed, f32[1024,2048]{1,0:T(8,128)} %integrals.1), custom_call_target="tpu_custom_call" | custom-call | bytes 8388608 | tf_op jit(solution)/shard_map/part/pallas_call | solution.py:268
  7.4 0.0 collective-permute-done.2.refs_3_
  7.4 1.2 %collective-permute-start.7 = (f32[1,16,2048]{2,1,0:T(8,128)S(1)}, f32[1,16,2048]{2,1,0:T(8,128)S(1)}, u32[]{:S(2)}, u32[]{:S(2)}) collective-permute-start(f32[1,16,2048]{2,1,0:T(8,128)S(1)} %collective-permute-done.2.refs_3_), channel_id=1, source_target_pairs={{4,0},{8,4},{12,8},{14,12},{10,14},{6,10},{2,6},{0,2},{5,1},{9,5},... | collective-permute-start | bytes 393224 | tf_op jit(solution)/shard_map/ppermute | solution.py:308
  8.7 0.0 collective-permute-done.refs_2_
  8.7 0.3 collective-permute-start.1
  9.0 0.6 %collective-permute-done.3.refs_4_ = f32[1,16,2048]{2,1,0:T(8,128)S(1)} collective-permute-done((f32[1,16,2048]{2,1,0:T(8,128)S(1)}, f32[1,16,2048]{2,1,0:T(8,128)S(1)}, u32[]{:S(2)}, u32[]{:S(2)}) %collective-permute-start.3) | collective-permute-done | bytes 131104 | tf_op jit(solution)/shard_map/ppermute | solution.py:308
  9.6 1.1 %collective-permute-start.11 = (f32[1,16,2048]{2,1,0:T(8,128)S(1)}, f32[1,16,2048]{2,1,0:T(8,128)S(1)}, u32[]{:S(2)}, u32[]{:S(2)}) collective-permute-start(f32[1,16,2048]{2,1,0:T(8,128)S(1)} %collective-permute-done.3.refs_4_), channel_id=1, source_target_pairs={{4,0},{8,4},{12,8},{14,12},{10,14},{6,10},{2,6},{0,2},{5,1},{9,5},... | collective-permute-start | bytes 393224 | tf_op jit(solution)/shard_map/ppermute | solution.py:308
  10.6 0.0 collective-permute-done.4.refs_5_
  10.6 0.4 %collective-permute-start.13 = (f32[1,16,2048]{2,1,0:T(8,128)S(1)}, f32[1,16,2048]{2,1,0:T(8,128)S(1)}, u32[]{:S(2)}, u32[]{:S(2)}) collective-permute-start(f32[1,16,2048]{2,1,0:T(8,128)S(1)} %collective-permute-done.4.refs_5_), channel_id=1, source_target_pairs={{0,4},{4,8},{8,12},{12,14},{14,10},{10,6},{6,2},{2,0},{1,5},{5,9},... | collective-permute-start | bytes 393224 | tf_op jit(solution)/shard_map/ppermute | solution.py:308
  11.0 1.4 %step.3 = (f32[2,64,1024]{2,1,0:T(8,128)S(1)}, f32[2,64,1024]{2,1,0:T(8,128)S(1)}) custom-call(s32[2,128]{1,0:T(2,128)S(1)} %get-tuple-element.20.listed, bf16[128,128,256]{2,1,0:T(8,128)(2,1)S(1)} %part.1.split, f32[1,16,2048]{2,1,0:T(8,128)S(1)} %get-tuple-element.21.refs_0_, f32[1,16,2048]{2,1,0:T(8,128)S(1)} %get-tuple-element.23.refs_1_, ...), custom_call_target="tpu_custom_call" | custom-call | flops 1073741824 | bytes 4194304 | tf_op jit(solution)/shard_map/step/pallas_call | solution.py:283
  12.5 0.0 collective-permute-done.7.refs_1_
  12.5 1.0 %collective-permute-start.8 = (f32[1,16,2048]{2,1,0:T(8,128)S(1)}, f32[1,16,2048]{2,1,0:T(8,128)S(1)}, u32[]{:S(2)}, u32[]{:S(2)}) collective-permute-start(f32[1,16,2048]{2,1,0:T(8,128)S(1)} %collective-permute-done.7.refs_1_), channel_id=1, source_target_pairs={{4,0},{8,4},{12,8},{14,12},{10,14},{6,10},{2,6},{0,2},{5,1},{9,5},... | collective-permute-start | bytes 393224 | tf_op jit(solution)/shard_map/ppermute | solution.py:308
  13.5 0.0 collective-permute-done.1.refs_0_
  13.5 0.5 %collective-permute-start.5 = (f32[1,16,2048]{2,1,0:T(8,128)S(1)}, f32[1,16,2048]{2,1,0:T(8,128)S(1)}, u32[]{:S(2)}, u32[]{:S(2)}) collective-permute-start(f32[1,16,2048]{2,1,0:T(8,128)S(1)} %collective-permute-done.1.refs_0_), channel_id=1, source_target_pairs={{0,4},{4,8},{8,12},{12,14},{14,10},{10,6},{6,2},{2,0},{1,5},{5,9},... | collective-permute-start | bytes 393224 | tf_op jit(solution)/shard_map/ppermute | solution.py:308
  14.0 1.1 %collective-permute-done.11.refs_2_ = f32[1,16,2048]{2,1,0:T(8,128)S(1)} collective-permute-done((f32[1,16,2048]{2,1,0:T(8,128)S(1)}, f32[1,16,2048]{2,1,0:T(8,128)S(1)}, u32[]{:S(2)}, u32[]{:S(2)}) %collective-permute-start.11) | collective-permute-done | bytes 131104 | tf_op jit(solution)/shard_map/ppermute | solution.py:308
  15.1 0.7 %collective-permute-start.12 = (f32[1,16,2048]{2,1,0:T(8,128)S(1)}, f32[1,16,2048]{2,1,0:T(8,128)S(1)}, u32[]{:S(2)}, u32[]{:S(2)}) collective-permute-start(f32[1,16,2048]{2,1,0:T(8,128)S(1)} %collective-permute-done.11.refs_2_), channel_id=1, source_target_pairs={{4,0},{8,4},{12,8},{14,12},{10,14},{6,10},{2,6},{0,2},{5,1},{9,5},... | collective-permute-start | bytes 393224 | tf_op jit(solution)/shard_map/ppermute | solution.py:308
  15.8 0.0 collective-permute-done.13.refs_3_
  15.8 0.7 %collective-permute-start.14 = (f32[1,16,2048]{2,1,0:T(8,128)S(1)}, f32[1,16,2048]{2,1,0:T(8,128)S(1)}, u32[]{:S(2)}, u32[]{:S(2)}) collective-permute-start(f32[1,16,2048]{2,1,0:T(8,128)S(1)} %collective-permute-done.13.refs_3_), channel_id=1, source_target_pairs={{0,4},{4,8},{8,12},{12,14},{14,10},{10,6},{6,2},{2,0},{1,5},{5,9},... | collective-permute-start | bytes 393224 | tf_op jit(solution)/shard_map/ppermute | solution.py:308
  16.5 1.2 %collective-permute-done.8.refs_5_ = f32[1,16,2048]{2,1,0:T(8,128)S(1)} collective-permute-done((f32[1,16,2048]{2,1,0:T(8,128)S(1)}, f32[1,16,2048]{2,1,0:T(8,128)S(1)}, u32[]{:S(2)}, u32[]{:S(2)}) %collective-permute-start.8) | collective-permute-done | bytes 131104 | tf_op jit(solution)/shard_map/ppermute | solution.py:308
  17.7 1.2 %collective-permute-start.9 = (f32[1,16,2048]{2,1,0:T(8,128)S(1)}, f32[1,16,2048]{2,1,0:T(8,128)S(1)}, u32[]{:S(2)}, u32[]{:S(2)}) collective-permute-start(f32[1,16,2048]{2,1,0:T(8,128)S(1)} %collective-permute-done.8.refs_5_), channel_id=1, source_target_pairs={{4,0},{8,4},{12,8},{14,12},{10,14},{6,10},{2,6},{0,2},{5,1},{9,5},... | collective-permute-start | bytes 393224 | tf_op jit(solution)/shard_map/ppermute | solution.py:308
  19.0 0.0 collective-permute-done.5.refs_4_
  19.0 0.2 collective-permute-start.6
  19.2 1.5 %step.4 = (f32[2,64,1024]{2,1,0:T(8,128)S(1)}, f32[2,64,1024]{2,1,0:T(8,128)S(1)}) custom-call(s32[2,128]{1,0:T(2,128)S(1)} %get-tuple-element.20.listed, bf16[128,128,256]{2,1,0:T(8,128)(2,1)S(1)} %part.1.split, f32[1,16,2048]{2,1,0:T(8,128)S(1)} %collective-permute-done.1.refs_0_, ...), custom_call_target="tpu_custom_call", output_to_operand_aliasing={{0}: (8, {}), {1}: (9, {})} | custom-call | flops 1073741824 | bytes 4194304 | tf_op jit(solution)/shard_map/step/pallas_call | solution.py:283
  20.7 0.0 collective-permute-done.12.refs_0_
  20.7 0.0 collective-permute-done.14.refs_1_
  20.7 1.1 %step.5 = (f32[2,64,1024]{2,1,0:T(8,128)S(1)}, f32[2,64,1024]{2,1,0:T(8,128)S(1)}) custom-call(s32[2,128]{1,0:T(2,128)S(1)} %get-tuple-element.20.listed, bf16[128,128,256]{2,1,0:T(8,128)(2,1)S(1)} %part.1.split, f32[1,16,2048]{2,1,0:T(8,128)S(1)} %collective-permute-done.12.refs_0_, ...), custom_call_target="tpu_custom_call", output_to_operand_aliasing={{0}: (4, {}), {1}: (5, {})} | custom-call | flops 1073741824 | bytes 4194304 | tf_op jit(solution)/shard_map/step/pallas_call | solution.py:283
  21.8 4.3 %collective-permute-start.15 = (f32[2,64,1024]{2,1,0:T(8,128)S(1)}, f32[2,64,1024]{2,1,0:T(8,128)S(1)}, u32[]{:S(2)}, u32[]{:S(2)}) collective-permute-start(f32[2,64,1024]{2,1,0:T(8,128)S(1)} %get-tuple-element.34), channel_id=1, source_target_pairs={{0,1},{1,0},{2,3},{3,2},{4,5},{5,4},{6,7},{7,6},{8,9},{9,8},{10,11... | collective-permute-start | bytes 1572872 | tf_op jit(solution)/shard_map/ppermute | solution.py:328
  26.1 0.0 collective-permute-done.9.refs_1_
  26.1 0.0 collective-permute-done.6.refs_0_
  26.1 1.0 %last.1 = f32[32,1024]{1,0:T(8,128)S(1)} custom-call(s32[2,128]{1,0:T(2,128)S(1)} %get-tuple-element.20.listed, bf16[128,128,256]{2,1,0:T(8,128)(2,1)S(1)} %part.1.split, f32[1,16,2048]{2,1,0:T(8,128)S(1)} %collective-permute-done.6.refs_0_, f32[1,16,2048]{2,1,0:T(8,128)S(1)} %collective-permute-done.9.refs_1_), custom_call_target="tpu_custom_call" | custom-call | flops 17179869184 | bytes 4194304 | tf_op jit(solution)/shard_map/last/pallas_call | solution.py:330
  27.1 1.4 %collective-permute-start.10 = (f32[32,1024]{1,0:T(8,128)S(1)}, f32[32,1024]{1,0:T(8,128)S(1)}, u32[]{:S(2)}, u32[]{:S(2)}) collective-permute-start(f32[32,1024]{1,0:T(8,128)S(1)} %last.1), channel_id=1, source_target_pairs={{0,1},{1,0},{2,3},{3,2},{4,5},{5,4},{6,7},{7,6},{8,9},{9,8},{10,11... | collective-permute-start | bytes 393224 | tf_op jit(solution)/shard_map/ppermute | solution.py:348
  28.5 0.0 collective-permute-done.15.received
  28.5 0.9 %merge.1.before = f32[2,64,1024]{2,1,0:T(8,128)} custom-call(f32[2,64,1024]{2,1,0:T(8,128)S(1)} %get-tuple-element.33.mine, f32[2,64,1024]{2,1,0:T(8,128)S(1)} %collective-permute-done.15.received), custom_call_target="tpu_custom_call" | custom-call | tf_op jit(solution)/shard_map/merge/pallas_call | solution.py:321
  29.4 0.1 collective-permute-done.10.received
  29.5 0.7 %final.1 = f32[2,64,1024]{2,1,0:T(8,128)} custom-call(f32[32,1024]{1,0:T(8,128)S(1)} %last.1, f32[32,1024]{1,0:T(8,128)S(1)} %collective-permute-done.10.received, f32[2,64,1024]{2,1,0:T(8,128)} %merge.1.before), custom_call_target="tpu_custom_call", output_to_operand_aliasing={{}: (2, {})} | custom-call | tf_op jit(solution)/shard_map/final/pallas_call | solution.py:339
Async XLA Ops:
  1.3 6.1 %collective-permute-start.2 = (f32[1,16,2048]{2,1,0:T(8,128)S(1)}, f32[1,16,2048]{2,1,0:T(8,128)S(1)}, u32[]{:S(2)}, u32[]{:S(2)}) collective-permute-start(f32[1,16,2048]{2,1,0:T(8,128)S(1)} %get-tuple-element.23.refs_1_), channel_id=1, source_target_pairs={{4,0},{8,4},{12,8},{14,12},{10,14},{6,10},{2,6},{0,2},{5,1},{9,5},... | collective-permute-start | bytes 393224 | tf_op jit(solution)/shard_map/ppermute | solution.py:308
  3.5 5.2 %collective-permute-start = (f32[1,16,2048]{2,1,0:T(8,128)S(1)}, f32[1,16,2048]{2,1,0:T(8,128)S(1)}, u32[]{:S(2)}, u32[]{:S(2)}) collective-permute-start(f32[1,16,2048]{2,1,0:T(8,128)S(1)} %get-tuple-element.21.refs_0_), channel_id=1, source_target_pairs={{0,4},{4,8},{8,12},{12,14},{14,10},{10,6},{6,2},{2,0},{1,5},{5,9},... | collective-permute-start | bytes 393224 | tf_op jit(solution)/shard_map/ppermute | solution.py:308
  3.6 6.0 %collective-permute-start.3 = (f32[1,16,2048]{2,1,0:T(8,128)S(1)}, f32[1,16,2048]{2,1,0:T(8,128)S(1)}, u32[]{:S(2)}, u32[]{:S(2)}) collective-permute-start(f32[1,16,2048]{2,1,0:T(8,128)S(1)} %get-tuple-element.21.refs_0_), channel_id=1, source_target_pairs={{4,0},{8,4},{12,8},{14,12},{10,14},{6,10},{2,6},{0,2},{5,1},{9,5},... | collective-permute-start | bytes 393224 | tf_op jit(solution)/shard_map/ppermute | solution.py:308
  4.9 5.7 %collective-permute-start.4 = (f32[1,16,2048]{2,1,0:T(8,128)S(1)}, f32[1,16,2048]{2,1,0:T(8,128)S(1)}, u32[]{:S(2)}, u32[]{:S(2)}) collective-permute-start(f32[1,16,2048]{2,1,0:T(8,128)S(1)} %get-tuple-element.23.refs_1_), channel_id=1, source_target_pairs={{0,4},{4,8},{8,12},{12,14},{14,10},{10,6},{6,2},{2,0},{1,5},{5,9},... | collective-permute-start | bytes 393224 | tf_op jit(solution)/shard_map/ppermute | solution.py:308
  7.4 5.0 %collective-permute-start.7 = (f32[1,16,2048]{2,1,0:T(8,128)S(1)}, f32[1,16,2048]{2,1,0:T(8,128)S(1)}, u32[]{:S(2)}, u32[]{:S(2)}) collective-permute-start(f32[1,16,2048]{2,1,0:T(8,128)S(1)} %collective-permute-done.2.refs_3_), channel_id=1, source_target_pairs={{4,0},{8,4},{12,8},{14,12},{10,14},{6,10},{2,6},{0,2},{5,1},{9,5},... | collective-permute-start | bytes 393224 | tf_op jit(solution)/shard_map/ppermute | solution.py:308
  8.7 4.8 %collective-permute-start.1 = (f32[1,16,2048]{2,1,0:T(8,128)S(1)}, f32[1,16,2048]{2,1,0:T(8,128)S(1)}, u32[]{:S(2)}, u32[]{:S(2)}) collective-permute-start(f32[1,16,2048]{2,1,0:T(8,128)S(1)} %collective-permute-done.refs_2_), channel_id=1, source_target_pairs={{0,4},{4,8},{8,12},{12,14},{14,10},{10,6},{6,2},{2,0},{1,5},{5,9},... | collective-permute-start | bytes 393224 | tf_op jit(solution)/shard_map/ppermute | solution.py:308
  9.6 5.5 %collective-permute-start.11 = (f32[1,16,2048]{2,1,0:T(8,128)S(1)}, f32[1,16,2048]{2,1,0:T(8,128)S(1)}, u32[]{:S(2)}, u32[]{:S(2)}) collective-permute-start(f32[1,16,2048]{2,1,0:T(8,128)S(1)} %collective-permute-done.3.refs_4_), channel_id=1, source_target_pairs={{4,0},{8,4},{12,8},{14,12},{10,14},{6,10},{2,6},{0,2},{5,1},{9,5},... | collective-permute-start | bytes 393224 | tf_op jit(solution)/shard_map/ppermute | solution.py:308
  10.6 5.2 %collective-permute-start.13 = (f32[1,16,2048]{2,1,0:T(8,128)S(1)}, f32[1,16,2048]{2,1,0:T(8,128)S(1)}, u32[]{:S(2)}, u32[]{:S(2)}) collective-permute-start(f32[1,16,2048]{2,1,0:T(8,128)S(1)} %collective-permute-done.4.refs_5_), channel_id=1, source_target_pairs={{0,4},{4,8},{8,12},{12,14},{14,10},{10,6},{6,2},{2,0},{1,5},{5,9},... | collective-permute-start | bytes 393224 | tf_op jit(solution)/shard_map/ppermute | solution.py:308
  12.5 5.3 %collective-permute-start.8 = (f32[1,16,2048]{2,1,0:T(8,128)S(1)}, f32[1,16,2048]{2,1,0:T(8,128)S(1)}, u32[]{:S(2)}, u32[]{:S(2)}) collective-permute-start(f32[1,16,2048]{2,1,0:T(8,128)S(1)} %collective-permute-done.7.refs_1_), channel_id=1, source_target_pairs={{4,0},{8,4},{12,8},{14,12},{10,14},{6,10},{2,6},{0,2},{5,1},{9,5},... | collective-permute-start | bytes 393224 | tf_op jit(solution)/shard_map/ppermute | solution.py:308
  13.5 5.5 %collective-permute-start.5 = (f32[1,16,2048]{2,1,0:T(8,128)S(1)}, f32[1,16,2048]{2,1,0:T(8,128)S(1)}, u32[]{:S(2)}, u32[]{:S(2)}) collective-permute-start(f32[1,16,2048]{2,1,0:T(8,128)S(1)} %collective-permute-done.1.refs_0_), channel_id=1, source_target_pairs={{0,4},{4,8},{8,12},{12,14},{14,10},{10,6},{6,2},{2,0},{1,5},{5,9},... | collective-permute-start | bytes 393224 | tf_op jit(solution)/shard_map/ppermute | solution.py:308
  15.1 5.6 %collective-permute-start.12 = (f32[1,16,2048]{2,1,0:T(8,128)S(1)}, f32[1,16,2048]{2,1,0:T(8,128)S(1)}, u32[]{:S(2)}, u32[]{:S(2)}) collective-permute-start(f32[1,16,2048]{2,1,0:T(8,128)S(1)} %collective-permute-done.11.refs_2_), channel_id=1, source_target_pairs={{4,0},{8,4},{12,8},{14,12},{10,14},{6,10},{2,6},{0,2},{5,1},{9,5},... | collective-permute-start | bytes 393224 | tf_op jit(solution)/shard_map/ppermute | solution.py:308
  15.8 4.9 %collective-permute-start.14 = (f32[1,16,2048]{2,1,0:T(8,128)S(1)}, f32[1,16,2048]{2,1,0:T(8,128)S(1)}, u32[]{:S(2)}, u32[]{:S(2)}) collective-permute-start(f32[1,16,2048]{2,1,0:T(8,128)S(1)} %collective-permute-done.13.refs_3_), channel_id=1, source_target_pairs={{0,4},{4,8},{8,12},{12,14},{14,10},{10,6},{6,2},{2,0},{1,5},{5,9},... | collective-permute-start | bytes 393224 | tf_op jit(solution)/shard_map/ppermute | solution.py:308
  17.7 8.4 %collective-permute-start.9 = (f32[1,16,2048]{2,1,0:T(8,128)S(1)}, f32[1,16,2048]{2,1,0:T(8,128)S(1)}, u32[]{:S(2)}, u32[]{:S(2)}) collective-permute-start(f32[1,16,2048]{2,1,0:T(8,128)S(1)} %collective-permute-done.8.refs_5_), channel_id=1, source_target_pairs={{4,0},{8,4},{12,8},{14,12},{10,14},{6,10},{2,6},{0,2},{5,1},{9,5},... | collective-permute-start | bytes 393224 | tf_op jit(solution)/shard_map/ppermute | solution.py:308
  19.0 7.1 %collective-permute-start.6 = (f32[1,16,2048]{2,1,0:T(8,128)S(1)}, f32[1,16,2048]{2,1,0:T(8,128)S(1)}, u32[]{:S(2)}, u32[]{:S(2)}) collective-permute-start(f32[1,16,2048]{2,1,0:T(8,128)S(1)} %collective-permute-done.5.refs_4_), channel_id=1, source_target_pairs={{0,4},{4,8},{8,12},{12,14},{14,10},{10,6},{6,2},{2,0},{1,5},{5,9},... | collective-permute-start | bytes 393224 | tf_op jit(solution)/shard_map/ppermute | solution.py:308
  21.8 6.7 %collective-permute-start.15 = (f32[2,64,1024]{2,1,0:T(8,128)S(1)}, f32[2,64,1024]{2,1,0:T(8,128)S(1)}, u32[]{:S(2)}, u32[]{:S(2)}) collective-permute-start(f32[2,64,1024]{2,1,0:T(8,128)S(1)} %get-tuple-element.34), channel_id=1, source_target_pairs={{0,1},{1,0},{2,3},{3,2},{4,5},{5,4},{6,7},{7,6},{8,9},{9,8},{10,11... | collective-permute-start | bytes 1572872 | tf_op jit(solution)/shard_map/ppermute | solution.py:328
  27.1 2.4 %collective-permute-start.10 = (f32[32,1024]{1,0:T(8,128)S(1)}, f32[32,1024]{1,0:T(8,128)S(1)}, u32[]{:S(2)}, u32[]{:S(2)}) collective-permute-start(f32[32,1024]{1,0:T(8,128)S(1)} %last.1), channel_id=1, source_target_pairs={{0,1},{1,0},{2,3},{3,2},{4,5},{5,4},{6,7},{7,6},{8,9},{9,8},{10,11... | collective-permute-start | bytes 393224 | tf_op jit(solution)/shard_map/ppermute | solution.py:348
